TPU v7x, 32 devices: a whole 2x2x4 slice. The times are simulated.
32 devices in a mesh: dp: 8 (over y, x, core), seq: 4 (over z).
Axes of the slice: x: 2, y: 2, z: 4, core: 2. Of those that a mesh axis runs over, the one named last changes fastest.
Arguments:
- tokens: bfloat16 [8, 1024, 2048], P('dp', 'seq'), may hold values from -6 to 6
- segments: int32 [8, 1024], P('dp'), may hold values from 0 to 3, as said below
- w_query: bfloat16 [2048, 2048], P(('dp', 'seq')), may hold values from -0.125 to 0.125
- w_key: bfloat16 [2048, 2048], P(('dp', 'seq')), may hold values from -0.125 to 0.125
- w_value: bfloat16 [2048, 2048], P(('dp', 'seq')), may hold values from -0.125 to 0.125
- w_out: bfloat16 [2048, 2048], P(('dp', 'seq')), may hold values from -0.125 to 0.125
- g_query: bfloat16 [2048], P(('dp', 'seq')), may hold values from 0.25 to 1.75
- g_key: bfloat16 [2048], P(('dp', 'seq')), may hold values from 0.25 to 1.75
- g_attn: bfloat16 [2048], P(('dp', 'seq')), may hold values from 0.5 to 1.5
- w_gate: bfloat16 [2048, 8192], P(('dp', 'seq')), may hold values from -0.125 to 0.125
- w_up: bfloat16 [2048, 8192], P(('dp', 'seq')), may hold values from -0.125 to 0.125
- w_down: bfloat16 [8192, 2048], P(('dp', 'seq')), may hold values from -0.0625 to 0.0625
- g_ffn: bfloat16 [2048], P(('dp', 'seq')), may hold values from 0.5 to 1.5
- d_out: bfloat16 [8, 1024, 2048], P('dp', 'seq'), may hold values from -6 to 6
Outputs:
- out: bfloat16 [8, 1024, 2048], P('dp', 'seq')
- d_tokens: float32 [8, 1024, 2048], P('dp', 'seq')
- d_w_query: float32 [2048, 2048], P(('dp', 'seq'))
- d_w_key: float32 [2048, 2048], P(('dp', 'seq'))
- d_w_value: float32 [2048, 2048], P(('dp', 'seq'))
- d_w_out: float32 [2048, 2048], P(('dp', 'seq'))
- d_g_query: float32 [2048], P(('dp', 'seq'))
- d_g_key: float32 [2048], P(('dp', 'seq'))
- d_g_attn: float32 [2048], P(('dp', 'seq'))
- d_w_gate: float32 [2048, 8192], P(('dp', 'seq'))
- d_w_up: float32 [2048, 8192], P(('dp', 'seq'))
- d_w_down: float32 [8192, 2048], P(('dp', 'seq'))
- d_g_ffn: float32 [2048], P(('dp', 'seq'))
Inputs may be any that keep to these rules, and one draw needn't show every extreme that they name: `segments`: each sequence packs 4 documents in order, numbered 0 to 3, each of 102 tokens or more.
All inputs are finite; a program needn't handle non-finite values.
Results may differ from a plain program's by a relative error of at most 0.023.
Values may be sent and summed in bfloat16 or wider, within the bound.
No kernel may reach another device: no remote copies, remote signals or barrier semaphores. Data moves between devices by JAX's collectives and lax.ppermute only.
A program may use at most 576 MiB of HBM per device.

v0:
```python
import jax
import jax.numpy as jnp
from jax import lax
from jax.sharding import PartitionSpec as P

H = 16
HD = 128
DOCS = 4


epsilon = 1e-06
rope_base = 500000.0
masked_score = -1e30


def shortened(x):
    return jax.tree.map(lambda a: a.astype(jnp.bfloat16) if a.dtype == jnp.float32 else a, x)


def product(left, right):
    return jnp.dot(left, right, preferred_element_type=jnp.float32)


def against(left, right):
    return lax.dot_general(
        left, right, (((1,), (1,)), ((), ())), preferred_element_type=jnp.float32
    )


def weight_grad(left, right):
    return lax.dot_general(
        left, right, (((0,), (0,)), ((), ())), preferred_element_type=jnp.float32
    )


def rms_scale(values):
    return lax.rsqrt(jnp.mean(values * values, -1, keepdims=True) + epsilon)


def norm_back(values, scale_rows, grad_vals):
    return scale_rows * grad_vals - values * scale_rows**3 * jnp.mean(
        grad_vals * values, -1, keepdims=True
    )


def positions(seg_ids):
    doc_ids = jnp.arange(DOCS, dtype=jnp.int32)
    one_hot = (seg_ids[..., None] == doc_ids).astype(jnp.int32)
    counts = jnp.sum(one_hot, axis=-2)
    starts = jnp.cumsum(counts, axis=-1) - counts
    token_start = jnp.sum(one_hot * starts[..., None, :], axis=-1)
    return jnp.arange(seg_ids.shape[-1], dtype=jnp.int32) - token_start


def rope_tables(position_ids):
    freqs = rope_base ** (-jnp.arange(HD // 2, dtype=jnp.float32) * 2.0 / HD)
    angles = position_ids.astype(jnp.float32)[..., None] * freqs
    cosine = jnp.cos(angles)
    sine_tab = jnp.sin(angles)
    return (
        jnp.concatenate([cosine, cosine], -1)[..., None, :],
        jnp.concatenate([sine_tab, sine_tab], -1)[..., None, :],
    )


def rotate(values):
    return jnp.concatenate([-values[..., HD // 2 :], values[..., : HD // 2]], -1)


def apply_rope(values, cosine, sine_tab):
    return values * cosine + rotate(values) * sine_tab


def rope_back(grad_vals, cosine, sine_tab):
    return grad_vals * cosine - rotate(grad_vals * sine_tab)


def mask_for(seg_ids, row_start, row_count):
    query_ids = row_start + jnp.arange(row_count)
    key_ids = jnp.arange(seg_ids.shape[0])
    same_doc = seg_ids[row_start : row_start + row_count, None] == seg_ids[None, :]
    return same_doc & (key_ids[None, :] <= query_ids[:, None])


def attend(query_vecs, key_vecs, value_vecs, seg_ids):
    length = query_vecs.shape[0]
    q_block = min(512, length)
    score_scale = HD ** (-0.5)
    outputs = []
    log_sums = []
    for row_start in range(0, length, q_block):
        q_part = query_vecs[row_start : row_start + q_block]
        scores = (
            jnp.einsum("qhd,khd->hqk", q_part, key_vecs, preferred_element_type=jnp.float32)
            * score_scale
        )
        scores = jnp.where(mask_for(seg_ids, row_start, q_block)[None], scores, masked_score)
        row_max = jnp.max(scores, -1, keepdims=True)
        expos = jnp.exp(scores - row_max)
        row_total = jnp.sum(expos, -1, keepdims=True)
        attn_probs = (expos / row_total).astype(jnp.bfloat16)
        block_out = jnp.einsum(
            "hqk,khd->qhd", attn_probs, value_vecs, preferred_element_type=jnp.float32
        )
        outputs.append(block_out.astype(jnp.bfloat16))
        log_sums.append((row_max + jnp.log(row_total))[..., 0])
    return (jnp.concatenate(outputs, 0), jnp.concatenate(log_sums, 1))


def attend_back(query_vecs, key_vecs, value_vecs, d_attended, seg_ids, log_totals):
    length = query_vecs.shape[0]
    q_block = min(512, length)
    score_scale = HD ** (-0.5)
    d_query_parts = []
    d_keys = jnp.zeros(key_vecs.shape, jnp.float32)
    d_values = jnp.zeros(value_vecs.shape, jnp.float32)
    for row_start in range(0, length, q_block):
        q_part = query_vecs[row_start : row_start + q_block]
        g_part = d_attended[row_start : row_start + q_block]
        scores = (
            jnp.einsum("qhd,khd->hqk", q_part, key_vecs, preferred_element_type=jnp.float32)
            * score_scale
        )
        scores = jnp.where(mask_for(seg_ids, row_start, q_block)[None], scores, masked_score)
        attn_probs = jnp.exp(scores - log_totals[:, row_start : row_start + q_block, None])
        d_probs = jnp.einsum("qhd,khd->hqk", g_part, value_vecs, preferred_element_type=jnp.float32)
        inner_sum = jnp.sum(attn_probs * d_probs, -1, keepdims=True)
        d_scores = (attn_probs * (d_probs - inner_sum)).astype(jnp.bfloat16)
        d_query_parts.append(
            jnp.einsum("hqk,khd->qhd", d_scores, key_vecs, preferred_element_type=jnp.float32)
            * score_scale
        )
        d_keys = (
            d_keys
            + jnp.einsum("hqk,qhd->khd", d_scores, q_part, preferred_element_type=jnp.float32)
            * score_scale
        )
        d_values = d_values + jnp.einsum(
            "hqk,qhd->khd",
            attn_probs.astype(jnp.bfloat16),
            g_part,
            preferred_element_type=jnp.float32,
        )
    d_query = jnp.concatenate(d_query_parts, 0)
    return (
        d_query.astype(jnp.bfloat16),
        d_keys.astype(jnp.bfloat16),
        d_values.astype(jnp.bfloat16),
    )


def local(
    tokens,
    segments,
    w_query,
    w_key,
    w_value,
    w_out,
    g_query,
    g_key,
    g_attn,
    w_gate,
    w_up,
    w_down,
    g_ffn,
    d_out,
):
    seq_count, local_len, model_width = tokens.shape
    row_count = seq_count * local_len
    head_shape = (seq_count, local_len, H, HD)
    tok_rows = tokens.reshape(row_count, model_width)
    attn_set = (
        lax.all_gather(w_query, ("dp", "seq"), axis=0, tiled=True),
        lax.all_gather(w_key, ("dp", "seq"), axis=0, tiled=True),
        lax.all_gather(w_value, ("dp", "seq"), axis=0, tiled=True),
        lax.all_gather(w_out, ("dp", "seq"), axis=0, tiled=True),
        lax.all_gather(g_query, ("dp", "seq"), axis=0, tiled=True),
        lax.all_gather(g_key, ("dp", "seq"), axis=0, tiled=True),
        lax.all_gather(g_attn, ("dp", "seq"), axis=0, tiled=True),
    )
    gain_query = attn_set[4].astype(jnp.float32)
    gain_key = attn_set[5].astype(jnp.float32)
    gain_attn = attn_set[6].astype(jnp.float32)
    q_raw = product(tok_rows, attn_set[0])
    k_raw = product(tok_rows, attn_set[1])
    v_raw = product(tok_rows, attn_set[2])
    q_scale = rms_scale(q_raw)
    k_scale = rms_scale(k_raw)
    all_pos = positions(segments)
    local_pos = lax.dynamic_slice_in_dim(all_pos, lax.axis_index("seq") * local_len, local_len, 1)
    cosine, sine_tab = rope_tables(local_pos)
    query_low = apply_rope(
        (q_raw * q_scale * gain_query).reshape(head_shape), cosine, sine_tab
    ).astype(jnp.bfloat16)
    key_low = apply_rope((k_raw * k_scale * gain_key).reshape(head_shape), cosine, sine_tab).astype(
        jnp.bfloat16
    )
    value_low = v_raw.astype(jnp.bfloat16).reshape(head_shape)
    query_heads, key_heads, value_heads = (
        lax.all_to_all(query_low, "seq", split_axis=2, concat_axis=1, tiled=True),
        lax.all_to_all(key_low, "seq", split_axis=2, concat_axis=1, tiled=True),
        lax.all_to_all(value_low, "seq", split_axis=2, concat_axis=1, tiled=True),
    )
    attended_heads, log_totals = lax.map(
        lambda seq_item: attend(seq_item[0], seq_item[1], seq_item[2], seq_item[3]),
        (query_heads, key_heads, value_heads, segments),
    )
    attended = jax.tree.map(
        lambda part, own: part.astype(own.dtype),
        lax.all_to_all(shortened(attended_heads), "seq", split_axis=1, concat_axis=2, tiled=True),
        attended_heads,
    ).reshape(row_count, model_width)
    a_proj = product(attended, attn_set[3])
    a_scale = rms_scale(a_proj)
    hidden = tok_rows.astype(jnp.float32) + a_proj * a_scale * gain_attn
    hidden_low = hidden.astype(jnp.bfloat16)
    mlp_set = (
        lax.all_gather(w_gate, ("dp", "seq"), axis=0, tiled=True),
        lax.all_gather(w_up, ("dp", "seq"), axis=0, tiled=True),
        lax.all_gather(w_down, ("dp", "seq"), axis=0, tiled=True),
        lax.all_gather(g_ffn, ("dp", "seq"), axis=0, tiled=True),
    )
    gain_ffn = mlp_set[3].astype(jnp.float32)
    gate_proj = product(hidden_low, mlp_set[0])
    up_proj = product(hidden_low, mlp_set[1])
    inner_act = (jax.nn.silu(gate_proj) * up_proj).astype(jnp.bfloat16)
    m_proj = product(inner_act, mlp_set[2])
    m_scale = rms_scale(m_proj)
    layer_out = (hidden + m_proj * m_scale * gain_ffn).astype(jnp.bfloat16).reshape(tokens.shape)
    grad_out = d_out.reshape(row_count, model_width).astype(jnp.float32)
    d_gain_ffn = jnp.sum(grad_out * m_proj * m_scale, 0)
    dm_low = norm_back(m_proj, m_scale, grad_out * gain_ffn).astype(jnp.bfloat16)
    d_inner = against(dm_low, mlp_set[2])
    sigmoid_gate = jax.nn.sigmoid(gate_proj)
    d_gate_low = (
        d_inner * up_proj * sigmoid_gate * (1.0 + gate_proj * (1.0 - sigmoid_gate))
    ).astype(jnp.bfloat16)
    d_up_low = (d_inner * jax.nn.silu(gate_proj)).astype(jnp.bfloat16)
    gateup_low = jnp.concatenate([d_gate_low, d_up_low], 1)
    d_hidden = grad_out + against(d_gate_low, mlp_set[0]) + against(d_up_low, mlp_set[1])
    d_gain_attn = jnp.sum(d_hidden * a_proj * a_scale, 0)
    da_low = norm_back(a_proj, a_scale, d_hidden * gain_attn).astype(jnp.bfloat16)
    d_attended = against(da_low, attn_set[3]).astype(jnp.bfloat16).reshape(head_shape)
    d_attended_heads = lax.all_to_all(d_attended, "seq", split_axis=2, concat_axis=1, tiled=True)
    dq_heads, dk_heads, dv_heads = lax.map(
        lambda seq_item: attend_back(
            seq_item[0], seq_item[1], seq_item[2], seq_item[3], seq_item[4], seq_item[5]
        ),
        (query_heads, key_heads, value_heads, d_attended_heads, segments, log_totals),
    )
    dq_back, dk_back, dv_back = (
        lax.all_to_all(shortened(dq_heads), "seq", split_axis=1, concat_axis=2, tiled=True).astype(
            dq_heads.dtype
        ),
        lax.all_to_all(shortened(dk_heads), "seq", split_axis=1, concat_axis=2, tiled=True).astype(
            dk_heads.dtype
        ),
        lax.all_to_all(shortened(dv_heads), "seq", split_axis=1, concat_axis=2, tiled=True).astype(
            dv_heads.dtype
        ),
    )
    dq_norm = rope_back(dq_back.astype(jnp.float32), cosine, sine_tab).reshape(
        row_count, model_width
    )
    dk_norm = rope_back(dk_back.astype(jnp.float32), cosine, sine_tab).reshape(
        row_count, model_width
    )
    d_gain_query = jnp.sum(dq_norm * q_raw * q_scale, 0)
    d_gain_key = jnp.sum(dk_norm * k_raw * k_scale, 0)
    dq_low = norm_back(q_raw, q_scale, dq_norm * gain_query).astype(jnp.bfloat16)
    dk_low = norm_back(k_raw, k_scale, dk_norm * gain_key).astype(jnp.bfloat16)
    dv_low = dv_back.reshape(row_count, model_width)
    d_inputs = (
        d_hidden
        + against(dq_low, attn_set[0])
        + against(dk_low, attn_set[1])
        + against(dv_low, attn_set[2])
    )
    qkv_low = jnp.concatenate([dq_low, dk_low, dv_low], 1)
    ff_width = inner_act.shape[1]
    replica_count = lax.axis_size("dp")
    down_part = lax.psum_scatter(
        weight_grad(inner_act, dm_low).astype(jnp.bfloat16), "dp", scatter_dimension=0, tiled=True
    )
    count = model_width // replica_count * lax.axis_size("dp")
    gateup_part, ffn_gain_part = jax.tree.map(
        lambda part: lax.psum_scatter(
            part.astype(jnp.bfloat16), "dp", scatter_dimension=0, tiled=True
        ).astype(jnp.float32),
        (
            weight_grad(lax.slice_in_dim(hidden_low, 0, count, axis=1), gateup_low),
            lax.slice_in_dim(d_gain_ffn, 0, count, axis=0),
        ),
    )
    count = model_width // replica_count * lax.axis_size("dp")
    qkv_part, out_part, query_gain_part, key_gain_part, attn_gain_part = jax.tree.map(
        lambda part: lax.psum_scatter(
            part.astype(jnp.bfloat16), "dp", scatter_dimension=0, tiled=True
        ).astype(jnp.float32),
        (
            weight_grad(tok_rows, qkv_low),
            weight_grad(lax.slice_in_dim(attended, 0, count, axis=1), da_low),
            d_gain_query,
            d_gain_key,
            lax.slice_in_dim(d_gain_attn, 0, count, axis=0),
        ),
    )
    (
        down_sum,
        gateup_sum,
        ffn_gain_sum,
        qkv_sum,
        out_sum,
        query_gain_sum,
        key_gain_sum,
        attn_gain_sum,
    ) = (
        lax.psum_scatter(down_part, "seq", scatter_dimension=0, tiled=True).astype(jnp.float32),
        lax.psum_scatter(
            gateup_part.astype(jnp.bfloat16), "seq", scatter_dimension=0, tiled=True
        ).astype(jnp.float32),
        lax.psum_scatter(
            ffn_gain_part.astype(jnp.bfloat16), "seq", scatter_dimension=0, tiled=True
        ).astype(jnp.float32),
        lax.psum_scatter(
            qkv_part.astype(jnp.bfloat16), "seq", scatter_dimension=0, tiled=True
        ).astype(jnp.float32),
        lax.psum_scatter(
            out_part.astype(jnp.bfloat16), "seq", scatter_dimension=0, tiled=True
        ).astype(jnp.float32),
        lax.psum_scatter(
            query_gain_part.astype(jnp.bfloat16), "seq", scatter_dimension=0, tiled=True
        ).astype(jnp.float32),
        lax.psum_scatter(
            key_gain_part.astype(jnp.bfloat16), "seq", scatter_dimension=0, tiled=True
        ).astype(jnp.float32),
        lax.psum_scatter(
            attn_gain_part.astype(jnp.bfloat16), "seq", scatter_dimension=0, tiled=True
        ).astype(jnp.float32),
    )
    return (
        layer_out,
        d_inputs.reshape(tokens.shape),
        qkv_sum[:, :model_width],
        qkv_sum[:, model_width : 2 * model_width],
        qkv_sum[:, 2 * model_width :],
        out_sum,
        query_gain_sum,
        key_gain_sum,
        attn_gain_sum,
        gateup_sum[:, :ff_width],
        gateup_sum[:, ff_width:],
        down_sum,
        ffn_gain_sum,
    )


def solution(mesh):
    in_specs = (
        P("dp", "seq", None),
        P("dp", None),
        P(("dp", "seq"), None),
        P(("dp", "seq"), None),
        P(("dp", "seq"), None),
        P(("dp", "seq"), None),
        P(("dp", "seq")),
        P(("dp", "seq")),
        P(("dp", "seq")),
        P(("dp", "seq"), None),
        P(("dp", "seq"), None),
        P(("dp", "seq"), None),
        P(("dp", "seq")),
        P("dp", "seq", None),
    )
    out_specs = (
        P("dp", "seq", None),
        P("dp", "seq", None),
        P(("dp", "seq"), None),
        P(("dp", "seq"), None),
        P(("dp", "seq"), None),
        P(("dp", "seq"), None),
        P(("dp", "seq")),
        P(("dp", "seq")),
        P(("dp", "seq")),
        P(("dp", "seq"), None),
        P(("dp", "seq"), None),
        P(("dp", "seq"), None),
        P(("dp", "seq")),
    )
    return jax.shard_map(local, mesh=mesh, in_specs=in_specs, out_specs=out_specs, check_vma=False)
```

profile of v0, /device:TPU:0, one launch (start us, length us, event | category | flops | bytes accessed | tf_op | source)
XLA Modules:
  0.0 2319.0 jit_solution(3211324311743623962)
XLA Ops:
  13.0 42.6 %all-reduce.12 = (bf16[2048]{0:T(1024)(128)(2,1)S(1)}, bf16[2048]{0:T(1024)(128)(2,1)S(1)}, bf16[2048]{0:T(1024)(128)(2,1)S(1)}, bf16[2048]{0:T(1024)(128)(2,1)S(1)}) all-reduce(bf16[2048]{0:T(1024)(128)(2,1)S(1)} %dynamic-update-slice, bf16[2048]{0:T(1024)(128)(2,1)S(1)} %dynamic-update-slice.1, ...), channel_id=1, replica_groups=mesh['dp'=8,'seq'=4] {'dp','seq'}, use_global_device_ids=true, to_apply=%add | all-reduce | flops 8192 | bytes 32768
  56.7 34.6 %all-gather.8.cloned.1.call-done = bf16[2048,2048]{1,0:T(8,128)(2,1)} async-done(((bf16[64,2048]{1,0:T(8,128)(2,1)}), bf16[2048,2048]{1,0:T(8,128)(2,1)}) %all-gather.8.cloned.1.call-update) | async-done | bytes 8388624 | tf_op jit(solution)/shard_map/all_gather | solution.py:175
  91.4 5.7 fusion.38
  98.6 4.4 all-to-all-start
  103.0 80.8 %all-gather.12.cloned.1.call-done = bf16[2048,2048]{1,0:T(8,128)(2,1)} async-done(((bf16[64,2048]{1,0:T(8,128)(2,1)}), bf16[2048,2048]{1,0:T(8,128)(2,1)}) %all-gather.12.cloned.1.call-update) | async-done | bytes 8388624 | tf_op jit(solution)/shard_map/all_gather | solution.py:174
  183.9 5.8 multiply_reduce_fusion.10
  190.2 72.6 %all-gather.10.cloned.1.call-done = bf16[2048,2048]{1,0:T(8,128)(2,1)} async-done(((bf16[64,2048]{1,0:T(8,128)(2,1)}), bf16[2048,2048]{1,0:T(8,128)(2,1)}) %all-gather.10.cloned.1.call-update) | async-done | bytes 8388624 | tf_op jit(solution)/shard_map/all_gather | solution.py:173
  262.8 5.8 multiply_reduce_fusion.11
  273.8 2.9 fusion.32
  276.7 42.1 %all_to_all.108 = bf16[1,256,16,128]{3,1,0,2:T(8,128)(2,1)} all-to-all(bf16[1,256,16,128]{3,1,0,2:T(8,128)(2,1)S(1)} %get-tuple-element.176), channel_id=1, replica_groups=mesh['dp'=8,'seq'=4] {'seq'}, dimensions={2} | all-to-all | bytes 2097152 | tf_op jit(solution)/shard_map/all_to_all | solution.py:200
  318.7 3.7 all-to-all-start.2
  328.7 2.7 copy.204
  331.3 38.5 %all-to-all-done.2 = bf16[1,256,16,128]{3,1,0,2:T(8,128)(2,1)S(1)} async-done(((bf16[1,256,16,128]{3,1,0,2:T(8,128)(2,1)}), bf16[1,256,16,128]{3,1,0,2:T(8,128)(2,1)S(1)}, u32[]{:S(2)}, u32[]{:S(2)}) %all-to-all-start.2) | async-done | bytes 1048608 | tf_op jit(solution)/shard_map/all_to_all | solution.py:201
  385.1 3.9 all-to-all-start.3
  389.1 42.8 %all-to-all-done.3 = bf16[1,1024,4,128]{3,2,0,1:T(4,128)(2,1)S(1)} async-done(((bf16[1,1024,4,128]{3,2,0,1:T(4,128)(2,1)}), bf16[1,1024,4,128]{3,2,0,1:T(4,128)(2,1)S(1)}, u32[]{:S(2)}, u32[]{:S(2)}) %all-to-all-start.3) | async-done | bytes 1048608 | tf_op jit(solution)/shard_map/all_to_all | solution.py:210
  432.5 6.7 multiply_reduce_fusion.9
  441.0 146.7 %all-gather.16.cloned.1.call-done = bf16[2048,8192]{1,0:T(8,128)(2,1)} async-done(((bf16[64,8192]{1,0:T(8,128)(2,1)}), bf16[2048,8192]{1,0:T(8,128)(2,1)}) %all-gather.16.cloned.1.call-update) | async-done | bytes 33554448 | tf_op jit(solution)/shard_map/all_gather | solution.py:218
  587.7 17.8 fusion.72
  605.5 177.9 %all-gather.18.cloned.1.call-done = bf16[2048,8192]{1,0:T(8,128)(2,1)} async-done(((bf16[64,8192]{1,0:T(8,128)(2,1)}), bf16[2048,8192]{1,0:T(8,128)(2,1)}) %all-gather.18.cloned.1.call-update) | async-done | bytes 33554448 | tf_op jit(solution)/shard_map/all_gather | solution.py:219
  783.5 23.7 %multiply_convert_fusion.4 = (bf16[256,8192]{1,0:T(8,128)(2,1)}, f32[256,8192]{1,0:T(8,128)}) fusion(f32[256,8192]{1,0:T(8,128)} %fusion.72, bf16[256,2048]{1,0:T(8,128)(2,1)S(1)} %fusion.51, bf16[2048,8192]{1,0:T(8,128)(2,1)} %all-gather.18.cloned.1.call-done), kind=kOutput, calls=%fused_computation.14 | convolution fusion | flops 8602517504 | bytes 55574528 | tf_op jit(solution)/shard_map/dot_general | solution.py:21
  807.2 172.2 %all-gather.20.cloned.1.call-done = bf16[8192,2048]{1,0:T(8,128)(2,1)} async-done(((bf16[256,2048]{1,0:T(8,128)(2,1)}), bf16[8192,2048]{1,0:T(8,128)(2,1)}) %all-gather.20.cloned.1.call-update) | async-done | bytes 33554448 | tf_op jit(solution)/shard_map/all_gather | solution.py:220
  979.4 16.6 multiply_reduce_fusion.8
  997.2 22.6 multiply_convert_fusion.2
  1019.8 17.4 convert_add_fusion
  1037.1 17.7 multiply_reduce_fusion.2
  1056.8 6.1 fusion.39
  1064.4 4.3 all-to-all-start.4
  1068.8 6.8 convolution_convert_fusion.2
  1075.7 19.5 all-to-all-done.4
  1096.7 4.9 multiply_reduce_fusion.1
  1101.7 4.5 multiply_convert_fusion.1
  1118.8 4.7 all-to-all-start.6
  1123.5 4.0 fusion.49
  1132.6 16.9 all-to-all-done.6
  1149.5 4.2 all-to-all-start.5
  1153.7 5.0 fusion.8
  1158.8 5.0 fusion.40
  1165.2 2.8 copy_bitcast_fusion
  1168.0 11.0 all-to-all-done.5
  1179.0 3.5 all-to-all-start.7
  1182.6 3.0 copy_bitcast_fusion.1
  1187.6 3.2 reshape.744
  1190.8 3.6 copy.155
  1194.4 3.1 reshape.742
  1201.4 2.5 copy.162
  1209.1 2.6 reshape.739
  1213.4 6.8 multiply_reduce_fusion.3
  1223.2 13.9 convert_bitcast_fusion
  1238.3 23.5 %convolution_convert_fusion.1 = bf16[8192,2048]{1,0:T(8,128)(2,1)} fusion(bf16[256,8192]{1,0:T(8,128)(2,1)} %get-tuple-element.203, f32[256,2048]{1,0:T(8,128)S(1)} %get-tuple-element.206, bf16[1,256,2048]{2,1,0:T(8,128)(2,1)S(1)} %copy-done.30, f32[256]{0:T(256)S(1)} %broadcast_multiply_fusion.5, f32[256]{0:T(256)S(1)} %get-tuple-element.191, ...), kind=kOutput, calls=%fused_computation.1 | convolution fusion | flops 8610381824 | bytes 40905728 | tf_op jit(solution)/shard_map/dot_general | solution.py:31
  1263.4 30.8 %convolution_convert_fusion = bf16[2048,16384]{1,0:T(8,128)(2,1)} fusion(bf16[256,2048]{1,0:T(8,128)(2,1)S(1)} %copy-done.28, bf16[256,8192]{1,0:T(8,128)(2,1)} %get-tuple-element.151, bf16[256,8192]{1,0:T(8,128)(2,1)} %get-tuple-element.152), kind=kOutput, calls=%fused_computation | convolution fusion | flops 17230200832 | bytes 76546048 | tf_op jit(solution)/shard_map/dot_general | solution.py:31
  1294.8 100.0 %reduce-scatter.11.cloned.1.call-done = bf16[256,6144]{0,1:T(8,128)(2,1)} async-done(((bf16[2048,6144]{0,1:T(8,128)(2,1)}), bf16[256,6144]{0,1:T(8,128)(2,1)}) %reduce-scatter.11.cloned.1.call-update) | async-done | bytes 3145744 | tf_op jit(solution)/shard_map/reduce_scatter | solution.py:297
  1394.8 4.8 copy.178
  1399.6 204.3 %reduce-scatter.21.cloned.1.call-done = bf16[1024,2048]{1,0:T(8,128)(2,1)} async-done(((bf16[8192,2048]{1,0:T(8,128)(2,1)}), bf16[1024,2048]{1,0:T(8,128)(2,1)}) %reduce-scatter.21.cloned.1.call-update) | async-done | bytes 4194320 | tf_op jit(solution)/shard_map/reduce_scatter | solution.py:282
  1604.0 387.3 %reduce-scatter.17.cloned.1.call-done = bf16[256,16384]{1,0:T(8,128)(2,1)} async-done(((bf16[2048,16384]{1,0:T(8,128)(2,1)}), bf16[256,16384]{1,0:T(8,128)(2,1)}) %reduce-scatter.17.cloned.1.call-update) | async-done | bytes 8388624 | tf_op jit(solution)/shard_map/reduce_scatter | solution.py:287
  1994.4 24.3 %all-reduce.13 = (bf16[2048]{0:T(1024)(128)(2,1)S(1)}, bf16[2048]{0:T(1024)(128)(2,1)S(1)}, bf16[2048]{0:T(1024)(128)(2,1)S(1)}, bf16[2048]{0:T(1024)(128)(2,1)S(1)}) all-reduce(bf16[2048]{0:T(1024)(128)(2,1)S(1)} %get-tuple-element.158, bf16[2048]{0:T(1024)(128)(2,1)S(1)} %get-tuple-element.131, ...), channel_id=6, replica_groups=mesh['dp'=8,'seq'=4] {'dp'}, use_global_device_ids=true, to_apply=%region_22.23.clone | all-reduce | flops 8192 | bytes 32768
  2019.0 11.7 all-reduce.14
  2033.1 6.0 convolution_add_fusion.3
  2039.1 5.9 convolution_add_fusion.2
  2045.0 3.7 fusion.21
  2050.5 31.4 %reduce-scatter.25.cloned.1.call-done = bf16[64,6144]{1,0:T(8,128)(2,1)} async-done(((bf16[256,6144]{1,0:T(8,128)(2,1)}), bf16[64,6144]{1,0:T(8,128)(2,1)}) %reduce-scatter.25.cloned.1.call-update) | async-done | bytes 786448
  2089.9 71.0 %reduce-scatter.23.cloned.1.call-done = bf16[256,2048]{1,0:T(8,128)(2,1)} async-done(((bf16[1024,2048]{1,0:T(8,128)(2,1)}), bf16[256,2048]{1,0:T(8,128)(2,1)}) %reduce-scatter.23.cloned.1.call-update) | async-done | bytes 1048592 | tf_op jit(solution)/shard_map/reduce_scatter | solution.py:318
  2160.9 2.8 convert_element_type.339
  2163.7 144.5 %reduce-scatter.19.cloned.1.call-done = bf16[64,16384]{1,0:T(8,128)(2,1)} async-done(((bf16[256,16384]{1,0:T(8,128)(2,1)}), bf16[64,16384]{1,0:T(8,128)(2,1)}) %reduce-scatter.19.cloned.1.call-update) | async-done | bytes 2097168 | tf_op jit(solution)/shard_map/reduce_scatter | solution.py:319
  2308.2 4.0 fusion.65
  (280 shorter events, 96.2 us)
Async XLA Ops:
  7.2 4.8 copy-start.62
  7.2 5.0 copy-start.63
  7.2 5.3 copy-start.64
  7.2 5.5 copy-start.65
  7.2 48.4 %copy-start.51 = (s32[1,1024]{1,0:T(1,128)S(1)}, s32[1,1024]{1,0:T(1,128)}, u32[]{:S(2)}) copy-start(s32[1,1024]{1,0:T(1,128)} %param.15) | copy-start | bytes 12292
  7.2 84.2 %all-gather.8.cloned.1.call-start = ((), (), s32[]{:S(2)}) async-start(), calls=%async_computation.16 | async-start | bytes 8650752 | tf_op jit(solution)/shard_map/all_gather | solution.py:175
  8.0 175.9 %all-gather.12.cloned.1.call-start = ((), (), s32[]{:S(2)}) async-start(), calls=%async_computation.18 | async-start | bytes 8650752 | tf_op jit(solution)/shard_map/all_gather | solution.py:174
  8.7 254.1 %all-gather.10.cloned.1.call-start = ((), (), s32[]{:S(2)}) async-start(), calls=%async_computation.17 | async-start | bytes 8650752 | tf_op jit(solution)/shard_map/all_gather | solution.py:173
  9.4 81.9 %copy-start.14 = (bf16[1,256,2048]{2,1,0:T(8,128)(2,1)S(1)}, bf16[1,256,2048]{2,1,0:T(8,128)(2,1)}, u32[]{:S(2)}) copy-start(bf16[1,256,2048]{2,1,0:T(8,128)(2,1)} %param.14) | copy-start | bytes 3145732
  9.5 423.1 %all-gather.14.cloned.1.call-start = ((), (), s32[]{:S(2)}) async-start(), calls=%async_computation.19 | async-start | bytes 8650752 | tf_op jit(solution)/shard_map/all_gather | solution.py:176
  10.0 577.6 %all-gather.16.cloned.1.call-start = ((), (), s32[]{:S(2)}) async-start(), calls=%async_computation.20 | async-start | bytes 34603008 | tf_op jit(solution)/shard_map/all_gather | solution.py:218
  10.6 772.8 %all-gather.18.cloned.1.call-start = ((), (), s32[]{:S(2)}) async-start(), calls=%async_computation.21 | async-start | bytes 34603008 | tf_op jit(solution)/shard_map/all_gather | solution.py:219
  11.2 968.2 %all-gather.20.cloned.1.call-start = ((), (), s32[]{:S(2)}) async-start(), calls=%async_computation.22 | async-start | bytes 34603008 | tf_op jit(solution)/shard_map/all_gather | solution.py:220
  55.6 213.0 %copy-start.45 = (f32[2048]{0:T(1024)}, f32[2048]{0:T(1024)S(1)}, u32[]{:S(2)}) copy-start(f32[2048]{0:T(1024)S(1)} %convert_element_type.283) | copy-start | bytes 24580
  55.6 215.0 %copy-start.47 = (f32[2048]{0:T(1024)}, f32[2048]{0:T(1024)S(1)}, u32[]{:S(2)}) copy-start(f32[2048]{0:T(1024)S(1)} %convert_element_type.278) | copy-start | bytes 24580
  56.7 217.0 %copy-start.41 = (f32[256,128]{1,0:T(8,128)}, f32[256,128]{1,0:T(8,128)S(1)}, u32[]{:S(2)}) copy-start(f32[256,128]{1,0:T(8,128)S(1)} %get-tuple-element.213) | copy-start | bytes 393220
  56.7 217.0 %copy-start.43 = (f32[256,128]{1,0:T(8,128)}, f32[256,128]{1,0:T(8,128)S(1)}, u32[]{:S(2)}) copy-start(f32[256,128]{1,0:T(8,128)S(1)} %get-tuple-element.212) | copy-start | bytes 393220
  98.6 178.1 %all-to-all-start = ((bf16[1,256,16,128]{3,1,0,2:T(8,128)(2,1)}), bf16[1,256,16,128]{3,1,0,2:T(8,128)(2,1)}, u32[]{:S(2)}, u32[]{:S(2)}) async-start(bf16[1,256,16,128]{3,1,0,2:T(8,128)(2,1)} %copy.134), calls=%async_computation | async-start | bytes 2097152 | tf_op jit(solution)/shard_map/all_to_all | solution.py:202
  189.7 79.0 %copy-start.8 = (f32[256,2048]{1,0:T(8,128)}, f32[256,2048]{1,0:T(8,128)S(1)}, u32[]{:S(2)}) copy-start(f32[256,2048]{1,0:T(8,128)S(1)} %get-tuple-element.194) | copy-start | bytes 6291460
  190.2 78.4 %copy-start.55 = (f32[256]{0:T(256)}, f32[256]{0:T(256)S(1)}, u32[]{:S(2)}) copy-start(f32[256]{0:T(256)S(1)} %get-tuple-element.186) | copy-start | bytes 3076
  318.7 51.1 %all-to-all-start.2 = ((bf16[1,256,16,128]{3,1,0,2:T(8,128)(2,1)}), bf16[1,256,16,128]{3,1,0,2:T(8,128)(2,1)S(1)}, u32[]{:S(2)}, u32[]{:S(2)}) async-start(bf16[1,256,16,128]{3,1,0,2:T(8,128)(2,1)} %get-tuple-element.175), calls=%async_computation.2 | async-start | bytes 2097152 | tf_op jit(solution)/shard_map/all_to_all | solution.py:201
  328.7 52.5 %copy-start.17 = (bf16[1024,4,128]{0,2,1:T(8,128)(2,1)}, bf16[1024,4,128]{0,2,1:T(8,128)(2,1)S(1)}, u32[]{:S(2)}) copy-start(bf16[1024,4,128]{0,2,1:T(8,128)(2,1)S(1)} %squeeze.31) | copy-start | bytes 3145732
  369.9 5.3 copy-start.5
  373.3 5.5 copy-start
  373.3 5.5 copy-start.49
  377.0 4.2 copy-start.1
  385.1 46.7 %all-to-all-start.3 = ((bf16[1,1024,4,128]{3,2,0,1:T(4,128)(2,1)}), bf16[1,1024,4,128]{3,2,0,1:T(4,128)(2,1)S(1)}, u32[]{:S(2)}, u32[]{:S(2)}) async-start(bf16[1,1024,4,128]{3,2,0,1:T(4,128)(2,1)} %copy.144), calls=%async_computation.3 | async-start | bytes 2097152 | tf_op jit(solution)/shard_map/all_to_all | solution.py:210
  441.0 342.5 %copy-start.27 = (bf16[256,2048]{1,0:T(8,128)(2,1)}, bf16[256,2048]{1,0:T(8,128)(2,1)S(1)}, u32[]{:S(2)}) copy-start(bf16[256,2048]{1,0:T(8,128)(2,1)S(1)} %fusion.51) | copy-start | bytes 3145732
  979.4 16.6 copy-start.29
  1037.1 17.7 copy-start.13
  1037.1 17.7 copy-start.15
  1056.8 6.1 copy-start.36
  1063.2 5.6 copy-start.50
  1063.2 5.6 copy-start.53
  1064.4 30.7 %all-to-all-start.4 = ((bf16[1,256,16,128]{3,1,0,2:T(8,128)(2,1)}), bf16[1,256,16,128]{3,1,0,2:T(8,128)(2,1)}, u32[]{:S(2)}, u32[]{:S(2)}) async-start(bf16[1,256,16,128]{3,1,0,2:T(8,128)(2,1)} %copy.147), calls=%async_computation.4 | async-start | bytes 2097152 | tf_op jit(solution)/shard_map/all_to_all | solution.py:244
  1068.7 225.5 %reduce-scatter.13.cloned.1.call-start = ((), (), s32[]{:S(2)}) async-start(), calls=%async_computation.24 | async-start | bytes 9437184 | tf_op jit(solution)/shard_map/reduce_scatter | solution.py:297
  1096.7 5.0 copy-start.23
  1096.7 11.5 copy-start.25
  1096.7 11.5 slice-start
  1101.7 4.5 copy-start.20
  1101.7 6.5 slice-start.1
  1116.3 7.2 copy-start.6
  1118.8 30.7 %all-to-all-start.6 = ((bf16[1,1024,4,128]{3,2,0,1:T(4,128)(2,1)}), bf16[1,1024,4,128]{3,2,0,1:T(4,128)(2,1)}, u32[]{:S(2)}, u32[]{:S(2)}) async-start(bf16[1,1024,4,128]{3,2,0,1:T(4,128)(2,1)} %copy.159), calls=%async_computation.6 | async-start | bytes 2097152 | tf_op jit(solution)/shard_map/all_to_all | solution.py:255
  1123.5 4.0 copy-start.3
  1130.1 23.6 %copy-start.26 = (bf16[1,2,256,4,128]{4,2,1,3,0:T(8,128)(2,1)S(1)}, bf16[1,2,256,4,128]{4,2,1,3,0:T(8,128)(2,1)}, u32[]{:S(2)}) copy-start(bf16[1,2,256,4,128]{4,2,1,3,0:T(8,128)(2,1)} %copy-done.25) | copy-start | bytes 1572868
  1149.5 29.6 %all-to-all-start.5 = ((bf16[1,1024,4,128]{3,2,0,1:T(4,128)(2,1)}), bf16[1,1024,4,128]{3,2,0,1:T(4,128)(2,1)}, u32[]{:S(2)}, u32[]{:S(2)}) async-start(bf16[1,1024,4,128]{3,2,0,1:T(4,128)(2,1)} %copy.153), calls=%async_computation.5 | async-start | bytes 2097152 | tf_op jit(solution)/shard_map/all_to_all | solution.py:252
  1153.7 5.0 copy-start.24
  1179.0 28.7 %all-to-all-start.7 = ((bf16[1,1024,4,128]{3,2,0,1:T(4,128)(2,1)}), bf16[1,1024,4,128]{3,2,0,1:T(4,128)(2,1)S(1)}, u32[]{:S(2)}, u32[]{:S(2)}) async-start(bf16[1,1024,4,128]{3,2,0,1:T(4,128)(2,1)} %copy.165), calls=%async_computation.7 | async-start | bytes 2097152 | tf_op jit(solution)/shard_map/all_to_all | solution.py:258
  1182.6 212.2 %reduce-scatter.11.cloned.1.call-start = ((), (), s32[]{:S(2)}) async-start(), calls=%async_computation.23 | async-start | bytes 28311552 | tf_op jit(solution)/shard_map/reduce_scatter | solution.py:297
  1207.8 4.0 copy-start.44
  1213.4 6.8 copy-start.11
  1213.4 6.8 copy-start.61
  1237.1 366.8 %reduce-scatter.21.cloned.1.call-start = ((), (), s32[]{:S(2)}) async-start(), calls=%async_computation.28 | async-start | bytes 37748736 | tf_op jit(solution)/shard_map/reduce_scatter | solution.py:282
  1261.9 729.4 %reduce-scatter.17.cloned.1.call-start = ((), (), s32[]{:S(2)}) async-start(), calls=%async_computation.26 | async-start | bytes 75497472 | tf_op jit(solution)/shard_map/reduce_scatter | solution.py:287
  1294.2 754.5 %reduce-scatter.15.cloned.1.call-start = ((), (), s32[]{:S(2)}) async-start(), calls=%async_computation.25 | async-start | bytes 1310720 | tf_op jit(solution)/shard_map/reduce_scatter | solution.py:328
  1294.8 787.2 %reduce-scatter.25.cloned.1.call-start = ((), (), s32[]{:S(2)}) async-start(), calls=%async_computation.30 | async-start | bytes 3932160
  1399.6 761.3 %reduce-scatter.23.cloned.1.call-start = ((), (), s32[]{:S(2)}) async-start(), calls=%async_computation.29 | async-start | bytes 5242880 | tf_op jit(solution)/shard_map/reduce_scatter | solution.py:318
  1603.9 704.3 %reduce-scatter.19.cloned.1.call-start = ((), (), s32[]{:S(2)}) async-start(), calls=%async_computation.27 | async-start | bytes 10485760 | tf_op jit(solution)/shard_map/reduce_scatter | solution.py:319
  1991.3 41.8 %copy-start.32 = (bf16[256,2048]{1,0:T(8,128)(2,1)S(1)}, bf16[256,2048]{1,0:T(8,128)(2,1)}, u32[]{:S(2)}) copy-start(bf16[256,2048]{1,0:T(8,128)(2,1)} %subtract_convert_fusion.1) | copy-start | bytes 3145732
  1991.3 41.8 %copy-start.40 = (f32[256,2048]{1,0:T(8,128)S(1)}, f32[256,2048]{1,0:T(8,128)}, u32[]{:S(2)}) copy-start(f32[256,2048]{1,0:T(8,128)} %copy-done.39) | copy-start | bytes 6291460
  2033.1 6.0 copy-start.33
  2033.1 12.0 slice-start.2
  2039.0 6.0 copy-start.31
  2039.1 6.0 slice-start.3
  (30 other events, 64.9 us)
Sparse Core Ops, SparseCore 0:
  11.0 80.3 all-gather.7
  94.3 89.5 all-gather.11
  186.8 75.9 all-gather.9
  265.6 105.5 all-gather.13
  374.0 213.6 all-gather.15
  590.5 192.9 all-gather.17
  786.4 192.9 all-gather.19
  1075.8 71.6 reduce-scatter.12
  1237.2 157.4 reduce-scatter.10
  1398.6 205.2 reduce-scatter.20
  1607.5 383.7 reduce-scatter.16
  1993.5 27.1 reduce-scatter.14
  2023.0 58.8 reduce-scatter.24
  2084.1 76.7 reduce-scatter.22
  2163.2 144.9 reduce-scatter.18
where the time goes:
time: 2330 us; the launch traced here: 2320 us
  waiting for transfers between devices  1760 us (76%)
  matrix products  270 us (12%)
  blocking collectives  121 us (5%)
  local copies, waits for them, and re-layouts  73.5 us (3%)
  other arithmetic  51.7 us (2%)
  starting transfers between devices  29.4 us (1%)
    reduce_scatter x3, waiting for transfers between devices, local(): lax.psum_scatter(part.astype(jnp.bfloat16), 'dp', scatter_dimension=0, ti...  487 us
    reduce_scatter x1, waiting for transfers between devices, local(): lax.psum_scatter(weight_grad(inner_act, dm_low).astype(jnp.bfloat16), 'dp...  204 us
    all_gather x1, waiting for transfers between devices, local(): lax.all_gather(w_up, ('dp', 'seq'), axis=0, tiled=True)  178 us
    all_gather x1, waiting for transfers between devices, local(): lax.all_gather(w_down, ('dp', 'seq'), axis=0, tiled=True)  172 us
    all_gather x1, waiting for transfers between devices, local(): lax.all_gather(w_gate, ('dp', 'seq'), axis=0, tiled=True)  147 us
    reduce_scatter x1, waiting for transfers between devices, local(): lax.psum_scatter(gateup_part.astype(jnp.bfloat16), 'seq', scatter_dimensi...  145 us
    dot_general x7, matrix products, product(): return jnp.dot(left, right, preferred_element_type=jnp.float32)  82.2 us
    all_gather x1, waiting for transfers between devices, local(): lax.all_gather(w_key, ('dp', 'seq'), axis=0, tiled=True)  80.8 us
  transfers between devices with their start and end apart: 22, of which 17 were waited for; matrix products, arithmetic and copies ran while one was open for 13% of the time, Pallas kernels for 0%

commit v1 on v0

v1 whole, which is shorter than its diff:
```python
import jax
import jax.numpy as jnp
from jax import lax
from jax.sharding import PartitionSpec as P

H = 16
HD = 128
DOCS = 4
CHUNKS = 2

epsilon = 1e-06
rope_base = 500000.0
masked_score = -1e30
bf16 = jnp.bfloat16
f32 = jnp.float32


def product(left, right):
    return jnp.dot(left, right, preferred_element_type=f32)


def against(left, right):
    return lax.dot_general(left, right, (((1,), (1,)), ((), ())), preferred_element_type=f32)


def weight_grad(left, right):
    return lax.dot_general(left, right, (((0,), (0,)), ((), ())), preferred_element_type=f32)


def rms_scale(values):
    return lax.rsqrt(jnp.mean(values * values, -1, keepdims=True) + epsilon)


def norm_back(values, scale_rows, grad_vals):
    return scale_rows * grad_vals - values * scale_rows**3 * jnp.mean(
        grad_vals * values, -1, keepdims=True
    )


def positions(seg_ids):
    doc_ids = jnp.arange(DOCS, dtype=jnp.int32)
    starts = jnp.sum((seg_ids[..., None, :] < doc_ids[:, None]).astype(jnp.int32), -1)
    one_hot = (seg_ids[..., None] == doc_ids).astype(jnp.int32)
    token_start = jnp.sum(one_hot * starts[..., None, :], axis=-1)
    return jnp.arange(seg_ids.shape[-1], dtype=jnp.int32) - token_start


def rope_tables(position_ids):
    freqs = rope_base ** (-jnp.arange(HD // 2, dtype=f32) * 2.0 / HD)
    angles = position_ids.astype(f32)[..., None] * freqs
    cosine = jnp.cos(angles)
    sine_tab = jnp.sin(angles)
    return (
        jnp.concatenate([cosine, cosine], -1)[..., None, :],
        jnp.concatenate([sine_tab, sine_tab], -1)[..., None, :],
    )


def rotate(values):
    return jnp.concatenate([-values[..., HD // 2 :], values[..., : HD // 2]], -1)


def apply_rope(values, cosine, sine_tab):
    return values * cosine + rotate(values) * sine_tab


def rope_back(grad_vals, cosine, sine_tab):
    return grad_vals * cosine - rotate(grad_vals * sine_tab)


def mask_for(seg_ids, row_start, row_count):
    query_ids = row_start + jnp.arange(row_count)
    key_ids = jnp.arange(seg_ids.shape[0])
    same_doc = seg_ids[row_start : row_start + row_count, None] == seg_ids[None, :]
    return same_doc & (key_ids[None, :] <= query_ids[:, None])


def attend(query_vecs, key_vecs, value_vecs, seg_ids):
    length = query_vecs.shape[0]
    q_block = min(512, length)
    score_scale = HD ** (-0.5)
    outputs = []
    log_sums = []
    for row_start in range(0, length, q_block):
        seen = row_start + q_block
        q_part = query_vecs[row_start:seen]
        scores = (
            jnp.einsum("qhd,khd->hqk", q_part, key_vecs[:seen], preferred_element_type=f32)
            * score_scale
        )
        scores = jnp.where(mask_for(seg_ids, row_start, q_block)[None, :, :seen], scores, masked_score)
        row_max = jnp.max(scores, -1, keepdims=True)
        expos = jnp.exp(scores - row_max)
        row_total = jnp.sum(expos, -1, keepdims=True)
        attn_probs = (expos / row_total).astype(bf16)
        block_out = jnp.einsum("hqk,khd->qhd", attn_probs, value_vecs[:seen], preferred_element_type=f32)
        outputs.append(block_out.astype(bf16))
        log_sums.append((row_max + jnp.log(row_total))[..., 0])
    return (jnp.concatenate(outputs, 0), jnp.concatenate(log_sums, 1))


def attend_back(query_vecs, key_vecs, value_vecs, d_attended, seg_ids, log_totals):
    length = query_vecs.shape[0]
    q_block = min(512, length)
    score_scale = HD ** (-0.5)
    d_query_parts = []
    d_keys = jnp.zeros(key_vecs.shape, f32)
    d_values = jnp.zeros(value_vecs.shape, f32)
    for row_start in range(0, length, q_block):
        seen = row_start + q_block
        q_part = query_vecs[row_start:seen]
        g_part = d_attended[row_start:seen]
        k_part = key_vecs[:seen]
        scores = jnp.einsum("qhd,khd->hqk", q_part, k_part, preferred_element_type=f32) * score_scale
        scores = jnp.where(mask_for(seg_ids, row_start, q_block)[None, :, :seen], scores, masked_score)
        attn_probs = jnp.exp(scores - log_totals[:, row_start:seen, None])
        d_probs = jnp.einsum("qhd,khd->hqk", g_part, value_vecs[:seen], preferred_element_type=f32)
        inner_sum = jnp.sum(attn_probs * d_probs, -1, keepdims=True)
        d_scores = (attn_probs * (d_probs - inner_sum)).astype(bf16)
        d_query_parts.append(
            jnp.einsum("hqk,khd->qhd", d_scores, k_part, preferred_element_type=f32) * score_scale
        )
        d_k_part = jnp.einsum("hqk,qhd->khd", d_scores, q_part, preferred_element_type=f32) * score_scale
        d_v_part = jnp.einsum("hqk,qhd->khd", attn_probs.astype(bf16), g_part, preferred_element_type=f32)
        d_keys = d_keys.at[:seen].add(d_k_part)
        d_values = d_values.at[:seen].add(d_v_part)
    return (jnp.concatenate(d_query_parts, 0), d_keys, d_values)


def line_gather(block, axis):
    size = lax.axis_size(axis)
    here = lax.axis_index(axis)
    up, down = [block], [block]
    for step in range(1, size):
        up.append(lax.ppermute(up[-1], axis, [(i, i + 1) for i in range(step - 1, size - 1)]))
        down.append(lax.ppermute(down[-1], axis, [(i, i - 1) for i in range(1, size - step + 1)]))
    return [block] + [
        jnp.where(here >= back, up[back], down[size - back]) for back in range(1, size)
    ]


def line_scatter_sum(parts, axis):
    size = lax.axis_size(axis)
    from_below = from_above = None
    for step in range(1, size):
        up, down = parts[step], parts[size - step]
        if step > 1:
            up = up.astype(f32) + from_below.astype(f32)
            down = down.astype(f32) + from_above.astype(f32)
        from_below = lax.ppermute(up.astype(bf16), axis, [(i, i + 1) for i in range(step)])
        from_above = lax.ppermute(down.astype(bf16), axis, [(i, i - 1) for i in range(size - step, size)])
    return parts[0].astype(f32) + from_below.astype(f32) + from_above.astype(f32)


def in_order(slots, axis):
    size = lax.axis_size(axis)
    rising = slots[:0:-1] + slots[:1]
    twice = jnp.concatenate([s[None] for s in rising + rising[: size - 1]], 0)
    start = lax.rem(2 * size - 1 - lax.axis_index(axis), size)
    return lax.dynamic_slice_in_dim(twice, start, size, 0)


def small_sum(values, axis):
    size = lax.axis_size(axis)
    total = values
    for step in range(1, size):
        total = total + lax.ppermute(values, axis, [(i, (i + step) % size) for i in range(size)])
    return total


def local(
    tokens,
    segments,
    w_query,
    w_key,
    w_value,
    w_out,
    g_query,
    g_key,
    g_attn,
    w_gate,
    w_up,
    w_down,
    g_ffn,
    d_out,
):
    seqs, local_len, width = tokens.shape
    rows = seqs * local_len
    copies, size = lax.axis_size("dp"), lax.axis_size("seq")
    here = lax.axis_index("seq")
    total_len = size * local_len
    part = width // size
    heads = H // size
    own_rows = w_gate.shape[0]
    ff_width = w_gate.shape[1]
    ff_part = ff_width // size
    ff_own = w_down.shape[0]
    everyone = ("dp", "seq")
    tok_rows = tokens.reshape(rows, width)

    qkv_own = jnp.stack([w_query, w_key, w_value], 1).reshape(own_rows, 3, size, part)
    qkv_own = lax.all_to_all(
        qkv_own.transpose(2, 0, 1, 3), "seq", split_axis=0, concat_axis=0, tiled=True
    ).reshape(size * own_rows, 3 * part)
    w_qkv = lax.all_gather(qkv_own, "dp", axis=0, tiled=True)
    gu_own = jnp.stack([w_gate, w_up], 1).reshape(own_rows, 2, copies, size, ff_own)
    gu_own = lax.all_to_all(
        gu_own.transpose(3, 0, 1, 2, 4), "seq", split_axis=0, concat_axis=0, tiled=True
    ).reshape(size * own_rows, 2 * ff_part)
    w_gu = lax.all_gather(gu_own, "dp", axis=0, tiled=True)
    w_gate_part, w_up_part = w_gu[:, :ff_part], w_gu[:, ff_part:]
    w_down_part = lax.all_gather(w_down, "dp", axis=0, tiled=True)
    w_out_all = lax.all_gather(
        lax.all_gather(w_out, "seq", axis=0, tiled=True), "dp", axis=0, tiled=True
    )
    gains = lax.all_gather(
        jnp.stack([g_query, g_key, g_attn, g_ffn], 0), everyone, axis=1, tiled=True
    ).astype(f32)
    gain_attn, gain_ffn = gains[2], gains[3]
    gain_qk = lax.dynamic_slice_in_dim(gains[:2], here * part, part, 1).reshape(2, heads, HD)

    x_all = in_order([s.reshape(seqs, local_len, width) for s in line_gather(tok_rows, "seq")], "seq")
    x_all = x_all.transpose(1, 0, 2, 3).reshape(seqs * total_len, width)
    qkv = product(x_all, w_qkv).reshape(seqs * total_len, 3, part)
    qk_raw = qkv[:, :2]
    squares = small_sum(jnp.sum(qk_raw * qk_raw, -1), "seq")
    qk_scale = lax.rsqrt(squares / width + epsilon)[..., None, None]
    qk_raw = qk_raw.reshape(seqs * total_len, 2, heads, HD)
    cosine, sine_tab = rope_tables(positions(segments).reshape(seqs * total_len))
    cosine, sine_tab = cosine[:, None], sine_tab[:, None]
    qk_unit = qk_raw * qk_scale
    qk_low = apply_rope(qk_unit * gain_qk, cosine, sine_tab).astype(bf16)
    head_shape = (seqs, total_len, heads, HD)
    query_low = qk_low[:, 0].reshape(head_shape)
    key_low = qk_low[:, 1].reshape(head_shape)
    value_low = qkv[:, 2].astype(bf16).reshape(head_shape)
    attended_heads, log_totals = jax.vmap(attend)(query_low, key_low, value_low, segments)
    attended = lax.all_to_all(
        attended_heads.reshape(seqs, total_len, part), "seq", split_axis=1, concat_axis=2, tiled=True
    ).reshape(rows, width)

    step = rows // CHUNKS
    cuts = [slice(at * step, (at + 1) * step) for at in range(CHUNKS)]
    d_out_rows = d_out.reshape(rows, width)
    a_parts, hidden_parts, hidden_all = [], [], []
    for cut in cuts:
        a_proj = product(attended[cut], w_out_all)
        a_scale = rms_scale(a_proj)
        hidden = tok_rows[cut].astype(f32) + a_proj * a_scale * gain_attn
        a_parts.append((a_proj, a_scale))
        hidden_parts.append(hidden)
        hidden_all.append(jnp.concatenate(line_gather(hidden.astype(bf16), "seq"), 0))
    gates, ups, inners, outs, dms, d_gain_ffn = [], [], [], [], [], 0.0
    for at, cut in enumerate(cuts):
        gate = product(hidden_all[at], w_gate_part)
        up = product(hidden_all[at], w_up_part)
        inner = (jax.nn.silu(gate) * up).astype(bf16)
        m_share = product(inner, w_down_part).astype(bf16)
        gates.append(gate)
        ups.append(up)
        inners.append(inner)
        m_proj = line_scatter_sum([m_share[o * step : (o + 1) * step] for o in range(size)], "seq")
        m_scale = rms_scale(m_proj)
        outs.append((hidden_parts[at] + m_proj * m_scale * gain_ffn).astype(bf16))
        grad_out = d_out_rows[cut].astype(f32)
        d_gain_ffn = d_gain_ffn + jnp.sum(grad_out * m_proj * m_scale, 0)
        dm_low = norm_back(m_proj, m_scale, grad_out * gain_ffn).astype(bf16)
        dms.append(jnp.concatenate(line_gather(dm_low, "seq"), 0))
    d_gates, d_ups, d_hiddens, das, d_attendeds, d_gain_attn = [], [], [], [], [], 0.0
    for at, cut in enumerate(cuts):
        gate, up = gates[at], ups[at]
        d_inner = against(dms[at], w_down_part)
        sigmoid_gate = jax.nn.sigmoid(gate)
        d_gate = (d_inner * up * sigmoid_gate * (1.0 + gate * (1.0 - sigmoid_gate))).astype(bf16)
        d_up = (d_inner * (gate * sigmoid_gate)).astype(bf16)
        d_gates.append(d_gate)
        d_ups.append(d_up)
        h_share = (against(d_gate, w_gate_part) + against(d_up, w_up_part)).astype(bf16)
        d_hidden = d_out_rows[cut].astype(f32) + line_scatter_sum(
            [h_share[o * step : (o + 1) * step] for o in range(size)], "seq"
        )
        a_proj, a_scale = a_parts[at]
        d_gain_attn = d_gain_attn + jnp.sum(d_hidden * a_proj * a_scale, 0)
        da_low = norm_back(a_proj, a_scale, d_hidden * gain_attn).astype(bf16)
        d_hiddens.append(d_hidden)
        das.append(da_low)
        d_attendeds.append(against(da_low, w_out_all).astype(bf16))
    out = jnp.concatenate(outs, 0).reshape(tokens.shape)
    d_hidden = jnp.concatenate(d_hiddens, 0)

    inner_all = jnp.concatenate(inners, 0)
    dm_all = jnp.concatenate(dms, 0)
    hidden_all = jnp.concatenate(hidden_all, 0)
    d_gu = jnp.concatenate(
        [
            weight_grad(hidden_all, jnp.concatenate(d_gates, 0)).astype(bf16),
            weight_grad(hidden_all, jnp.concatenate(d_ups, 0)).astype(bf16),
        ],
        1,
    )
    d_down = weight_grad(inner_all, dm_all).astype(bf16)
    d_w_out = weight_grad(attended, jnp.concatenate(das, 0)).astype(bf16)
    d_down = lax.psum_scatter(d_down, "dp", scatter_dimension=0, tiled=True).astype(f32)
    d_gu = lax.psum_scatter(d_gu, "dp", scatter_dimension=0, tiled=True)
    d_gu = lax.all_to_all(
        d_gu.reshape(size, own_rows, 2, copies, ff_own), "seq", split_axis=0, concat_axis=0, tiled=True
    )
    d_gu = d_gu.transpose(2, 1, 3, 0, 4).reshape(2, own_rows, ff_width).astype(f32)
    d_w_out = lax.psum_scatter(
        lax.psum_scatter(d_w_out, "dp", scatter_dimension=0, tiled=True),
        "seq",
        scatter_dimension=0,
        tiled=True,
    ).astype(f32)

    d_attended = jnp.concatenate(d_attendeds, 0).reshape(seqs, local_len, width)
    d_attended = lax.all_to_all(d_attended, "seq", split_axis=2, concat_axis=1, tiled=True).reshape(head_shape)
    dq, dk, dv = jax.vmap(attend_back)(query_low, key_low, value_low, d_attended, segments, log_totals)
    d_qk = jnp.stack([dq, dk], 2).reshape(seqs * total_len, 2, heads, HD).astype(bf16).astype(f32)
    d_qk = rope_back(d_qk, cosine, sine_tab)
    d_gain_qk = jnp.sum(d_qk * qk_unit, 0)
    d_qk = d_qk * gain_qk
    dots = small_sum(jnp.sum(d_qk * qk_raw, (-2, -1)), "seq")[..., None, None] / width
    d_qk = (qk_scale * d_qk - qk_raw * qk_scale**3 * dots).astype(bf16)
    d_qkv = jnp.concatenate(
        [d_qk.reshape(seqs * total_len, 2 * part), dv.astype(bf16).reshape(seqs * total_len, part)], 1
    )
    x_share = against(d_qkv, w_qkv).astype(bf16).reshape(seqs, size, local_len, width)
    x_share = [
        lax.dynamic_index_in_dim(x_share, lax.rem(here + size - o, size), 1, keepdims=False).reshape(rows, width)
        for o in range(size)
    ]
    d_tokens = d_hidden + line_scatter_sum(x_share, "seq")
    d_w_qkv = weight_grad(x_all, d_qkv).astype(bf16)
    d_w_qkv = lax.psum_scatter(d_w_qkv, "dp", scatter_dimension=0, tiled=True)
    d_w_qkv = lax.all_to_all(
        d_w_qkv.reshape(size, own_rows, 3, part), "seq", split_axis=0, concat_axis=0, tiled=True
    )
    d_w_qkv = d_w_qkv.transpose(2, 1, 0, 3).reshape(3, own_rows, width).astype(f32)

    d_gain_qk = lax.dynamic_update_slice_in_dim(
        jnp.zeros((2, width), f32), d_gain_qk.reshape(2, part), here * part, 1
    )
    d_gains = jnp.concatenate([d_gain_qk, d_gain_attn[None], d_gain_ffn[None]], 0)
    d_gains = lax.psum_scatter(d_gains, everyone, scatter_dimension=1, tiled=True)
    return (
        out,
        d_tokens.reshape(tokens.shape),
        d_w_qkv[0],
        d_w_qkv[1],
        d_w_qkv[2],
        d_w_out,
        d_gains[0],
        d_gains[1],
        d_gains[2],
        d_gu[0],
        d_gu[1],
        d_down,
        d_gains[3],
    )


def solution(mesh):
    rows = P("dp", "seq", None)
    mat = P(("dp", "seq"), None)
    vec = P(("dp", "seq"))
    in_specs = (rows, P("dp", None), mat, mat, mat, mat, vec, vec, vec, mat, mat, mat, vec, rows)
    out_specs = (rows, rows, mat, mat, mat, mat, vec, vec, vec, mat, mat, mat, vec)
    return jax.shard_map(local, mesh=mesh, in_specs=in_specs, out_specs=out_specs, check_vma=False)
```

time: 2330 us -> 1430 us (0.61)
  waiting for transfers between devices: 1760 us -> 588 us
  starting transfers between devices: 29.4 us -> 163 us
  other arithmetic: 51.7 us -> 127 us
  blocking collectives: 121 us -> 175 us
  local copies, waits for them, and re-layouts: 73.5 us -> 117 us
  matrix products: 270 us -> 228 us
    reduce_scatter x7 -> x5, waiting for transfers between devices: 907 us -> 200 us  [the longest x1 64.5 us: local(): lax.psum_scatter(d_down, 'dp', scatter_dimension=0, tiled=True).astype(f32)]
    all_gather x7 -> x5, waiting for transfers between devices: 685 us -> 0.04 us  [the longest x1 0.02 us: local(): lax.all_gather(lax.all_gather(w_out, 'seq', axis=0, tiled=True), 'dp', ax...]
    ppermute x0 -> x66, waiting for transfers between devices: none -> 218 us  [the longest x15 123 us: line_gather(): lax.ppermute(down[-1], axis, [(i, i - 1) for i in range(1, size - step +...]
    ppermute x0 -> x66, starting transfers between devices: none -> 141 us  [the longest x15 72.9 us: line_scatter_sum(): lax.ppermute(up.astype(bf16), axis, [(i, i + 1) for i in range(step)])]
    unnamed x16 -> x12, waiting for transfers between devices: 36.4 us -> 137 us
    all_to_all x6 -> x3, waiting for transfers between devices: 109 us -> 17.6 us  [the longest x1 17.6 us: local(): lax.all_to_all(attended_heads.reshape(seqs, total_len, part), 'seq', spli...]
    all_gather x0 -> x1, blocking collectives: none -> 82.4 us  [local(): lax.all_gather(jnp.stack([g_query, g_key, g_attn, g_ffn], 0), everyone, a...]
    unnamed x3 -> x0, blocking collectives: 78.6 us -> none
  transfers between devices with their start and end apart: 22 -> 81, of which waited for: 17 -> 31; matrix products, arithmetic and copies ran while one was open for 13% -> 24% of each run, Pallas kernels for 0% -> 0%
where the time goes in v1:
time: 1430 us; the launch traced here: 1420 us
  waiting for transfers between devices  588 us (41%)
  matrix products  228 us (16%)
  blocking collectives  175 us (12%)
  starting transfers between devices  163 us (11%)
  other arithmetic  127 us (9%)
  local copies, waits for them, and re-layouts  117 us (8%)
  between operations  16.7 us (1%)
    unnamed x12, waiting for transfers between devices  137 us
    ppermute x15, waiting for transfers between devices, line_gather(): lax.ppermute(down[-1], axis, [(i, i - 1) for i in range(1, size - step +...  123 us
    all_gather x1, blocking collectives, local(): lax.all_gather(jnp.stack([g_query, g_key, g_attn, g_ffn], 0), everyone, a...  82.4 us
    dot_general x9, matrix products, product(): return jnp.dot(left, right, preferred_element_type=f32)  75.9 us
    dot_general x9, matrix products, against(): lax.dot_general(left, right, (((1,), (1,)), ((), ())), preferred_element_...  75.3 us
    ppermute x15, starting transfers between devices, line_scatter_sum(): lax.ppermute(up.astype(bf16), axis, [(i, i + 1) for i in range(step)])  72.9 us
    reduce_scatter x1, waiting for transfers between devices, local(): lax.psum_scatter(d_down, 'dp', scatter_dimension=0, tiled=True).astype(f32)  64.5 us
    ppermute x15, waiting for transfers between devices, line_scatter_sum(): lax.ppermute(up.astype(bf16), axis, [(i, i + 1) for i in range(step)])  61.7 us
  transfers between devices with their start and end apart: 81, of which 31 were waited for; matrix products, arithmetic and copies ran while one was open for 24% of the time, Pallas kernels for 0%

profile of v1, /device:TPU:0, one launch (start us, length us, event | category | flops | bytes accessed | tf_op | source)
XLA Modules:
  0.0 1416.2 jit_solution(6645091355991819317)
XLA Ops:
  12.2 43.1 %all_to_all.50 = bf16[4,64,3,512]{3,1,2,0:T(8,128)(2,1)S(1)} all-to-all(bf16[4,64,3,512]{3,1,2,0:T(8,128)(2,1)S(1)} %copy.272), channel_id=1, replica_groups=mesh['dp'=8,'seq'=4] {'seq'}, dimensions={0} | all-to-all | bytes 1572864 | tf_op jit(solution)/shard_map/all_to_all | solution.py:202
  60.1 49.9 %all_to_all.51 = bf16[4,64,2,8,256]{4,3,2,1,0:T(8,128)(2,1)} all-to-all(bf16[4,64,2,8,256]{4,3,2,1,0:T(8,128)(2,1)S(1)} %maximum_bitcast_fusion), channel_id=1, replica_groups=mesh['dp'=8,'seq'=4] {'seq'}, dimensions={0} | all-to-all | bytes 4194304 | tf_op jit(solution)/shard_map/all_to_all | solution.py:207
  117.9 19.2 %collective-permute-done = bf16[256,2048]{1,0:T(8,128)(2,1)S(1)} collective-permute-done((bf16[256,2048]{1,0:T(8,128)(2,1)S(1)}, bf16[256,2048]{1,0:T(8,128)(2,1)S(1)}, u32[]{:S(2)}, u32[]{:S(2)}) %collective-permute-start) | collective-permute-done | bytes 1048608 | tf_op jit(solution)/shard_map/ppermute | solution.py:135
  138.9 82.4 %all-gather = bf16[32,64,4]{1,2,0:T(4,128)(2,1)S(1)} all-gather(bf16[1,64,4]{1,2,0:T(4,128)(2,1)S(1)} %maximum_bitcast_fusion.4), channel_id=1, replica_groups=mesh['dp'=8,'seq'=4] {'dp','seq'}, dimensions={0}, use_global_device_ids=true | all-gather | bytes 16896 | tf_op jit(solution)/shard_map/all_gather | solution.py:216
  227.6 17.5 %collective-permute-done.4 = bf16[256,2048]{1,0:T(8,128)(2,1)S(1)} collective-permute-done((bf16[256,2048]{1,0:T(8,128)(2,1)}, bf16[256,2048]{1,0:T(8,128)(2,1)S(1)}, u32[]{:S(2)}, u32[]{:S(2)}) %collective-permute-start.4) | collective-permute-done | bytes 1048608 | tf_op jit(solution)/shard_map/ppermute | solution.py:136
  248.9 17.7 %collective-permute-done.5 = bf16[256,2048]{1,0:T(8,128)(2,1)S(1)} collective-permute-done((bf16[256,2048]{1,0:T(8,128)(2,1)S(1)}, bf16[256,2048]{1,0:T(8,128)(2,1)S(1)}, u32[]{:S(2)}, u32[]{:S(2)}) %collective-permute-start.5) | collective-permute-done | bytes 1048608 | tf_op jit(solution)/shard_map/ppermute | solution.py:136
  271.8 8.8 copy.274
  280.6 11.2 fusion.156
  300.3 5.9 copy.275
  329.9 8.0 reduce.23
  344.0 17.6 %all-to-all-done.1 = bf16[4,2,65536]{2,1,0:T(2,128)(2,1)S(1)} async-done(((bf16[4,2,65536]{2,1,0:T(2,128)(2,1)}), bf16[4,2,65536]{2,1,0:T(2,128)(2,1)S(1)}, u32[]{:S(2)}, u32[]{:S(2)}) %all-to-all-start.1) | async-done | bytes 1048608 | tf_op jit(solution)/shard_map/all_to_all | solution.py:238
  379.9 7.8 collective-permute-done.10
  390.0 12.1 collective-permute-done.11
  424.5 10.6 collective-permute-done.22
  437.6 13.2 collective-permute-done.23
  452.7 9.1 collective-permute-done.24
  465.3 10.3 fusion.16
  475.6 9.9 multiply_convert_fusion.7
  485.5 8.6 convolution_convert_fusion.7
  496.6 10.0 fusion.14
  506.7 11.5 multiply_convert_fusion.6
  527.5 9.3 collective-permute-done.27
  542.4 5.6 collective-permute-done.16
  549.7 5.0 collective-permute-start.17
  559.2 5.3 collective-permute-start.29
  564.9 9.2 collective-permute-done.32
  580.8 5.0 collective-permute-start.33
  585.9 6.2 collective-permute-done.34
  594.1 9.1 collective-permute-done.35
  605.2 11.8 collective-permute-done.36
  626.5 14.0 multiply_convert_fusion.5
  641.9 7.8 fusion.4
  655.8 8.4 add_convert_fusion.1
  665.4 7.2 collective-permute-start.39
  679.3 14.0 multiply_convert_fusion.3
  693.2 7.8 fusion.2
  701.0 8.6 add_convert_fusion
  719.1 8.9 collective-permute-start.52
  731.7 12.2 collective-permute-start.41
  745.7 8.3 collective-permute-start.53
  754.0 4.9 collective-permute-done.56
  771.5 11.6 reduce.24
  786.6 5.2 all-to-all-start.3
  792.7 15.1 %all-to-all-done.3 = bf16[4,2,65536]{2,1,0:T(2,128)(2,1)} async-done(((bf16[4,2,65536]{2,1,0:T(2,128)(2,1)}), bf16[4,2,65536]{2,1,0:T(2,128)(2,1)}, u32[]{:S(2)}, u32[]{:S(2)}) %all-to-all-start.3) | async-done | bytes 1048608 | tf_op jit(solution)/shard_map/all_to_all | solution.py:317
  842.2 5.4 copy.302
  856.9 5.9 fusion.74
  865.1 5.5 copy.300
  870.6 6.0 fusion.32
  877.9 9.3 convolution_convert_fusion.4
  888.8 12.0 convolution_convert_fusion.1
  900.8 10.9 convolution_convert_fusion.2
  911.7 7.6 pad_maximum_fusion
  921.2 5.6 convolution_convert_fusion.3
  929.0 13.8 convolution_convert_fusion
  944.8 8.9 convolution_convert_fusion.5
  960.6 18.0 %collective-permute-done.60 = bf16[256,2048]{1,0:T(8,128)(2,1)S(1)} collective-permute-done((bf16[256,2048]{1,0:T(8,128)(2,1)S(1)}, bf16[256,2048]{1,0:T(8,128)(2,1)S(1)}, u32[]{:S(2)}, u32[]{:S(2)}) %collective-permute-start.60) | collective-permute-done | bytes 1048608 | tf_op jit(solution)/shard_map/ppermute | solution.py:150
  985.1 18.2 %collective-permute-done.61 = bf16[256,2048]{1,0:T(8,128)(2,1)S(1)} collective-permute-done((bf16[256,2048]{1,0:T(8,128)(2,1)S(1)}, bf16[256,2048]{1,0:T(8,128)(2,1)S(1)}, u32[]{:S(2)}, u32[]{:S(2)}) %collective-permute-start.61) | collective-permute-done | bytes 1048608 | tf_op jit(solution)/shard_map/ppermute | solution.py:150
  1011.4 8.0 all-to-all-start.4
  1024.0 57.2 %reduce-scatter.15.cloned.1.call-done = bf16[256,4096]{0,1:T(8,128)(2,1)} async-done(((bf16[2048,4096]{0,1:T(8,128)(2,1)}), bf16[256,4096]{0,1:T(8,128)(2,1)}) %reduce-scatter.15.cloned.1.call-update) | async-done | bytes 2097168 | tf_op jit(solution)/shard_map/reduce_scatter | solution.py:304
  1090.9 5.0 collective-permute-start.62
  1100.5 55.9 %reduce-scatter.11.cloned.1.call-done = bf16[256,2048]{1,0:T(8,128)(2,1)} async-done(((bf16[2048,2048]{1,0:T(8,128)(2,1)}), bf16[256,2048]{1,0:T(8,128)(2,1)}) %reduce-scatter.11.cloned.1.call-update) | async-done | bytes 1048592 | tf_op jit(solution)/shard_map/reduce_scatter | solution.py:310
  1158.5 135.4 %reduce-scatter.19.cloned.1.call-done = f32[64,4]{1,0:T(8,128)} async-done(((f32[2048,4]{1,0:T(8,128)}), f32[64,4]{1,0:T(8,128)}) %reduce-scatter.19.cloned.1.call-update) | async-done | bytes 1040
  1301.1 64.5 %reduce-scatter.17.cloned.1.call-done = bf16[256,2048]{1,0:T(8,128)(2,1)} async-done(((bf16[2048,2048]{1,0:T(8,128)(2,1)}), bf16[256,2048]{1,0:T(8,128)(2,1)}) %reduce-scatter.17.cloned.1.call-update) | async-done | bytes 1048592 | tf_op jit(solution)/shard_map/reduce_scatter | solution.py:303
  1372.6 22.4 %reduce-scatter.13.cloned.1.call-done = bf16[64,2048]{1,0:T(8,128)(2,1)} async-done(((bf16[256,2048]{1,0:T(8,128)(2,1)}), bf16[64,2048]{1,0:T(8,128)(2,1)}) %reduce-scatter.13.cloned.1.call-update) | async-done | bytes 262160 | tf_op jit(solution)/shard_map/reduce_scatter | solution.py:309
  (510 shorter events, 338.8 us)
Async XLA Ops:
  7.2 50.0 %all-gather.9.cloned.1.call-start = ((), (), s32[]{:S(2)}) async-start(), calls=%async_computation.13 | async-start | bytes 1310720 | tf_op jit(solution)/shard_map/all_gather | solution.py:214
  7.9 263.9 %all-gather.7.cloned.1.call-start = ((), (), s32[]{:S(2)}) async-start(), calls=%async_computation.12 | async-start | bytes 7077888 | tf_op jit(solution)/shard_map/all_gather | solution.py:205
  57.1 310.0 %all-gather.11.cloned.1.call-start = ((), (), s32[]{:S(2)}) async-start(), calls=%async_computation.14 | async-start | bytes 9437184 | tf_op jit(solution)/shard_map/all_gather | solution.py:213
  57.8 407.4 %all-gather.13.cloned.1.call-start = ((), (), s32[]{:S(2)}) async-start(), calls=%async_computation.15 | async-start | bytes 18874368 | tf_op jit(solution)/shard_map/all_gather | solution.py:210
  114.4 371.1 %all-gather.15.cloned.1.call-start = ((), (), s32[]{:S(2)}) async-start(), calls=%async_computation.16 | async-start | bytes 9437184 | tf_op jit(solution)/shard_map/all_gather | solution.py:212
  114.5 22.7 %collective-permute-start = (bf16[256,2048]{1,0:T(8,128)(2,1)S(1)}, bf16[256,2048]{1,0:T(8,128)(2,1)S(1)}, u32[]{:S(2)}, u32[]{:S(2)}) collective-permute-start(bf16[256,2048]{1,0:T(8,128)(2,1)S(1)} %bitcast.315), channel_id=1, source_target_pairs={{0,1},{1,2},{2,3},{4,5},{5,6},{6,7},{8,9},{9,10},{10,11},{12,13},{... | collective-permute-start | bytes 3145736 | tf_op jit(solution)/shard_map/ppermute | solution.py:135
  116.6 105.0 %collective-permute-start.3 = (bf16[256,2048]{1,0:T(8,128)(2,1)S(1)}, bf16[256,2048]{1,0:T(8,128)(2,1)}, u32[]{:S(2)}, u32[]{:S(2)}) collective-permute-start(bf16[256,2048]{1,0:T(8,128)(2,1)S(1)} %bitcast.316), channel_id=1, source_target_pairs={{1,0},{2,1},{3,2},{5,4},{6,5},{7,6},{9,8},{10,9},{11,10},{13,12},{... | collective-permute-start | bytes 3145736 | tf_op jit(solution)/shard_map/ppermute | solution.py:136
  137.1 85.8 %collective-permute-start.1 = (bf16[256,2048]{1,0:T(8,128)(2,1)S(1)}, bf16[256,2048]{1,0:T(8,128)(2,1)}, u32[]{:S(2)}, u32[]{:S(2)}) collective-permute-start(bf16[256,2048]{1,0:T(8,128)(2,1)S(1)} %collective-permute-done), channel_id=1, source_target_pairs={{1,2},{2,3},{5,6},{6,7},{9,10},{10,11},{13,14},{14,15},{17,18},{18... | collective-permute-start | bytes 3145736 | tf_op jit(solution)/shard_map/ppermute | solution.py:135
  221.7 23.4 %collective-permute-start.4 = (bf16[256,2048]{1,0:T(8,128)(2,1)}, bf16[256,2048]{1,0:T(8,128)(2,1)S(1)}, u32[]{:S(2)}, u32[]{:S(2)}) collective-permute-start(bf16[256,2048]{1,0:T(8,128)(2,1)} %collective-permute-done.3), channel_id=1, source_target_pairs={{1,0},{2,1},{5,4},{6,5},{9,8},{10,9},{13,12},{14,13},{17,16},{18,1... | collective-permute-start | bytes 3145736 | tf_op jit(solution)/shard_map/ppermute | solution.py:136
  223.0 23.9 %collective-permute-start.2 = (bf16[256,2048]{1,0:T(8,128)(2,1)}, bf16[256,2048]{1,0:T(8,128)(2,1)S(1)}, u32[]{:S(2)}, u32[]{:S(2)}) collective-permute-start(bf16[256,2048]{1,0:T(8,128)(2,1)} %collective-permute-done.1), channel_id=1, source_target_pairs={{2,3},{6,7},{10,11},{14,15},{18,19},{22,23},{26,27},{30,31}} | collective-permute-start | bytes 3145736 | tf_op jit(solution)/shard_map/ppermute | solution.py:135
  245.1 21.4 %collective-permute-start.5 = (bf16[256,2048]{1,0:T(8,128)(2,1)S(1)}, bf16[256,2048]{1,0:T(8,128)(2,1)S(1)}, u32[]{:S(2)}, u32[]{:S(2)}) collective-permute-start(bf16[256,2048]{1,0:T(8,128)(2,1)S(1)} %collective-permute-done.4), channel_id=1, source_target_pairs={{1,0},{5,4},{9,8},{13,12},{17,16},{21,20},{25,24},{29,28}} | collective-permute-start | bytes 3145736 | tf_op jit(solution)/shard_map/ppermute | solution.py:136
  339.9 21.7 %all-to-all-start.1 = ((bf16[4,2,65536]{2,1,0:T(2,128)(2,1)}), bf16[4,2,65536]{2,1,0:T(2,128)(2,1)S(1)}, u32[]{:S(2)}, u32[]{:S(2)}) async-start(bf16[4,2,65536]{2,1,0:T(2,128)(2,1)} %reshape.911), calls=%async_computation.1 | async-start | bytes 2097152 | tf_op jit(solution)/shard_map/all_to_all | solution.py:238
  374.0 13.7 collective-permute-start.10
  375.3 14.0 collective-permute-start.9
  387.7 14.4 %collective-permute-start.11 = (bf16[128,2048]{1,0:T(8,128)(2,1)S(1)}, bf16[128,2048]{1,0:T(8,128)(2,1)}, u32[]{:S(2)}, u32[]{:S(2)}) collective-permute-start(bf16[128,2048]{1,0:T(8,128)(2,1)S(1)} %collective-permute-done.10), channel_id=1, source_target_pairs={{1,0},{2,1},{5,4},{6,5},{9,8},{10,9},{13,12},{14,13},{17,16},{18,1... | collective-permute-start | bytes 1572872 | tf_op jit(solution)/shard_map/ppermute | solution.py:136
  389.3 19.4 %collective-permute-start.13 = (bf16[128,2048]{1,0:T(8,128)(2,1)S(1)}, bf16[128,2048]{1,0:T(8,128)(2,1)S(1)}, u32[]{:S(2)}, u32[]{:S(2)}) collective-permute-start(bf16[128,2048]{1,0:T(8,128)(2,1)S(1)} %collective-permute-done.9), channel_id=1, source_target_pairs={{1,2},{2,3},{5,6},{6,7},{9,10},{10,11},{13,14},{14,15},{17,18},{18... | collective-permute-start | bytes 1572872 | tf_op jit(solution)/shard_map/ppermute | solution.py:135
  418.7 16.5 %collective-permute-start.22 = (bf16[128,2048]{1,0:T(8,128)(2,1)S(1)}, bf16[128,2048]{1,0:T(8,128)(2,1)S(1)}, u32[]{:S(2)}, u32[]{:S(2)}) collective-permute-start(bf16[128,2048]{1,0:T(8,128)(2,1)S(1)} %get-tuple-element.110), channel_id=1, source_target_pairs={{1,0},{2,1},{3,2},{5,4},{6,5},{7,6},{9,8},{10,9},{11,10},{13,12},{... | collective-permute-start | bytes 1572872 | tf_op jit(solution)/shard_map/ppermute | solution.py:136
  420.0 16.9 %collective-permute-start.21 = (bf16[128,2048]{1,0:T(8,128)(2,1)S(1)}, bf16[128,2048]{1,0:T(8,128)(2,1)S(1)}, u32[]{:S(2)}, u32[]{:S(2)}) collective-permute-start(bf16[128,2048]{1,0:T(8,128)(2,1)S(1)} %get-tuple-element.110), channel_id=1, source_target_pairs={{0,1},{1,2},{2,3},{4,5},{5,6},{6,7},{8,9},{9,10},{10,11},{12,13},{... | collective-permute-start | bytes 1572872 | tf_op jit(solution)/shard_map/ppermute | solution.py:135
  435.1 15.6 %collective-permute-start.23 = (bf16[128,2048]{1,0:T(8,128)(2,1)S(1)}, bf16[128,2048]{1,0:T(8,128)(2,1)S(1)}, u32[]{:S(2)}, u32[]{:S(2)}) collective-permute-start(bf16[128,2048]{1,0:T(8,128)(2,1)S(1)} %collective-permute-done.22), channel_id=1, source_target_pairs={{1,0},{2,1},{5,4},{6,5},{9,8},{10,9},{13,12},{14,13},{17,16},{18,1... | collective-permute-start | bytes 1572872 | tf_op jit(solution)/shard_map/ppermute | solution.py:136
  436.8 15.2 %collective-permute-start.25 = (bf16[128,2048]{1,0:T(8,128)(2,1)S(1)}, bf16[128,2048]{1,0:T(8,128)(2,1)S(1)}, u32[]{:S(2)}, u32[]{:S(2)}) collective-permute-start(bf16[128,2048]{1,0:T(8,128)(2,1)S(1)} %collective-permute-done.21), channel_id=1, source_target_pairs={{1,2},{2,3},{5,6},{6,7},{9,10},{10,11},{13,14},{14,15},{17,18},{18... | collective-permute-start | bytes 1572872 | tf_op jit(solution)/shard_map/ppermute | solution.py:135
  494.2 30.9 %collective-permute-start.15 = (bf16[128,2048]{1,0:T(8,128)(2,1)S(1)}, bf16[128,2048]{1,0:T(8,128)(2,1)S(1)}, u32[]{:S(2)}, u32[]{:S(2)}) collective-permute-start(bf16[128,2048]{1,0:T(8,128)(2,1)S(1)} %get-tuple-element.156), channel_id=1, source_target_pairs={{0,1},{4,5},{8,9},{12,13},{16,17},{20,21},{24,25},{28,29}} | collective-permute-start | bytes 1572872 | tf_op jit(solution)/shard_map/ppermute | solution.py:150
  495.7 29.4 %collective-permute-start.18 = (bf16[128,2048]{1,0:T(8,128)(2,1)S(1)}, bf16[128,2048]{1,0:T(8,128)(2,1)S(1)}, u32[]{:S(2)}, u32[]{:S(2)}) collective-permute-start(bf16[128,2048]{1,0:T(8,128)(2,1)S(1)} %get-tuple-element.157), channel_id=1, source_target_pairs={{3,2},{7,6},{11,10},{15,14},{19,18},{23,22},{27,26},{31,30}} | collective-permute-start | bytes 1572872 | tf_op jit(solution)/shard_map/ppermute | solution.py:151
  523.1 13.7 collective-permute-start.27
  525.4 22.6 %collective-permute-start.16 = (bf16[128,2048]{1,0:T(8,128)(2,1)S(1)}, bf16[128,2048]{1,0:T(8,128)(2,1)S(1)}, u32[]{:S(2)}, u32[]{:S(2)}) collective-permute-start(bf16[128,2048]{1,0:T(8,128)(2,1)S(1)} %get-tuple-element.154), channel_id=1, source_target_pairs={{0,1},{1,2},{4,5},{5,6},{8,9},{9,10},{12,13},{13,14},{16,17},{17,1... | collective-permute-start | bytes 1572872 | tf_op jit(solution)/shard_map/ppermute | solution.py:150
  526.8 21.2 %collective-permute-start.19 = (bf16[128,2048]{1,0:T(8,128)(2,1)S(1)}, bf16[128,2048]{1,0:T(8,128)(2,1)S(1)}, u32[]{:S(2)}, u32[]{:S(2)}) collective-permute-start(bf16[128,2048]{1,0:T(8,128)(2,1)S(1)} %get-tuple-element.155), channel_id=1, source_target_pairs={{2,1},{3,2},{6,5},{7,6},{10,9},{11,10},{14,13},{15,14},{18,17},{19... | collective-permute-start | bytes 1572872 | tf_op jit(solution)/shard_map/ppermute | solution.py:151
  537.1 20.4 %collective-permute-start.28 = (bf16[128,2048]{1,0:T(8,128)(2,1)S(1)}, bf16[128,2048]{1,0:T(8,128)(2,1)S(1)}, u32[]{:S(2)}, u32[]{:S(2)}) collective-permute-start(bf16[128,2048]{1,0:T(8,128)(2,1)S(1)} %get-tuple-element.160), channel_id=1, source_target_pairs={{0,1},{1,2},{4,5},{5,6},{8,9},{9,10},{12,13},{13,14},{16,17},{17,1... | collective-permute-start | bytes 1572872 | tf_op jit(solution)/shard_map/ppermute | solution.py:150
  541.5 16.0 %collective-permute-start.31 = (bf16[128,2048]{1,0:T(8,128)(2,1)S(1)}, bf16[128,2048]{1,0:T(8,128)(2,1)S(1)}, u32[]{:S(2)}, u32[]{:S(2)}) collective-permute-start(bf16[128,2048]{1,0:T(8,128)(2,1)S(1)} %get-tuple-element.161), channel_id=1, source_target_pairs={{2,1},{3,2},{6,5},{7,6},{10,9},{11,10},{14,13},{15,14},{18,17},{19... | collective-permute-start | bytes 1572872 | tf_op jit(solution)/shard_map/ppermute | solution.py:151
  548.4 16.1 %collective-permute-start.20 = (bf16[128,2048]{1,0:T(8,128)(2,1)S(1)}, bf16[128,2048]{1,0:T(8,128)(2,1)S(1)}, u32[]{:S(2)}, u32[]{:S(2)}) collective-permute-start(bf16[128,2048]{1,0:T(8,128)(2,1)S(1)} %get-tuple-element.153), channel_id=1, source_target_pairs={{1,0},{2,1},{3,2},{5,4},{6,5},{7,6},{9,8},{10,9},{11,10},{13,12},{... | collective-permute-start | bytes 1572872 | tf_op jit(solution)/shard_map/ppermute | solution.py:151
  549.7 14.8 %collective-permute-start.17 = (bf16[128,2048]{1,0:T(8,128)(2,1)S(1)}, bf16[128,2048]{1,0:T(8,128)(2,1)S(1)}, u32[]{:S(2)}, u32[]{:S(2)}) collective-permute-start(bf16[128,2048]{1,0:T(8,128)(2,1)S(1)} %get-tuple-element.152), channel_id=1, source_target_pairs={{0,1},{1,2},{2,3},{4,5},{5,6},{6,7},{8,9},{9,10},{10,11},{12,13},{... | collective-permute-start | bytes 1572872 | tf_op jit(solution)/shard_map/ppermute | solution.py:150
  557.9 16.2 %collective-permute-start.32 = (bf16[128,2048]{1,0:T(8,128)(2,1)S(1)}, bf16[128,2048]{1,0:T(8,128)(2,1)S(1)}, u32[]{:S(2)}, u32[]{:S(2)}) collective-permute-start(bf16[128,2048]{1,0:T(8,128)(2,1)S(1)} %get-tuple-element.159), channel_id=1, source_target_pairs={{1,0},{2,1},{3,2},{5,4},{6,5},{7,6},{9,8},{10,9},{11,10},{13,12},{... | collective-permute-start | bytes 1572872 | tf_op jit(solution)/shard_map/ppermute | solution.py:151
  559.2 16.7 %collective-permute-start.29 = (bf16[128,2048]{1,0:T(8,128)(2,1)S(1)}, bf16[128,2048]{1,0:T(8,128)(2,1)S(1)}, u32[]{:S(2)}, u32[]{:S(2)}) collective-permute-start(bf16[128,2048]{1,0:T(8,128)(2,1)S(1)} %get-tuple-element.158), channel_id=1, source_target_pairs={{0,1},{1,2},{2,3},{4,5},{5,6},{6,7},{8,9},{9,10},{10,11},{12,13},{... | collective-permute-start | bytes 1572872 | tf_op jit(solution)/shard_map/ppermute | solution.py:150
  603.2 13.8 collective-permute-start.36
  604.5 14.4 %collective-permute-start.38 = (bf16[128,2048]{1,0:T(8,128)(2,1)S(1)}, bf16[128,2048]{1,0:T(8,128)(2,1)S(1)}, u32[]{:S(2)}, u32[]{:S(2)}) collective-permute-start(bf16[128,2048]{1,0:T(8,128)(2,1)S(1)} %collective-permute-done.37), channel_id=1, source_target_pairs={{2,3},{6,7},{10,11},{14,15},{18,19},{22,23},{26,27},{30,31}} | collective-permute-start | bytes 1572872 | tf_op jit(solution)/shard_map/ppermute | solution.py:135
  623.0 26.6 %collective-permute-start.45 = (bf16[128,2048]{1,0:T(8,128)(2,1)}, bf16[128,2048]{1,0:T(8,128)(2,1)}, u32[]{:S(2)}, u32[]{:S(2)}) collective-permute-start(bf16[128,2048]{1,0:T(8,128)(2,1)} %get-tuple-element.94), channel_id=1, source_target_pairs={{0,1},{1,2},{2,3},{4,5},{5,6},{6,7},{8,9},{9,10},{10,11},{12,13},{... | collective-permute-start | bytes 1572872 | tf_op jit(solution)/shard_map/ppermute | solution.py:135
  625.3 15.3 %collective-permute-start.46 = (bf16[128,2048]{1,0:T(8,128)(2,1)}, bf16[128,2048]{1,0:T(8,128)(2,1)}, u32[]{:S(2)}, u32[]{:S(2)}) collective-permute-start(bf16[128,2048]{1,0:T(8,128)(2,1)} %get-tuple-element.94), channel_id=1, source_target_pairs={{1,0},{2,1},{3,2},{5,4},{6,5},{7,6},{9,8},{10,9},{11,10},{13,12},{... | collective-permute-start | bytes 1572872 | tf_op jit(solution)/shard_map/ppermute | solution.py:136
  649.7 24.4 %collective-permute-start.49 = (bf16[128,2048]{1,0:T(8,128)(2,1)}, bf16[128,2048]{1,0:T(8,128)(2,1)S(1)}, u32[]{:S(2)}, u32[]{:S(2)}) collective-permute-start(bf16[128,2048]{1,0:T(8,128)(2,1)} %collective-permute-done.45), channel_id=1, source_target_pairs={{1,2},{2,3},{5,6},{6,7},{9,10},{10,11},{13,14},{14,15},{17,18},{18... | collective-permute-start | bytes 1572872 | tf_op jit(solution)/shard_map/ppermute | solution.py:135
  654.1 20.6 %collective-permute-start.48 = (bf16[128,2048]{1,0:T(8,128)(2,1)S(1)}, bf16[128,2048]{1,0:T(8,128)(2,1)S(1)}, u32[]{:S(2)}, u32[]{:S(2)}) collective-permute-start(bf16[128,2048]{1,0:T(8,128)(2,1)S(1)} %collective-permute-done.47), channel_id=1, source_target_pairs={{1,0},{5,4},{9,8},{13,12},{17,16},{21,20},{25,24},{29,28}} | collective-permute-start | bytes 1572872 | tf_op jit(solution)/shard_map/ppermute | solution.py:136
  665.4 46.8 %collective-permute-start.39 = (bf16[128,2048]{1,0:T(8,128)(2,1)}, bf16[128,2048]{1,0:T(8,128)(2,1)}, u32[]{:S(2)}, u32[]{:S(2)}) collective-permute-start(bf16[128,2048]{1,0:T(8,128)(2,1)} %get-tuple-element.144), channel_id=1, source_target_pairs={{0,1},{4,5},{8,9},{12,13},{16,17},{20,21},{24,25},{28,29}} | collective-permute-start | bytes 1572872 | tf_op jit(solution)/shard_map/ppermute | solution.py:150
  672.6 39.6 %collective-permute-start.42 = (bf16[128,2048]{1,0:T(8,128)(2,1)}, bf16[128,2048]{1,0:T(8,128)(2,1)}, u32[]{:S(2)}, u32[]{:S(2)}) collective-permute-start(bf16[128,2048]{1,0:T(8,128)(2,1)} %get-tuple-element.145), channel_id=1, source_target_pairs={{3,2},{7,6},{11,10},{15,14},{19,18},{23,22},{27,26},{31,30}} | collective-permute-start | bytes 1572872 | tf_op jit(solution)/shard_map/ppermute | solution.py:151
  713.7 16.3 %collective-permute-start.40 = (bf16[128,2048]{1,0:T(8,128)(2,1)S(1)}, bf16[128,2048]{1,0:T(8,128)(2,1)S(1)}, u32[]{:S(2)}, u32[]{:S(2)}) collective-permute-start(bf16[128,2048]{1,0:T(8,128)(2,1)S(1)} %get-tuple-element.142), channel_id=1, source_target_pairs={{0,1},{1,2},{4,5},{5,6},{8,9},{9,10},{12,13},{13,14},{16,17},{17,1... | collective-permute-start | bytes 1572872 | tf_op jit(solution)/shard_map/ppermute | solution.py:150
  715.1 15.0 %collective-permute-start.43 = (bf16[128,2048]{1,0:T(8,128)(2,1)S(1)}, bf16[128,2048]{1,0:T(8,128)(2,1)S(1)}, u32[]{:S(2)}, u32[]{:S(2)}) collective-permute-start(bf16[128,2048]{1,0:T(8,128)(2,1)S(1)} %get-tuple-element.143), channel_id=1, source_target_pairs={{2,1},{3,2},{6,5},{7,6},{10,9},{11,10},{14,13},{15,14},{18,17},{19... | collective-permute-start | bytes 1572872 | tf_op jit(solution)/shard_map/ppermute | solution.py:151
  719.1 24.8 %collective-permute-start.52 = (bf16[128,2048]{1,0:T(8,128)(2,1)S(1)}, bf16[128,2048]{1,0:T(8,128)(2,1)S(1)}, u32[]{:S(2)}, u32[]{:S(2)}) collective-permute-start(bf16[128,2048]{1,0:T(8,128)(2,1)S(1)} %get-tuple-element.148), channel_id=1, source_target_pairs={{0,1},{1,2},{4,5},{5,6},{8,9},{9,10},{12,13},{13,14},{16,17},{17,1... | collective-permute-start | bytes 1572872 | tf_op jit(solution)/shard_map/ppermute | solution.py:150
  728.0 15.9 %collective-permute-start.55 = (bf16[128,2048]{1,0:T(8,128)(2,1)S(1)}, bf16[128,2048]{1,0:T(8,128)(2,1)S(1)}, u32[]{:S(2)}, u32[]{:S(2)}) collective-permute-start(bf16[128,2048]{1,0:T(8,128)(2,1)S(1)} %get-tuple-element.149), channel_id=1, source_target_pairs={{2,1},{3,2},{6,5},{7,6},{10,9},{11,10},{14,13},{15,14},{18,17},{19... | collective-permute-start | bytes 1572872 | tf_op jit(solution)/shard_map/ppermute | solution.py:151
  730.4 23.6 %collective-permute-start.44 = (bf16[128,2048]{1,0:T(8,128)(2,1)S(1)}, bf16[128,2048]{1,0:T(8,128)(2,1)S(1)}, u32[]{:S(2)}, u32[]{:S(2)}) collective-permute-start(bf16[128,2048]{1,0:T(8,128)(2,1)S(1)} %get-tuple-element.141), channel_id=1, source_target_pairs={{1,0},{2,1},{3,2},{5,4},{6,5},{7,6},{9,8},{10,9},{11,10},{13,12},{... | collective-permute-start | bytes 1572872 | tf_op jit(solution)/shard_map/ppermute | solution.py:151
  731.7 22.3 %collective-permute-start.41 = (bf16[128,2048]{1,0:T(8,128)(2,1)S(1)}, bf16[128,2048]{1,0:T(8,128)(2,1)S(1)}, u32[]{:S(2)}, u32[]{:S(2)}) collective-permute-start(bf16[128,2048]{1,0:T(8,128)(2,1)S(1)} %get-tuple-element.140), channel_id=1, source_target_pairs={{0,1},{1,2},{2,3},{4,5},{5,6},{6,7},{8,9},{9,10},{10,11},{12,13},{... | collective-permute-start | bytes 1572872 | tf_op jit(solution)/shard_map/ppermute | solution.py:150
  744.4 14.5 %collective-permute-start.56 = (bf16[128,2048]{1,0:T(8,128)(2,1)S(1)}, bf16[128,2048]{1,0:T(8,128)(2,1)S(1)}, u32[]{:S(2)}, u32[]{:S(2)}) collective-permute-start(bf16[128,2048]{1,0:T(8,128)(2,1)S(1)} %get-tuple-element.147), channel_id=1, source_target_pairs={{1,0},{2,1},{3,2},{5,4},{6,5},{7,6},{9,8},{10,9},{11,10},{13,12},{... | collective-permute-start | bytes 1572872 | tf_op jit(solution)/shard_map/ppermute | solution.py:151
  745.7 14.9 %collective-permute-start.53 = (bf16[128,2048]{1,0:T(8,128)(2,1)S(1)}, bf16[128,2048]{1,0:T(8,128)(2,1)S(1)}, u32[]{:S(2)}, u32[]{:S(2)}) collective-permute-start(bf16[128,2048]{1,0:T(8,128)(2,1)S(1)} %get-tuple-element.146), channel_id=1, source_target_pairs={{0,1},{1,2},{2,3},{4,5},{5,6},{6,7},{8,9},{9,10},{10,11},{12,13},{... | collective-permute-start | bytes 1572872 | tf_op jit(solution)/shard_map/ppermute | solution.py:150
  786.6 21.3 %all-to-all-start.3 = ((bf16[4,2,65536]{2,1,0:T(2,128)(2,1)}), bf16[4,2,65536]{2,1,0:T(2,128)(2,1)}, u32[]{:S(2)}, u32[]{:S(2)}) async-start(bf16[4,2,65536]{2,1,0:T(2,128)(2,1)} %reshape.913), calls=%async_computation.3 | async-start | bytes 2097152 | tf_op jit(solution)/shard_map/all_to_all | solution.py:317
  791.8 215.8 %reduce-scatter.9.cloned.1.call-start = ((), (), s32[]{:S(2)}) async-start(), calls=%async_computation.17 | async-start | bytes 7077888 | tf_op jit(solution)/shard_map/reduce_scatter | solution.py:335
  854.8 15.7 %collective-permute-start.59 = (f32[1024,2]{0,1:T(2,128)S(1)}, f32[1024,2]{0,1:T(2,128)S(1)}, u32[]{:S(2)}, u32[]{:S(2)}) collective-permute-start(f32[1024,2]{0,1:T(2,128)S(1)} %fusion.35), channel_id=1, source_target_pairs={{0,3},{1,0},{2,1},{3,2},{4,7},{5,4},{6,5},{7,6},{8,11},{9,8},{10,9... | collective-permute-start | bytes 24584 | tf_op jit(solution)/shard_map/ppermute | solution.py:167
  856.3 14.3 %collective-permute-start.58 = (f32[1024,2]{0,1:T(2,128)S(1)}, f32[1024,2]{0,1:T(2,128)S(1)}, u32[]{:S(2)}, u32[]{:S(2)}) collective-permute-start(f32[1024,2]{0,1:T(2,128)S(1)} %fusion.35), channel_id=1, source_target_pairs={{0,2},{1,3},{2,0},{3,1},{4,6},{5,7},{6,4},{7,5},{8,10},{9,11},{10,... | collective-permute-start | bytes 24584 | tf_op jit(solution)/shard_map/ppermute | solution.py:167
  856.3 14.3 %collective-permute-start.57 = (f32[1024,2]{0,1:T(2,128)S(1)}, f32[1024,2]{0,1:T(2,128)S(1)}, u32[]{:S(2)}, u32[]{:S(2)}) collective-permute-start(f32[1024,2]{0,1:T(2,128)S(1)} %fusion.35), channel_id=1, source_target_pairs={{0,1},{1,2},{2,3},{3,0},{4,5},{5,6},{6,7},{7,4},{8,9},{9,10},{10,1... | collective-permute-start | bytes 24584 | tf_op jit(solution)/shard_map/ppermute | solution.py:167
  887.2 194.0 %reduce-scatter.15.cloned.1.call-start = ((), (), s32[]{:S(2)}) async-start(), calls=%async_computation.20 | async-start | bytes 18874368 | tf_op jit(solution)/shard_map/reduce_scatter | solution.py:304
  919.3 237.1 %reduce-scatter.11.cloned.1.call-start = ((), (), s32[]{:S(2)}) async-start(), calls=%async_computation.18 | async-start | bytes 9437184 | tf_op jit(solution)/shard_map/reduce_scatter | solution.py:310
  926.9 367.1 %reduce-scatter.19.cloned.1.call-start = ((), (), s32[]{:S(2)}) async-start(), calls=%async_computation.22 | async-start | bytes 1081344
  929.0 436.6 %reduce-scatter.17.cloned.1.call-start = ((), (), s32[]{:S(2)}) async-start(), calls=%async_computation.21 | async-start | bytes 9437184 | tf_op jit(solution)/shard_map/reduce_scatter | solution.py:303
  955.7 22.9 %collective-permute-start.60 = (bf16[256,2048]{1,0:T(8,128)(2,1)S(1)}, bf16[256,2048]{1,0:T(8,128)(2,1)S(1)}, u32[]{:S(2)}, u32[]{:S(2)}) collective-permute-start(bf16[256,2048]{1,0:T(8,128)(2,1)S(1)} %dynamic-slice_bitcast_fusion), channel_id=1, source_target_pairs={{0,1},{4,5},{8,9},{12,13},{16,17},{20,21},{24,25},{28,29}} | collective-permute-start | bytes 3145736 | tf_op jit(solution)/shard_map/ppermute | solution.py:150
  980.3 23.0 %collective-permute-start.61 = (bf16[256,2048]{1,0:T(8,128)(2,1)S(1)}, bf16[256,2048]{1,0:T(8,128)(2,1)S(1)}, u32[]{:S(2)}, u32[]{:S(2)}) collective-permute-start(bf16[256,2048]{1,0:T(8,128)(2,1)S(1)} %fusion.51), channel_id=1, source_target_pairs={{0,1},{1,2},{4,5},{5,6},{8,9},{9,10},{12,13},{13,14},{16,17},{17,1... | collective-permute-start | bytes 3145736 | tf_op jit(solution)/shard_map/ppermute | solution.py:150
  1011.4 74.7 %all-to-all-start.4 = ((bf16[4,64,3,512]{3,1,2,0:T(8,128)(2,1)}), bf16[4,64,3,512]{3,1,2,0:T(8,128)(2,1)S(1)}, u32[]{:S(2)}, u32[]{:S(2)}) async-start(bf16[4,64,3,512]{3,1,2,0:T(8,128)(2,1)} %copy.310), calls=%async_computation.5 | async-start | bytes 1572864 | tf_op jit(solution)/shard_map/all_to_all | solution.py:336
  1022.4 73.5 %collective-permute-start.64 = (bf16[256,2048]{1,0:T(8,128)(2,1)}, bf16[256,2048]{1,0:T(8,128)(2,1)}, u32[]{:S(2)}, u32[]{:S(2)}) collective-permute-start(bf16[256,2048]{1,0:T(8,128)(2,1)} %fusion.52), channel_id=1, source_target_pairs={{2,1},{3,2},{6,5},{7,6},{10,9},{11,10},{14,13},{15,14},{18,17},{19... | collective-permute-start | bytes 3145736 | tf_op jit(solution)/shard_map/ppermute | solution.py:151
  1086.1 310.7 %all-to-all-start.5 = ((bf16[4,64,2,8,256]{4,3,2,1,0:T(8,128)(2,1)}), bf16[4,64,2,8,256]{4,3,2,1,0:T(8,128)(2,1)}, u32[]{:S(2)}, u32[]{:S(2)}) async-start(bf16[4,64,2,8,256]{4,3,2,1,0:T(8,128)(2,1)} %bitcast.136), calls=%async_computation.9 | async-start | bytes 4194304 | tf_op jit(solution)/shard_map/all_to_all | solution.py:305
  1090.8 304.2 %reduce-scatter.13.cloned.1.call-start = ((), (), s32[]{:S(2)}) async-start(), calls=%async_computation.19 | async-start | bytes 1310720 | tf_op jit(solution)/shard_map/reduce_scatter | solution.py:309
  1090.9 206.4 %collective-permute-start.62 = (bf16[256,2048]{1,0:T(8,128)(2,1)}, bf16[256,2048]{1,0:T(8,128)(2,1)}, u32[]{:S(2)}, u32[]{:S(2)}) collective-permute-start(bf16[256,2048]{1,0:T(8,128)(2,1)} %get-tuple-element.121), channel_id=1, source_target_pairs={{0,1},{1,2},{2,3},{4,5},{5,6},{6,7},{8,9},{9,10},{10,11},{12,13},{... | collective-permute-start | bytes 3145736 | tf_op jit(solution)/shard_map/ppermute | solution.py:150
  1099.2 198.1 %collective-permute-start.65 = (bf16[256,2048]{1,0:T(8,128)(2,1)}, bf16[256,2048]{1,0:T(8,128)(2,1)}, u32[]{:S(2)}, u32[]{:S(2)}) collective-permute-start(bf16[256,2048]{1,0:T(8,128)(2,1)} %add_convert_fusion.2), channel_id=1, source_target_pairs={{1,0},{2,1},{3,2},{5,4},{6,5},{7,6},{9,8},{10,9},{11,10},{13,12},{... | collective-permute-start | bytes 3145736 | tf_op jit(solution)/shard_map/ppermute | solution.py:151
  (112 other events, 1940.3 us)
Sparse Core Ops, SparseCore 0:
  9.6 46.1 all-gather.8
  58.3 44.6 all-gather.6
  104.8 54.3 all-gather.10
  161.6 89.9 all-gather.12
  253.3 54.3 all-gather.14
  887.3 73.8 reduce-scatter.8
  965.2 115.9 reduce-scatter.14
  1085.1 71.2 reduce-scatter.10
  1158.6 135.2 reduce-scatter.18
  1297.7 67.8 reduce-scatter.16
  1367.9 27.1 reduce-scatter.12

commit v2 on v1

v2 whole, which is shorter than its diff:
```python
import jax
import jax.numpy as jnp
from jax import lax
from jax.sharding import PartitionSpec as P

H = 16
HD = 128
DOCS = 4

epsilon = 1e-06
rope_base = 500000.0
masked_score = -1e30
bf16 = jnp.bfloat16
f32 = jnp.float32


def product(left, right):
    return jnp.dot(left, right, preferred_element_type=f32)


def against(left, right):
    return lax.dot_general(left, right, (((1,), (1,)), ((), ())), preferred_element_type=f32)


def weight_grad(left, right):
    return lax.dot_general(left, right, (((0,), (0,)), ((), ())), preferred_element_type=f32)


def rms_scale(values):
    return lax.rsqrt(jnp.mean(values * values, -1, keepdims=True) + epsilon)


def norm_back(values, scale_rows, grad_vals):
    return scale_rows * grad_vals - values * scale_rows**3 * jnp.mean(
        grad_vals * values, -1, keepdims=True
    )


def positions(seg_ids):
    doc_ids = jnp.arange(DOCS, dtype=jnp.int32)
    starts = jnp.sum((seg_ids[..., None, :] < doc_ids[:, None]).astype(jnp.int32), -1)
    one_hot = (seg_ids[..., None] == doc_ids).astype(jnp.int32)
    token_start = jnp.sum(one_hot * starts[..., None, :], axis=-1)
    return jnp.arange(seg_ids.shape[-1], dtype=jnp.int32) - token_start


def rope_tables(position_ids):
    freqs = rope_base ** (-jnp.arange(HD // 2, dtype=f32) * 2.0 / HD)
    angles = position_ids.astype(f32)[..., None] * freqs
    cosine = jnp.cos(angles)
    sine_tab = jnp.sin(angles)
    return (
        jnp.concatenate([cosine, cosine], -1)[..., None, :],
        jnp.concatenate([sine_tab, sine_tab], -1)[..., None, :],
    )


def rotate(values):
    return jnp.concatenate([-values[..., HD // 2 :], values[..., : HD // 2]], -1)


def apply_rope(values, cosine, sine_tab):
    return values * cosine + rotate(values) * sine_tab


def rope_back(grad_vals, cosine, sine_tab):
    return grad_vals * cosine - rotate(grad_vals * sine_tab)


def mask_for(seg_ids, row_start, row_count):
    query_ids = row_start + jnp.arange(row_count)
    key_ids = jnp.arange(seg_ids.shape[0])
    same_doc = seg_ids[row_start : row_start + row_count, None] == seg_ids[None, :]
    return same_doc & (key_ids[None, :] <= query_ids[:, None])


def attend(query_vecs, key_vecs, value_vecs, seg_ids):
    length = query_vecs.shape[0]
    q_block = min(512, length)
    score_scale = HD ** (-0.5)
    outputs = []
    log_sums = []
    for row_start in range(0, length, q_block):
        seen = row_start + q_block
        q_part = query_vecs[row_start:seen]
        scores = (
            jnp.einsum("qhd,khd->hqk", q_part, key_vecs[:seen], preferred_element_type=f32)
            * score_scale
        )
        scores = jnp.where(mask_for(seg_ids, row_start, q_block)[None, :, :seen], scores, masked_score)
        row_max = jnp.max(scores, -1, keepdims=True)
        expos = jnp.exp(scores - row_max)
        row_total = jnp.sum(expos, -1, keepdims=True)
        attn_probs = (expos / row_total).astype(bf16)
        block_out = jnp.einsum("hqk,khd->qhd", attn_probs, value_vecs[:seen], preferred_element_type=f32)
        outputs.append(block_out.astype(bf16))
        log_sums.append((row_max + jnp.log(row_total))[..., 0])
    return (jnp.concatenate(outputs, 0), jnp.concatenate(log_sums, 1))


def attend_back(query_vecs, key_vecs, value_vecs, d_attended, seg_ids, log_totals):
    length = query_vecs.shape[0]
    q_block = min(512, length)
    score_scale = HD ** (-0.5)
    d_query_parts = []
    d_keys = jnp.zeros(key_vecs.shape, f32)
    d_values = jnp.zeros(value_vecs.shape, f32)
    for row_start in range(0, length, q_block):
        seen = row_start + q_block
        q_part = query_vecs[row_start:seen]
        g_part = d_attended[row_start:seen]
        k_part = key_vecs[:seen]
        scores = jnp.einsum("qhd,khd->hqk", q_part, k_part, preferred_element_type=f32) * score_scale
        scores = jnp.where(mask_for(seg_ids, row_start, q_block)[None, :, :seen], scores, masked_score)
        attn_probs = jnp.exp(scores - log_totals[:, row_start:seen, None])
        d_probs = jnp.einsum("qhd,khd->hqk", g_part, value_vecs[:seen], preferred_element_type=f32)
        inner_sum = jnp.sum(attn_probs * d_probs, -1, keepdims=True)
        d_scores = (attn_probs * (d_probs - inner_sum)).astype(bf16)
        d_query_parts.append(
            jnp.einsum("hqk,khd->qhd", d_scores, k_part, preferred_element_type=f32) * score_scale
        )
        d_k_part = jnp.einsum("hqk,qhd->khd", d_scores, q_part, preferred_element_type=f32) * score_scale
        d_v_part = jnp.einsum("hqk,qhd->khd", attn_probs.astype(bf16), g_part, preferred_element_type=f32)
        d_keys = d_keys.at[:seen].add(d_k_part)
        d_values = d_values.at[:seen].add(d_v_part)
    return (jnp.concatenate(d_query_parts, 0), d_keys, d_values)


def after(value, *done):
    ends = [lax.slice(d, (0,) * d.ndim, (1,) * d.ndim) for d in done]
    return lax.optimization_barrier((value, *ends))[0]


def next_one(block, axis):
    size = lax.axis_size(axis)
    return lax.ppermute(block, axis, [(i, (i + 1) % size) for i in range(size)])


def in_order(slots, axis):
    size, here = lax.axis_size(axis), lax.axis_index(axis)
    joined = jnp.zeros((size,) + slots[0].shape, slots[0].dtype)
    for back, slot in enumerate(slots):
        joined = lax.dynamic_update_index_in_dim(joined, slot, lax.rem(here + size - back, size), 0)
    return joined


def exchange(blocks, axis):
    size, here = lax.axis_size(axis), lax.axis_index(axis)
    got = []
    for step in range(size):
        block = lax.dynamic_index_in_dim(blocks, lax.rem(here + step, size), 0, keepdims=False)
        if step:
            block = lax.ppermute(block, axis, [(i, (i + step) % size) for i in range(size)])
        got.append(block)
    return got


def flipped(block, bit):
    size = lax.axis_size("dp")
    return lax.ppermute(block, "dp", [(i, i ^ bit) for i in range(size)])


def cube_bits():
    bits = [1 << b for b in range(1, (lax.axis_size("dp") - 1).bit_length())]
    return bits, bits[1:] + bits[:1]


class CubeGather:
    def __init__(self, pair):
        self.tables = [{0: block} for block in pair]
        self.orders = [bits + [1] for bits in cube_bits()]
        self.steps = len(self.orders[0])

    def step(self):
        got = []
        for table, order in zip(self.tables, self.orders):
            bit = order.pop(0)
            new = {m ^ bit: flipped(v, bit) for m, v in table.items()}
            table.update(new)
            got.extend(new.values())
        return got


def cube_rows(have):
    here, rows = lax.axis_index("dp"), have[0].shape[0]
    joined = jnp.zeros((len(have) * rows,) + have[0].shape[1:], have[0].dtype)
    for mask, block in have.items():
        joined = lax.dynamic_update_slice_in_dim(joined, block, (here ^ mask) * rows, 0)
    return joined


def cube_rows_halves(halves):
    here, rows = lax.axis_index("dp"), halves[0][0].shape[0]
    count = len(halves[0])
    joined = jnp.zeros((2 * count * rows,) + halves[0][0].shape[1:], halves[0][0].dtype)
    for at, have in enumerate(halves):
        for mask, block in have.items():
            joined = lax.dynamic_update_slice_in_dim(joined, block, ((here ^ mask) * 2 + at) * rows, 0)
    return joined


def split_columns(left):
    size, here = lax.axis_size("dp"), lax.axis_index("dp")
    block = left.shape[1] // size
    bits = (size - 1).bit_length()
    sides = []
    for side in (1, 0):
        masks = []
        for at in range(size // 2):
            mask = side
            for b in range(1, bits):
                mask |= ((at >> (bits - 1 - b)) & 1) << b
            masks.append(mask)
        sides.append(
            jnp.concatenate(
                [lax.dynamic_slice_in_dim(left, (here ^ m) * block, block, 1) for m in masks], 1
            )
        )
    return sides


def split_grad(sides, right):
    bits = (lax.axis_size("dp") - 1).bit_length()
    shape = (2,) * (bits - 1) + (-1, right.shape[1])
    return [weight_grad(side, right).astype(bf16).reshape(shape) for side in sides]


class CubeScatter:
    def __init__(self, pairs):
        self.pairs, self.orders = pairs, [list(bits) for bits in cube_bits()]
        self.dims = [sorted(bits) for bits in self.orders]
        self.totals = None
        self.steps = 1 + len(self.orders[0])

    def step(self, *done):
        if self.totals is None:
            got = [flipped(after(sent, *done) if done else sent, 1) for sent, _ in self.pairs]
            self.totals = [keep.astype(f32) + g.astype(f32) for (_, keep), g in zip(self.pairs, got)]
            return got
        got = []
        for which, total in enumerate(self.totals):
            bit = self.orders[which].pop(0)
            at = self.dims[which].index(bit)
            self.dims[which].remove(bit)
            away = lax.index_in_dim(total, 1, at, keepdims=False).astype(bf16)
            got.append(flipped(away, bit))
            self.totals[which] = lax.index_in_dim(total, 0, at, keepdims=False) + got[-1].astype(f32)
        return got


def halves_of(grad):
    cut = grad[0].shape[-1] // 2
    return [[g[..., :cut] for g in grad], [g[..., cut:] for g in grad]]


def gather_small(block):
    slots = in_order(exchange(jnp.broadcast_to(block, (lax.axis_size("seq"),) + block.shape), "seq"), "seq")
    block = slots.transpose(1, 0, 2).reshape(block.shape[0], -1)
    here, wide = lax.axis_index("dp"), block.shape[1]
    table = {0: block}
    for bit in cube_bits()[0] + [1]:
        table.update({m ^ bit: flipped(v, bit) for m, v in table.items()})
    joined = jnp.zeros((block.shape[0], wide * len(table)), block.dtype)
    for mask, piece in table.items():
        joined = lax.dynamic_update_slice_in_dim(joined, piece, (here ^ mask) * wide, 1)
    return joined


def scatter_small(values):
    copies, size, here = lax.axis_size("dp"), lax.axis_size("seq"), lax.axis_index("dp")
    blocks = values.reshape(values.shape[0], copies, size, -1).transpose(2, 1, 0, 3)
    total = sum(exchange(blocks, "seq"))
    for bit in reversed([1] + cube_bits()[0]):
        total = total.reshape((2, total.shape[0] // 2) + total.shape[1:])
        mine = (here // bit) % 2
        away = lax.dynamic_index_in_dim(total, 1 - mine, 0, keepdims=False)
        total = lax.dynamic_index_in_dim(total, mine, 0, keepdims=False) + flipped(away, bit)
    return total[0]


def small_sum(values, axis):
    size = lax.axis_size(axis)
    total = values
    for step in range(1, size):
        total = total + lax.ppermute(values, axis, [(i, (i + step) % size) for i in range(size)])
    return total


def local(
    tokens,
    segments,
    w_query,
    w_key,
    w_value,
    w_out,
    g_query,
    g_key,
    g_attn,
    w_gate,
    w_up,
    w_down,
    g_ffn,
    d_out,
):
    seqs, local_len, width = tokens.shape
    rows = seqs * local_len
    copies, size = lax.axis_size("dp"), lax.axis_size("seq")
    here = lax.axis_index("seq")
    total_len = size * local_len
    part = width // size
    heads = H // size
    own_rows = w_gate.shape[0]
    ff_width = w_gate.shape[1]
    ff_part = ff_width // size
    ff_own = w_down.shape[0]
    everyone = ("dp", "seq")
    tok_rows = tokens.reshape(rows, width)

    gains = gather_small(jnp.stack([g_query, g_key, g_attn, g_ffn], 0)).astype(f32)
    gain_attn, gain_ffn = gains[2], gains[3]
    gain_qk = lax.dynamic_slice_in_dim(gains[:2], here * part, part, 1).reshape(2, heads, HD)
    w_down_part = lax.all_gather(w_down, "dp", axis=0, tiled=True)
    w_out_all = lax.all_gather(w_out, everyone, axis=0, tiled=True)
    qkv_own = jnp.stack([w_query, w_key, w_value], 1).reshape(own_rows, 3, size, part)
    qkv_own = exchange(qkv_own.transpose(2, 0, 1, 3).reshape(size, own_rows, 3 * part), "seq")
    qkv_got = qkv_own[1:]
    qkv_own = in_order(qkv_own, "seq").reshape(size * own_rows, 3 * part)
    half = size * own_rows // 2
    cube_qkv = CubeGather([qkv_own[:half], qkv_own[half:]])
    for _ in range(cube_qkv.steps):
        cube_qkv.step()
    w_qkv = cube_rows_halves(cube_qkv.tables)

    def to_columns(weight, *done):
        blocks = weight.reshape(own_rows, copies, size, ff_own).transpose(2, 0, 1, 3)
        got = exchange(after(blocks.reshape(size, own_rows, ff_part), *done), "seq")
        return got[1:], in_order(got, "seq").reshape(size * own_rows, ff_part)

    gate_got, gate_own = to_columns(w_gate, *qkv_got)
    half_gate = [gate_own[:half], gate_own[half:]]
    cube_gate = CubeGather(half_gate)
    gate_done = [cube_gate.step()]
    x_slots = [tok_rows]
    for at in range(size - 1):
        block = x_slots[-1]
        if at == 0:
            block = after(block, *gate_got)
        if at == size - 2:
            block = after(block, *gate_done[0])
        x_slots.append(next_one(block, "seq"))
    for _ in range(cube_gate.steps - 1):
        gate_done.append(cube_gate.step())
    w_gate_part = cube_rows_halves(cube_gate.tables)
    up_got, up_own = to_columns(w_up, x_slots[-1])
    cube_up = CubeGather([up_own[:half], up_own[half:]])
    up_done = [cube_up.step() for _ in range(cube_up.steps)]
    w_up_part = cube_rows_halves(cube_up.tables)

    x_all = in_order([s.reshape(seqs, local_len, width) for s in x_slots], "seq")
    x_all = x_all.transpose(1, 0, 2, 3).reshape(seqs * total_len, width)
    qkv = product(after(x_all, w_down_part, *gate_done[-2]), w_qkv).reshape(seqs * total_len, 3, part)
    qk_raw = qkv[:, :2]
    squares = small_sum(jnp.sum(qk_raw * qk_raw, -1), "seq")
    qk_scale = lax.rsqrt(squares / width + epsilon)[..., None, None]
    qk_raw = qk_raw.reshape(seqs * total_len, 2, heads, HD)
    cosine, sine_tab = rope_tables(positions(segments).reshape(seqs * total_len))
    cosine, sine_tab = cosine[:, None], sine_tab[:, None]
    qk_unit = qk_raw * qk_scale
    qk_low = apply_rope(qk_unit * gain_qk, cosine, sine_tab).astype(bf16)
    head_shape = (seqs, total_len, heads, HD)
    qk_low = after(qk_low, *gate_done[-1], *up_got)
    query_low = qk_low[:, 0].reshape(head_shape)
    key_low = qk_low[:, 1].reshape(head_shape)
    value_low = qkv[:, 2].astype(bf16).reshape(head_shape)
    attended_heads, log_totals = jax.vmap(attend)(query_low, key_low, value_low, segments)
    attended_heads = after(attended_heads, w_out_all, *up_done[0])
    attended = lax.all_to_all(
        attended_heads.reshape(seqs, total_len, part), "seq", split_axis=1, concat_axis=2, tiled=True
    ).reshape(rows, width)
    attended = after(attended, *up_done[1])

    a_proj = product(attended, w_out_all)
    a_scale = rms_scale(a_proj)
    hidden = tok_rows.astype(f32) + a_proj * a_scale * gain_attn

    def ring(block, work):
        got, own = None, None
        for at in range(size):
            later = next_one(block, "seq") if at < size - 1 else None
            share = work(block)
            if at == 0:
                own = share
            else:
                if at > 1:
                    share = share + got.astype(f32)
                got = next_one(share.astype(bf16), "seq")
            block = later
        return own + got.astype(f32)

    h_slots, gates, ups, inners = [], [], [], []

    def forward(h_low):
        gate = product(h_low, w_gate_part)
        up = product(h_low, w_up_part)
        inner = (jax.nn.silu(gate) * up).astype(bf16)
        h_slots.append(h_low)
        gates.append(gate)
        ups.append(up)
        inners.append(inner)
        return product(inner, w_down_part)

    m_proj = ring(hidden.astype(bf16), forward)
    m_scale = rms_scale(m_proj)
    out = (hidden + m_proj * m_scale * gain_ffn).astype(bf16).reshape(tokens.shape)
    grad_out = d_out.reshape(rows, width).astype(f32)
    d_gain_ffn = jnp.sum(grad_out * m_proj * m_scale, 0)
    dm_low = norm_back(m_proj, m_scale, grad_out * gain_ffn).astype(bf16)
    dms, d_gates, d_ups = [], [], []

    def backward(dm_slot):
        at = len(dms)
        gate, up = gates[at], ups[at]
        d_inner = against(dm_slot, w_down_part)
        sigmoid_gate = jax.nn.sigmoid(gate)
        d_gate = (d_inner * up * sigmoid_gate * (1.0 + gate * (1.0 - sigmoid_gate))).astype(bf16)
        d_up = (d_inner * (gate * sigmoid_gate)).astype(bf16)
        dms.append(dm_slot)
        d_gates.append(d_gate)
        d_ups.append(d_up)
        return against(d_gate, w_gate_part) + against(d_up, w_up_part)

    d_sum = ring(dm_low, backward)
    d_down = weight_grad(jnp.concatenate(inners, 0), jnp.concatenate(dms, 0)).astype(bf16)
    h_sides = split_columns(jnp.concatenate(h_slots, 0))
    d_gate = split_grad(h_sides, jnp.concatenate(d_gates, 0))
    d_up = split_grad(h_sides, jnp.concatenate(d_ups, 0))
    d_hidden = grad_out + after(d_sum, d_down, *d_gate)
    d_gain_attn = jnp.sum(d_hidden * a_proj * a_scale, 0)
    da_low = norm_back(a_proj, a_scale, d_hidden * gain_attn).astype(bf16)
    d_attended = against(da_low, w_out_all).astype(bf16).reshape(seqs, local_len, width)
    d_attended = lax.all_to_all(d_attended, "seq", split_axis=2, concat_axis=1, tiled=True).reshape(head_shape)
    d_w_out = weight_grad(attended, da_low).astype(bf16)

    d_down = lax.psum_scatter(d_down, "dp", scatter_dimension=0, tiled=True).astype(f32)
    d_w_out = lax.psum_scatter(d_w_out, everyone, scatter_dimension=0, tiled=True).astype(f32)
    cube_gu = CubeScatter([d_gate, d_up])
    gu_done = [cube_gu.step() for _ in range(cube_gu.steps)]
    d_gu = jnp.stack(cube_gu.totals, 0).astype(bf16).reshape(2, size, own_rows, copies, ff_own)
    d_gu = lax.all_to_all(d_gu.transpose(1, 0, 2, 3, 4), "seq", split_axis=0, concat_axis=0, tiled=True)
    d_gu = d_gu.transpose(1, 2, 3, 0, 4).reshape(2, own_rows, ff_width).astype(f32)

    d_attended = after(d_attended, d_w_out, *gu_done[0])
    dq, dk, dv = jax.vmap(attend_back)(query_low, key_low, value_low, d_attended, segments, log_totals)
    d_qk = jnp.stack([dq, dk], 2).reshape(seqs * total_len, 2, heads, HD).astype(bf16)
    d_qk = after(d_qk, d_down, *gu_done[1]).astype(f32)
    d_qk = rope_back(d_qk, cosine, sine_tab)
    d_gain_qk = jnp.sum(d_qk * qk_unit, 0)
    d_qk = d_qk * gain_qk
    dots = small_sum(jnp.sum(d_qk * qk_raw, (-2, -1)), "seq")[..., None, None] / width
    d_qk = (qk_scale * d_qk - qk_raw * qk_scale**3 * dots).astype(bf16)
    d_qkv = jnp.concatenate(
        [d_qk.reshape(seqs * total_len, 2 * part), dv.astype(bf16).reshape(seqs * total_len, part)], 1
    )
    d_qkv = after(d_qkv, *gu_done[-1])
    x_share = against(d_qkv, w_qkv).astype(bf16).reshape(seqs, size, local_len, width)
    x_share = [
        lax.dynamic_index_in_dim(x_share, lax.rem(here + size - o, size), 1, keepdims=False).reshape(rows, width)
        for o in range(size)
    ]
    got = next_one(x_share[1], "seq")
    for o in range(2, size):
        got = next_one((x_share[o].astype(f32) + got.astype(f32)).astype(bf16), "seq")
    d_tokens = d_hidden + x_share[0].astype(f32) + got.astype(f32)
    cube_qkv = CubeScatter(halves_of(split_grad(split_columns(x_all), d_qkv)))
    for _ in range(cube_qkv.steps):
        cube_qkv.step()
    d_w_qkv = jnp.concatenate(cube_qkv.totals, 1).astype(bf16)
    d_w_qkv = in_order(exchange(d_w_qkv.reshape(size, own_rows, 3 * part), "seq"), "seq")
    d_w_qkv = d_w_qkv.reshape(size, own_rows, 3, part).transpose(2, 1, 0, 3).reshape(3, own_rows, width).astype(f32)

    d_gain_qk = lax.dynamic_update_slice_in_dim(
        jnp.zeros((2, width), f32), d_gain_qk.reshape(2, part), here * part, 1
    )
    d_gains = scatter_small(jnp.concatenate([d_gain_qk, d_gain_attn[None], d_gain_ffn[None]], 0))
    return (
        out,
        d_tokens.reshape(tokens.shape),
        d_w_qkv[0],
        d_w_qkv[1],
        d_w_qkv[2],
        d_w_out,
        d_gains[0],
        d_gains[1],
        d_gains[2],
        d_gu[0],
        d_gu[1],
        d_down,
        d_gains[3],
    )


def solution(mesh):
    rows = P("dp", "seq", None)
    mat = P(("dp", "seq"), None)
    vec = P(("dp", "seq"))
    in_specs = (rows, P("dp", None), mat, mat, mat, mat, vec, vec, vec, mat, mat, mat, vec, rows)
    out_specs = (rows, rows, mat, mat, mat, mat, vec, vec, vec, mat, mat, mat, vec)
    return jax.shard_map(local, mesh=mesh, in_specs=in_specs, out_specs=out_specs, check_vma=False)
```

time: 1430 us -> 1150 us (0.80)
  blocking collectives: 175 us -> 0 us
  waiting for transfers between devices: 588 us -> 513 us
  starting transfers between devices: 163 us -> 131 us
  other arithmetic: 127 us -> 98 us
  local copies, waits for them, and re-layouts: 117 us -> 144 us
    ppermute x60 -> x100, waiting for transfers between devices: 218 us -> 506 us  [the longest x64 204 us: flipped(): return lax.ppermute(block, 'dp', [(i, i ^ bit) for i in range(size)])]
    unnamed x12 -> x4, waiting for transfers between devices: 137 us -> 0.73 us
    reduce_scatter x4 -> x1, waiting for transfers between devices: 136 us -> 0.01 us  [local(): lax.psum_scatter(d_w_out, everyone, scatter_dimension=0, tiled=True)]
    all_to_all x2 -> x0, blocking collectives: 93 us -> none  [the longest x1 49.9 us: local(): lax.all_to_all(gu_own.transpose(3, 0, 1, 2, 4), 'seq', split_axis=0, conc...]
    all_gather x1 -> x0, blocking collectives: 82.4 us -> none  [local(): lax.all_gather(jnp.stack([g_query, g_key, g_attn, g_ffn], 0), everyone, a...]
    reduce_scatter x1, waiting for transfers between devices: 64.5 us -> 0.01 us  [local(): lax.psum_scatter(d_down, 'dp', scatter_dimension=0, tiled=True).astype(f32)]
    dynamic_update_slice x0 -> x76, local copies, waits for them, and re-layouts: none -> 45.8 us  [the longest x48 35.8 us: cube_rows_halves(): lax.dynamic_update_slice_in_dim(joined, block, ((here ^ mask) * 2 + at) *...]
    ppermute x60 -> x100, starting transfers between devices: 137 us -> 113 us  [the longest x64 47.9 us: flipped(): return lax.ppermute(block, 'dp', [(i, i ^ bit) for i in range(size)])]
  transfers between devices with their start and end apart: 81 -> 113, of which waited for: 31 -> 46; matrix products, arithmetic and copies ran while one was open for 24% -> 39% of each run, Pallas kernels for 0% -> 0%
where the time goes in v2:
time: 1150 us; the launch traced here: 1140 us
  waiting for transfers between devices  513 us (45%)
  matrix products  233 us (20%)
  local copies, waits for them, and re-layouts  144 us (13%)
  starting transfers between devices  131 us (11%)
  other arithmetic  98 us (9%)
  between operations  17.4 us (2%)
    ppermute x64, waiting for transfers between devices, flipped(): return lax.ppermute(block, 'dp', [(i, i ^ bit) for i in range(size)])  204 us
    ppermute x18, waiting for transfers between devices, next_one(): return lax.ppermute(block, axis, [(i, (i + 1) % size) for i in range(size)])  198 us
    ppermute x18, waiting for transfers between devices, exchange(): lax.ppermute(block, axis, [(i, (i + step) % size) for i in range(size)])  104 us
    dot_general x14, matrix products, against(): lax.dot_general(left, right, (((1,), (1,)), ((), ())), preferred_element_...  85.3 us
    dot_general x14, matrix products, product(): return jnp.dot(left, right, preferred_element_type=f32)  71.6 us
    dot_general x8, matrix products, weight_grad(): lax.dot_general(left, right, (((0,), (0,)), ((), ())), preferred_element_...  56.6 us
    ppermute x64, starting transfers between devices, flipped(): return lax.ppermute(block, 'dp', [(i, i ^ bit) for i in range(size)])  47.9 us
    ppermute x18, starting transfers between devices, exchange(): lax.ppermute(block, axis, [(i, (i + step) % size) for i in range(size)])  45.4 us
  transfers between devices with their start and end apart: 113, of which 46 were waited for; matrix products, arithmetic and copies ran while one was open for 39% of the time, Pallas kernels for 0%

profile of v2, /device:TPU:0, one launch (start us, length us, event | category | flops | bytes accessed | tf_op | source)
XLA Modules:
  0.0 1135.9 jit_solution(8893205594893064846)
XLA Ops:
  65.0 5.1 collective-permute-start.35
  71.5 9.5 collective-permute-start.50
  84.3 7.3 collective-permute-start.51
  91.7 18.5 %collective-permute-done.34 = bf16[64,2048]{1,0:T(8,128)(2,1)S(1)} collective-permute-done((bf16[64,2048]{1,0:T(8,128)(2,1)}, bf16[64,2048]{1,0:T(8,128)(2,1)S(1)}, u32[]{:S(2)}, u32[]{:S(2)}) %collective-permute-start.34) | collective-permute-done | bytes 262176 | tf_op jit(solution)/shard_map/ppermute | solution.py:153
  114.5 23.0 %collective-permute-done.51 = bf16[64,2048]{1,0:T(8,128)(2,1)S(1)} collective-permute-done((bf16[64,2048]{1,0:T(8,128)(2,1)S(1)}, bf16[64,2048]{1,0:T(8,128)(2,1)S(1)}, u32[]{:S(2)}, u32[]{:S(2)}) %collective-permute-start.51) | collective-permute-done | bytes 262176 | tf_op jit(solution)/shard_map/ppermute | solution.py:153
  154.8 12.7 %collective-permute-done.37 = bf16[128,2048]{1,0:T(8,128)(2,1)S(1)} collective-permute-done((bf16[128,2048]{1,0:T(8,128)(2,1)S(1)}, bf16[128,2048]{1,0:T(8,128)(2,1)S(1)}, u32[]{:S(2)}, u32[]{:S(2)}) %collective-permute-start.37) | collective-permute-done | bytes 524320 | tf_op jit(solution)/shard_map/ppermute | solution.py:160
  173.7 10.1 collective-permute-done.54
  184.3 30.8 %collective-permute-done.8 = bf16[128,1536]{1,0:T(8,128)(2,1)S(1)} collective-permute-done((bf16[128,1536]{1,0:T(8,128)(2,1)S(1)}, bf16[128,1536]{1,0:T(8,128)(2,1)S(1)}, u32[]{:S(2)}, u32[]{:S(2)}) %collective-permute-start.8) | collective-permute-done | bytes 393248 | tf_op jit(solution)/shard_map/ppermute | solution.py:160
  222.9 10.6 collective-permute-done.38
  238.9 9.8 collective-permute-done.55
  252.2 8.2 collective-permute-done.15
  261.1 8.2 collective-permute-start.1
  274.8 17.5 %collective-permute-done.1 = bf16[256,2048]{1,0:T(8,128)(2,1)S(1)} collective-permute-done((bf16[256,2048]{1,0:T(8,128)(2,1)}, bf16[256,2048]{1,0:T(8,128)(2,1)S(1)}, u32[]{:S(2)}, u32[]{:S(2)}) %collective-permute-start.1) | collective-permute-done | bytes 1048608 | tf_op jit(solution)/shard_map/ppermute | solution.py:136
  301.5 18.3 %collective-permute-done.2 = bf16[256,2048]{1,0:T(8,128)(2,1)S(1)} collective-permute-done((bf16[256,2048]{1,0:T(8,128)(2,1)S(1)}, bf16[256,2048]{1,0:T(8,128)(2,1)S(1)}, u32[]{:S(2)}, u32[]{:S(2)}) %collective-permute-start.2) | collective-permute-done | bytes 1048608 | tf_op jit(solution)/shard_map/ppermute | solution.py:136
  320.8 10.4 fusion.145
  331.2 4.9 multiply_reduce_fusion.4
  341.9 5.8 copy.235
  369.8 7.0 reduce.22
  393.0 8.7 collective-permute-done.62
  412.9 6.2 multiply_reduce_fusion.8
  429.9 16.3 %collective-permute-done.67 = bf16[256,2048]{1,0:T(8,128)(2,1)} collective-permute-done((bf16[256,2048]{1,0:T(8,128)(2,1)S(1)}, bf16[256,2048]{1,0:T(8,128)(2,1)}, u32[]{:S(2)}, u32[]{:S(2)}) %collective-permute-start.67) | collective-permute-done | bytes 1048608 | tf_op jit(solution)/shard_map/ppermute | solution.py:136
  446.6 6.0 fusion.150
  454.0 5.4 multiply_convert_fusion.10
  459.4 6.2 convolution_convert_fusion.10
  465.7 9.1 collective-permute-done.68
  474.8 6.2 fusion.149
  481.0 5.9 multiply_convert_fusion.11
  486.9 10.3 collective-permute-done.70
  499.9 19.8 %collective-permute-done.69 = bf16[256,2048]{1,0:T(8,128)(2,1)S(1)} collective-permute-done((bf16[256,2048]{1,0:T(8,128)(2,1)}, bf16[256,2048]{1,0:T(8,128)(2,1)S(1)}, u32[]{:S(2)}, u32[]{:S(2)}) %collective-permute-start.69) | collective-permute-done | bytes 1048608 | tf_op jit(solution)/shard_map/ppermute | solution.py:136
  519.6 5.7 fusion.147
  531.7 7.6 collective-permute-done.71
  539.7 5.7 fusion.146
  548.1 15.7 %collective-permute-done.72 = bf16[256,2048]{1,0:T(8,128)(2,1)S(1)} collective-permute-done((bf16[256,2048]{1,0:T(8,128)(2,1)S(1)}, bf16[256,2048]{1,0:T(8,128)(2,1)S(1)}, u32[]{:S(2)}, u32[]{:S(2)}) %collective-permute-start.72) | collective-permute-done | bytes 1048608 | tf_op jit(solution)/shard_map/ppermute | solution.py:136
  579.0 14.1 %collective-permute-done.73 = bf16[256,2048]{1,0:T(8,128)(2,1)} collective-permute-done((bf16[256,2048]{1,0:T(8,128)(2,1)S(1)}, bf16[256,2048]{1,0:T(8,128)(2,1)}, u32[]{:S(2)}, u32[]{:S(2)}) %collective-permute-start.73) | collective-permute-done | bytes 1048608 | tf_op jit(solution)/shard_map/ppermute | solution.py:136
  598.5 7.5 fusion.151
  606.0 10.8 collective-permute-done.74
  616.8 7.7 multiply_convert_fusion.3
  628.3 10.1 collective-permute-done.75
  639.5 12.5 %convolution_convert_fusion = bf16[2048,2048]{1,0:T(8,128)(2,1)} fusion(bf16[256,2048]{1,0:T(8,128)(2,1)S(1)} %copy-done.110, bf16[256,2048]{1,0:T(8,128)(2,1)S(1)} %copy-done.114, bf16[256,2048]{1,0:T(8,128)(2,1)S(1)} %copy-done.115, bf16[256,2048]{1,0:T(8,128)(2,1)S(1)} %copy-done.108, bf16[256,2048]{1,0:T(8,128)(2,1)S(1)} %collective-permute-done.75, ...), kind=kOutput, calls=%fused_computation.8 | convolution fusion | flops 8627683328 | bytes 16777216 | tf_op jit(solution)/shard_map/dot_general | solution.py:26
  652.0 8.3 fusion.30
  660.6 9.0 multiply_convert_fusion.5
  673.3 6.2 collective-permute-done.76
  680.5 7.0 fusion.32
  687.6 6.8 multiply_convert_fusion.7
  698.2 8.0 collective-permute-done.77
  706.2 6.2 fusion.31
  713.0 6.6 convolution_convert_fusion.5
  719.7 6.7 convolution_convert_fusion.7
  730.5 5.8 fusion.29
  743.0 10.6 reduce.23
  759.0 8.9 convolution_convert_fusion.6
  768.0 6.6 convolution_convert_fusion.8
  774.8 5.7 convolution_convert_fusion.1
  809.2 6.4 multiply_reduce_fusion.1
  824.8 5.0 subtract_convert_fusion
  833.2 9.1 convolution_convert_fusion.2
  854.5 5.3 convolution_convert_fusion.4
  860.8 30.9 %collective-permute-done.82 = bf16[256,2048]{1,0:T(8,128)(2,1)S(1)} collective-permute-done((bf16[256,2048]{1,0:T(8,128)(2,1)S(1)}, bf16[256,2048]{1,0:T(8,128)(2,1)S(1)}, u32[]{:S(2)}, u32[]{:S(2)}) %collective-permute-start.82) | collective-permute-done | bytes 1048608 | tf_op jit(solution)/shard_map/ppermute | solution.py:136
  915.3 19.1 %collective-permute-done.86 = bf16[2,256,768]{2,1,0:T(8,128)(2,1)S(1)} collective-permute-done((bf16[2,256,768]{2,1,0:T(8,128)(2,1)S(1)}, bf16[2,256,768]{2,1,0:T(8,128)(2,1)S(1)}, u32[]{:S(2)}, u32[]{:S(2)}) %collective-permute-start.86) | collective-permute-done | bytes 786464 | tf_op jit(solution)/shard_map/ppermute | solution.py:160
  935.9 45.4 %collective-permute-done.89 = bf16[2,256,768]{2,1,0:T(8,128)(2,1)S(1)} collective-permute-done((bf16[2,256,768]{2,1,0:T(8,128)(2,1)S(1)}, bf16[2,256,768]{2,1,0:T(8,128)(2,1)S(1)}, u32[]{:S(2)}, u32[]{:S(2)}) %collective-permute-start.89) | collective-permute-done | bytes 786464 | tf_op jit(solution)/shard_map/ppermute | solution.py:160
  984.5 8.4 collective-permute-done.101
  997.5 21.0 %collective-permute-done.105 = bf16[256,2048]{1,0:T(8,128)(2,1)S(1)} collective-permute-done((bf16[256,2048]{1,0:T(8,128)(2,1)S(1)}, bf16[256,2048]{1,0:T(8,128)(2,1)S(1)}, u32[]{:S(2)}, u32[]{:S(2)}) %collective-permute-start.105) | collective-permute-done | bytes 1048608 | tf_op jit(solution)/shard_map/ppermute | solution.py:160
  1036.9 31.6 %collective-permute-done.91 = bf16[64,1536]{1,0:T(8,128)(2,1)S(1)} collective-permute-done((bf16[64,1536]{1,0:T(8,128)(2,1)S(1)}, bf16[64,1536]{1,0:T(8,128)(2,1)S(1)}, u32[]{:S(2)}, u32[]{:S(2)}) %collective-permute-start.91) | collective-permute-done | bytes 196640 | tf_op jit(solution)/shard_map/ppermute | solution.py:153
  1068.5 30.7 %collective-permute-done.92 = bf16[64,1536]{1,0:T(8,128)(2,1)S(1)} collective-permute-done((bf16[64,1536]{1,0:T(8,128)(2,1)S(1)}, bf16[64,1536]{1,0:T(8,128)(2,1)S(1)}, u32[]{:S(2)}, u32[]{:S(2)}) %collective-permute-start.92) | collective-permute-done | bytes 196640 | tf_op jit(solution)/shard_map/ppermute | solution.py:153
  (723 shorter events, 388.0 us)
Async XLA Ops:
  7.2 405.7 %all-gather.3.cloned.1.call-start = ((), (), s32[]{:S(2)}) async-start(), calls=%async_computation.5 | async-start | bytes 8650752 | tf_op jit(solution)/shard_map/all_gather | solution.py:323
  7.9 451.5 %all-gather.5.cloned.1.call-start = ((), (), s32[]{:S(2)}) async-start(), calls=%async_computation.6 | async-start | bytes 9437184 | tf_op jit(solution)/shard_map/all_gather | solution.py:322
  8.7 32.3 %collective-permute-start.23 = (bf16[4,64]{1,0:T(4,128)(2,1)S(1)}, bf16[4,64]{1,0:T(4,128)(2,1)S(1)}, u32[]{:S(2)}, u32[]{:S(2)}) collective-permute-start(bf16[4,64]{1,0:T(4,128)(2,1)S(1)} %pad_maximum_fusion.17), channel_id=1, source_target_pairs={{0,1},{1,2},{2,3},{3,0},{4,5},{5,6},{6,7},{7,4},{8,9},{9,10},{10,1... | collective-permute-start | bytes 1544 | tf_op jit(solution)/shard_map/ppermute | solution.py:153
  11.8 32.9 %collective-permute-start.24 = (bf16[4,64]{1,0:T(4,128)(2,1)S(1)}, bf16[4,64]{1,0:T(4,128)(2,1)S(1)}, u32[]{:S(2)}, u32[]{:S(2)}) collective-permute-start(bf16[4,64]{1,0:T(4,128)(2,1)S(1)} %pad_maximum_fusion.17), channel_id=1, source_target_pairs={{0,2},{1,3},{2,0},{3,1},{4,6},{5,7},{6,4},{7,5},{8,10},{9,11},{10,... | collective-permute-start | bytes 1544 | tf_op jit(solution)/shard_map/ppermute | solution.py:153
  14.3 30.5 %collective-permute-start.25 = (bf16[4,64]{1,0:T(4,128)(2,1)S(1)}, bf16[4,64]{1,0:T(4,128)(2,1)S(1)}, u32[]{:S(2)}, u32[]{:S(2)}) collective-permute-start(bf16[4,64]{1,0:T(4,128)(2,1)S(1)} %pad_maximum_fusion.17), channel_id=1, source_target_pairs={{0,3},{1,0},{2,1},{3,2},{4,7},{5,4},{6,5},{7,6},{8,11},{9,8},{10,9... | collective-permute-start | bytes 1544 | tf_op jit(solution)/shard_map/ppermute | solution.py:153
  15.7 204.8 %collective-permute-start = (bf16[256,2048]{1,0:T(8,128)(2,1)}, bf16[256,2048]{1,0:T(8,128)(2,1)}, u32[]{:S(2)}, u32[]{:S(2)}) collective-permute-start(bf16[256,2048]{1,0:T(8,128)(2,1)} %bitcast.447), channel_id=1, source_target_pairs={{0,1},{1,2},{2,3},{3,0},{4,5},{5,6},{6,7},{7,4},{8,9},{9,10},{10,1... | collective-permute-start | bytes 3145736 | tf_op jit(solution)/shard_map/ppermute | solution.py:136
  25.8 37.3 %collective-permute-start.3 = (bf16[64,1536]{1,0:T(8,128)(2,1)}, bf16[64,1536]{1,0:T(8,128)(2,1)}, u32[]{:S(2)}, u32[]{:S(2)}) collective-permute-start(bf16[64,1536]{1,0:T(8,128)(2,1)} %get-tuple-element.151), channel_id=1, source_target_pairs={{0,1},{1,2},{2,3},{3,0},{4,5},{5,6},{6,7},{7,4},{8,9},{9,10},{10,1... | collective-permute-start | bytes 589832 | tf_op jit(solution)/shard_map/ppermute | solution.py:153
  41.0 24.0 %collective-permute-start.4 = (bf16[64,1536]{1,0:T(8,128)(2,1)}, bf16[64,1536]{1,0:T(8,128)(2,1)S(1)}, u32[]{:S(2)}, u32[]{:S(2)}) collective-permute-start(bf16[64,1536]{1,0:T(8,128)(2,1)} %get-tuple-element.150), channel_id=1, source_target_pairs={{0,2},{1,3},{2,0},{3,1},{4,6},{5,7},{6,4},{7,5},{8,10},{9,11},{10,... | collective-permute-start | bytes 589832 | tf_op jit(solution)/shard_map/ppermute | solution.py:153
  44.7 26.1 %collective-permute-start.5 = (bf16[64,1536]{1,0:T(8,128)(2,1)}, bf16[64,1536]{1,0:T(8,128)(2,1)S(1)}, u32[]{:S(2)}, u32[]{:S(2)}) collective-permute-start(bf16[64,1536]{1,0:T(8,128)(2,1)} %get-tuple-element.149), channel_id=1, source_target_pairs={{0,3},{1,0},{2,1},{3,2},{4,7},{5,4},{6,5},{7,6},{8,11},{9,8},{10,9... | collective-permute-start | bytes 589832 | tf_op jit(solution)/shard_map/ppermute | solution.py:153
  63.2 47.1 %collective-permute-start.34 = (bf16[64,2048]{1,0:T(8,128)(2,1)}, bf16[64,2048]{1,0:T(8,128)(2,1)S(1)}, u32[]{:S(2)}, u32[]{:S(2)}) collective-permute-start(bf16[64,2048]{1,0:T(8,128)(2,1)} %get-tuple-element.134), channel_id=1, source_target_pairs={{0,2},{1,3},{2,0},{3,1},{4,6},{5,7},{6,4},{7,5},{8,10},{9,11},{10,... | collective-permute-start | bytes 786440 | tf_op jit(solution)/shard_map/ppermute | solution.py:153
  65.0 45.3 %collective-permute-start.35 = (bf16[64,2048]{1,0:T(8,128)(2,1)}, bf16[64,2048]{1,0:T(8,128)(2,1)S(1)}, u32[]{:S(2)}, u32[]{:S(2)}) collective-permute-start(bf16[64,2048]{1,0:T(8,128)(2,1)} %get-tuple-element.133), channel_id=1, source_target_pairs={{0,3},{1,0},{2,1},{3,2},{4,7},{5,4},{6,5},{7,6},{8,11},{9,8},{10,9... | collective-permute-start | bytes 786440 | tf_op jit(solution)/shard_map/ppermute | solution.py:153
  71.5 41.3 %collective-permute-start.50 = (bf16[64,2048]{1,0:T(8,128)(2,1)}, bf16[64,2048]{1,0:T(8,128)(2,1)S(1)}, u32[]{:S(2)}, u32[]{:S(2)}) collective-permute-start(bf16[64,2048]{1,0:T(8,128)(2,1)} %get-tuple-element.141), channel_id=1, source_target_pairs={{0,1},{1,2},{2,3},{3,0},{4,5},{5,6},{6,7},{7,4},{8,9},{9,10},{10,1... | collective-permute-start | bytes 786440 | tf_op jit(solution)/shard_map/ppermute | solution.py:153
  84.3 53.1 %collective-permute-start.51 = (bf16[64,2048]{1,0:T(8,128)(2,1)S(1)}, bf16[64,2048]{1,0:T(8,128)(2,1)S(1)}, u32[]{:S(2)}, u32[]{:S(2)}) collective-permute-start(bf16[64,2048]{1,0:T(8,128)(2,1)S(1)} %copy-done.67), channel_id=1, source_target_pairs={{0,2},{1,3},{2,0},{3,1},{4,6},{5,7},{6,4},{7,5},{8,10},{9,11},{10,... | collective-permute-start | bytes 786440 | tf_op jit(solution)/shard_map/ppermute | solution.py:153
  110.3 27.3 %collective-permute-start.52 = (bf16[64,2048]{1,0:T(8,128)(2,1)S(1)}, bf16[64,2048]{1,0:T(8,128)(2,1)S(1)}, u32[]{:S(2)}, u32[]{:S(2)}) collective-permute-start(bf16[64,2048]{1,0:T(8,128)(2,1)S(1)} %copy-done.66), channel_id=1, source_target_pairs={{0,3},{1,0},{2,1},{3,2},{4,7},{5,4},{6,5},{7,6},{8,11},{9,8},{10,9... | collective-permute-start | bytes 786440 | tf_op jit(solution)/shard_map/ppermute | solution.py:153
  110.3 36.1 %collective-permute-start.6 = (bf16[128,1536]{1,0:T(8,128)(2,1)S(1)}, bf16[128,1536]{1,0:T(8,128)(2,1)S(1)}, u32[]{:S(2)}, u32[]{:S(2)}) collective-permute-start(bf16[128,1536]{1,0:T(8,128)(2,1)S(1)} %bitcast.500), channel_id=1, source_target_pairs={{0,8},{4,12},{8,0},{12,4},{16,24},{20,28},{24,16},{28,20},{1,9},{5... | collective-permute-start | bytes 1179656 | tf_op jit(solution)/shard_map/ppermute | solution.py:160
  112.8 35.3 %collective-permute-start.7 = (bf16[128,1536]{1,0:T(8,128)(2,1)S(1)}, bf16[128,1536]{1,0:T(8,128)(2,1)S(1)}, u32[]{:S(2)}, u32[]{:S(2)}) collective-permute-start(bf16[128,1536]{1,0:T(8,128)(2,1)S(1)} %bitcast.501), channel_id=1, source_target_pairs={{0,16},{4,20},{8,24},{12,28},{16,0},{20,4},{24,8},{28,12},{1,17},{... | collective-permute-start | bytes 1179656 | tf_op jit(solution)/shard_map/ppermute | solution.py:160
  137.4 77.7 %collective-permute-start.9 = (bf16[128,1536]{1,0:T(8,128)(2,1)S(1)}, bf16[128,1536]{1,0:T(8,128)(2,1)S(1)}, u32[]{:S(2)}, u32[]{:S(2)}) collective-permute-start(bf16[128,1536]{1,0:T(8,128)(2,1)S(1)} %bitcast.502), channel_id=1, source_target_pairs={{0,4},{4,0},{8,12},{12,8},{16,20},{20,16},{24,28},{28,24},{1,5},{5... | collective-permute-start | bytes 1179656 | tf_op jit(solution)/shard_map/ppermute | solution.py:160
  148.1 24.2 %collective-permute-start.53 = (bf16[128,2048]{1,0:T(8,128)(2,1)S(1)}, bf16[128,2048]{1,0:T(8,128)(2,1)S(1)}, u32[]{:S(2)}, u32[]{:S(2)}) collective-permute-start(bf16[128,2048]{1,0:T(8,128)(2,1)S(1)} %bitcast.488), channel_id=1, source_target_pairs={{0,8},{4,12},{8,0},{12,4},{16,24},{20,28},{24,16},{28,20},{1,9},{5... | collective-permute-start | bytes 1572872 | tf_op jit(solution)/shard_map/ppermute | solution.py:160
  152.4 31.3 %collective-permute-start.54 = (bf16[128,2048]{1,0:T(8,128)(2,1)S(1)}, bf16[128,2048]{1,0:T(8,128)(2,1)S(1)}, u32[]{:S(2)}, u32[]{:S(2)}) collective-permute-start(bf16[128,2048]{1,0:T(8,128)(2,1)S(1)} %bitcast.489), channel_id=1, source_target_pairs={{0,16},{4,20},{8,24},{12,28},{16,0},{20,4},{24,8},{28,12},{1,17},{... | collective-permute-start | bytes 1572872 | tf_op jit(solution)/shard_map/ppermute | solution.py:160
  167.5 81.2 %collective-permute-start.13 = (bf16[128,1536]{1,0:T(8,128)(2,1)S(1)}, bf16[128,1536]{1,0:T(8,128)(2,1)S(1)}, u32[]{:S(2)}, u32[]{:S(2)}) collective-permute-start(bf16[128,1536]{1,0:T(8,128)(2,1)S(1)} %bitcast.495), channel_id=1, source_target_pairs={{0,16},{4,20},{8,24},{12,28},{16,0},{20,4},{24,8},{28,12},{1,17},{... | collective-permute-start | bytes 1179656 | tf_op jit(solution)/shard_map/ppermute | solution.py:160
  172.2 42.9 %collective-permute-start.8 = (bf16[128,1536]{1,0:T(8,128)(2,1)S(1)}, bf16[128,1536]{1,0:T(8,128)(2,1)S(1)}, u32[]{:S(2)}, u32[]{:S(2)}) collective-permute-start(bf16[128,1536]{1,0:T(8,128)(2,1)S(1)} %collective-permute-done.6), channel_id=1, source_target_pairs={{0,16},{4,20},{8,24},{12,28},{16,0},{20,4},{24,8},{28,12},{1,17},{... | collective-permute-start | bytes 1179656 | tf_op jit(solution)/shard_map/ppermute | solution.py:160
  183.7 68.4 %collective-permute-start.14 = (bf16[128,1536]{1,0:T(8,128)(2,1)S(1)}, bf16[128,1536]{1,0:T(8,128)(2,1)S(1)}, u32[]{:S(2)}, u32[]{:S(2)}) collective-permute-start(bf16[128,1536]{1,0:T(8,128)(2,1)S(1)} %bitcast.496), channel_id=1, source_target_pairs={{0,8},{4,12},{8,0},{12,4},{16,24},{20,28},{24,16},{28,20},{1,9},{5... | collective-permute-start | bytes 1179656 | tf_op jit(solution)/shard_map/ppermute | solution.py:160
  250.6 47.0 %collective-permute-start.43 = (bf16[128,2048]{1,0:T(8,128)(2,1)}, bf16[128,2048]{1,0:T(8,128)(2,1)}, u32[]{:S(2)}, u32[]{:S(2)}) collective-permute-start(bf16[128,2048]{1,0:T(8,128)(2,1)} %bitcast.55), channel_id=1, source_target_pairs={{0,16},{4,20},{8,24},{12,28},{16,0},{20,4},{24,8},{28,12},{1,17},{... | collective-permute-start | bytes 1572872 | tf_op jit(solution)/shard_map/ppermute | solution.py:160
  261.1 31.1 %collective-permute-start.1 = (bf16[256,2048]{1,0:T(8,128)(2,1)}, bf16[256,2048]{1,0:T(8,128)(2,1)S(1)}, u32[]{:S(2)}, u32[]{:S(2)}) collective-permute-start(bf16[256,2048]{1,0:T(8,128)(2,1)} %collective-permute-done), channel_id=1, source_target_pairs={{0,1},{1,2},{2,3},{3,0},{4,5},{5,6},{6,7},{7,4},{8,9},{9,10},{10,1... | collective-permute-start | bytes 3145736 | tf_op jit(solution)/shard_map/ppermute | solution.py:136
  269.5 68.9 %collective-permute-start.44 = (bf16[128,2048]{1,0:T(8,128)(2,1)}, bf16[128,2048]{1,0:T(8,128)(2,1)S(1)}, u32[]{:S(2)}, u32[]{:S(2)}) collective-permute-start(bf16[128,2048]{1,0:T(8,128)(2,1)} %bitcast.55), channel_id=1, source_target_pairs={{0,8},{4,12},{8,0},{12,4},{16,24},{20,28},{24,16},{28,20},{1,9},{5... | collective-permute-start | bytes 1572872 | tf_op jit(solution)/shard_map/ppermute | solution.py:160
  269.9 24.1 %collective-permute-start.59 = (bf16[128,2048]{1,0:T(8,128)(2,1)S(1)}, bf16[128,2048]{1,0:T(8,128)(2,1)S(1)}, u32[]{:S(2)}, u32[]{:S(2)}) collective-permute-start(bf16[128,2048]{1,0:T(8,128)(2,1)S(1)} %collective-permute-done.55), channel_id=1, source_target_pairs={{0,4},{4,0},{8,12},{12,8},{16,20},{20,16},{24,28},{28,24},{1,5},{5... | collective-permute-start | bytes 1572872 | tf_op jit(solution)/shard_map/ppermute | solution.py:160
  271.4 116.2 %collective-permute-start.46 = (bf16[128,2048]{1,0:T(8,128)(2,1)}, bf16[128,2048]{1,0:T(8,128)(2,1)}, u32[]{:S(2)}, u32[]{:S(2)}) collective-permute-start(bf16[128,2048]{1,0:T(8,128)(2,1)} %bitcast.55), channel_id=1, source_target_pairs={{0,4},{4,0},{8,12},{12,8},{16,20},{20,16},{24,28},{28,24},{1,5},{5... | collective-permute-start | bytes 1572872 | tf_op jit(solution)/shard_map/ppermute | solution.py:160
  292.3 92.9 %collective-permute-start.60 = (bf16[128,2048]{1,0:T(8,128)(2,1)}, bf16[128,2048]{1,0:T(8,128)(2,1)}, u32[]{:S(2)}, u32[]{:S(2)}) collective-permute-start(bf16[128,2048]{1,0:T(8,128)(2,1)} %bitcast.64), channel_id=1, source_target_pairs={{0,16},{4,20},{8,24},{12,28},{16,0},{20,4},{24,8},{28,12},{1,17},{... | collective-permute-start | bytes 1572872 | tf_op jit(solution)/shard_map/ppermute | solution.py:160
  294.0 25.7 %collective-permute-start.2 = (bf16[256,2048]{1,0:T(8,128)(2,1)S(1)}, bf16[256,2048]{1,0:T(8,128)(2,1)S(1)}, u32[]{:S(2)}, u32[]{:S(2)}) collective-permute-start(bf16[256,2048]{1,0:T(8,128)(2,1)S(1)} %collective-permute-done.1), channel_id=1, source_target_pairs={{0,1},{1,2},{2,3},{3,0},{4,5},{5,6},{6,7},{7,4},{8,9},{9,10},{10,1... | collective-permute-start | bytes 3145736 | tf_op jit(solution)/shard_map/ppermute | solution.py:136
  347.6 42.1 %collective-permute-start.61 = (bf16[128,2048]{1,0:T(8,128)(2,1)}, bf16[128,2048]{1,0:T(8,128)(2,1)}, u32[]{:S(2)}, u32[]{:S(2)}) collective-permute-start(bf16[128,2048]{1,0:T(8,128)(2,1)} %bitcast.64), channel_id=1, source_target_pairs={{0,8},{4,12},{8,0},{12,4},{16,24},{20,28},{24,16},{28,20},{1,9},{5... | collective-permute-start | bytes 1572872 | tf_op jit(solution)/shard_map/ppermute | solution.py:160
  347.9 74.4 %collective-permute-start.63 = (bf16[128,2048]{1,0:T(8,128)(2,1)}, bf16[128,2048]{1,0:T(8,128)(2,1)}, u32[]{:S(2)}, u32[]{:S(2)}) collective-permute-start(bf16[128,2048]{1,0:T(8,128)(2,1)} %bitcast.64), channel_id=1, source_target_pairs={{0,4},{4,0},{8,12},{12,8},{16,20},{20,16},{24,28},{28,24},{1,5},{5... | collective-permute-start | bytes 1572872 | tf_op jit(solution)/shard_map/ppermute | solution.py:160
  347.9 35.2 %collective-permute-start.45 = (bf16[128,2048]{1,0:T(8,128)(2,1)}, bf16[128,2048]{1,0:T(8,128)(2,1)}, u32[]{:S(2)}, u32[]{:S(2)}) collective-permute-start(bf16[128,2048]{1,0:T(8,128)(2,1)} %collective-permute-done.43), channel_id=1, source_target_pairs={{0,8},{4,12},{8,0},{12,4},{16,24},{20,28},{24,16},{28,20},{1,9},{5... | collective-permute-start | bytes 1572872 | tf_op jit(solution)/shard_map/ppermute | solution.py:160
  378.8 30.3 %all-to-all-start = ((bf16[4,2,65536]{2,1,0:T(2,128)(2,1)}), bf16[4,2,65536]{2,1,0:T(2,128)(2,1)S(1)}, u32[]{:S(2)}, u32[]{:S(2)}) async-start(bf16[4,2,65536]{2,1,0:T(2,128)(2,1)} %reshape.901), calls=%async_computation | async-start | bytes 2097152 | tf_op jit(solution)/shard_map/all_to_all | solution.py:377
  383.1 741.2 %reduce-scatter.5.cloned.1.call-start = ((), (), s32[]{:S(2)}) async-start(), calls=%async_computation.8 | async-start | bytes 9437184 | tf_op jit(solution)/shard_map/reduce_scatter | solution.py:444
  389.8 34.5 %collective-permute-start.64 = (bf16[128,2048]{1,0:T(8,128)(2,1)}, bf16[128,2048]{1,0:T(8,128)(2,1)}, u32[]{:S(2)}, u32[]{:S(2)}) collective-permute-start(bf16[128,2048]{1,0:T(8,128)(2,1)} %collective-permute-done.60), channel_id=1, source_target_pairs={{0,4},{4,0},{8,12},{12,8},{16,20},{20,16},{24,28},{28,24},{1,5},{5... | collective-permute-start | bytes 1572872 | tf_op jit(solution)/shard_map/ppermute | solution.py:160
  391.7 34.5 %collective-permute-start.65 = (bf16[128,2048]{1,0:T(8,128)(2,1)}, bf16[128,2048]{1,0:T(8,128)(2,1)}, u32[]{:S(2)}, u32[]{:S(2)}) collective-permute-start(bf16[128,2048]{1,0:T(8,128)(2,1)} %collective-permute-done.61), channel_id=1, source_target_pairs={{0,4},{4,0},{8,12},{12,8},{16,20},{20,16},{24,28},{28,24},{1,5},{5... | collective-permute-start | bytes 1572872 | tf_op jit(solution)/shard_map/ppermute | solution.py:160
  403.6 24.4 %collective-permute-start.66 = (bf16[128,2048]{1,0:T(8,128)(2,1)}, bf16[128,2048]{1,0:T(8,128)(2,1)}, u32[]{:S(2)}, u32[]{:S(2)}) collective-permute-start(bf16[128,2048]{1,0:T(8,128)(2,1)} %collective-permute-done.62), channel_id=1, source_target_pairs={{0,4},{4,0},{8,12},{12,8},{16,20},{20,16},{24,28},{28,24},{1,5},{5... | collective-permute-start | bytes 1572872 | tf_op jit(solution)/shard_map/ppermute | solution.py:160
  420.1 26.1 %collective-permute-start.67 = (bf16[256,2048]{1,0:T(8,128)(2,1)S(1)}, bf16[256,2048]{1,0:T(8,128)(2,1)}, u32[]{:S(2)}, u32[]{:S(2)}) collective-permute-start(bf16[256,2048]{1,0:T(8,128)(2,1)S(1)} %fusion.93), channel_id=1, source_target_pairs={{0,1},{1,2},{2,3},{3,0},{4,5},{5,6},{6,7},{7,4},{8,9},{9,10},{10,1... | collective-permute-start | bytes 3145736 | tf_op jit(solution)/shard_map/ppermute | solution.py:136
  446.2 28.6 %collective-permute-start.68 = (bf16[256,2048]{1,0:T(8,128)(2,1)}, bf16[256,2048]{1,0:T(8,128)(2,1)}, u32[]{:S(2)}, u32[]{:S(2)}) collective-permute-start(bf16[256,2048]{1,0:T(8,128)(2,1)} %collective-permute-done.67), channel_id=1, source_target_pairs={{0,1},{1,2},{2,3},{3,0},{4,5},{5,6},{6,7},{7,4},{8,9},{9,10},{10,1... | collective-permute-start | bytes 3145736 | tf_op jit(solution)/shard_map/ppermute | solution.py:136
  465.6 31.5 %collective-permute-start.70 = (bf16[256,2048]{1,0:T(8,128)(2,1)S(1)}, bf16[256,2048]{1,0:T(8,128)(2,1)S(1)}, u32[]{:S(2)}, u32[]{:S(2)}) collective-permute-start(bf16[256,2048]{1,0:T(8,128)(2,1)S(1)} %convolution_convert_fusion.10), channel_id=1, source_target_pairs={{0,1},{1,2},{2,3},{3,0},{4,5},{5,6},{6,7},{7,4},{8,9},{9,10},{10,1... | collective-permute-start | bytes 3145736 | tf_op jit(solution)/shard_map/ppermute | solution.py:136
  474.8 44.8 %collective-permute-start.69 = (bf16[256,2048]{1,0:T(8,128)(2,1)}, bf16[256,2048]{1,0:T(8,128)(2,1)S(1)}, u32[]{:S(2)}, u32[]{:S(2)}) collective-permute-start(bf16[256,2048]{1,0:T(8,128)(2,1)} %collective-permute-done.68), channel_id=1, source_target_pairs={{0,1},{1,2},{2,3},{3,0},{4,5},{5,6},{6,7},{7,4},{8,9},{9,10},{10,1... | collective-permute-start | bytes 3145736 | tf_op jit(solution)/shard_map/ppermute | solution.py:136
  499.6 39.6 %collective-permute-start.71 = (bf16[256,2048]{1,0:T(8,128)(2,1)S(1)}, bf16[256,2048]{1,0:T(8,128)(2,1)S(1)}, u32[]{:S(2)}, u32[]{:S(2)}) collective-permute-start(bf16[256,2048]{1,0:T(8,128)(2,1)S(1)} %add_convert_fusion.2), channel_id=1, source_target_pairs={{0,1},{1,2},{2,3},{3,0},{4,5},{5,6},{6,7},{7,4},{8,9},{9,10},{10,1... | collective-permute-start | bytes 3145736 | tf_op jit(solution)/shard_map/ppermute | solution.py:136
  539.6 24.2 %collective-permute-start.72 = (bf16[256,2048]{1,0:T(8,128)(2,1)S(1)}, bf16[256,2048]{1,0:T(8,128)(2,1)S(1)}, u32[]{:S(2)}, u32[]{:S(2)}) collective-permute-start(bf16[256,2048]{1,0:T(8,128)(2,1)S(1)} %add_convert_fusion.1), channel_id=1, source_target_pairs={{0,1},{1,2},{2,3},{3,0},{4,5},{5,6},{6,7},{7,4},{8,9},{9,10},{10,1... | collective-permute-start | bytes 3145736 | tf_op jit(solution)/shard_map/ppermute | solution.py:136
  593.1 23.7 %collective-permute-start.74 = (bf16[256,2048]{1,0:T(8,128)(2,1)}, bf16[256,2048]{1,0:T(8,128)(2,1)}, u32[]{:S(2)}, u32[]{:S(2)}) collective-permute-start(bf16[256,2048]{1,0:T(8,128)(2,1)} %collective-permute-done.73), channel_id=1, source_target_pairs={{0,1},{1,2},{2,3},{3,0},{4,5},{5,6},{6,7},{7,4},{8,9},{9,10},{10,1... | collective-permute-start | bytes 3145736 | tf_op jit(solution)/shard_map/ppermute | solution.py:136
  719.6 176.8 %collective-permute-start.103 = (bf16[2,2,256,2048]{3,2,1,0:T(8,128)(2,1)}, bf16[2,2,256,2048]{3,2,1,0:T(8,128)(2,1)}, u32[]{:S(2)}, u32[]{:S(2)}) collective-permute-start(bf16[2,2,256,2048]{3,2,1,0:T(8,128)(2,1)} %bitcast.139), channel_id=1, source_target_pairs={{0,4},{4,0},{8,12},{12,8},{16,20},{20,16},{24,28},{28,24},{1,5},{5... | collective-permute-start | bytes 12582920 | tf_op jit(solution)/shard_map/ppermute | solution.py:160
  726.4 177.7 %collective-permute-start.100 = (bf16[2,2,256,2048]{3,2,1,0:T(8,128)(2,1)}, bf16[2,2,256,2048]{3,2,1,0:T(8,128)(2,1)}, u32[]{:S(2)}, u32[]{:S(2)}) collective-permute-start(bf16[2,2,256,2048]{3,2,1,0:T(8,128)(2,1)} %bitcast.133), channel_id=1, source_target_pairs={{0,4},{4,0},{8,12},{12,8},{16,20},{20,16},{24,28},{28,24},{1,5},{5... | collective-permute-start | bytes 12582920 | tf_op jit(solution)/shard_map/ppermute | solution.py:160
  755.3 27.3 %all-to-all-start.1 = ((bf16[4,2,65536]{2,1,0:T(2,128)(2,1)}), bf16[4,2,65536]{2,1,0:T(2,128)(2,1)S(1)}, u32[]{:S(2)}, u32[]{:S(2)}) async-start(bf16[4,2,65536]{2,1,0:T(2,128)(2,1)} %reshape.903), calls=%async_computation.1 | async-start | bytes 2097152 | tf_op jit(solution)/shard_map/all_to_all | solution.py:441
  758.8 368.3 %reduce-scatter.3.cloned.1.call-start = ((), (), s32[]{:S(2)}) async-start(), calls=%async_computation.7 | async-start | bytes 8650752 | tf_op jit(solution)/shard_map/reduce_scatter | solution.py:445
  842.3 49.3 %collective-permute-start.82 = (bf16[256,2048]{1,0:T(8,128)(2,1)S(1)}, bf16[256,2048]{1,0:T(8,128)(2,1)S(1)}, u32[]{:S(2)}, u32[]{:S(2)}) collective-permute-start(bf16[256,2048]{1,0:T(8,128)(2,1)S(1)} %dynamic-slice_bitcast_fusion), channel_id=1, source_target_pairs={{0,1},{1,2},{2,3},{3,0},{4,5},{5,6},{6,7},{7,4},{8,9},{9,10},{10,1... | collective-permute-start | bytes 3145736 | tf_op jit(solution)/shard_map/ppermute | solution.py:136
  853.9 54.2 %collective-permute-start.88 = (bf16[2,2,256,768]{3,2,1,0:T(8,128)(2,1)}, bf16[2,2,256,768]{3,2,1,0:T(8,128)(2,1)S(1)}, u32[]{:S(2)}, u32[]{:S(2)}) collective-permute-start(bf16[2,2,256,768]{3,2,1,0:T(8,128)(2,1)} %get-tuple-element.122), channel_id=1, source_target_pairs={{0,4},{4,0},{8,12},{12,8},{16,20},{20,16},{24,28},{28,24},{1,5},{5... | collective-permute-start | bytes 4718600 | tf_op jit(solution)/shard_map/ppermute | solution.py:160
  859.9 48.3 %collective-permute-start.85 = (bf16[2,2,256,768]{3,2,1,0:T(8,128)(2,1)}, bf16[2,2,256,768]{3,2,1,0:T(8,128)(2,1)}, u32[]{:S(2)}, u32[]{:S(2)}) collective-permute-start(bf16[2,2,256,768]{3,2,1,0:T(8,128)(2,1)} %get-tuple-element.123), channel_id=1, source_target_pairs={{0,4},{4,0},{8,12},{12,8},{16,20},{20,16},{24,28},{28,24},{1,5},{5... | collective-permute-start | bytes 4718600 | tf_op jit(solution)/shard_map/ppermute | solution.py:160
  893.0 135.4 %collective-permute-start.83 = (bf16[256,2048]{1,0:T(8,128)(2,1)}, bf16[256,2048]{1,0:T(8,128)(2,1)}, u32[]{:S(2)}, u32[]{:S(2)}) collective-permute-start(bf16[256,2048]{1,0:T(8,128)(2,1)} %fusion.63), channel_id=1, source_target_pairs={{0,1},{1,2},{2,3},{3,0},{4,5},{5,6},{6,7},{7,4},{8,9},{9,10},{10,1... | collective-permute-start | bytes 3145736 | tf_op jit(solution)/shard_map/ppermute | solution.py:136
  902.0 79.5 %collective-permute-start.104 = (bf16[2,256,2048]{2,1,0:T(8,128)(2,1)}, bf16[2,256,2048]{2,1,0:T(8,128)(2,1)}, u32[]{:S(2)}, u32[]{:S(2)}) collective-permute-start(bf16[2,256,2048]{2,1,0:T(8,128)(2,1)} %fusion.44), channel_id=1, source_target_pairs={{0,16},{4,20},{8,24},{12,28},{16,0},{20,4},{24,8},{28,12},{1,17},{... | collective-permute-start | bytes 6291464 | tf_op jit(solution)/shard_map/ppermute | solution.py:160
  913.4 67.9 %collective-permute-start.89 = (bf16[2,256,768]{2,1,0:T(8,128)(2,1)S(1)}, bf16[2,256,768]{2,1,0:T(8,128)(2,1)S(1)}, u32[]{:S(2)}, u32[]{:S(2)}) collective-permute-start(bf16[2,256,768]{2,1,0:T(8,128)(2,1)S(1)} %fusion.104), channel_id=1, source_target_pairs={{0,16},{4,20},{8,24},{12,28},{16,0},{20,4},{24,8},{28,12},{1,17},{... | collective-permute-start | bytes 2359304 | tf_op jit(solution)/shard_map/ppermute | solution.py:160
  914.5 78.5 %collective-permute-start.101 = (bf16[2,256,2048]{2,1,0:T(8,128)(2,1)S(1)}, bf16[2,256,2048]{2,1,0:T(8,128)(2,1)S(1)}, u32[]{:S(2)}, u32[]{:S(2)}) collective-permute-start(bf16[2,256,2048]{2,1,0:T(8,128)(2,1)S(1)} %fusion.43), channel_id=1, source_target_pairs={{0,8},{4,12},{8,0},{12,4},{16,24},{20,28},{24,16},{28,20},{1,9},{5... | collective-permute-start | bytes 6291464 | tf_op jit(solution)/shard_map/ppermute | solution.py:160
  934.6 61.8 %collective-permute-start.87 = (bf16[256,768]{1,0:T(8,128)(2,1)S(1)}, bf16[256,768]{1,0:T(8,128)(2,1)}, u32[]{:S(2)}, u32[]{:S(2)}) collective-permute-start(bf16[256,768]{1,0:T(8,128)(2,1)S(1)} %fusion.111), channel_id=1, source_target_pairs={{0,16},{4,20},{8,24},{12,28},{16,0},{20,4},{24,8},{28,12},{1,17},{... | collective-permute-start | bytes 1179656 | tf_op jit(solution)/shard_map/ppermute | solution.py:160
  984.5 34.1 %collective-permute-start.105 = (bf16[256,2048]{1,0:T(8,128)(2,1)S(1)}, bf16[256,2048]{1,0:T(8,128)(2,1)S(1)}, u32[]{:S(2)}, u32[]{:S(2)}) collective-permute-start(bf16[256,2048]{1,0:T(8,128)(2,1)S(1)} %fusion.96), channel_id=1, source_target_pairs={{0,8},{4,12},{8,0},{12,4},{16,24},{20,28},{24,16},{28,20},{1,9},{5... | collective-permute-start | bytes 3145736 | tf_op jit(solution)/shard_map/ppermute | solution.py:160
  993.6 25.2 %collective-permute-start.102 = (bf16[256,2048]{1,0:T(8,128)(2,1)S(1)}, bf16[256,2048]{1,0:T(8,128)(2,1)S(1)}, u32[]{:S(2)}, u32[]{:S(2)}) collective-permute-start(bf16[256,2048]{1,0:T(8,128)(2,1)S(1)} %fusion.95), channel_id=1, source_target_pairs={{0,16},{4,20},{8,24},{12,28},{16,0},{20,4},{24,8},{28,12},{1,17},{... | collective-permute-start | bytes 3145736 | tf_op jit(solution)/shard_map/ppermute | solution.py:160
  994.9 30.0 %collective-permute-start.90 = (bf16[256,768]{1,0:T(8,128)(2,1)S(1)}, bf16[256,768]{1,0:T(8,128)(2,1)}, u32[]{:S(2)}, u32[]{:S(2)}) collective-permute-start(bf16[256,768]{1,0:T(8,128)(2,1)S(1)} %fusion.112), channel_id=1, source_target_pairs={{0,8},{4,12},{8,0},{12,4},{16,24},{20,28},{24,16},{28,20},{1,9},{5... | collective-permute-start | bytes 1179656 | tf_op jit(solution)/shard_map/ppermute | solution.py:160
  1021.3 92.5 %all-to-all-start.2 = ((bf16[4,2,64,8,256]{4,3,2,1,0:T(8,128)(2,1)}), bf16[4,2,64,8,256]{4,3,2,1,0:T(8,128)(2,1)S(1)}, u32[]{:S(2)}, u32[]{:S(2)}) async-start(bf16[4,2,64,8,256]{4,3,2,1,0:T(8,128)(2,1)} %maximum_bitcast_fusion.1), calls=%async_computation.3 | async-start | bytes 4194304 | tf_op jit(solution)/shard_map/all_to_all | solution.py:449
  1026.4 42.1 %collective-permute-start.91 = (bf16[64,1536]{1,0:T(8,128)(2,1)S(1)}, bf16[64,1536]{1,0:T(8,128)(2,1)S(1)}, u32[]{:S(2)}, u32[]{:S(2)}) collective-permute-start(bf16[64,1536]{1,0:T(8,128)(2,1)S(1)} %get-tuple-element.145), channel_id=1, source_target_pairs={{0,1},{1,2},{2,3},{3,0},{4,5},{5,6},{6,7},{7,4},{8,9},{9,10},{10,1... | collective-permute-start | bytes 589832 | tf_op jit(solution)/shard_map/ppermute | solution.py:153
  1031.3 78.9 %collective-permute-start.84 = (bf16[256,2048]{1,0:T(8,128)(2,1)}, bf16[256,2048]{1,0:T(8,128)(2,1)}, u32[]{:S(2)}, u32[]{:S(2)}) collective-permute-start(bf16[256,2048]{1,0:T(8,128)(2,1)} %fusion.64), channel_id=1, source_target_pairs={{0,1},{1,2},{2,3},{3,0},{4,5},{5,6},{6,7},{7,4},{8,9},{9,10},{10,1... | collective-permute-start | bytes 3145736 | tf_op jit(solution)/shard_map/ppermute | solution.py:136
  1032.8 66.4 %collective-permute-start.92 = (bf16[64,1536]{1,0:T(8,128)(2,1)S(1)}, bf16[64,1536]{1,0:T(8,128)(2,1)S(1)}, u32[]{:S(2)}, u32[]{:S(2)}) collective-permute-start(bf16[64,1536]{1,0:T(8,128)(2,1)S(1)} %get-tuple-element.146), channel_id=1, source_target_pairs={{0,2},{1,3},{2,0},{3,1},{4,6},{5,7},{6,4},{7,5},{8,10},{9,11},{10,... | collective-permute-start | bytes 589832 | tf_op jit(solution)/shard_map/ppermute | solution.py:153
  1033.8 65.5 %collective-permute-start.93 = (bf16[64,1536]{1,0:T(8,128)(2,1)S(1)}, bf16[64,1536]{1,0:T(8,128)(2,1)S(1)}, u32[]{:S(2)}, u32[]{:S(2)}) collective-permute-start(bf16[64,1536]{1,0:T(8,128)(2,1)S(1)} %get-tuple-element.143), channel_id=1, source_target_pairs={{0,3},{1,0},{2,1},{3,2},{4,7},{5,4},{6,5},{7,6},{8,11},{9,8},{10,9... | collective-permute-start | bytes 589832 | tf_op jit(solution)/shard_map/ppermute | solution.py:153
  (179 other events, 2769.1 us)
Sparse Core Ops, SparseCore 0:
  10.9 125.7 all-gather.2
  138.6 86.2 all-gather.4
  652.1 67.3 reduce-scatter.4
  780.6 233.9 reduce-scatter.2

commit v3 on v2

v3 whole, which is shorter than its diff:
```python
import functools

import jax
import jax.numpy as jnp
from jax import lax
from jax.experimental import pallas as pl
from jax.experimental.pallas import tpu as pltpu
from jax.sharding import PartitionSpec as P

H = 16
HD = 128
DOCS = 4

epsilon = 1e-06
rope_base = 500000.0
masked_score = -1e30
bf16 = jnp.bfloat16
f32 = jnp.float32


def product(left, right):
    return jnp.dot(left, right, preferred_element_type=f32)


def against(left, right):
    return lax.dot_general(left, right, (((1,), (1,)), ((), ())), preferred_element_type=f32)


def weight_grad(left, right):
    return lax.dot_general(left, right, (((0,), (0,)), ((), ())), preferred_element_type=f32)


def rms_scale(values):
    return lax.rsqrt(jnp.mean(values * values, -1, keepdims=True) + epsilon)


def norm_back(values, scale_rows, grad_vals):
    return scale_rows * grad_vals - values * scale_rows**3 * jnp.mean(
        grad_vals * values, -1, keepdims=True
    )


def positions(seg_ids):
    doc_ids = jnp.arange(DOCS, dtype=jnp.int32)
    starts = jnp.sum((seg_ids[..., None, :] < doc_ids[:, None]).astype(jnp.int32), -1)
    one_hot = (seg_ids[..., None] == doc_ids).astype(jnp.int32)
    token_start = jnp.sum(one_hot * starts[..., None, :], axis=-1)
    return jnp.arange(seg_ids.shape[-1], dtype=jnp.int32) - token_start


def rope_tables(position_ids):
    freqs = rope_base ** (-jnp.arange(HD // 2, dtype=f32) * 2.0 / HD)
    angles = position_ids.astype(f32)[..., None] * freqs
    cosine = jnp.cos(angles)
    sine_tab = jnp.sin(angles)
    return (
        jnp.concatenate([cosine, cosine], -1),
        jnp.concatenate([sine_tab, sine_tab], -1),
    )


def contract(left, right, left_dim, right_dim):
    return lax.dot_general(left, right, (((left_dim,), (right_dim,)), ((), ())), preferred_element_type=f32)


def vmem(shape, index=None):
    return pl.BlockSpec(shape, index or (lambda *_: (0,) * len(shape)))


def kernel_params(grid=0):
    return pltpu.CompilerParams(vmem_limit_bytes=48 * 2**20)


def relayout_body(moves, count, *refs):
    ins, outs = refs[:count], refs[count:]
    for (src, src_row, src_col), (dst, dst_row, dst_col), (rows, cols) in moves():
        outs[dst][pl.ds(dst_row, rows), pl.ds(dst_col, cols)] = ins[src][
            pl.ds(src_row, rows), pl.ds(src_col, cols)
        ].astype(outs[dst].dtype)


def relayout(arrays, shapes, dtype, moves):
    outs = [jax.ShapeDtypeStruct(shape, dtype) for shape in shapes]
    size = sum(a.size * a.dtype.itemsize for a in [*arrays, *outs])
    return pl.pallas_call(
        functools.partial(relayout_body, moves, len(arrays)),
        in_specs=[vmem(a.shape) for a in arrays],
        out_specs=[vmem(o.shape) for o in outs],
        out_shape=outs,
        compiler_params=kernel_params(),
        cost_estimate=pl.CostEstimate(flops=0, bytes_accessed=size, transcendentals=0),
    )(*arrays)


def turned(values):
    lane = lax.broadcasted_iota(jnp.int32, values.shape, 1)
    rolled = pltpu.roll(values, HD // 2, 1)
    return jnp.where(lane < HD // 2, -rolled, rolled)


def query_key_body(width, raw_ref, squares_ref, cos_ref, sin_ref, gain_ref, q_ref, k_ref, v_ref):
    part = q_ref.shape[1]
    scales = lax.rsqrt(squares_ref[...] / width + epsilon)
    for which, out in enumerate((q_ref, k_ref)):
        for first in range(0, part, HD):
            gain = gain_ref[which : which + 1, first : first + HD]
            unit = raw_ref[:, which * part + first : which * part + first + HD] * scales[:, which : which + 1] * gain
            out[:, first : first + HD] = (unit * cos_ref[...] + turned(unit) * sin_ref[...]).astype(bf16)
    v_ref[...] = raw_ref[:, 2 * part :].astype(bf16)


def query_key(raw, squares, cosine, sine_tab, gains, width):
    tokens, part = raw.shape[0], raw.shape[1] // 3
    block = min(256, tokens)
    shape = jax.ShapeDtypeStruct((tokens, part), bf16)

    def by_rows(cols):
        return vmem((block, cols), lambda at: (at, 0))

    return pl.pallas_call(
        functools.partial(query_key_body, width),
        grid=(tokens // block,),
        in_specs=[by_rows(3 * part), by_rows(2), by_rows(HD), by_rows(HD), vmem(gains.shape)],
        out_specs=[by_rows(part)] * 3,
        out_shape=[shape] * 3,
        compiler_params=kernel_params(),
    )(raw, squares, cosine, sine_tab, gains)


def key_weights(query, key, seg_query, seg_key, first, count):
    scores = contract(key, query, 1, 1) * HD ** (-0.5)
    shape = scores.shape
    allowed = (seg_key == seg_query) & (
        lax.broadcasted_iota(jnp.int32, shape, 0) <= first + lax.broadcasted_iota(jnp.int32, shape, 1)
    )
    scores = jnp.where(allowed, scores, masked_score)
    expos = jnp.exp(scores - jnp.max(scores, 0, keepdims=True))
    return expos * (1.0 / jnp.sum(expos, 0, keepdims=True))


def attend_body(blocks, q_ref, k_ref, v_ref, seg_q_ref, seg_k_ref, out_ref):
    rows = q_ref.shape[0]
    for at in range(blocks):
        seen = (at + 1) * rows

        @pl.when(pl.program_id(1) == at)
        def _():
            probs = key_weights(
                q_ref[...], k_ref[:seen], seg_q_ref[...], seg_k_ref[:seen], at * rows, seen
            ).astype(bf16)
            out_ref[...] = contract(probs, v_ref[:seen], 0, 0).astype(bf16)


def attention_specs(tokens, block):
    by_query = vmem((block, HD), lambda head, at: (at, head))
    by_head = vmem((tokens, HD), lambda head, at: (0, head))
    return by_query, by_head, [vmem((1, block), lambda head, at: (0, at)), vmem((tokens, 1))]


def attend(query, key, value, seg_ids):
    tokens, part = query.shape
    block = min(256, tokens)
    by_query, by_head, segs = attention_specs(tokens, block)
    return pl.pallas_call(
        functools.partial(attend_body, tokens // block),
        grid=(part // HD, tokens // block),
        in_specs=[by_query, by_head, by_head, *segs],
        out_specs=by_query,
        out_shape=jax.ShapeDtypeStruct(query.shape, bf16),
        compiler_params=kernel_params(),
    )(query, key, value, seg_ids[None, :], seg_ids[:, None])


def attend_back_body(
    blocks, q_ref, k_ref, v_ref, g_ref, seg_q_ref, seg_k_ref, dq_ref, dk_ref, dv_ref, dk_sum, dv_sum
):
    rows = q_ref.shape[0]
    scale = HD ** (-0.5)
    for at in range(blocks):
        seen = (at + 1) * rows

        @pl.when(pl.program_id(1) == at)
        def _():
            query, grad = q_ref[...], g_ref[...]
            probs = key_weights(query, k_ref[:seen], seg_q_ref[...], seg_k_ref[:seen], at * rows, seen)
            d_probs = contract(v_ref[:seen], grad, 1, 1)
            inner = jnp.sum(probs * d_probs, 0, keepdims=True)
            d_scores = (probs * (d_probs - inner)).astype(bf16)
            dq_ref[...] = (contract(d_scores, k_ref[:seen], 0, 0) * scale).astype(bf16)
            d_key = contract(d_scores, query, 1, 0) * scale
            d_value = contract(probs.astype(bf16), grad, 1, 0)
            old = seen - rows
            dk_sum[old:seen] = d_key[old:]
            dv_sum[old:seen] = d_value[old:]
            if at:
                dk_sum[:old] += d_key[:old]
                dv_sum[:old] += d_value[:old]
            if at == blocks - 1:
                dk_ref[...] = dk_sum[...].astype(bf16)
                dv_ref[...] = dv_sum[...].astype(bf16)


def attend_back(query, key, value, grad, seg_ids):
    tokens, part = query.shape
    block = min(256, tokens)
    by_query, by_head, segs = attention_specs(tokens, block)
    shape = jax.ShapeDtypeStruct(query.shape, bf16)
    return pl.pallas_call(
        functools.partial(attend_back_body, tokens // block),
        grid=(part // HD, tokens // block),
        in_specs=[by_query, by_head, by_head, by_query, *segs],
        out_specs=[by_query, by_head, by_head],
        out_shape=[shape] * 3,
        scratch_shapes=[pltpu.VMEM((tokens, HD), f32)] * 2,
        compiler_params=kernel_params(),
    )(query, key, value, grad, seg_ids[None, :], seg_ids[:, None])


def rope_back(grad, cosine, sine_tab):
    return grad * cosine - turned(grad * sine_tab)


def unrope_body(width, dq_ref, dk_ref, raw_ref, squares_ref, cos_ref, sin_ref, gain_ref, dots_ref, gains_ref):
    part = dq_ref.shape[1]
    scales = lax.rsqrt(squares_ref[...] / width + epsilon)

    @pl.when(pl.program_id(0) == 0)
    def _():
        gains_ref[...] = jnp.zeros_like(gains_ref)

    for which, ref in enumerate((dq_ref, dk_ref)):
        dots = 0.0
        for first in range(0, part, HD):
            raw = raw_ref[:, which * part + first : which * part + first + HD]
            grad = rope_back(ref[:, first : first + HD].astype(f32), cos_ref[...], sin_ref[...])
            both = grad * raw
            gain = gain_ref[which : which + 1, first : first + HD]
            dots = dots + jnp.sum(both * gain, 1, keepdims=True)
            gains_ref[which : which + 1, first : first + HD] += jnp.sum(
                both * scales[:, which : which + 1], 0, keepdims=True
            )
        dots_ref[:, which : which + 1] = dots


def unrope(d_query, d_key, raw, squares, cosine, sine_tab, gains, width):
    tokens, part = d_query.shape
    block = min(256, tokens)

    def by_rows(cols):
        return vmem((block, cols), lambda at: (at, 0))

    return pl.pallas_call(
        functools.partial(unrope_body, width),
        grid=(tokens // block,),
        in_specs=[by_rows(part)] * 2
        + [by_rows(3 * part), by_rows(2), by_rows(HD), by_rows(HD), vmem(gains.shape)],
        out_specs=[by_rows(2), vmem((2, part))],
        out_shape=[jax.ShapeDtypeStruct((tokens, 2), f32), jax.ShapeDtypeStruct((2, part), f32)],
        compiler_params=kernel_params(),
    )(d_query, d_key, raw, squares, cosine, sine_tab, gains)


def raw_grad_body(width, dq_ref, dk_ref, dv_ref, raw_ref, squares_ref, dots_ref, cos_ref, sin_ref, gain_ref, out_ref):
    part = dq_ref.shape[1]
    scales = lax.rsqrt(squares_ref[...] / width + epsilon)
    cubes = scales * scales * scales * dots_ref[...] / width
    for which, ref in enumerate((dq_ref, dk_ref)):
        for first in range(0, part, HD):
            at = slice(which * part + first, which * part + first + HD)
            grad = rope_back(ref[:, first : first + HD].astype(f32), cos_ref[...], sin_ref[...])
            grad = grad * gain_ref[which : which + 1, first : first + HD]
            out_ref[:, at] = (
                scales[:, which : which + 1] * grad - raw_ref[:, at] * cubes[:, which : which + 1]
            ).astype(bf16)
    out_ref[:, 2 * part :] = dv_ref[...]


def raw_grad(d_query, d_key, d_value, raw, squares, dots, cosine, sine_tab, gains, width):
    tokens, part = d_query.shape
    block = min(256, tokens)

    def by_rows(cols):
        return vmem((block, cols), lambda at: (at, 0))

    return pl.pallas_call(
        functools.partial(raw_grad_body, width),
        grid=(tokens // block,),
        in_specs=[by_rows(part)] * 3
        + [by_rows(3 * part), by_rows(2), by_rows(2), by_rows(HD), by_rows(HD), vmem(gains.shape)],
        out_specs=by_rows(3 * part),
        out_shape=jax.ShapeDtypeStruct((tokens, 3 * part), bf16),
        compiler_params=kernel_params(),
    )(d_query, d_key, d_value, raw, squares, dots, cosine, sine_tab, gains)


def together(*trees):
    return lax.optimization_barrier(trees)


def next_one(block, axis):
    size = lax.axis_size(axis)
    return lax.ppermute(block, axis, [(i, (i + 1) % size) for i in range(size)])


def flipped(block, bit):
    size = lax.axis_size("dp")
    return lax.ppermute(block, "dp", [(i, i ^ bit) for i in range(size)])


def exchange(blocks, axis):
    size, here = lax.axis_size(axis), lax.axis_index(axis)
    got = []
    for step in range(size):
        block = lax.dynamic_index_in_dim(blocks, lax.rem(here + step, size), 0, keepdims=False)
        if step:
            block = lax.ppermute(block, axis, [(i, (i + step) % size) for i in range(size)])
        got.append(block)
    return got


def send_ahead(blocks, axis):
    size = lax.axis_size(axis)
    return [blocks[0]] + [
        lax.ppermute(blocks[step], axis, [(i, (i + step) % size) for i in range(size)]) for step in range(1, size)
    ]


def share_out(block, axis):
    size = lax.axis_size(axis)
    return [block] + [
        lax.ppermute(block, axis, [(i, (i + step) % size) for i in range(size)]) for step in range(1, size)
    ]


def assemble_body(parts, places, count, *refs):
    pieces, out, held, in_sems, out_sems = refs[:count], *refs[count:]
    reads, writes, first = [], [], 0
    for at, ((which, start, rows), place) in enumerate(zip(parts, places())):
        here = held.at[pl.ds(first, rows)]
        reads.append(pltpu.make_async_copy(pieces[which].at[pl.ds(start, rows)], here, in_sems.at[at]))
        writes.append(pltpu.make_async_copy(here, out.at[pl.ds(place, rows)], out_sems.at[at]))
        first += rows
    for read in reads:
        read.start()
    for read, write in zip(reads, writes):
        read.wait()
        write.start()
    for write in writes:
        write.wait()


def assemble(pieces, parts, places):
    shape = (sum(rows for _, _, rows in parts), pieces[0].shape[1])
    anywhere = pl.BlockSpec(memory_space=pl.ANY)
    sems = pltpu.SemaphoreType.DMA((len(parts),))
    size = shape[0] * shape[1] * pieces[0].dtype.itemsize
    return pl.pallas_call(
        functools.partial(assemble_body, parts, places, len(pieces)),
        in_specs=[anywhere] * len(pieces),
        out_specs=anywhere,
        out_shape=jax.ShapeDtypeStruct(shape, pieces[0].dtype),
        scratch_shapes=[pltpu.VMEM(shape, pieces[0].dtype), sems, sems],
        compiler_params=pltpu.CompilerParams(vmem_limit_bytes=size + 2**20),
        cost_estimate=pl.CostEstimate(flops=0, bytes_accessed=2 * size, transcendentals=0),
    )(*pieces)


def stacked(pieces, parts=None):
    parts = parts or [(at, 0, p.shape[0]) for at, p in enumerate(pieces)]
    places = [sum(rows for _, _, rows in parts[:at]) for at in range(len(parts))]
    return assemble(pieces, parts, lambda: places)


def in_order(slots, axis, first=0, rows=None):
    size, rows = len(slots), rows or slots[0].shape[0]

    def places():
        here = lax.axis_index(axis)
        return [pl.multiple_of(lax.rem(here + (size - back), size) * rows, rows) for back in range(size)]

    return assemble(slots, [(at, first, rows) for at in range(size)], places)


def cube_bits():
    bits = [1 << b for b in range(1, (lax.axis_size("dp") - 1).bit_length())]
    return bits, bits[1:] + bits[:1]


class CubeGather:
    def __init__(self, pair, core=False):
        self.arrays = [[block] for block in pair]
        self.masks = [[[0]] for _ in pair]
        self.orders = [list(bits) + [1] * core for bits in cube_bits()]
        self.new = []

    def step(self):
        for at, arrays in enumerate(self.arrays):
            if len(arrays) > 1:
                self.arrays[at] = [stacked(arrays)]
                self.masks[at] = [sum(self.masks[at], [])]
        self.new = [flipped(arrays[0], order[0]) for arrays, order in zip(self.arrays, self.orders)]

    def set(self, new):
        for at, block in enumerate(new):
            bit = self.orders[at].pop(0)
            self.arrays[at].append(block)
            self.masks[at].append([m ^ bit for m in self.masks[at][0]])
        self.new = []

    def finish(self):
        self.set(self.new)
        while self.orders[0]:
            self.step()
            self.set(self.new)


def cube_join(cube, firsts, rows, fold=1):
    pieces, parts, where = [], [], []
    for (own, first), arrays, masks in zip(firsts, cube.arrays, cube.masks):
        step = arrays[0].shape[0] // len(masks[0])
        for array, blocks in zip(arrays, masks):
            for at, mask in enumerate(blocks):
                parts.append((len(pieces), at * step, step))
                where.append((own ^ mask, first))
            pieces.append(array)

    def places():
        here = lax.axis_index("dp")
        return [pl.multiple_of((here ^ mask) // fold * rows + first, step) for mask, first in where]

    return assemble(pieces, parts, places)


class CubeScatter:
    def __init__(self, pair, core=False):
        self.totals, self.got = list(pair), None
        self.orders = [[1] * core + list(bits) for bits in cube_bits()]
        self.dims = [sorted(order, reverse=True) for order in self.orders]

    def add(self):
        if self.got:
            self.totals = [t.astype(f32) + g.astype(f32) for t, g in zip(self.totals, self.got)]
        self.got = None
        return self.totals

    def step(self):
        self.add()
        got = []
        for which, total in enumerate(self.totals):
            bit = self.orders[which].pop(0)
            at = self.dims[which].index(bit)
            self.dims[which].remove(bit)
            mine = (lax.axis_index("dp") // bit) % 2
            away = lax.dynamic_index_in_dim(total, 1 - mine, at, keepdims=False).astype(bf16)
            got.append(flipped(away, bit))
            self.totals[which] = lax.dynamic_index_in_dim(total, mine, at, keepdims=False)
        self.got = got

    def finish(self):
        while self.orders[0]:
            self.step()
        return jnp.concatenate(self.add(), 1)


def column_halves(grad, core):
    bits = (lax.axis_size("dp") - 1).bit_length() - (not core)
    cut = grad.shape[1] // 2
    shape = (2,) * bits + (-1, cut)
    return [grad[:, :cut].reshape(shape), grad[:, cut:].reshape(shape)]


def gather_small(block):
    size, here = lax.axis_size("seq"), lax.axis_index("seq")
    joined = jnp.zeros((size,) + block.shape, block.dtype)
    for back, slot in enumerate(share_out(block, "seq")):
        joined = lax.dynamic_update_index_in_dim(joined, slot, lax.rem(here + size - back, size), 0)
    block = joined.transpose(1, 0, 2).reshape(block.shape[0], -1)
    here, wide = lax.axis_index("dp"), block.shape[1]
    table = {0: block}
    for bit in cube_bits()[0] + [1]:
        table.update({m ^ bit: flipped(v, bit) for m, v in table.items()})
    joined = jnp.zeros((block.shape[0], wide * len(table)), block.dtype)
    for mask, piece in table.items():
        joined = lax.dynamic_update_slice_in_dim(joined, piece, (here ^ mask) * wide, 1)
    return joined


def scatter_small(values):
    copies, size, here = lax.axis_size("dp"), lax.axis_size("seq"), lax.axis_index("dp")
    blocks = values.reshape(values.shape[0], copies, size, -1).transpose(2, 1, 0, 3)
    total = sum(exchange(blocks, "seq"))
    for bit in reversed([1] + cube_bits()[0]):
        total = total.reshape((2, total.shape[0] // 2) + total.shape[1:])
        mine = (here // bit) % 2
        away = lax.dynamic_index_in_dim(total, 1 - mine, 0, keepdims=False)
        total = lax.dynamic_index_in_dim(total, mine, 0, keepdims=False) + flipped(away, bit)
    return total[0]


def small_sum(values, axis):
    return sum(share_out(values.reshape(-1), axis)).reshape(values.shape)


def local(
    tokens,
    segments,
    w_query,
    w_key,
    w_value,
    w_out,
    g_query,
    g_key,
    g_attn,
    w_gate,
    w_up,
    w_down,
    g_ffn,
    d_out,
):
    seqs, local_len, width = tokens.shape
    rows = seqs * local_len
    copies, size = lax.axis_size("dp"), lax.axis_size("seq")
    here = lax.axis_index("seq")
    total_len = size * local_len
    part = width // size
    heads = H // size
    own_rows = w_gate.shape[0]
    ff_width = w_gate.shape[1]
    ff_part = ff_width // size
    ff_own = w_down.shape[0]
    tok_rows = tokens.reshape(rows, width)

    side = width // copies
    pairs = copies // 2
    ff_half = ff_part // 2
    slots = range(size)

    def before(back):
        return lax.rem(lax.axis_index("seq") + (size - back), size)

    def behind(ahead):
        return lax.rem(lax.axis_index("seq") + ahead, size)

    def ff_column(pair, other, seq_at):
        return pl.multiple_of(((pair * 2 + (lax.rem(lax.axis_index("dp"), 2) ^ other)) * size + seq_at) * ff_own, ff_own)

    def ff_pack(weight):
        if ff_own % 128:
            core = lax.rem(lax.axis_index("dp"), 2)
            blocks = weight.reshape(own_rows, pairs, 2, size, ff_own).transpose(2, 3, 0, 1, 4)
            blocks = blocks.reshape(2, size, own_rows, ff_half)
            blocks = jnp.concatenate(
                [lax.dynamic_index_in_dim(blocks, c, 0, keepdims=False) for c in (core, 1 - core)], 1
            )
            return [lax.dynamic_index_in_dim(blocks, behind(ahead), 0, keepdims=False) for ahead in slots]
        return relayout(
            [weight],
            [(2 * own_rows, ff_half)] * size,
            bf16,
            lambda: [
                ((0, 0, ff_column(pair, other, behind(ahead))), (ahead, other * own_rows, pair * ff_own), (own_rows, ff_own))
                for ahead in slots
                for other in (0, 1)
                for pair in range(pairs)
            ],
        )

    def ff_unpack(got):
        if ff_own % 128:
            core = lax.rem(lax.axis_index("dp"), 2)
            joined = in_order(got, "seq").reshape(size, 2, own_rows, pairs, ff_own)
            joined = jnp.where(core == 0, joined, joined[:, ::-1])
            return joined.transpose(2, 3, 1, 0, 4).reshape(own_rows, ff_width).astype(f32)
        return relayout(
            got,
            [(own_rows, ff_width)],
            f32,
            lambda: [
                ((back, other * own_rows, pair * ff_own), (0, 0, ff_column(pair, other, before(back))), (own_rows, ff_own))
                for back in slots
                for other in (0, 1)
                for pair in range(pairs)
            ],
        )[0]

    def ff_pair(got):
        mine, away = [in_order(got, "seq", first, own_rows) for first in (0, own_rows)]
        return [mine, flipped(away, 1)]

    def two_parts(got):
        joined = in_order(got, "seq")
        return [joined[: side // 2], joined[side // 2 :]]

    def part_column(seq_at):
        return pl.multiple_of(seq_at * part, part)

    def part_row(seq_at):
        return pl.multiple_of(seq_at * rows, rows)

    gains, w_down_own = together(gather_small(jnp.stack([g_query, g_key, g_attn, g_ffn], 0)), w_down)
    gains = gains.astype(f32)
    qkv_send = relayout(
        [w_query, w_key, w_value],
        [(own_rows, 3 * part)] * size,
        bf16,
        lambda: [
            ((which, 0, part_column(behind(ahead))), (ahead, 0, which * part), (own_rows, part))
            for ahead in slots
            for which in range(3)
        ],
    )
    qkv_got = send_ahead(qkv_send, "seq")
    cube_down = CubeGather([w_down_own[: ff_own // 2], w_down_own[ff_own // 2 :]])
    cube_down.step()
    gate_send, up_send = ff_pack(w_gate), ff_pack(w_up)
    qkv_got, new, gate_send, x_own, w_out_own = together(qkv_got, cube_down.new, gate_send, tok_rows, w_out)
    cube_down.set(new)

    gate_got = send_ahead(gate_send, "seq")
    cube_qkv = CubeGather(two_parts(qkv_got), core=True)
    cube_qkv.step()
    gate_got, new, x_own = together(gate_got, cube_qkv.new, x_own)
    cube_qkv.set(new)

    x_slots = [x_own]
    cube_qkv.step()
    cube_gate = CubeGather(ff_pair(gate_got))
    cube_gate.step()
    for at in range(size - 1):
        x_next = next_one(x_slots[-1], "seq")
        if at == 0:
            x_next, new, more = together(x_next, cube_qkv.new, cube_gate.new)
            cube_qkv.set(new)
            cube_gate.set(more)
            cube_qkv.step()
            cube_gate.step()
        elif at == 1:
            x_next, new, more = together(x_next, cube_qkv.new, cube_gate.new)
            cube_qkv.set(new)
            cube_gate.set(more)
            cube_down.step()
        x_slots.append(x_next)
    cube_qkv.finish()
    cube_gate.finish()
    w_qkv = cube_join(cube_qkv, ((0, 0), (0, side // 2)), side)

    x_all = in_order(x_slots, "seq")
    gain_attn, gain_ffn = gains[2], gains[3]
    gain_qk = lax.dynamic_slice_in_dim(gains[:2], here * part, part, 1)
    cosine, sine_tab = rope_tables(positions(segments).reshape(total_len))
    qkv = product(x_all, w_qkv)
    squares = jnp.stack([jnp.sum(jnp.square(qkv[:, first : first + part]), -1) for first in (0, part)], 0)
    squares = small_sum(squares, "seq")
    squares, new, w_out_own, up_send = together(squares, cube_down.new, w_out_own, up_send)
    cube_down.set(new)
    out_got = share_out(w_out_own, "seq")
    w_gate_part = cube_join(cube_gate, ((0, 0), (1, 0)), side)
    squares = squares.T
    query, key, value = query_key(qkv, squares, cosine, sine_tab, gain_qk, width)
    query, out_got, w_gate_part = together(query, out_got, w_gate_part)
    cube_out = CubeGather(two_parts(out_got), core=True)
    cube_out.step()
    up_got = send_ahead(up_send, "seq")
    seg_ids = segments.reshape(total_len)
    attended = attend(query, key, value, seg_ids)
    attended = relayout(
        [attended],
        [(rows, part)] * size,
        bf16,
        lambda: [((0, part_row(behind(ahead)), 0), (ahead, 0, 0), (rows, part)) for ahead in slots],
    )
    attended, up_got, new = together(attended, up_got, cube_out.new)
    cube_out.set(new)
    attended = send_ahead(attended, "seq")
    cube_out.step()
    cube_up = CubeGather(ff_pair(up_got))
    cube_down.finish()
    w_down_part = cube_join(cube_down, ((0, 0), (0, ff_own // 2)), ff_own, 2)
    attended, new, w_down_part = together(attended, cube_out.new, w_down_part)
    cube_out.set(new)
    cube_out.finish()
    cube_up.step()
    w_out_all = cube_join(cube_out, ((0, 0), (0, side // 2)), side)
    attended = relayout(
        attended,
        [(rows, width)],
        bf16,
        lambda: [((back, 0, 0), (0, 0, part_column(before(back))), (rows, part)) for back in slots],
    )[0]

    cube_up.finish()
    w_up_part = cube_join(cube_up, ((0, 0), (1, 0)), side)
    a_proj = product(attended, w_out_all)
    a_scale = rms_scale(a_proj)
    hidden = tok_rows.astype(f32) + a_proj * a_scale * gain_attn

    def ring(block, work, last=lambda: (), beside=lambda early: ()):
        got, own = None, None
        for at in range(size):
            later = next_one(block, "seq") if at < size - 1 else None
            share = work(stacked([block, flipped(block, 1)]))
            if later is None:
                share, early = together(share, last())
            share, away = share[:rows], share[rows:].astype(bf16)
            if later is not None:
                later, share, away = together(later, share, away)
            share = share + flipped(away, 1).astype(f32)
            if at == 0:
                own = share
            else:
                if at > 1:
                    share = share + got.astype(f32)
                got = next_one(share.astype(bf16), "seq")
            block = later
        got, extra = together(got, beside(early))
        return own + got.astype(f32), extra

    h_slots, gates, ups, inners = [], [], [], []

    def forward(h_low):
        gate = product(h_low, w_gate_part)
        up = product(h_low, w_up_part)
        inner = (jax.nn.silu(gate) * up).astype(bf16)
        h_slots.append(h_low)
        gates.append(gate)
        ups.append(up)
        inners.append(inner)
        return product(inner, w_down_part)

    m_proj, _ = ring(hidden.astype(bf16), forward)
    m_scale = rms_scale(m_proj)
    out = (hidden + m_proj * m_scale * gain_ffn).astype(bf16).reshape(tokens.shape)
    grad_out = d_out.reshape(rows, width).astype(f32)
    d_gain_ffn = jnp.sum(grad_out * m_proj * m_scale, 0)
    dm_low = norm_back(m_proj, m_scale, grad_out * gain_ffn).astype(bf16)
    dms, d_gates, d_ups = [], [], []

    def backward(dm_slot):
        at = len(dms)
        gate, up = gates[at], ups[at]
        d_inner = against(dm_slot, w_down_part)
        sigmoid_gate = jax.nn.sigmoid(gate)
        d_gate = (d_inner * up * sigmoid_gate * (1.0 + gate * (1.0 - sigmoid_gate))).astype(bf16)
        d_up = (d_inner * (gate * sigmoid_gate)).astype(bf16)
        dms.append(dm_slot)
        d_gates.append(d_gate)
        d_ups.append(d_up)
        return against(d_gate, w_gate_part) + against(d_up, w_up_part)

    def down_grad():
        return weight_grad(stacked(inners), stacked(dms)).astype(bf16)

    def grads(d_down):
        cube = CubeScatter(column_halves(d_down, False))
        cube.step()
        sums.append(cube)
        h_all = stacked(h_slots)
        d_gate = weight_grad(h_all, stacked(d_gates)).astype(bf16)
        d_up = weight_grad(h_all, stacked(d_ups)).astype(bf16)
        return d_gate, d_up, cube.got

    sums = []

    d_sum, (d_gate, d_up, got) = ring(dm_low, backward, down_grad, grads)
    cube_down = sums[0]
    cube_down.got = got

    def ff_rows(total):
        core = lax.rem(lax.axis_index("dp"), 2)
        total = total.astype(bf16).reshape(2, side, ff_half)
        mine, away = [lax.dynamic_index_in_dim(total, c, 0, keepdims=False) for c in (core, 1 - core)]
        away = flipped(away, 1)

        def moves():
            return [
                ((which, pl.multiple_of(behind(ahead) * own_rows, own_rows), 0), (ahead, which * own_rows, 0), (own_rows, ff_half))
                for ahead in slots
                for which in (0, 1)
            ]

        return relayout([mine, away], [(2 * own_rows, ff_half)] * size, bf16, moves)

    cube_down.step()
    cube_gate = CubeScatter(column_halves(d_gate, False))
    cube_gate.step()
    d_hidden = grad_out + d_sum
    d_gain_attn = jnp.sum(d_hidden * a_proj * a_scale, 0)
    da_low = norm_back(a_proj, a_scale, d_hidden * gain_attn).astype(bf16)
    d_attended = against(da_low, w_out_all).astype(bf16)
    d_attended = relayout(
        [d_attended],
        [(rows, part)] * size,
        bf16,
        lambda: [((0, 0, part_column(behind(ahead))), (ahead, 0, 0), (rows, part)) for ahead in slots],
    )
    d_attended = send_ahead(d_attended, "seq")
    d_w_out = weight_grad(attended, da_low).astype(bf16)
    d_attended, cube_gate.got, cube_down.got, d_w_out = together(d_attended, cube_gate.got, cube_down.got, d_w_out)
    d_down = cube_down.finish()
    cube_gate.step()
    cube_up = CubeScatter(column_halves(d_up, False))
    cube_up.step()
    d_attended = in_order(d_attended, "seq")

    d_query, d_key, d_value = attend_back(query, key, value, d_attended, seg_ids)
    d_query, cube_gate.got, cube_up.got = together(d_query, cube_gate.got, cube_up.got)
    cube_up.step()
    dots, d_gain_qk = unrope(d_query, d_key, qkv, squares, cosine, sine_tab, gain_qk, width)
    dots = small_sum(dots.T, "seq")
    gate_send = ff_rows(cube_gate.finish())
    dots, gate_send, cube_up.got = together(dots, gate_send, cube_up.got)
    gate_got = send_ahead(gate_send, "seq")
    d_qkv = raw_grad(d_query, d_key, d_value, qkv, squares, dots.T, cosine, sine_tab, gain_qk, width)
    up_send = ff_rows(cube_up.finish())
    d_slots = relayout(
        [d_qkv],
        [(rows, 3 * part)] * size,
        bf16,
        lambda: [((0, part_row(before(back)), 0), (back, 0, 0), (rows, 3 * part)) for back in slots],
    )
    cube_qkv = CubeScatter(column_halves(weight_grad(x_all, d_qkv).astype(bf16), True), core=True)
    cube_qkv.step()
    shares = [against(d_slots[back], w_qkv) for back in [*slots[1:], 0]]
    shares, gate_got, up_send, cube_qkv.got = together(shares, gate_got, up_send, cube_qkv.got)
    got = next_one(shares[0].astype(bf16), "seq")
    cube_qkv.step()
    up_got = send_ahead(up_send, "seq")
    got, cube_qkv.got, up_got = together(got, cube_qkv.got, up_got)
    cube_qkv.step()
    cube_out = CubeScatter(column_halves(d_w_out, True), core=True)
    cube_out.step()
    for back in range(2, size):
        got = next_one((shares[back - 1] + got.astype(f32)).astype(bf16), "seq")
        if back == 2:
            got, cube_qkv.got, cube_out.got = together(got, cube_qkv.got, cube_out.got)
            cube_out.step()
    d_w_qkv = cube_qkv.finish()
    d_w_out = cube_out.finish()
    d_tokens = d_hidden + shares[-1] + got.astype(f32)

    def row_blocks(total):
        wide = total.shape[1]
        return relayout(
            [total],
            [(own_rows, wide)] * size,
            bf16,
            lambda: [
                ((0, pl.multiple_of(behind(ahead) * own_rows, own_rows), 0), (ahead, 0, 0), (own_rows, wide))
                for ahead in slots
            ],
        )

    d_w_qkv = send_ahead(row_blocks(d_w_qkv), "seq")
    d_w_out = sum(g.astype(f32) for g in send_ahead(row_blocks(d_w_out), "seq"))
    d_w_qkv = relayout(
        d_w_qkv,
        [(own_rows, width)] * 3,
        f32,
        lambda: [
            ((back, 0, which * part), (which, 0, part_column(before(back))), (own_rows, part))
            for back in slots
            for which in range(3)
        ],
    )
    d_w_gate, d_w_up = ff_unpack(gate_got), ff_unpack(up_got)

    d_gain_qk = lax.dynamic_update_slice_in_dim(jnp.zeros((2, width), f32), d_gain_qk, here * part, 1)
    d_gains = scatter_small(jnp.concatenate([d_gain_qk, d_gain_attn[None], d_gain_ffn[None]], 0))
    return (
        out,
        d_tokens.reshape(tokens.shape),
        d_w_qkv[0],
        d_w_qkv[1],
        d_w_qkv[2],
        d_w_out,
        d_gains[0],
        d_gains[1],
        d_gains[2],
        d_w_gate,
        d_w_up,
        d_down,
        d_gains[3],
    )


def solution(mesh):
    rows = P("dp", "seq", None)
    mat = P(("dp", "seq"), None)
    vec = P(("dp", "seq"))
    in_specs = (rows, P("dp", None), mat, mat, mat, mat, vec, vec, vec, mat, mat, mat, vec, rows)
    out_specs = (rows, rows, mat, mat, mat, mat, vec, vec, vec, mat, mat, mat, vec)
    return jax.shard_map(local, mesh=mesh, in_specs=in_specs, out_specs=out_specs, check_vma=False)
```

time: 1150 us -> 1020 us (0.89)
  Pallas kernels: 0 us -> 102 us
  matrix products: 233 us -> 141 us
  waiting for transfers between devices: 513 us -> 461 us
  other arithmetic: 98 us -> 56.6 us
  local copies, waits for them, and re-layouts: 144 us -> 103 us
  between operations: 17.4 us -> 4.33 us
    pallas_call x0 -> x59, Pallas kernels: none -> 102 us  [the longest x40 40.7 us: assemble(): pl.pallas_call(functools.partial(assemble_body, parts, places, len(pieces...]
    ppermute x18 -> x3, waiting for transfers between devices: 104 us -> 5.01 us  [exchange(): lax.ppermute(block, axis, [(i, (i + step) % size) for i in range(size)])]
    ppermute x6 -> x39, waiting for transfers between devices: 0.02 us -> 91.5 us  [the longest x27 86.4 us: send_ahead(): lax.ppermute(blocks[step], axis, [(i, (i + step) % size) for i in range(s...]
    ppermute x64 -> x78, waiting for transfers between devices: 204 us -> 135 us  [flipped(): return lax.ppermute(block, 'dp', [(i, i ^ bit) for i in range(size)])]
    ppermute x6 -> x39, starting transfers between devices: 5.69 us -> 60.2 us  [the longest x27 42.4 us: send_ahead(): lax.ppermute(blocks[step], axis, [(i, (i + step) % size) for i in range(s...]
    dynamic_update_slice x69 -> x5, local copies, waits for them, and re-layouts: 45.7 us -> 0.16 us  [the longest x4 0.15 us: gather_small(): lax.dynamic_update_index_in_dim(joined, slot, lax.rem(here + size - back,...]
    ppermute x18 -> x3, starting transfers between devices: 45.4 us -> 4.37 us  [exchange(): lax.ppermute(block, axis, [(i, (i + step) % size) for i in range(size)])]
    dot_general x14 -> x17, matrix products: 85.3 us -> 52.5 us  [against(): lax.dot_general(left, right, (((1,), (1,)), ((), ())), preferred_element_...]
  transfers between devices with their start and end apart: 113 -> 138, of which waited for: 46 -> 59; matrix products, arithmetic and copies ran while one was open for 39% -> 22% of each run, Pallas kernels for 0% -> 8%
where the time goes in v3:
time: 1020 us; the launch traced here: 1010 us
  waiting for transfers between devices  461 us (45%)
  starting transfers between devices  142 us (14%)
  matrix products  141 us (14%)
  local copies, waits for them, and re-layouts  103 us (10%)
  Pallas kernels  102 us (10%)
  other arithmetic  56.6 us (6%)
    ppermute x18, waiting for transfers between devices, next_one(): return lax.ppermute(block, axis, [(i, (i + 1) % size) for i in range(size)])  229 us
    ppermute x78, waiting for transfers between devices, flipped(): return lax.ppermute(block, 'dp', [(i, i ^ bit) for i in range(size)])  135 us
    ppermute x27, waiting for transfers between devices, send_ahead(): lax.ppermute(blocks[step], axis, [(i, (i + step) % size) for i in range(s...  86.4 us
    ppermute x78, starting transfers between devices, flipped(): return lax.ppermute(block, 'dp', [(i, i ^ bit) for i in range(size)])  54 us
    unnamed x347, local copies, waits for them, and re-layouts  53.8 us
    dot_general x17, matrix products, against(): lax.dot_general(left, right, (((1,), (1,)), ((), ())), preferred_element_...  52.5 us
    dot_general x5, matrix products, weight_grad(): lax.dot_general(left, right, (((0,), (0,)), ((), ())), preferred_element_...  47.7 us
    ppermute x27, starting transfers between devices, send_ahead(): lax.ppermute(blocks[step], axis, [(i, (i + step) % size) for i in range(s...  42.4 us
  transfers between devices with their start and end apart: 138, of which 59 were waited for; matrix products, arithmetic and copies ran while one was open for 22% of the time, Pallas kernels for 8%

profile of v3, /device:TPU:0, one launch (start us, length us, event | category | flops | bytes accessed | tf_op | source)
XLA Modules:
  0.0 1009.4 jit_solution(3524074343517381747)
XLA Ops:
  24.0 3.5 collective-permute-start.1
  27.8 5.7 collective-permute-done.refs_1_
  33.5 7.1 collective-permute-done.1.refs_2_
  43.9 4.5 collective-permute-start.15
  50.8 4.5 collective-permute-done.15.refs_1_
  55.3 9.0 collective-permute-done.16.refs_2_
  64.8 5.9 collective-permute-start.20
  79.4 26.9 %collective-permute-done.23.refs_1_ = bf16[256,1024]{1,0:T(8,128)(2,1)S(1)} collective-permute-done((bf16[256,1024]{1,0:T(8,128)(2,1)S(1)}, bf16[256,1024]{1,0:T(8,128)(2,1)S(1)}, u32[]{:S(2)}, u32[]{:S(2)}) %collective-permute-start.23) | collective-permute-done | bytes 524320 | tf_op jit(solution)/shard_map/ppermute | solution.py:307
  111.1 23.4 %collective-permute-done.26.refs_2_ = bf16[256,2048]{1,0:T(8,128)(2,1)S(1)} collective-permute-done((bf16[256,2048]{1,0:T(8,128)(2,1)S(1)}, bf16[256,2048]{1,0:T(8,128)(2,1)S(1)}, u32[]{:S(2)}, u32[]{:S(2)}) %collective-permute-start.26) | collective-permute-done | bytes 1048608 | tf_op jit(solution)/shard_map/ppermute | solution.py:302
  141.9 6.3 shard_map.252
  148.3 13.4 %collective-permute-done.31.refs_3_ = bf16[256,2048]{1,0:T(8,128)(2,1)S(1)} collective-permute-done((bf16[256,2048]{1,0:T(8,128)(2,1)S(1)}, bf16[256,2048]{1,0:T(8,128)(2,1)S(1)}, u32[]{:S(2)}, u32[]{:S(2)}) %collective-permute-start.31) | collective-permute-done | bytes 1048608 | tf_op jit(solution)/shard_map/ppermute | solution.py:302
  162.3 6.6 fusion.57.raw_ref
  190.9 4.6 shard_map.256
  200.9 4.0 collective-permute-start.40
  211.2 13.9 %shard_map.258.refs_0_ = bf16[1024,512]{1,0:T(8,128)(2,1)S(1)} custom-call(bf16[1024,512]{1,0:T(8,128)(2,1)S(1)} %copy-done.34, bf16[1024,512]{1,0:T(8,128)(2,1)S(1)} %copy-done.37, bf16[1024,512]{1,0:T(8,128)(2,1)S(1)} %copy-done.40, s32[1,1024]{1,0:T(1,128)S(1)} %copy-done.90, s32[1024,1]{1,0:T(8,128)S(1)} %copy.80.seg_k_ref), custom_call_target="tpu_custom_call" | custom-call | tf_op jit(solution)/shard_map/pallas_call | solution.py:164
  236.1 4.9 collective-permute-done.45.refs_1_
  241.7 7.2 collective-permute-done.46.refs_2_
  259.1 11.6 %collective-permute-done.54.refs_1_ = bf16[256,1024]{1,0:T(8,128)(2,1)S(1)} collective-permute-done((bf16[256,1024]{1,0:T(8,128)(2,1)S(1)}, bf16[256,1024]{1,0:T(8,128)(2,1)S(1)}, u32[]{:S(2)}, u32[]{:S(2)}) %collective-permute-start.54) | collective-permute-done | bytes 524320 | tf_op jit(solution)/shard_map/ppermute | solution.py:307
  281.5 14.2 %collective-permute-done.55.refs_1_ = bf16[512,1024]{1,0:T(8,128)(2,1)} collective-permute-done((bf16[512,1024]{1,0:T(8,128)(2,1)S(1)}, bf16[512,1024]{1,0:T(8,128)(2,1)}, u32[]{:S(2)}, u32[]{:S(2)}) %collective-permute-start.55) | collective-permute-done | bytes 1048608 | tf_op jit(solution)/shard_map/ppermute | solution.py:307
  300.2 4.6 collective-permute-start.52
  314.5 13.9 %collective-permute-done.52.refs_0_ = bf16[256,2048]{1,0:T(8,128)(2,1)S(1)} collective-permute-done((bf16[256,2048]{1,0:T(8,128)(2,1)S(1)}, bf16[256,2048]{1,0:T(8,128)(2,1)S(1)}, u32[]{:S(2)}, u32[]{:S(2)}) %collective-permute-start.52) | collective-permute-done | bytes 1048608 | tf_op jit(solution)/shard_map/ppermute | solution.py:302
  333.8 3.8 multiply_convert_fusion.10
  342.1 13.7 %collective-permute-done.60.refs_0_ = bf16[256,2048]{1,0:T(8,128)(2,1)S(1)} collective-permute-done((bf16[256,2048]{1,0:T(8,128)(2,1)S(1)}, bf16[256,2048]{1,0:T(8,128)(2,1)S(1)}, u32[]{:S(2)}, u32[]{:S(2)}) %collective-permute-start.60) | collective-permute-done | bytes 1048608 | tf_op jit(solution)/shard_map/ppermute | solution.py:302
  368.1 15.1 %collective-permute-done.62.refs_0_ = bf16[256,2048]{1,0:T(8,128)(2,1)S(1)} collective-permute-done((bf16[256,2048]{1,0:T(8,128)(2,1)S(1)}, bf16[256,2048]{1,0:T(8,128)(2,1)S(1)}, u32[]{:S(2)}, u32[]{:S(2)}) %collective-permute-start.62) | collective-permute-done | bytes 1048608 | tf_op jit(solution)/shard_map/ppermute | solution.py:302
  388.7 3.8 multiply_convert_fusion.8
  394.8 16.2 %collective-permute-done.68 = bf16[256,2048]{1,0:T(8,128)(2,1)S(1)} collective-permute-done((bf16[256,2048]{1,0:T(8,128)(2,1)S(1)}, bf16[256,2048]{1,0:T(8,128)(2,1)S(1)}, u32[]{:S(2)}, u32[]{:S(2)}) %collective-permute-start.68) | collective-permute-done | bytes 1048608 | tf_op jit(solution)/shard_map/ppermute | solution.py:302
  411.8 26.3 %collective-permute-done.69 = bf16[256,2048]{1,0:T(8,128)(2,1)S(1)} collective-permute-done((bf16[256,2048]{1,0:T(8,128)(2,1)S(1)}, bf16[256,2048]{1,0:T(8,128)(2,1)S(1)}, u32[]{:S(2)}, u32[]{:S(2)}) %collective-permute-start.69) | collective-permute-done | bytes 1048608 | tf_op jit(solution)/shard_map/ppermute | solution.py:302
  438.9 25.6 %collective-permute-done.70 = bf16[256,2048]{1,0:T(8,128)(2,1)S(1)} collective-permute-done((bf16[256,2048]{1,0:T(8,128)(2,1)S(1)}, bf16[256,2048]{1,0:T(8,128)(2,1)S(1)}, u32[]{:S(2)}, u32[]{:S(2)}) %collective-permute-start.70) | collective-permute-done | bytes 1048608 | tf_op jit(solution)/shard_map/ppermute | solution.py:302
  480.3 13.7 %collective-permute-done.71.refs_0_ = bf16[256,2048]{1,0:T(8,128)(2,1)S(1)} collective-permute-done((bf16[256,2048]{1,0:T(8,128)(2,1)S(1)}, bf16[256,2048]{1,0:T(8,128)(2,1)S(1)}, u32[]{:S(2)}, u32[]{:S(2)}) %collective-permute-start.71) | collective-permute-done | bytes 1048608 | tf_op jit(solution)/shard_map/ppermute | solution.py:302
  507.4 14.4 %collective-permute-done.74.refs_0_ = bf16[256,2048]{1,0:T(8,128)(2,1)S(1)} collective-permute-done((bf16[256,2048]{1,0:T(8,128)(2,1)S(1)}, bf16[256,2048]{1,0:T(8,128)(2,1)S(1)}, u32[]{:S(2)}, u32[]{:S(2)}) %collective-permute-start.74) | collective-permute-done | bytes 1048608 | tf_op jit(solution)/shard_map/ppermute | solution.py:302
  535.7 13.6 %collective-permute-done.76.refs_0_ = bf16[256,2048]{1,0:T(8,128)(2,1)S(1)} collective-permute-done((bf16[256,2048]{1,0:T(8,128)(2,1)S(1)}, bf16[256,2048]{1,0:T(8,128)(2,1)S(1)}, u32[]{:S(2)}, u32[]{:S(2)}) %collective-permute-start.76) | collective-permute-done | bytes 1048608 | tf_op jit(solution)/shard_map/ppermute | solution.py:302
  559.7 3.3 copy-done.3
  563.6 3.3 add_convert_fusion.4
  576.8 4.4 fusion.69
  581.2 12.9 %collective-permute-done.82 = bf16[256,2048]{1,0:T(8,128)(2,1)S(1)} collective-permute-done((bf16[256,2048]{1,0:T(8,128)(2,1)}, bf16[256,2048]{1,0:T(8,128)(2,1)S(1)}, u32[]{:S(2)}, u32[]{:S(2)}) %collective-permute-start.82) | collective-permute-done | bytes 1048608 | tf_op jit(solution)/shard_map/ppermute | solution.py:302
  599.3 7.1 convolution_add_fusion
  606.5 11.0 %convolution_convert_fusion.2 = bf16[1024,2048]{1,0:T(8,128)(2,1)} fusion(bf16[2048,1024]{1,0:T(8,128)(2,1)S(1)} %copy-done.31, bf16[2048,2048]{1,0:T(8,128)(2,1)S(1)} %shard_map.282), kind=kOutput, calls=%fused_computation.4 | convolution fusion | flops 8592031744 | bytes 16777216 | tf_op jit(solution)/shard_map/dot_general | solution.py:30
  626.5 11.4 %convolution_convert_fusion.4 = bf16[2048,1024]{1,0:T(8,128)(2,1)} fusion(bf16[2048,2048]{1,0:T(8,128)(2,1)S(1)} %bitcast.315, bf16[2048,1024]{1,0:T(8,128)(2,1)S(1)} %shard_map.284), kind=kOutput, calls=%fused_computation.6 | convolution fusion | flops 8592031744 | bytes 16777216 | tf_op jit(solution)/shard_map/dot_general | solution.py:30
  639.8 10.9 %convolution_convert_fusion.3 = bf16[2048,1024]{1,0:T(8,128)(2,1)} fusion(bf16[2048,2048]{1,0:T(8,128)(2,1)S(1)} %bitcast.315, bf16[2048,1024]{1,0:T(8,128)(2,1)S(1)} %shard_map.285), kind=kOutput, calls=%fused_computation.5 | convolution fusion | flops 8592031744 | bytes 16777216 | tf_op jit(solution)/shard_map/dot_general | solution.py:30
  651.2 15.7 %collective-permute-done.84 = bf16[256,2048]{1,0:T(8,128)(2,1)S(1)} collective-permute-done((bf16[256,2048]{1,0:T(8,128)(2,1)S(1)}, bf16[256,2048]{1,0:T(8,128)(2,1)S(1)}, u32[]{:S(2)}, u32[]{:S(2)}) %collective-permute-start.84) | collective-permute-done | bytes 1048608 | tf_op jit(solution)/shard_map/ppermute | solution.py:302
  694.7 3.6 convolution_convert_fusion.1
  706.1 13.6 %collective-permute-done.92 = bf16[256,1024]{1,0:T(8,128)(2,1)} collective-permute-done((bf16[256,1024]{1,0:T(8,128)(2,1)}, bf16[256,1024]{1,0:T(8,128)(2,1)}, u32[]{:S(2)}, u32[]{:S(2)}) %collective-permute-start.92) | collective-permute-done | bytes 524320 | tf_op jit(solution)/shard_map/ppermute | solution.py:307
  723.9 20.1 %shard_map.288 = (bf16[1024,512]{1,0:T(8,128)(2,1)S(1)}, bf16[1024,512]{1,0:T(8,128)(2,1)S(1)}, bf16[1024,512]{1,0:T(8,128)(2,1)S(1)}) custom-call(bf16[1024,512]{1,0:T(8,128)(2,1)S(1)} %copy-done.35, bf16[1024,512]{1,0:T(8,128)(2,1)S(1)} %copy-done.38, bf16[1024,512]{1,0:T(8,128)(2,1)} %copy-done.39, bf16[1024,512]{1,0:T(8,128)(2,1)} %copy-done.32, ...), custom_call_target="tpu_custom_call" | custom-call | tf_op jit(solution)/shard_map/pallas_call | solution.py:208
  754.2 3.8 fusion.48
  759.3 3.7 collective-permute-done.95
  763.8 6.3 shard_map.289
  786.2 3.8 collective-permute-start.134
  790.0 4.7 constant_dynamic-slice_fusion.10
  795.3 4.0 collective-permute-done.133
  806.2 6.9 shard_map.291.refs_0_
  815.2 10.8 %convolution_convert_fusion = bf16[2048,1536]{1,0:T(8,128)(2,1)} fusion(bf16[1024,2048]{1,0:T(8,128)(2,1)S(1)} %copy-done.22, bf16[1024,1536]{1,0:T(8,128)(2,1)} %shard_map.291.refs_0_), kind=kOutput, calls=%fused_computation | convolution fusion | flops 6445596672 | bytes 13631488 | tf_op jit(solution)/shard_map/dot_general | solution.py:30
  833.1 3.3 fusion.49
  853.4 4.0 collective-permute-done.106.refs_3_
  868.7 14.0 %collective-permute-done.135 = f32[4,4,64]{2,1,0:T(4,128)S(1)} collective-permute-done((f32[4,4,64]{2,1,0:T(4,128)S(1)}, f32[4,4,64]{2,1,0:T(4,128)S(1)}, u32[]{:S(2)}, u32[]{:S(2)}) %collective-permute-start.135) | collective-permute-done | bytes 4128 | tf_op jit(solution)/shard_map/ppermute | solution.py:307
  884.6 6.6 collective-permute-done.113.refs_1_
  893.3 8.2 collective-permute-done.114.refs_2_
  905.0 4.5 collective-permute-start.116
  913.3 7.4 collective-permute-done.117
  921.8 11.0 %collective-permute-done.116 = bf16[256,2048]{1,0:T(8,128)(2,1)S(1)} collective-permute-done((bf16[256,2048]{1,0:T(8,128)(2,1)S(1)}, bf16[256,2048]{1,0:T(8,128)(2,1)S(1)}, u32[]{:S(2)}, u32[]{:S(2)}) %collective-permute-start.116) | collective-permute-done | bytes 1048608 | tf_op jit(solution)/shard_map/ppermute | solution.py:302
  942.7 20.0 %collective-permute-done.127 = bf16[2,256,1024]{2,1,0:T(8,128)(2,1)} collective-permute-done((bf16[2,256,1024]{2,1,0:T(8,128)(2,1)}, bf16[2,256,1024]{2,1,0:T(8,128)(2,1)}, u32[]{:S(2)}, u32[]{:S(2)}) %collective-permute-start.127) | collective-permute-done | bytes 1048608 | tf_op jit(solution)/shard_map/ppermute | solution.py:307
  974.9 4.4 collective-permute-done.123.refs_2_
  981.3 4.1 collective-permute-start.131
  988.2 4.0 collective-permute-done.131
  992.2 15.8 %collective-permute-done.130 = bf16[64,2048]{1,0:T(8,128)(2,1)S(1)} collective-permute-done((bf16[64,2048]{1,0:T(8,128)(2,1)S(1)}, bf16[64,2048]{1,0:T(8,128)(2,1)S(1)}, u32[]{:S(2)}, u32[]{:S(2)}) %collective-permute-start.130) | collective-permute-done | bytes 262176 | tf_op jit(solution)/shard_map/ppermute | solution.py:324
  (814 shorter events, 394.8 us)
Async XLA Ops:
  42.8 22.0 %collective-permute-start.18 = (bf16[128,1536]{1,0:T(8,128)(2,1)S(1)}, bf16[128,1536]{1,0:T(8,128)(2,1)S(1)}, u32[]{:S(2)}, u32[]{:S(2)}) collective-permute-start(bf16[128,1536]{1,0:T(8,128)(2,1)S(1)} %get-tuple-element.425.refs_0_), channel_id=1, source_target_pairs={{0,8},{4,12},{8,0},{12,4},{16,24},{20,28},{24,16},{28,20},{1,9},{5... | collective-permute-start | bytes 1179656 | tf_op jit(solution)/shard_map/ppermute | solution.py:307
  64.8 41.5 %collective-permute-start.20 = (bf16[256,2048]{1,0:T(8,128)(2,1)S(1)}, bf16[256,2048]{1,0:T(8,128)(2,1)S(1)}, u32[]{:S(2)}, u32[]{:S(2)}) collective-permute-start(bf16[256,2048]{1,0:T(8,128)(2,1)S(1)} %bitcast.307), channel_id=1, source_target_pairs={{0,1},{1,2},{2,3},{3,0},{4,5},{5,6},{6,7},{7,4},{8,9},{9,10},{10,1... | collective-permute-start | bytes 3145736 | tf_op jit(solution)/shard_map/ppermute | solution.py:302
  73.0 33.3 %collective-permute-start.21 = (bf16[256,1536]{1,0:T(8,128)(2,1)S(1)}, bf16[256,1536]{1,0:T(8,128)(2,1)S(1)}, u32[]{:S(2)}, u32[]{:S(2)}) collective-permute-start(bf16[256,1536]{1,0:T(8,128)(2,1)S(1)} %shard_map.243.refs_0_), channel_id=1, source_target_pairs={{0,16},{4,20},{8,24},{12,28},{16,0},{20,4},{24,8},{28,12},{1,17},{... | collective-permute-start | bytes 2359304 | tf_op jit(solution)/shard_map/ppermute | solution.py:307
  75.4 31.0 %collective-permute-start.22 = (bf16[256,1536]{1,0:T(8,128)(2,1)S(1)}, bf16[256,1536]{1,0:T(8,128)(2,1)S(1)}, u32[]{:S(2)}, u32[]{:S(2)}) collective-permute-start(bf16[256,1536]{1,0:T(8,128)(2,1)S(1)} %shard_map.244.refs_0_), channel_id=1, source_target_pairs={{0,8},{4,12},{8,0},{12,4},{16,24},{20,28},{24,16},{28,20},{1,9},{5... | collective-permute-start | bytes 2359304 | tf_op jit(solution)/shard_map/ppermute | solution.py:307
  78.3 28.0 %collective-permute-start.23 = (bf16[256,1024]{1,0:T(8,128)(2,1)S(1)}, bf16[256,1024]{1,0:T(8,128)(2,1)S(1)}, u32[]{:S(2)}, u32[]{:S(2)}) collective-permute-start(bf16[256,1024]{1,0:T(8,128)(2,1)S(1)} %shard_map.245.refs_0_), channel_id=1, source_target_pairs={{0,8},{4,12},{8,0},{12,4},{16,24},{20,28},{24,16},{28,20},{1,9},{5... | collective-permute-start | bytes 1572872 | tf_op jit(solution)/shard_map/ppermute | solution.py:307
  78.9 27.4 %collective-permute-start.25 = (bf16[256,1024]{1,0:T(8,128)(2,1)S(1)}, bf16[256,1024]{1,0:T(8,128)(2,1)S(1)}, u32[]{:S(2)}, u32[]{:S(2)}) collective-permute-start(bf16[256,1024]{1,0:T(8,128)(2,1)S(1)} %collective-permute-done.24.refs_0_), channel_id=1, source_target_pairs={{0,16},{4,20},{8,24},{12,28},{16,0},{20,4},{24,8},{28,12},{1,17},{... | collective-permute-start | bytes 1572872 | tf_op jit(solution)/shard_map/ppermute | solution.py:307
  106.6 28.9 %collective-permute-start.27 = (bf16[512,1536]{1,0:T(8,128)(2,1)S(1)}, bf16[512,1536]{1,0:T(8,128)(2,1)S(1)}, u32[]{:S(2)}, u32[]{:S(2)}) collective-permute-start(bf16[512,1536]{1,0:T(8,128)(2,1)S(1)} %shard_map.247.refs_0_), channel_id=1, source_target_pairs={{0,4},{4,0},{8,12},{12,8},{16,20},{20,16},{24,28},{28,24},{1,5},{5... | collective-permute-start | bytes 4718600 | tf_op jit(solution)/shard_map/ppermute | solution.py:307
  107.0 28.5 %collective-permute-start.28 = (bf16[512,1536]{1,0:T(8,128)(2,1)S(1)}, bf16[512,1536]{1,0:T(8,128)(2,1)S(1)}, u32[]{:S(2)}, u32[]{:S(2)}) collective-permute-start(bf16[512,1536]{1,0:T(8,128)(2,1)S(1)} %shard_map.248.refs_2_), channel_id=1, source_target_pairs={{0,4},{4,0},{8,12},{12,8},{16,20},{20,16},{24,28},{28,24},{1,5},{5... | collective-permute-start | bytes 4718600 | tf_op jit(solution)/shard_map/ppermute | solution.py:307
  107.5 26.9 %collective-permute-start.26 = (bf16[256,2048]{1,0:T(8,128)(2,1)S(1)}, bf16[256,2048]{1,0:T(8,128)(2,1)S(1)}, u32[]{:S(2)}, u32[]{:S(2)}) collective-permute-start(bf16[256,2048]{1,0:T(8,128)(2,1)S(1)} %collective-permute-done.20.refs_1_), channel_id=1, source_target_pairs={{0,1},{1,2},{2,3},{3,0},{4,5},{5,6},{6,7},{7,4},{8,9},{9,10},{10,1... | collective-permute-start | bytes 3145736 | tf_op jit(solution)/shard_map/ppermute | solution.py:302
  107.8 26.7 %collective-permute-start.29 = (bf16[512,1024]{1,0:T(8,128)(2,1)S(1)}, bf16[512,1024]{1,0:T(8,128)(2,1)S(1)}, u32[]{:S(2)}, u32[]{:S(2)}) collective-permute-start(bf16[512,1024]{1,0:T(8,128)(2,1)S(1)} %shard_map.249.refs_0_), channel_id=1, source_target_pairs={{0,16},{4,20},{8,24},{12,28},{16,0},{20,4},{24,8},{28,12},{1,17},{... | collective-permute-start | bytes 3145736 | tf_op jit(solution)/shard_map/ppermute | solution.py:307
  108.6 25.9 %collective-permute-start.30 = (bf16[512,1024]{1,0:T(8,128)(2,1)S(1)}, bf16[512,1024]{1,0:T(8,128)(2,1)S(1)}, u32[]{:S(2)}, u32[]{:S(2)}) collective-permute-start(bf16[512,1024]{1,0:T(8,128)(2,1)S(1)} %shard_map.250.refs_2_), channel_id=1, source_target_pairs={{0,8},{4,12},{8,0},{12,4},{16,24},{20,28},{24,16},{28,20},{1,9},{5... | collective-permute-start | bytes 3145736 | tf_op jit(solution)/shard_map/ppermute | solution.py:307
  135.5 26.1 %collective-permute-start.31 = (bf16[256,2048]{1,0:T(8,128)(2,1)S(1)}, bf16[256,2048]{1,0:T(8,128)(2,1)S(1)}, u32[]{:S(2)}, u32[]{:S(2)}) collective-permute-start(bf16[256,2048]{1,0:T(8,128)(2,1)S(1)} %collective-permute-done.26.refs_2_), channel_id=1, source_target_pairs={{0,1},{1,2},{2,3},{3,0},{4,5},{5,6},{6,7},{7,4},{8,9},{9,10},{10,1... | collective-permute-start | bytes 3145736 | tf_op jit(solution)/shard_map/ppermute | solution.py:302
  138.5 38.1 %collective-permute-start.35 = (bf16[256,2048]{1,0:T(8,128)(2,1)S(1)}, bf16[256,2048]{1,0:T(8,128)(2,1)}, u32[]{:S(2)}, u32[]{:S(2)}) collective-permute-start(bf16[256,2048]{1,0:T(8,128)(2,1)S(1)} %shard_map.253.refs_0_), channel_id=1, source_target_pairs={{0,16},{4,20},{8,24},{12,28},{16,0},{20,4},{24,8},{28,12},{1,17},{... | collective-permute-start | bytes 3145736 | tf_op jit(solution)/shard_map/ppermute | solution.py:307
  140.3 36.3 %collective-permute-start.36 = (bf16[256,2048]{1,0:T(8,128)(2,1)S(1)}, bf16[256,2048]{1,0:T(8,128)(2,1)}, u32[]{:S(2)}, u32[]{:S(2)}) collective-permute-start(bf16[256,2048]{1,0:T(8,128)(2,1)S(1)} %shard_map.254.refs_2_), channel_id=1, source_target_pairs={{0,8},{4,12},{8,0},{12,4},{16,24},{20,28},{24,16},{28,20},{1,9},{5... | collective-permute-start | bytes 3145736 | tf_op jit(solution)/shard_map/ppermute | solution.py:307
  198.0 27.2 %collective-permute-start.43 = (bf16[128,2048]{1,0:T(8,128)(2,1)}, bf16[128,2048]{1,0:T(8,128)(2,1)}, u32[]{:S(2)}, u32[]{:S(2)}) collective-permute-start(bf16[128,2048]{1,0:T(8,128)(2,1)} %get-tuple-element.421.refs_0_), channel_id=1, source_target_pairs={{0,8},{4,12},{8,0},{12,4},{16,24},{20,28},{24,16},{28,20},{1,9},{5... | collective-permute-start | bytes 1572872 | tf_op jit(solution)/shard_map/ppermute | solution.py:307
  199.6 25.6 %collective-permute-start.44 = (bf16[128,2048]{1,0:T(8,128)(2,1)}, bf16[128,2048]{1,0:T(8,128)(2,1)}, u32[]{:S(2)}, u32[]{:S(2)}) collective-permute-start(bf16[128,2048]{1,0:T(8,128)(2,1)} %get-tuple-element.420.refs_0_), channel_id=1, source_target_pairs={{0,16},{4,20},{8,24},{12,28},{16,0},{20,4},{24,8},{28,12},{1,17},{... | collective-permute-start | bytes 1572872 | tf_op jit(solution)/shard_map/ppermute | solution.py:307
  200.9 24.2 %collective-permute-start.40 = (bf16[128,1024]{1,0:T(8,128)(2,1)}, bf16[128,1024]{1,0:T(8,128)(2,1)}, u32[]{:S(2)}, u32[]{:S(2)}) collective-permute-start(bf16[128,1024]{1,0:T(8,128)(2,1)} %get-tuple-element.252), channel_id=1, source_target_pairs={{0,1},{1,2},{2,3},{3,0},{4,5},{5,6},{6,7},{7,4},{8,9},{9,10},{10,1... | collective-permute-start | bytes 786440 | tf_op jit(solution)/shard_map/ppermute | solution.py:324
  226.7 23.7 %collective-permute-start.48 = (bf16[256,2048]{1,0:T(8,128)(2,1)S(1)}, bf16[256,2048]{1,0:T(8,128)(2,1)S(1)}, u32[]{:S(2)}, u32[]{:S(2)}) collective-permute-start(bf16[256,2048]{1,0:T(8,128)(2,1)S(1)} %shard_map.261.refs_0_), channel_id=1, source_target_pairs={{0,16},{4,20},{8,24},{12,28},{16,0},{20,4},{24,8},{28,12},{1,17},{... | collective-permute-start | bytes 3145736 | tf_op jit(solution)/shard_map/ppermute | solution.py:307
  228.8 22.9 %collective-permute-start.49 = (bf16[256,2048]{1,0:T(8,128)(2,1)S(1)}, bf16[256,2048]{1,0:T(8,128)(2,1)S(1)}, u32[]{:S(2)}, u32[]{:S(2)}) collective-permute-start(bf16[256,2048]{1,0:T(8,128)(2,1)S(1)} %shard_map.262.refs_0_), channel_id=1, source_target_pairs={{0,8},{4,12},{8,0},{12,4},{16,24},{20,28},{24,16},{28,20},{1,9},{5... | collective-permute-start | bytes 3145736 | tf_op jit(solution)/shard_map/ppermute | solution.py:307
  252.0 21.9 %collective-permute-start.50 = (bf16[512,2048]{1,0:T(8,128)(2,1)S(1)}, bf16[512,2048]{1,0:T(8,128)(2,1)}, u32[]{:S(2)}, u32[]{:S(2)}) collective-permute-start(bf16[512,2048]{1,0:T(8,128)(2,1)S(1)} %shard_map.265.refs_0_), channel_id=1, source_target_pairs={{0,4},{4,0},{8,12},{12,8},{16,20},{20,16},{24,28},{28,24},{1,5},{5... | collective-permute-start | bytes 6291464 | tf_op jit(solution)/shard_map/ppermute | solution.py:307
  270.8 24.9 %collective-permute-start.55 = (bf16[512,1024]{1,0:T(8,128)(2,1)S(1)}, bf16[512,1024]{1,0:T(8,128)(2,1)}, u32[]{:S(2)}, u32[]{:S(2)}) collective-permute-start(bf16[512,1024]{1,0:T(8,128)(2,1)S(1)} %shard_map.270.refs_0_), channel_id=1, source_target_pairs={{0,16},{4,20},{8,24},{12,28},{16,0},{20,4},{24,8},{28,12},{1,17},{... | collective-permute-start | bytes 3145736 | tf_op jit(solution)/shard_map/ppermute | solution.py:307
  273.2 24.8 %collective-permute-start.58 = (bf16[512,1024]{1,0:T(8,128)(2,1)}, bf16[512,1024]{1,0:T(8,128)(2,1)}, u32[]{:S(2)}, u32[]{:S(2)}) collective-permute-start(bf16[512,1024]{1,0:T(8,128)(2,1)} %shard_map.272.refs_2_), channel_id=1, source_target_pairs={{0,8},{4,12},{8,0},{12,4},{16,24},{20,28},{24,16},{28,20},{1,9},{5... | collective-permute-start | bytes 3145736 | tf_op jit(solution)/shard_map/ppermute | solution.py:307
  281.5 23.2 %collective-permute-start.53 = (bf16[256,2048]{1,0:T(8,128)(2,1)S(1)}, bf16[256,2048]{1,0:T(8,128)(2,1)S(1)}, u32[]{:S(2)}, u32[]{:S(2)}) collective-permute-start(bf16[256,2048]{1,0:T(8,128)(2,1)S(1)} %fusion.15.refs_0_), channel_id=1, source_target_pairs={{0,4},{4,0},{8,12},{12,8},{16,20},{20,16},{24,28},{28,24},{1,5},{5... | collective-permute-start | bytes 3145736 | tf_op jit(solution)/shard_map/ppermute | solution.py:307
  300.2 28.2 %collective-permute-start.52 = (bf16[256,2048]{1,0:T(8,128)(2,1)S(1)}, bf16[256,2048]{1,0:T(8,128)(2,1)S(1)}, u32[]{:S(2)}, u32[]{:S(2)}) collective-permute-start(bf16[256,2048]{1,0:T(8,128)(2,1)S(1)} %fusion.15.refs_0_), channel_id=1, source_target_pairs={{0,1},{1,2},{2,3},{3,0},{4,5},{5,6},{6,7},{7,4},{8,9},{9,10},{10,1... | collective-permute-start | bytes 3145736 | tf_op jit(solution)/shard_map/ppermute | solution.py:302
  328.4 27.4 %collective-permute-start.60 = (bf16[256,2048]{1,0:T(8,128)(2,1)S(1)}, bf16[256,2048]{1,0:T(8,128)(2,1)S(1)}, u32[]{:S(2)}, u32[]{:S(2)}) collective-permute-start(bf16[256,2048]{1,0:T(8,128)(2,1)S(1)} %collective-permute-done.52.refs_0_), channel_id=1, source_target_pairs={{0,1},{1,2},{2,3},{3,0},{4,5},{5,6},{6,7},{7,4},{8,9},{9,10},{10,1... | collective-permute-start | bytes 3145736 | tf_op jit(solution)/shard_map/ppermute | solution.py:302
  355.7 27.5 %collective-permute-start.62 = (bf16[256,2048]{1,0:T(8,128)(2,1)S(1)}, bf16[256,2048]{1,0:T(8,128)(2,1)S(1)}, u32[]{:S(2)}, u32[]{:S(2)}) collective-permute-start(bf16[256,2048]{1,0:T(8,128)(2,1)S(1)} %collective-permute-done.60.refs_0_), channel_id=1, source_target_pairs={{0,1},{1,2},{2,3},{3,0},{4,5},{5,6},{6,7},{7,4},{8,9},{9,10},{10,1... | collective-permute-start | bytes 3145736 | tf_op jit(solution)/shard_map/ppermute | solution.py:302
  355.9 27.4 %collective-permute-start.67 = (bf16[256,2048]{1,0:T(8,128)(2,1)S(1)}, bf16[256,2048]{1,0:T(8,128)(2,1)S(1)}, u32[]{:S(2)}, u32[]{:S(2)}) collective-permute-start(bf16[256,2048]{1,0:T(8,128)(2,1)S(1)} %slice.232), channel_id=1, source_target_pairs={{0,4},{4,0},{8,12},{12,8},{16,20},{20,16},{24,28},{28,24},{1,5},{5... | collective-permute-start | bytes 3145736 | tf_op jit(solution)/shard_map/ppermute | solution.py:307
  383.6 27.4 %collective-permute-start.68 = (bf16[256,2048]{1,0:T(8,128)(2,1)S(1)}, bf16[256,2048]{1,0:T(8,128)(2,1)S(1)}, u32[]{:S(2)}, u32[]{:S(2)}) collective-permute-start(bf16[256,2048]{1,0:T(8,128)(2,1)S(1)} %add_convert_fusion.7), channel_id=1, source_target_pairs={{0,1},{1,2},{2,3},{3,0},{4,5},{5,6},{6,7},{7,4},{8,9},{9,10},{10,1... | collective-permute-start | bytes 3145736 | tf_op jit(solution)/shard_map/ppermute | solution.py:302
  383.7 27.4 %collective-permute-start.66 = (bf16[256,2048]{1,0:T(8,128)(2,1)S(1)}, bf16[256,2048]{1,0:T(8,128)(2,1)S(1)}, u32[]{:S(2)}, u32[]{:S(2)}) collective-permute-start(bf16[256,2048]{1,0:T(8,128)(2,1)S(1)} %slice.231), channel_id=1, source_target_pairs={{0,4},{4,0},{8,12},{12,8},{16,20},{20,16},{24,28},{28,24},{1,5},{5... | collective-permute-start | bytes 3145736 | tf_op jit(solution)/shard_map/ppermute | solution.py:307
  411.5 26.6 %collective-permute-start.69 = (bf16[256,2048]{1,0:T(8,128)(2,1)S(1)}, bf16[256,2048]{1,0:T(8,128)(2,1)S(1)}, u32[]{:S(2)}, u32[]{:S(2)}) collective-permute-start(bf16[256,2048]{1,0:T(8,128)(2,1)S(1)} %add_convert_fusion.6), channel_id=1, source_target_pairs={{0,1},{1,2},{2,3},{3,0},{4,5},{5,6},{6,7},{7,4},{8,9},{9,10},{10,1... | collective-permute-start | bytes 3145736 | tf_op jit(solution)/shard_map/ppermute | solution.py:302
  411.8 26.4 %collective-permute-start.65 = (bf16[256,2048]{1,0:T(8,128)(2,1)S(1)}, bf16[256,2048]{1,0:T(8,128)(2,1)S(1)}, u32[]{:S(2)}, u32[]{:S(2)}) collective-permute-start(bf16[256,2048]{1,0:T(8,128)(2,1)S(1)} %slice.230), channel_id=1, source_target_pairs={{0,4},{4,0},{8,12},{12,8},{16,20},{20,16},{24,28},{28,24},{1,5},{5... | collective-permute-start | bytes 3145736 | tf_op jit(solution)/shard_map/ppermute | solution.py:307
  438.7 25.7 %collective-permute-start.70 = (bf16[256,2048]{1,0:T(8,128)(2,1)S(1)}, bf16[256,2048]{1,0:T(8,128)(2,1)S(1)}, u32[]{:S(2)}, u32[]{:S(2)}) collective-permute-start(bf16[256,2048]{1,0:T(8,128)(2,1)S(1)} %fusion.8), channel_id=1, source_target_pairs={{0,1},{1,2},{2,3},{3,0},{4,5},{5,6},{6,7},{7,4},{8,9},{9,10},{10,1... | collective-permute-start | bytes 3145736 | tf_op jit(solution)/shard_map/ppermute | solution.py:302
  438.8 25.7 %collective-permute-start.59 = (bf16[256,2048]{1,0:T(8,128)(2,1)S(1)}, bf16[256,2048]{1,0:T(8,128)(2,1)S(1)}, u32[]{:S(2)}, u32[]{:S(2)}) collective-permute-start(bf16[256,2048]{1,0:T(8,128)(2,1)S(1)} %slice.233), channel_id=1, source_target_pairs={{0,4},{4,0},{8,12},{12,8},{16,20},{20,16},{24,28},{28,24},{1,5},{5... | collective-permute-start | bytes 3145736 | tf_op jit(solution)/shard_map/ppermute | solution.py:307
  466.4 27.6 %collective-permute-start.71 = (bf16[256,2048]{1,0:T(8,128)(2,1)S(1)}, bf16[256,2048]{1,0:T(8,128)(2,1)S(1)}, u32[]{:S(2)}, u32[]{:S(2)}) collective-permute-start(bf16[256,2048]{1,0:T(8,128)(2,1)S(1)} %fusion.3.refs_0_), channel_id=1, source_target_pairs={{0,1},{1,2},{2,3},{3,0},{4,5},{5,6},{6,7},{7,4},{8,9},{9,10},{10,1... | collective-permute-start | bytes 3145736 | tf_op jit(solution)/shard_map/ppermute | solution.py:302
  494.0 27.8 %collective-permute-start.74 = (bf16[256,2048]{1,0:T(8,128)(2,1)S(1)}, bf16[256,2048]{1,0:T(8,128)(2,1)S(1)}, u32[]{:S(2)}, u32[]{:S(2)}) collective-permute-start(bf16[256,2048]{1,0:T(8,128)(2,1)S(1)} %collective-permute-done.71.refs_0_), channel_id=1, source_target_pairs={{0,1},{1,2},{2,3},{3,0},{4,5},{5,6},{6,7},{7,4},{8,9},{9,10},{10,1... | collective-permute-start | bytes 3145736 | tf_op jit(solution)/shard_map/ppermute | solution.py:302
  521.8 27.5 %collective-permute-start.76 = (bf16[256,2048]{1,0:T(8,128)(2,1)S(1)}, bf16[256,2048]{1,0:T(8,128)(2,1)S(1)}, u32[]{:S(2)}, u32[]{:S(2)}) collective-permute-start(bf16[256,2048]{1,0:T(8,128)(2,1)S(1)} %collective-permute-done.74.refs_0_), channel_id=1, source_target_pairs={{0,1},{1,2},{2,3},{3,0},{4,5},{5,6},{6,7},{7,4},{8,9},{9,10},{10,1... | collective-permute-start | bytes 3145736 | tf_op jit(solution)/shard_map/ppermute | solution.py:302
  521.9 41.7 %collective-permute-start.81 = (bf16[256,2048]{1,0:T(8,128)(2,1)}, bf16[256,2048]{1,0:T(8,128)(2,1)}, u32[]{:S(2)}, u32[]{:S(2)}) collective-permute-start(bf16[256,2048]{1,0:T(8,128)(2,1)} %slice.228), channel_id=1, source_target_pairs={{0,4},{4,0},{8,12},{12,8},{16,20},{20,16},{24,28},{28,24},{1,5},{5... | collective-permute-start | bytes 3145736 | tf_op jit(solution)/shard_map/ppermute | solution.py:307
  563.1 103.8 %collective-permute-start.73 = (bf16[256,2048]{1,0:T(8,128)(2,1)}, bf16[256,2048]{1,0:T(8,128)(2,1)}, u32[]{:S(2)}, u32[]{:S(2)}) collective-permute-start(bf16[256,2048]{1,0:T(8,128)(2,1)} %slice.229), channel_id=1, source_target_pairs={{0,4},{4,0},{8,12},{12,8},{16,20},{20,16},{24,28},{28,24},{1,5},{5... | collective-permute-start | bytes 3145736 | tf_op jit(solution)/shard_map/ppermute | solution.py:307
  566.8 27.3 %collective-permute-start.82 = (bf16[256,2048]{1,0:T(8,128)(2,1)}, bf16[256,2048]{1,0:T(8,128)(2,1)S(1)}, u32[]{:S(2)}, u32[]{:S(2)}) collective-permute-start(bf16[256,2048]{1,0:T(8,128)(2,1)} %add_convert_fusion.4), channel_id=1, source_target_pairs={{0,1},{1,2},{2,3},{3,0},{4,5},{5,6},{6,7},{7,4},{8,9},{9,10},{10,1... | collective-permute-start | bytes 3145736 | tf_op jit(solution)/shard_map/ppermute | solution.py:302
  567.0 27.1 %collective-permute-start.80 = (bf16[256,2048]{1,0:T(8,128)(2,1)}, bf16[256,2048]{1,0:T(8,128)(2,1)}, u32[]{:S(2)}, u32[]{:S(2)}) collective-permute-start(bf16[256,2048]{1,0:T(8,128)(2,1)} %slice.227), channel_id=1, source_target_pairs={{0,4},{4,0},{8,12},{12,8},{16,20},{20,16},{24,28},{28,24},{1,5},{5... | collective-permute-start | bytes 3145736 | tf_op jit(solution)/shard_map/ppermute | solution.py:307
  596.9 41.1 %collective-permute-start.83 = (bf16[256,2048]{1,0:T(8,128)(2,1)}, bf16[256,2048]{1,0:T(8,128)(2,1)}, u32[]{:S(2)}, u32[]{:S(2)}) collective-permute-start(bf16[256,2048]{1,0:T(8,128)(2,1)} %add_convert_fusion.3), channel_id=1, source_target_pairs={{0,1},{1,2},{2,3},{3,0},{4,5},{5,6},{6,7},{7,4},{8,9},{9,10},{10,1... | collective-permute-start | bytes 3145736 | tf_op jit(solution)/shard_map/ppermute | solution.py:302
  623.1 27.6 %collective-permute-start.85 = (bf16[2,256,1024]{2,1,0:T(8,128)(2,1)}, bf16[2,256,1024]{2,1,0:T(8,128)(2,1)S(1)}, u32[]{:S(2)}, u32[]{:S(2)}) collective-permute-start(bf16[2,256,1024]{2,1,0:T(8,128)(2,1)} %dynamic-slice_bitcast_fusion.7), channel_id=1, source_target_pairs={{0,8},{4,12},{8,0},{12,4},{16,24},{20,28},{24,16},{28,20},{1,9},{5... | collective-permute-start | bytes 3145736 | tf_op jit(solution)/shard_map/ppermute | solution.py:307
  625.7 25.5 %collective-permute-start.86 = (bf16[2,256,1024]{2,1,0:T(8,128)(2,1)}, bf16[2,256,1024]{2,1,0:T(8,128)(2,1)S(1)}, u32[]{:S(2)}, u32[]{:S(2)}) collective-permute-start(bf16[2,256,1024]{2,1,0:T(8,128)(2,1)} %dynamic-slice_bitcast_fusion.6), channel_id=1, source_target_pairs={{0,16},{4,20},{8,24},{12,28},{16,0},{20,4},{24,8},{28,12},{1,17},{... | collective-permute-start | bytes 3145736 | tf_op jit(solution)/shard_map/ppermute | solution.py:307
  639.7 27.1 %collective-permute-start.84 = (bf16[256,2048]{1,0:T(8,128)(2,1)S(1)}, bf16[256,2048]{1,0:T(8,128)(2,1)S(1)}, u32[]{:S(2)}, u32[]{:S(2)}) collective-permute-start(bf16[256,2048]{1,0:T(8,128)(2,1)S(1)} %add_convert_fusion.2), channel_id=1, source_target_pairs={{0,1},{1,2},{2,3},{3,0},{4,5},{5,6},{6,7},{7,4},{8,9},{9,10},{10,1... | collective-permute-start | bytes 3145736 | tf_op jit(solution)/shard_map/ppermute | solution.py:302
  682.6 38.3 %collective-permute-start.90 = (bf16[2,512,512]{2,1,0:T(8,128)(2,1)}, bf16[2,512,512]{2,1,0:T(8,128)(2,1)}, u32[]{:S(2)}, u32[]{:S(2)}) collective-permute-start(bf16[2,512,512]{2,1,0:T(8,128)(2,1)} %dynamic-slice_bitcast_fusion.5), channel_id=1, source_target_pairs={{0,8},{4,12},{8,0},{12,4},{16,24},{20,28},{24,16},{28,20},{1,9},{5... | collective-permute-start | bytes 3145736 | tf_op jit(solution)/shard_map/ppermute | solution.py:307
  684.6 36.3 %collective-permute-start.91 = (bf16[2,512,512]{2,1,0:T(8,128)(2,1)}, bf16[2,512,512]{2,1,0:T(8,128)(2,1)}, u32[]{:S(2)}, u32[]{:S(2)}) collective-permute-start(bf16[2,512,512]{2,1,0:T(8,128)(2,1)} %dynamic-slice_bitcast_fusion.4), channel_id=1, source_target_pairs={{0,16},{4,20},{8,24},{12,28},{16,0},{20,4},{24,8},{28,12},{1,17},{... | collective-permute-start | bytes 3145736 | tf_op jit(solution)/shard_map/ppermute | solution.py:307
  687.1 32.6 %collective-permute-start.92 = (bf16[256,1024]{1,0:T(8,128)(2,1)}, bf16[256,1024]{1,0:T(8,128)(2,1)}, u32[]{:S(2)}, u32[]{:S(2)}) collective-permute-start(bf16[256,1024]{1,0:T(8,128)(2,1)} %fusion.25), channel_id=1, source_target_pairs={{0,16},{4,20},{8,24},{12,28},{16,0},{20,4},{24,8},{28,12},{1,17},{... | collective-permute-start | bytes 1572872 | tf_op jit(solution)/shard_map/ppermute | solution.py:307
  693.5 27.4 %collective-permute-start.93 = (bf16[256,1024]{1,0:T(8,128)(2,1)S(1)}, bf16[256,1024]{1,0:T(8,128)(2,1)S(1)}, u32[]{:S(2)}, u32[]{:S(2)}) collective-permute-start(bf16[256,1024]{1,0:T(8,128)(2,1)S(1)} %fusion.26), channel_id=1, source_target_pairs={{0,8},{4,12},{8,0},{12,4},{16,24},{20,28},{24,16},{28,20},{1,9},{5... | collective-permute-start | bytes 1572872 | tf_op jit(solution)/shard_map/ppermute | solution.py:307
  704.8 53.1 %collective-permute-start.96 = (bf16[2,512,512]{2,1,0:T(8,128)(2,1)}, bf16[2,512,512]{2,1,0:T(8,128)(2,1)}, u32[]{:S(2)}, u32[]{:S(2)}) collective-permute-start(bf16[2,512,512]{2,1,0:T(8,128)(2,1)} %dynamic-slice_bitcast_fusion.3), channel_id=1, source_target_pairs={{0,8},{4,12},{8,0},{12,4},{16,24},{20,28},{24,16},{28,20},{1,9},{5... | collective-permute-start | bytes 3145736 | tf_op jit(solution)/shard_map/ppermute | solution.py:307
  719.7 38.2 %collective-permute-start.97 = (bf16[2,512,512]{2,1,0:T(8,128)(2,1)}, bf16[2,512,512]{2,1,0:T(8,128)(2,1)}, u32[]{:S(2)}, u32[]{:S(2)}) collective-permute-start(bf16[2,512,512]{2,1,0:T(8,128)(2,1)} %dynamic-slice_bitcast_fusion.2), channel_id=1, source_target_pairs={{0,16},{4,20},{8,24},{12,28},{16,0},{20,4},{24,8},{28,12},{1,17},{... | collective-permute-start | bytes 3145736 | tf_op jit(solution)/shard_map/ppermute | solution.py:307
  781.2 22.3 %collective-permute-start.102 = (bf16[512,512]{1,0:T(8,128)(2,1)}, bf16[512,512]{1,0:T(8,128)(2,1)}, u32[]{:S(2)}, u32[]{:S(2)}) collective-permute-start(bf16[512,512]{1,0:T(8,128)(2,1)} %fusion.29), channel_id=1, source_target_pairs={{0,16},{4,20},{8,24},{12,28},{16,0},{20,4},{24,8},{28,12},{1,17},{... | collective-permute-start | bytes 1572872 | tf_op jit(solution)/shard_map/ppermute | solution.py:307
  829.0 24.3 %collective-permute-start.104 = (bf16[128,1024]{1,0:T(8,128)(2,1)S(1)}, bf16[128,1024]{1,0:T(8,128)(2,1)S(1)}, u32[]{:S(2)}, u32[]{:S(2)}) collective-permute-start(bf16[128,1024]{1,0:T(8,128)(2,1)S(1)} %copy-done.96), channel_id=1, source_target_pairs={{0,1},{1,2},{2,3},{3,0},{4,5},{5,6},{6,7},{7,4},{8,9},{9,10},{10,1... | collective-permute-start | bytes 786440 | tf_op jit(solution)/shard_map/ppermute | solution.py:324
  829.3 24.1 %collective-permute-start.105 = (bf16[128,1024]{1,0:T(8,128)(2,1)S(1)}, bf16[128,1024]{1,0:T(8,128)(2,1)S(1)}, u32[]{:S(2)}, u32[]{:S(2)}) collective-permute-start(bf16[128,1024]{1,0:T(8,128)(2,1)S(1)} %copy-done.94), channel_id=1, source_target_pairs={{0,2},{1,3},{2,0},{3,1},{4,6},{5,7},{6,4},{7,5},{8,10},{9,11},{10,... | collective-permute-start | bytes 786440 | tf_op jit(solution)/shard_map/ppermute | solution.py:324
  857.4 47.2 %collective-permute-start.110 = (bf16[256,2048]{1,0:T(8,128)(2,1)}, bf16[256,2048]{1,0:T(8,128)(2,1)S(1)}, u32[]{:S(2)}, u32[]{:S(2)}) collective-permute-start(bf16[256,2048]{1,0:T(8,128)(2,1)} %fusion.70), channel_id=1, source_target_pairs={{0,1},{1,2},{2,3},{3,0},{4,5},{5,6},{6,7},{7,4},{8,9},{9,10},{10,1... | collective-permute-start | bytes 3145736 | tf_op jit(solution)/shard_map/ppermute | solution.py:302
  861.7 41.5 %collective-permute-start.111 = (bf16[2,256,768]{2,1,0:T(8,128)(2,1)S(1)}, bf16[2,256,768]{2,1,0:T(8,128)(2,1)S(1)}, u32[]{:S(2)}, u32[]{:S(2)}) collective-permute-start(bf16[2,256,768]{2,1,0:T(8,128)(2,1)S(1)} %fusion.23), channel_id=1, source_target_pairs={{0,8},{4,12},{8,0},{12,4},{16,24},{20,28},{24,16},{28,20},{1,9},{5... | collective-permute-start | bytes 2359304 | tf_op jit(solution)/shard_map/ppermute | solution.py:307
  863.6 41.0 %collective-permute-start.112 = (bf16[2,256,768]{2,1,0:T(8,128)(2,1)S(1)}, bf16[2,256,768]{2,1,0:T(8,128)(2,1)S(1)}, u32[]{:S(2)}, u32[]{:S(2)}) collective-permute-start(bf16[2,256,768]{2,1,0:T(8,128)(2,1)S(1)} %fusion.24), channel_id=1, source_target_pairs={{0,16},{4,20},{8,24},{12,28},{16,0},{20,4},{24,8},{28,12},{1,17},{... | collective-permute-start | bytes 2359304 | tf_op jit(solution)/shard_map/ppermute | solution.py:307
  864.6 26.6 %collective-permute-start.113 = (bf16[128,1024]{1,0:T(8,128)(2,1)S(1)}, bf16[128,1024]{1,0:T(8,128)(2,1)S(1)}, u32[]{:S(2)}, u32[]{:S(2)}) collective-permute-start(bf16[128,1024]{1,0:T(8,128)(2,1)S(1)} %get-tuple-element.349), channel_id=1, source_target_pairs={{0,1},{1,2},{2,3},{3,0},{4,5},{5,6},{6,7},{7,4},{8,9},{9,10},{10,1... | collective-permute-start | bytes 786440 | tf_op jit(solution)/shard_map/ppermute | solution.py:324
  905.0 27.8 %collective-permute-start.116 = (bf16[256,2048]{1,0:T(8,128)(2,1)S(1)}, bf16[256,2048]{1,0:T(8,128)(2,1)S(1)}, u32[]{:S(2)}, u32[]{:S(2)}) collective-permute-start(bf16[256,2048]{1,0:T(8,128)(2,1)S(1)} %add_convert_fusion.1), channel_id=1, source_target_pairs={{0,1},{1,2},{2,3},{3,0},{4,5},{5,6},{6,7},{7,4},{8,9},{9,10},{10,1... | collective-permute-start | bytes 3145736 | tf_op jit(solution)/shard_map/ppermute | solution.py:302
  913.2 55.2 %collective-permute-start.137 = (f32[1,4,64]{2,1,0:T(4,128)S(1)}, f32[1,4,64]{2,1,0:T(4,128)S(1)}, u32[]{:S(2)}, u32[]{:S(2)}) collective-permute-start(f32[1,4,64]{2,1,0:T(4,128)S(1)} %constant_dynamic-slice_fusion), channel_id=1, source_target_pairs={{0,4},{4,0},{8,12},{12,8},{16,20},{20,16},{24,28},{28,24},{1,5},{5... | collective-permute-start | bytes 3080 | tf_op jit(solution)/shard_map/ppermute | solution.py:307
  934.0 52.2 %collective-permute-start.121 = (bf16[256,2048]{1,0:T(8,128)(2,1)}, bf16[256,2048]{1,0:T(8,128)(2,1)S(1)}, u32[]{:S(2)}, u32[]{:S(2)}) collective-permute-start(bf16[256,2048]{1,0:T(8,128)(2,1)} %add_convert_fusion), channel_id=1, source_target_pairs={{0,1},{1,2},{2,3},{3,0},{4,5},{5,6},{6,7},{7,4},{8,9},{9,10},{10,1... | collective-permute-start | bytes 3145736 | tf_op jit(solution)/shard_map/ppermute | solution.py:302
  938.3 24.5 %collective-permute-start.127 = (bf16[2,256,1024]{2,1,0:T(8,128)(2,1)}, bf16[2,256,1024]{2,1,0:T(8,128)(2,1)}, u32[]{:S(2)}, u32[]{:S(2)}) collective-permute-start(bf16[2,256,1024]{2,1,0:T(8,128)(2,1)} %fusion.18), channel_id=1, source_target_pairs={{0,16},{4,20},{8,24},{12,28},{16,0},{20,4},{24,8},{28,12},{1,17},{... | collective-permute-start | bytes 3145736 | tf_op jit(solution)/shard_map/ppermute | solution.py:307
  941.3 24.4 %collective-permute-start.125 = (bf16[2,256,1024]{2,1,0:T(8,128)(2,1)}, bf16[2,256,1024]{2,1,0:T(8,128)(2,1)}, u32[]{:S(2)}, u32[]{:S(2)}) collective-permute-start(bf16[2,256,1024]{2,1,0:T(8,128)(2,1)} %fusion.17), channel_id=1, source_target_pairs={{0,8},{4,12},{8,0},{12,4},{16,24},{20,28},{24,16},{28,20},{1,9},{5... | collective-permute-start | bytes 3145736 | tf_op jit(solution)/shard_map/ppermute | solution.py:307
  942.4 26.4 %collective-permute-start.122 = (bf16[64,1536]{1,0:T(8,128)(2,1)S(1)}, bf16[64,1536]{1,0:T(8,128)(2,1)S(1)}, u32[]{:S(2)}, u32[]{:S(2)}) collective-permute-start(bf16[64,1536]{1,0:T(8,128)(2,1)S(1)} %get-tuple-element.360), channel_id=1, source_target_pairs={{0,1},{1,2},{2,3},{3,0},{4,5},{5,6},{6,7},{7,4},{8,9},{9,10},{10,1... | collective-permute-start | bytes 589832 | tf_op jit(solution)/shard_map/ppermute | solution.py:324
  985.4 22.6 %collective-permute-start.130 = (bf16[64,2048]{1,0:T(8,128)(2,1)S(1)}, bf16[64,2048]{1,0:T(8,128)(2,1)S(1)}, u32[]{:S(2)}, u32[]{:S(2)}) collective-permute-start(bf16[64,2048]{1,0:T(8,128)(2,1)S(1)} %get-tuple-element.370), channel_id=1, source_target_pairs={{0,2},{1,3},{2,0},{3,1},{4,6},{5,7},{6,4},{7,5},{8,10},{9,11},{10,... | collective-permute-start | bytes 786440 | tf_op jit(solution)/shard_map/ppermute | solution.py:324
  (250 other events, 2745.1 us)

commit v4 on v3

--- a/solution.py
+++ b/solution.py
@@ -332,37 +332,54 @@
     ]
 
 
-def assemble_body(parts, places, count, *refs):
-    pieces, out, held, in_sems, out_sems = refs[:count], *refs[count:]
+def assemble_body(parts, places, count, cuts, *refs):
+    pieces, outs, (held, in_sems, out_sems) = refs[:count], refs[count : count + len(cuts)], refs[count + len(cuts) :]
     reads, writes, first = [], [], 0
     for at, ((which, start, rows), place) in enumerate(zip(parts, places())):
         here = held.at[pl.ds(first, rows)]
         reads.append(pltpu.make_async_copy(pieces[which].at[pl.ds(start, rows)], here, in_sems.at[at]))
-        writes.append(pltpu.make_async_copy(here, out.at[pl.ds(place, rows)], out_sems.at[at]))
+        writes.append(
+            [
+                pltpu.make_async_copy(
+                    held.at[pl.ds(first, rows), pl.ds(left, wide)],
+                    out.at[pl.ds(place, rows)],
+                    out_sems.at[at * len(cuts) + n],
+                )
+                for n, (out, (left, wide)) in enumerate(zip(outs, cuts))
+            ]
+        )
         first += rows
     for read in reads:
         read.start()
-    for read, write in zip(reads, writes):
+    for read, copies in zip(reads, writes):
         read.wait()
-        write.start()
-    for write in writes:
-        write.wait()
-
-
-def assemble(pieces, parts, places):
+        for write in copies:
+            write.start()
+    for copies in writes:
+        for write in copies:
+            write.wait()
+
+
+def assemble(pieces, parts, places, cuts=None):
     shape = (sum(rows for _, _, rows in parts), pieces[0].shape[1])
+    several, cuts = cuts is not None, cuts or [(0, shape[1])]
     anywhere = pl.BlockSpec(memory_space=pl.ANY)
-    sems = pltpu.SemaphoreType.DMA((len(parts),))
-    size = shape[0] * shape[1] * pieces[0].dtype.itemsize
-    return pl.pallas_call(
-        functools.partial(assemble_body, parts, places, len(pieces)),
+    dtype = pieces[0].dtype
+    size = shape[0] * shape[1] * dtype.itemsize
+    results = pl.pallas_call(
+        functools.partial(assemble_body, parts, places, len(pieces), cuts),
         in_specs=[anywhere] * len(pieces),
-        out_specs=anywhere,
-        out_shape=jax.ShapeDtypeStruct(shape, pieces[0].dtype),
-        scratch_shapes=[pltpu.VMEM(shape, pieces[0].dtype), sems, sems],
+        out_specs=[anywhere] * len(cuts),
+        out_shape=[jax.ShapeDtypeStruct((shape[0], wide), dtype) for _, wide in cuts],
+        scratch_shapes=[
+            pltpu.VMEM(shape, dtype),
+            pltpu.SemaphoreType.DMA((len(parts),)),
+            pltpu.SemaphoreType.DMA((len(parts) * len(cuts),)),
+        ],
         compiler_params=pltpu.CompilerParams(vmem_limit_bytes=size + 2**20),
         cost_estimate=pl.CostEstimate(flops=0, bytes_accessed=2 * size, transcendentals=0),
     )(*pieces)
+    return results if several else results[0]
 
 
 def stacked(pieces, parts=None):
@@ -414,7 +431,7 @@
             self.set(self.new)
 
 
-def cube_join(cube, firsts, rows, fold=1):
+def cube_join(cube, firsts, rows, fold=1, cuts=None):
     pieces, parts, where = [], [], []
     for (own, first), arrays, masks in zip(firsts, cube.arrays, cube.masks):
         step = arrays[0].shape[0] // len(masks[0])
@@ -428,7 +445,7 @@
         here = lax.axis_index("dp")
         return [pl.multiple_of((here ^ mask) // fold * rows + first, step) for mask, first in where]
 
-    return assemble(pieces, parts, places)
+    return assemble(pieces, parts, places, cuts)
 
 
 class CubeScatter:
@@ -462,39 +479,13 @@
         return jnp.concatenate(self.add(), 1)
 
 
-def column_halves(grad, core):
+def column_halves(grad, core, more=None):
     bits = (lax.axis_size("dp") - 1).bit_length() - (not core)
     cut = grad.shape[1] // 2
-    shape = (2,) * bits + (-1, cut)
-    return [grad[:, :cut].reshape(shape), grad[:, cut:].reshape(shape)]
-
-
-def gather_small(block):
-    size, here = lax.axis_size("seq"), lax.axis_index("seq")
-    joined = jnp.zeros((size,) + block.shape, block.dtype)
-    for back, slot in enumerate(share_out(block, "seq")):
-        joined = lax.dynamic_update_index_in_dim(joined, slot, lax.rem(here + size - back, size), 0)
-    block = joined.transpose(1, 0, 2).reshape(block.shape[0], -1)
-    here, wide = lax.axis_index("dp"), block.shape[1]
-    table = {0: block}
-    for bit in cube_bits()[0] + [1]:
-        table.update({m ^ bit: flipped(v, bit) for m, v in table.items()})
-    joined = jnp.zeros((block.shape[0], wide * len(table)), block.dtype)
-    for mask, piece in table.items():
-        joined = lax.dynamic_update_slice_in_dim(joined, piece, (here ^ mask) * wide, 1)
-    return joined
-
-
-def scatter_small(values):
-    copies, size, here = lax.axis_size("dp"), lax.axis_size("seq"), lax.axis_index("dp")
-    blocks = values.reshape(values.shape[0], copies, size, -1).transpose(2, 1, 0, 3)
-    total = sum(exchange(blocks, "seq"))
-    for bit in reversed([1] + cube_bits()[0]):
-        total = total.reshape((2, total.shape[0] // 2) + total.shape[1:])
-        mine = (here // bit) % 2
-        away = lax.dynamic_index_in_dim(total, 1 - mine, 0, keepdims=False)
-        total = lax.dynamic_index_in_dim(total, mine, 0, keepdims=False) + flipped(away, bit)
-    return total[0]
+    halves = [grad[:, :cut], grad[:, cut:]]
+    if more is not None:
+        halves[1] = jnp.concatenate([halves[1], more], 1)
+    return [half.reshape((2,) * bits + (-1, half.shape[1])) for half in halves]
 
 
 def small_sum(values, axis):
@@ -597,70 +588,80 @@
     def part_row(seq_at):
         return pl.multiple_of(seq_at * rows, rows)
 
-    gains, w_down_own = together(gather_small(jnp.stack([g_query, g_key, g_attn, g_ffn], 0)), w_down)
-    gains = gains.astype(f32)
+    lanes = 128
+    own_gains = jnp.stack([g_query, g_key, g_attn, g_ffn], 1)
+    own_gains = jnp.pad(own_gains, ((0, 0), (0, lanes - own_gains.shape[1])))
     qkv_send = relayout(
-        [w_query, w_key, w_value],
-        [(own_rows, 3 * part)] * size,
+        [w_query, w_key, w_value, own_gains],
+        [(own_rows, 3 * part + lanes)] * size,
         bf16,
         lambda: [
             ((which, 0, part_column(behind(ahead))), (ahead, 0, which * part), (own_rows, part))
             for ahead in slots
             for which in range(3)
-        ],
+        ]
+        + [((3, 0, 0), (ahead, 0, 3 * part), (own_rows, lanes)) for ahead in slots],
     )
     qkv_got = send_ahead(qkv_send, "seq")
-    cube_down = CubeGather([w_down_own[: ff_own // 2], w_down_own[ff_own // 2 :]])
+    cube_down = CubeGather([w_down[: ff_own // 2], w_down[ff_own // 2 :]])
     cube_down.step()
     gate_send, up_send = ff_pack(w_gate), ff_pack(w_up)
-    qkv_got, new, gate_send, x_own, w_out_own = together(qkv_got, cube_down.new, gate_send, tok_rows, w_out)
+    qkv_got, new, gate_send, up_send, x_own = together(qkv_got, cube_down.new, gate_send, up_send, tok_rows)
     cube_down.set(new)
 
     gate_got = send_ahead(gate_send, "seq")
     cube_qkv = CubeGather(two_parts(qkv_got), core=True)
     cube_qkv.step()
-    gate_got, new, x_own = together(gate_got, cube_qkv.new, x_own)
+    gate_got, new, up_send = together(gate_got, cube_qkv.new, up_send)
     cube_qkv.set(new)
-
-    x_slots = [x_own]
+    up_got = send_ahead(up_send, "seq")
     cube_qkv.step()
     cube_gate = CubeGather(ff_pair(gate_got))
-    cube_gate.step()
+    up_got, new, x_own, gate_own = together(up_got, cube_qkv.new, x_own, cube_gate.arrays)
+    cube_qkv.set(new)
+    cube_gate.arrays = gate_own
+    cube_up = CubeGather(ff_pair(up_got))
+    cosine, sine_tab = rope_tables(positions(segments).reshape(total_len))
+
+    x_slots = [x_own]
     for at in range(size - 1):
         x_next = next_one(x_slots[-1], "seq")
         if at == 0:
-            x_next, new, more = together(x_next, cube_qkv.new, cube_gate.new)
-            cube_qkv.set(new)
-            cube_gate.set(more)
+            cube_gate.step()
+            cube_down.step()
+            x_next, new = together(x_next, cube_gate.new)
+            cube_gate.set(new)
+        elif at == 1:
+            cube_gate.step()
             cube_qkv.step()
-            cube_gate.step()
-        elif at == 1:
-            x_next, new, more = together(x_next, cube_qkv.new, cube_gate.new)
-            cube_qkv.set(new)
-            cube_gate.set(more)
-            cube_down.step()
+            x_next, new, more, cosine, sine_tab = together(x_next, cube_down.new, cube_qkv.new, cosine, sine_tab)
+            cube_down.set(new)
+            cube_qkv.set(more)
+        elif at == size - 2:
+            cube_up.step()
+            x_next, new, more, w_out_own = together(x_next, cube_gate.new, cube_up.new, w_out)
+            cube_gate.set(new)
+            cube_up.set(more)
         x_slots.append(x_next)
     cube_qkv.finish()
-    cube_gate.finish()
-    w_qkv = cube_join(cube_qkv, ((0, 0), (0, side // 2)), side)
+    w_qkv, gains = cube_join(
+        cube_qkv, ((0, 0), (0, side // 2)), side, cuts=[(0, 3 * part), (3 * part, lanes)]
+    )
 
     x_all = in_order(x_slots, "seq")
-    gain_attn, gain_ffn = gains[2], gains[3]
-    gain_qk = lax.dynamic_slice_in_dim(gains[:2], here * part, part, 1)
-    cosine, sine_tab = rope_tables(positions(segments).reshape(total_len))
+    out_got = share_out(w_out_own, "seq")
+    cube_up.step()
     qkv = product(x_all, w_qkv)
     squares = jnp.stack([jnp.sum(jnp.square(qkv[:, first : first + part]), -1) for first in (0, part)], 0)
     squares = small_sum(squares, "seq")
-    squares, new, w_out_own, up_send = together(squares, cube_down.new, w_out_own, up_send)
-    cube_down.set(new)
-    out_got = share_out(w_out_own, "seq")
-    w_gate_part = cube_join(cube_gate, ((0, 0), (1, 0)), side)
+    gains = gains[:, :4].T.astype(f32)
+    gain_attn, gain_ffn = gains[2], gains[3]
+    gain_qk = lax.dynamic_slice_in_dim(gains[:2], here * part, part, 1)
+    squares, out_got, gain_qk = together(squares, out_got, gain_qk)
+    cube_out = CubeGather(two_parts(out_got), core=True)
+    cube_out.step()
     squares = squares.T
     query, key, value = query_key(qkv, squares, cosine, sine_tab, gain_qk, width)
-    query, out_got, w_gate_part = together(query, out_got, w_gate_part)
-    cube_out = CubeGather(two_parts(out_got), core=True)
-    cube_out.step()
-    up_got = send_ahead(up_send, "seq")
     seg_ids = segments.reshape(total_len)
     attended = attend(query, key, value, seg_ids)
     attended = relayout(
@@ -669,17 +670,20 @@
         bf16,
         lambda: [((0, part_row(behind(ahead)), 0), (ahead, 0, 0), (rows, part)) for ahead in slots],
     )
-    attended, up_got, new = together(attended, up_got, cube_out.new)
+    attended, new, more = together(attended, cube_out.new, cube_up.new)
     cube_out.set(new)
+    cube_up.set(more)
     attended = send_ahead(attended, "seq")
     cube_out.step()
-    cube_up = CubeGather(ff_pair(up_got))
-    cube_down.finish()
+    for cube in (cube_down, cube_gate, cube_up):
+        cube.finish()
     w_down_part = cube_join(cube_down, ((0, 0), (0, ff_own // 2)), ff_own, 2)
-    attended, new, w_down_part = together(attended, cube_out.new, w_down_part)
+    w_gate_part, w_up_part = [cube_join(cube, ((0, 0), (1, 0)), side) for cube in (cube_gate, cube_up)]
+    attended, new, w_down_part, w_gate_part, w_up_part = together(
+        attended, cube_out.new, w_down_part, w_gate_part, w_up_part
+    )
     cube_out.set(new)
     cube_out.finish()
-    cube_up.step()
     w_out_all = cube_join(cube_out, ((0, 0), (0, side // 2)), side)
     attended = relayout(
         attended,
@@ -688,8 +692,6 @@
         lambda: [((back, 0, 0), (0, 0, part_column(before(back))), (rows, part)) for back in slots],
     )[0]
 
-    cube_up.finish()
-    w_up_part = cube_join(cube_up, ((0, 0), (1, 0)), side)
     a_proj = product(attended, w_out_all)
     a_scale = rms_scale(a_proj)
     hidden = tok_rows.astype(f32) + a_proj * a_scale * gain_attn
@@ -751,19 +753,16 @@
         return weight_grad(stacked(inners), stacked(dms)).astype(bf16)
 
     def grads(d_down):
-        cube = CubeScatter(column_halves(d_down, False))
-        cube.step()
-        sums.append(cube)
-        h_all = stacked(h_slots)
-        d_gate = weight_grad(h_all, stacked(d_gates)).astype(bf16)
-        d_up = weight_grad(h_all, stacked(d_ups)).astype(bf16)
-        return d_gate, d_up, cube.got
-
-    sums = []
-
-    d_sum, (d_gate, d_up, got) = ring(dm_low, backward, down_grad, grads)
-    cube_down = sums[0]
-    cube_down.got = got
+        for grad in (d_down, weight_grad(h_alls[0], stacked(d_gates)).astype(bf16)):
+            cubes.append(CubeScatter(column_halves(grad, False)))
+            cubes[-1].step()
+        d_up = weight_grad(h_alls[0], stacked(d_ups)).astype(bf16)
+        return d_up, [cube.got for cube in cubes]
+
+    h_alls, cubes = [stacked(h_slots)], []
+    d_sum, (d_up, gots) = ring(dm_low, backward, down_grad, grads)
+    cube_down, cube_gate = cubes
+    cube_down.got, cube_gate.got = gots
 
     def ff_rows(total):
         core = lax.rem(lax.axis_index("dp"), 2)
@@ -779,64 +778,6 @@
             ]
 
         return relayout([mine, away], [(2 * own_rows, ff_half)] * size, bf16, moves)
-
-    cube_down.step()
-    cube_gate = CubeScatter(column_halves(d_gate, False))
-    cube_gate.step()
-    d_hidden = grad_out + d_sum
-    d_gain_attn = jnp.sum(d_hidden * a_proj * a_scale, 0)
-    da_low = norm_back(a_proj, a_scale, d_hidden * gain_attn).astype(bf16)
-    d_attended = against(da_low, w_out_all).astype(bf16)
-    d_attended = relayout(
-        [d_attended],
-        [(rows, part)] * size,
-        bf16,
-        lambda: [((0, 0, part_column(behind(ahead))), (ahead, 0, 0), (rows, part)) for ahead in slots],
-    )
-    d_attended = send_ahead(d_attended, "seq")
-    d_w_out = weight_grad(attended, da_low).astype(bf16)
-    d_attended, cube_gate.got, cube_down.got, d_w_out = together(d_attended, cube_gate.got, cube_down.got, d_w_out)
-    d_down = cube_down.finish()
-    cube_gate.step()
-    cube_up = CubeScatter(column_halves(d_up, False))
-    cube_up.step()
-    d_attended = in_order(d_attended, "seq")
-
-    d_query, d_key, d_value = attend_back(query, key, value, d_attended, seg_ids)
-    d_query, cube_gate.got, cube_up.got = together(d_query, cube_gate.got, cube_up.got)
-    cube_up.step()
-    dots, d_gain_qk = unrope(d_query, d_key, qkv, squares, cosine, sine_tab, gain_qk, width)
-    dots = small_sum(dots.T, "seq")
-    gate_send = ff_rows(cube_gate.finish())
-    dots, gate_send, cube_up.got = together(dots, gate_send, cube_up.got)
-    gate_got = send_ahead(gate_send, "seq")
-    d_qkv = raw_grad(d_query, d_key, d_value, qkv, squares, dots.T, cosine, sine_tab, gain_qk, width)
-    up_send = ff_rows(cube_up.finish())
-    d_slots = relayout(
-        [d_qkv],
-        [(rows, 3 * part)] * size,
-        bf16,
-        lambda: [((0, part_row(before(back)), 0), (back, 0, 0), (rows, 3 * part)) for back in slots],
-    )
-    cube_qkv = CubeScatter(column_halves(weight_grad(x_all, d_qkv).astype(bf16), True), core=True)
-    cube_qkv.step()
-    shares = [against(d_slots[back], w_qkv) for back in [*slots[1:], 0]]
-    shares, gate_got, up_send, cube_qkv.got = together(shares, gate_got, up_send, cube_qkv.got)
-    got = next_one(shares[0].astype(bf16), "seq")
-    cube_qkv.step()
-    up_got = send_ahead(up_send, "seq")
-    got, cube_qkv.got, up_got = together(got, cube_qkv.got, up_got)
-    cube_qkv.step()
-    cube_out = CubeScatter(column_halves(d_w_out, True), core=True)
-    cube_out.step()
-    for back in range(2, size):
-        got = next_one((shares[back - 1] + got.astype(f32)).astype(bf16), "seq")
-        if back == 2:
-            got, cube_qkv.got, cube_out.got = together(got, cube_qkv.got, cube_out.got)
-            cube_out.step()
-    d_w_qkv = cube_qkv.finish()
-    d_w_out = cube_out.finish()
-    d_tokens = d_hidden + shares[-1] + got.astype(f32)
 
     def row_blocks(total):
         wide = total.shape[1]
@@ -850,8 +791,69 @@
             ],
         )
 
-    d_w_qkv = send_ahead(row_blocks(d_w_qkv), "seq")
-    d_w_out = sum(g.astype(f32) for g in send_ahead(row_blocks(d_w_out), "seq"))
+    cube_gate.step()
+    d_hidden = grad_out + d_sum
+    d_gain_attn = jnp.sum(d_hidden * a_proj * a_scale, 0)
+    da_low = norm_back(a_proj, a_scale, d_hidden * gain_attn).astype(bf16)
+    d_attended = against(da_low, w_out_all).astype(bf16)
+    d_attended = relayout(
+        [d_attended],
+        [(rows, part)] * size,
+        bf16,
+        lambda: [((0, 0, part_column(behind(ahead))), (ahead, 0, 0), (rows, part)) for ahead in slots],
+    )
+    d_attended, cube_gate.got, d_up = together(d_attended, cube_gate.got, d_up)
+    d_attended = send_ahead(d_attended, "seq")
+    cube_up = CubeScatter(column_halves(d_up, False))
+    cube_up.step()
+    d_w_out = weight_grad(attended, da_low).astype(bf16)
+    gate_send = ff_rows(cube_gate.finish())
+    d_attended, cube_up.got, d_w_out, gate_send = together(d_attended, cube_up.got, d_w_out, gate_send)
+    d_attended = in_order(d_attended, "seq")
+
+    gate_got = send_ahead(gate_send, "seq")
+    cube_up.step()
+    d_query, d_key, d_value = attend_back(query, key, value, d_attended, seg_ids)
+    d_query, gate_got, cube_up.got = together(d_query, gate_got, cube_up.got)
+    up_send = ff_rows(cube_up.finish())
+    dots, d_gain_qk = unrope(d_query, d_key, qkv, squares, cosine, sine_tab, gain_qk, width)
+    dots = small_sum(dots.T, "seq")
+    d_gain_qk = lax.dynamic_update_slice_in_dim(jnp.zeros((2, width), f32), d_gain_qk, here * part, 1)
+    d_gains = jnp.concatenate([d_gain_qk, d_gain_attn[None], d_gain_ffn[None]], 0).T.astype(bf16)
+    d_gains = jnp.pad(d_gains, ((0, 0), (0, lanes - d_gains.shape[1])))
+    cube_out = CubeScatter(column_halves(d_w_out, True, d_gains), core=True)
+    cube_out.step()
+    d_qkv = raw_grad(d_query, d_key, d_value, qkv, squares, dots.T, cosine, sine_tab, gain_qk, width)
+    d_qkv, up_send, cube_out.got = together(d_qkv, up_send, cube_out.got)
+    d_slots = relayout(
+        [d_qkv],
+        [(rows, 3 * part)] * size,
+        bf16,
+        lambda: [((0, part_row(before(back)), 0), (back, 0, 0), (rows, 3 * part)) for back in slots],
+    )
+    got = next_one(against(d_slots[1], w_qkv).astype(bf16), "seq")
+    up_got = send_ahead(up_send, "seq")
+    cube_out.step()
+    cube_qkv = CubeScatter(column_halves(weight_grad(x_all, d_qkv).astype(bf16), True), core=True)
+    cube_qkv.step()
+    shares = [against(d_slots[back], w_qkv) for back in [*slots[2:], 0]]
+    got, up_got, cube_out.got, cube_qkv.got, shares = together(got, up_got, cube_out.got, cube_qkv.got, shares)
+    for back in range(2, size):
+        got = next_one((shares[back - 2] + got.astype(f32)).astype(bf16), "seq")
+        if back == 2:
+            cube_qkv.step()
+            cube_out.step()
+            got, cube_qkv.got, cube_out.got = together(got, cube_qkv.got, cube_out.got)
+        elif back == 3:
+            cube_qkv.step()
+            out_send = row_blocks(cube_out.finish())
+            got, cube_qkv.got, out_send = together(got, cube_qkv.got, out_send)
+    out_got = send_ahead(out_send, "seq")
+    d_w_qkv = send_ahead(row_blocks(cube_qkv.finish()), "seq")
+    d_down = cube_down.finish()
+    d_tokens = d_hidden + shares[-1] + got.astype(f32)
+    out_sum = sum(g.astype(f32) for g in out_got)
+    d_w_out, d_gains = out_sum[:, :width], out_sum[:, width : width + 4].T
     d_w_qkv = relayout(
         d_w_qkv,
         [(own_rows, width)] * 3,
@@ -863,9 +865,6 @@
         ],
     )
     d_w_gate, d_w_up = ff_unpack(gate_got), ff_unpack(up_got)
-
-    d_gain_qk = lax.dynamic_update_slice_in_dim(jnp.zeros((2, width), f32), d_gain_qk, here * part, 1)
-    d_gains = scatter_small(jnp.concatenate([d_gain_qk, d_gain_attn[None], d_gain_ffn[None]], 0))
     return (
         out,
         d_tokens.reshape(tokens.shape),

time: 1020 us -> 982 us (0.963)
  waiting for transfers between devices: 461 us -> 421 us
    ppermute x27, starting transfers between devices: 42.4 us -> 62.7 us  [send_ahead(): lax.ppermute(blocks[step], axis, [(i, (i + step) % size) for i in range(s...]
    ppermute x78 -> x68, waiting for transfers between devices: 135 us -> 116 us  [flipped(): return lax.ppermute(block, 'dp', [(i, i ^ bit) for i in range(size)])]
    ppermute x18, waiting for transfers between devices: 229 us -> 214 us  [next_one(): return lax.ppermute(block, axis, [(i, (i + 1) % size) for i in range(size)])]
    unnamed x347 -> x352, local copies, waits for them, and re-layouts: 53.8 us -> 62.2 us
    ppermute x78 -> x68, starting transfers between devices: 54 us -> 45.9 us  [flipped(): return lax.ppermute(block, 'dp', [(i, i ^ bit) for i in range(size)])]
  transfers between devices with their start and end apart: 138 -> 122, of which waited for: 59 -> 56; matrix products, arithmetic and copies ran while one was open for 22% -> 21% of each run, Pallas kernels for 8% -> 9%
where the time goes in v4:
time: 982 us; the launch traced here: 975 us
  waiting for transfers between devices  421 us (43%)
  matrix products  139 us (14%)
  starting transfers between devices  135 us (14%)
  local copies, waits for them, and re-layouts  111 us (11%)
  Pallas kernels  109 us (11%)
  other arithmetic  55.5 us (6%)
    ppermute x18, waiting for transfers between devices, next_one(): return lax.ppermute(block, axis, [(i, (i + 1) % size) for i in range(size)])  214 us
    ppermute x68, waiting for transfers between devices, flipped(): return lax.ppermute(block, 'dp', [(i, i ^ bit) for i in range(size)])  116 us
    ppermute x27, waiting for transfers between devices, send_ahead(): lax.ppermute(blocks[step], axis, [(i, (i + step) % size) for i in range(s...  79 us
    ppermute x27, starting transfers between devices, send_ahead(): lax.ppermute(blocks[step], axis, [(i, (i + step) % size) for i in range(s...  62.7 us
    unnamed x352, local copies, waits for them, and re-layouts  62.2 us
    dot_general x17, matrix products, against(): lax.dot_general(left, right, (((1,), (1,)), ((), ())), preferred_element_...  50.6 us
    dot_general x5, matrix products, weight_grad(): lax.dot_general(left, right, (((0,), (0,)), ((), ())), preferred_element_...  47.9 us
    pallas_call x40, Pallas kernels, assemble(): pl.pallas_call(functools.partial(assemble_body, parts, places, len(pieces...  46.9 us
  transfers between devices with their start and end apart: 122, of which 56 were waited for; matrix products, arithmetic and copies ran while one was open for 21% of the time, Pallas kernels for 9%

profile of v4, /device:TPU:0, one launch (start us, length us, event | category | flops | bytes accessed | tf_op | source)
XLA Modules:
  0.0 974.7 jit_solution(31829084005741623)
XLA Ops:
  14.7 4.2 collective-permute-done.refs_1_
  19.0 7.4 collective-permute-done.1.refs_2_
  30.6 5.0 collective-permute-start.5
  38.0 6.0 collective-permute-done.5.refs_1_
  44.0 8.3 collective-permute-done.6.refs_2_
  57.4 6.1 collective-permute-start.10
  68.0 4.6 collective-permute-done.10.refs_1_
  75.1 6.9 collective-permute-done.11.refs_2_
  83.7 4.5 collective-permute-start.16
  91.6 12.4 %collective-permute-done.17.refs_1_ = bf16[256,1024]{1,0:T(8,128)(2,1)S(1)} collective-permute-done((bf16[256,1024]{1,0:T(8,128)(2,1)S(1)}, bf16[256,1024]{1,0:T(8,128)(2,1)S(1)}, u32[]{:S(2)}, u32[]{:S(2)}) %collective-permute-start.17) | collective-permute-done | bytes 524320 | tf_op jit(solution)/shard_map/ppermute | solution.py:307
  105.7 6.1 collective-permute-done.16.refs_1_
  119.6 8.7 collective-permute-done.20.refs_1_
  134.0 4.1 collective-permute-done.19.refs_2_
  146.7 4.7 shard_map.257
  155.1 13.7 %collective-permute-done.27.refs_1_ = bf16[256,1024]{1,0:T(8,128)(2,1)} collective-permute-done((bf16[256,1024]{1,0:T(8,128)(2,1)S(1)}, bf16[256,1024]{1,0:T(8,128)(2,1)}, u32[]{:S(2)}, u32[]{:S(2)}) %collective-permute-start.27) | collective-permute-done | bytes 524320 | tf_op jit(solution)/shard_map/ppermute | solution.py:307
  174.6 6.6 fusion.54.raw_ref
  196.8 8.7 collective-permute-done.34.refs_2_
  210.3 4.5 shard_map.258
  214.8 13.9 %shard_map.259.refs_0_ = bf16[1024,512]{1,0:T(8,128)(2,1)S(1)} custom-call(bf16[1024,512]{1,0:T(8,128)(2,1)S(1)} %get-tuple-element.281.q_ref, bf16[1024,512]{1,0:T(8,128)(2,1)S(1)} %get-tuple-element.282.k_ref, bf16[1024,512]{1,0:T(8,128)(2,1)S(1)} %get-tuple-element.283.v_ref, s32[1,1024]{1,0:T(1,128)S(1)} %copy-done.100, s32[1024,1]{1,0:T(8,128)S(1)} %copy.72.seg_k_ref), custom_call_target="tpu_custom_call" | custom-call | tf_op jit(solution)/shard_map/pallas_call | solution.py:164
  234.6 6.0 collective-permute-start.40
  248.5 3.9 shard_map.268
  252.3 4.2 collective-permute-done.41.refs_2_
  258.5 3.2 collective-permute-done.45.refs_1_
  271.7 6.3 collective-permute-start.47
  288.3 15.2 %collective-permute-done.47.refs_0_ = bf16[256,2048]{1,0:T(8,128)(2,1)S(1)} collective-permute-done((bf16[256,2048]{1,0:T(8,128)(2,1)S(1)}, bf16[256,2048]{1,0:T(8,128)(2,1)S(1)}, u32[]{:S(2)}, u32[]{:S(2)}) %collective-permute-start.47) | collective-permute-done | bytes 1048608 | tf_op jit(solution)/shard_map/ppermute | solution.py:302
  308.9 3.8 multiply_convert_fusion.10
  317.2 13.8 %collective-permute-done.50.refs_0_ = bf16[256,2048]{1,0:T(8,128)(2,1)S(1)} collective-permute-done((bf16[256,2048]{1,0:T(8,128)(2,1)S(1)}, bf16[256,2048]{1,0:T(8,128)(2,1)S(1)}, u32[]{:S(2)}, u32[]{:S(2)}) %collective-permute-start.50) | collective-permute-done | bytes 1048608 | tf_op jit(solution)/shard_map/ppermute | solution.py:302
  343.6 14.8 %collective-permute-done.52.refs_0_ = bf16[256,2048]{1,0:T(8,128)(2,1)S(1)} collective-permute-done((bf16[256,2048]{1,0:T(8,128)(2,1)S(1)}, bf16[256,2048]{1,0:T(8,128)(2,1)S(1)}, u32[]{:S(2)}, u32[]{:S(2)}) %collective-permute-start.52) | collective-permute-done | bytes 1048608 | tf_op jit(solution)/shard_map/ppermute | solution.py:302
  363.8 3.8 multiply_convert_fusion.8
  369.9 16.4 %collective-permute-done.58 = bf16[256,2048]{1,0:T(8,128)(2,1)S(1)} collective-permute-done((bf16[256,2048]{1,0:T(8,128)(2,1)S(1)}, bf16[256,2048]{1,0:T(8,128)(2,1)S(1)}, u32[]{:S(2)}, u32[]{:S(2)}) %collective-permute-start.58) | collective-permute-done | bytes 1048608 | tf_op jit(solution)/shard_map/ppermute | solution.py:302
  387.2 26.3 %collective-permute-done.59 = bf16[256,2048]{1,0:T(8,128)(2,1)S(1)} collective-permute-done((bf16[256,2048]{1,0:T(8,128)(2,1)S(1)}, bf16[256,2048]{1,0:T(8,128)(2,1)S(1)}, u32[]{:S(2)}, u32[]{:S(2)}) %collective-permute-start.59) | collective-permute-done | bytes 1048608 | tf_op jit(solution)/shard_map/ppermute | solution.py:302
  414.2 25.6 %collective-permute-done.60 = bf16[256,2048]{1,0:T(8,128)(2,1)S(1)} collective-permute-done((bf16[256,2048]{1,0:T(8,128)(2,1)S(1)}, bf16[256,2048]{1,0:T(8,128)(2,1)S(1)}, u32[]{:S(2)}, u32[]{:S(2)}) %collective-permute-start.60) | collective-permute-done | bytes 1048608 | tf_op jit(solution)/shard_map/ppermute | solution.py:302
  456.2 13.7 %collective-permute-done.61.refs_0_ = bf16[256,2048]{1,0:T(8,128)(2,1)S(1)} collective-permute-done((bf16[256,2048]{1,0:T(8,128)(2,1)S(1)}, bf16[256,2048]{1,0:T(8,128)(2,1)S(1)}, u32[]{:S(2)}, u32[]{:S(2)}) %collective-permute-start.61) | collective-permute-done | bytes 1048608 | tf_op jit(solution)/shard_map/ppermute | solution.py:302
  483.9 13.8 %collective-permute-done.64.refs_0_ = bf16[256,2048]{1,0:T(8,128)(2,1)S(1)} collective-permute-done((bf16[256,2048]{1,0:T(8,128)(2,1)S(1)}, bf16[256,2048]{1,0:T(8,128)(2,1)S(1)}, u32[]{:S(2)}, u32[]{:S(2)}) %collective-permute-start.64) | collective-permute-done | bytes 1048608 | tf_op jit(solution)/shard_map/ppermute | solution.py:302
  511.6 13.6 %collective-permute-done.66.refs_0_ = bf16[256,2048]{1,0:T(8,128)(2,1)S(1)} collective-permute-done((bf16[256,2048]{1,0:T(8,128)(2,1)S(1)}, bf16[256,2048]{1,0:T(8,128)(2,1)S(1)}, u32[]{:S(2)}, u32[]{:S(2)}) %collective-permute-start.66) | collective-permute-done | bytes 1048608 | tf_op jit(solution)/shard_map/ppermute | solution.py:302
  542.0 3.9 multiply_convert_fusion.1
  550.0 4.4 fusion.66
  554.4 12.8 %collective-permute-done.72 = bf16[256,2048]{1,0:T(8,128)(2,1)} collective-permute-done((bf16[256,2048]{1,0:T(8,128)(2,1)}, bf16[256,2048]{1,0:T(8,128)(2,1)}, u32[]{:S(2)}, u32[]{:S(2)}) %collective-permute-start.72) | collective-permute-done | bytes 1048608 | tf_op jit(solution)/shard_map/ppermute | solution.py:302
  574.3 7.1 convolution_add_fusion
  581.4 9.6 convolution_convert_fusion.2
  599.2 9.7 convolution_convert_fusion.3
  615.3 6.3 collective-permute-done.75
  621.6 10.9 %convolution_convert_fusion.4 = bf16[2048,1024]{1,0:T(8,128)(2,1)} fusion(bf16[2048,2048]{1,0:T(8,128)(2,1)S(1)} %shard_map.283, bf16[2048,1024]{1,0:T(8,128)(2,1)S(1)} %shard_map.284), kind=kOutput, calls=%fused_computation.9 | convolution fusion | flops 8592031744 | bytes 16777216 | tf_op jit(solution)/shard_map/dot_general | solution.py:30
  632.5 11.1 %collective-permute-done.77 = bf16[2,512,512]{2,1,0:T(8,128)(2,1)S(1)} collective-permute-done((bf16[2,512,512]{2,1,0:T(8,128)(2,1)}, bf16[2,512,512]{2,1,0:T(8,128)(2,1)S(1)}, u32[]{:S(2)}, u32[]{:S(2)}) %collective-permute-start.77) | collective-permute-done | bytes 1048608 | tf_op jit(solution)/shard_map/ppermute | solution.py:307
  660.4 3.3 collective-permute-done.79
  672.2 3.9 collective-permute-start.82
  677.9 6.9 convolution_convert_fusion.1
  685.9 8.2 collective-permute-done.82.refs_2_
  694.2 11.8 %collective-permute-start.87 = (bf16[128,1024]{1,0:T(8,128)(2,1)S(1)}, bf16[128,1024]{1,0:T(8,128)(2,1)S(1)}, u32[]{:S(2)}, u32[]{:S(2)}) collective-permute-start(bf16[128,1024]{1,0:T(8,128)(2,1)S(1)} %get-tuple-element.360), channel_id=1, source_target_pairs={{0,1},{1,2},{2,3},{3,0},{4,5},{5,6},{6,7},{7,4},{8,9},{9,10},{10,1... | collective-permute-start | bytes 786440 | tf_op jit(solution)/shard_map/ppermute | solution.py:324
  716.9 3.7 fusion.45
  722.6 20.1 %shard_map.289 = (bf16[1024,512]{1,0:T(8,128)(2,1)S(1)}, bf16[1024,512]{1,0:T(8,128)(2,1)S(1)}, bf16[1024,512]{1,0:T(8,128)(2,1)S(1)}) custom-call(bf16[1024,512]{1,0:T(8,128)(2,1)S(1)} %copy-done.39, bf16[1024,512]{1,0:T(8,128)(2,1)S(1)} %copy-done.41, bf16[1024,512]{1,0:T(8,128)(2,1)} %copy-done.42, bf16[1024,512]{1,0:T(8,128)(2,1)} %copy-done.37, ...), custom_call_target="tpu_custom_call" | custom-call | tf_op jit(solution)/shard_map/pallas_call | solution.py:208
  744.5 6.4 shard_map.290
  758.7 4.0 constant_dynamic-slice_fusion.2
  786.3 6.4 shard_map.291.refs_0_
  796.3 10.6 %convolution_convert_fusion = bf16[2048,1536]{1,0:T(8,128)(2,1)} fusion(bf16[1024,2048]{1,0:T(8,128)(2,1)S(1)} %copy-done.24, bf16[1024,1536]{1,0:T(8,128)(2,1)} %shard_map.291.refs_0_), kind=kOutput, calls=%fused_computation.2 | convolution fusion | flops 6445596672 | bytes 13631488 | tf_op jit(solution)/shard_map/dot_general | solution.py:30
  816.7 4.9 fusion.46
  821.6 3.2 constant_dynamic-slice_fusion
  835.4 3.2 fusion.69
  838.6 21.0 %collective-permute-done.98 = bf16[256,2048]{1,0:T(8,128)(2,1)} collective-permute-done((bf16[256,2048]{1,0:T(8,128)(2,1)}, bf16[256,2048]{1,0:T(8,128)(2,1)}, u32[]{:S(2)}, u32[]{:S(2)}) %collective-permute-start.98) | collective-permute-done | bytes 1048608 | tf_op jit(solution)/shard_map/ppermute | solution.py:302
  868.3 6.2 collective-permute-done.121
  878.5 22.3 %collective-permute-done.109 = bf16[256,1024]{1,0:T(8,128)(2,1)S(1)} collective-permute-done((bf16[256,1024]{1,0:T(8,128)(2,1)S(1)}, bf16[256,1024]{1,0:T(8,128)(2,1)S(1)}, u32[]{:S(2)}, u32[]{:S(2)}) %collective-permute-start.109) | collective-permute-done | bytes 524320 | tf_op jit(solution)/shard_map/ppermute | solution.py:307
  905.9 6.5 collective-permute-done.112
  913.4 14.8 %collective-permute-done.111 = bf16[256,2048]{1,0:T(8,128)(2,1)} collective-permute-done((bf16[256,2048]{1,0:T(8,128)(2,1)}, bf16[256,2048]{1,0:T(8,128)(2,1)}, u32[]{:S(2)}, u32[]{:S(2)}) %collective-permute-start.111) | collective-permute-done | bytes 1048608 | tf_op jit(solution)/shard_map/ppermute | solution.py:302
  950.8 21.9 %collective-permute-done.118 = bf16[64,2176]{1,0:T(8,128)(2,1)S(1)} collective-permute-done((bf16[64,2176]{1,0:T(8,128)(2,1)S(1)}, bf16[64,2176]{1,0:T(8,128)(2,1)S(1)}, u32[]{:S(2)}, u32[]{:S(2)}) %collective-permute-start.118) | collective-permute-done | bytes 278560 | tf_op jit(solution)/shard_map/ppermute | solution.py:324
  (766 shorter events, 384.3 us)
Async XLA Ops:
  2.1 24.3 %collective-permute-start.3 = (bf16[128,2048]{1,0:T(8,128)(2,1)S(1)}, bf16[128,2048]{1,0:T(8,128)(2,1)S(1)}, u32[]{:S(2)}, u32[]{:S(2)}) collective-permute-start(bf16[128,2048]{1,0:T(8,128)(2,1)S(1)} %get-tuple-element.473.refs_0_), channel_id=1, source_target_pairs={{0,8},{4,12},{8,0},{12,4},{16,24},{20,28},{24,16},{28,20},{1,9},{5... | collective-permute-start | bytes 1572872 | tf_op jit(solution)/shard_map/ppermute | solution.py:307
  29.5 22.8 %collective-permute-start.8 = (bf16[128,1664]{1,0:T(8,128)(2,1)S(1)}, bf16[128,1664]{1,0:T(8,128)(2,1)S(1)}, u32[]{:S(2)}, u32[]{:S(2)}) collective-permute-start(bf16[128,1664]{1,0:T(8,128)(2,1)S(1)} %get-tuple-element.475.refs_0_), channel_id=1, source_target_pairs={{0,8},{4,12},{8,0},{12,4},{16,24},{20,28},{24,16},{28,20},{1,9},{5... | collective-permute-start | bytes 1277960 | tf_op jit(solution)/shard_map/ppermute | solution.py:307
  53.3 30.4 %collective-permute-start.13 = (bf16[256,1664]{1,0:T(8,128)(2,1)S(1)}, bf16[256,1664]{1,0:T(8,128)(2,1)S(1)}, u32[]{:S(2)}, u32[]{:S(2)}) collective-permute-start(bf16[256,1664]{1,0:T(8,128)(2,1)S(1)} %shard_map.244.refs_0_), channel_id=1, source_target_pairs={{0,16},{4,20},{8,24},{12,28},{16,0},{20,4},{24,8},{28,12},{1,17},{... | collective-permute-start | bytes 2555912 | tf_op jit(solution)/shard_map/ppermute | solution.py:307
  55.9 27.8 %collective-permute-start.14 = (bf16[256,1664]{1,0:T(8,128)(2,1)S(1)}, bf16[256,1664]{1,0:T(8,128)(2,1)S(1)}, u32[]{:S(2)}, u32[]{:S(2)}) collective-permute-start(bf16[256,1664]{1,0:T(8,128)(2,1)S(1)} %shard_map.245.refs_0_), channel_id=1, source_target_pairs={{0,8},{4,12},{8,0},{12,4},{16,24},{20,28},{24,16},{28,20},{1,9},{5... | collective-permute-start | bytes 2555912 | tf_op jit(solution)/shard_map/ppermute | solution.py:307
  83.7 28.1 %collective-permute-start.16 = (bf16[256,2048]{1,0:T(8,128)(2,1)S(1)}, bf16[256,2048]{1,0:T(8,128)(2,1)S(1)}, u32[]{:S(2)}, u32[]{:S(2)}) collective-permute-start(bf16[256,2048]{1,0:T(8,128)(2,1)S(1)} %bitcast.265), channel_id=1, source_target_pairs={{0,1},{1,2},{2,3},{3,0},{4,5},{5,6},{6,7},{7,4},{8,9},{9,10},{10,1... | collective-permute-start | bytes 3145736 | tf_op jit(solution)/shard_map/ppermute | solution.py:302
  88.8 42.2 %collective-permute-start.22 = (bf16[512,1664]{1,0:T(8,128)(2,1)S(1)}, bf16[512,1664]{1,0:T(8,128)(2,1)S(1)}, u32[]{:S(2)}, u32[]{:S(2)}) collective-permute-start(bf16[512,1664]{1,0:T(8,128)(2,1)S(1)} %shard_map.250.refs_0_), channel_id=1, source_target_pairs={{0,4},{4,0},{8,12},{12,8},{16,20},{20,16},{24,28},{28,24},{1,5},{5... | collective-permute-start | bytes 5111816 | tf_op jit(solution)/shard_map/ppermute | solution.py:307
  89.5 43.2 %collective-permute-start.23 = (bf16[512,1664]{1,0:T(8,128)(2,1)S(1)}, bf16[512,1664]{1,0:T(8,128)(2,1)S(1)}, u32[]{:S(2)}, u32[]{:S(2)}) collective-permute-start(bf16[512,1664]{1,0:T(8,128)(2,1)S(1)} %shard_map.251.refs_2_), channel_id=1, source_target_pairs={{0,4},{4,0},{8,12},{12,8},{16,20},{20,16},{24,28},{28,24},{1,5},{5... | collective-permute-start | bytes 5111816 | tf_op jit(solution)/shard_map/ppermute | solution.py:307
  104.0 24.3 %collective-permute-start.20 = (bf16[256,2048]{1,0:T(8,128)(2,1)S(1)}, bf16[256,2048]{1,0:T(8,128)(2,1)S(1)}, u32[]{:S(2)}, u32[]{:S(2)}) collective-permute-start(bf16[256,2048]{1,0:T(8,128)(2,1)S(1)} %shard_map.248.refs_0_), channel_id=1, source_target_pairs={{0,16},{4,20},{8,24},{12,28},{16,0},{20,4},{24,8},{28,12},{1,17},{... | collective-permute-start | bytes 3145736 | tf_op jit(solution)/shard_map/ppermute | solution.py:307
  104.5 24.8 %collective-permute-start.21 = (bf16[256,2048]{1,0:T(8,128)(2,1)S(1)}, bf16[256,2048]{1,0:T(8,128)(2,1)S(1)}, u32[]{:S(2)}, u32[]{:S(2)}) collective-permute-start(bf16[256,2048]{1,0:T(8,128)(2,1)S(1)} %shard_map.249.refs_2_), channel_id=1, source_target_pairs={{0,8},{4,12},{8,0},{12,4},{16,24},{20,28},{24,16},{28,20},{1,9},{5... | collective-permute-start | bytes 3145736 | tf_op jit(solution)/shard_map/ppermute | solution.py:307
  111.9 26.2 %collective-permute-start.19 = (bf16[256,2048]{1,0:T(8,128)(2,1)S(1)}, bf16[256,2048]{1,0:T(8,128)(2,1)}, u32[]{:S(2)}, u32[]{:S(2)}) collective-permute-start(bf16[256,2048]{1,0:T(8,128)(2,1)S(1)} %collective-permute-done.16.refs_1_), channel_id=1, source_target_pairs={{0,1},{1,2},{2,3},{3,0},{4,5},{5,6},{6,7},{7,4},{8,9},{9,10},{10,1... | collective-permute-start | bytes 3145736 | tf_op jit(solution)/shard_map/ppermute | solution.py:302
  130.3 38.5 %collective-permute-start.25 = (bf16[512,1024]{1,0:T(8,128)(2,1)}, bf16[512,1024]{1,0:T(8,128)(2,1)}, u32[]{:S(2)}, u32[]{:S(2)}) collective-permute-start(bf16[512,1024]{1,0:T(8,128)(2,1)} %shard_map.252.refs_0_), channel_id=1, source_target_pairs={{0,16},{4,20},{8,24},{12,28},{16,0},{20,4},{24,8},{28,12},{1,17},{... | collective-permute-start | bytes 3145736 | tf_op jit(solution)/shard_map/ppermute | solution.py:307
  132.2 36.6 %collective-permute-start.26 = (bf16[512,1024]{1,0:T(8,128)(2,1)}, bf16[512,1024]{1,0:T(8,128)(2,1)}, u32[]{:S(2)}, u32[]{:S(2)}) collective-permute-start(bf16[512,1024]{1,0:T(8,128)(2,1)} %shard_map.253.refs_2_), channel_id=1, source_target_pairs={{0,8},{4,12},{8,0},{12,4},{16,24},{20,28},{24,16},{28,20},{1,9},{5... | collective-permute-start | bytes 3145736 | tf_op jit(solution)/shard_map/ppermute | solution.py:307
  138.1 30.8 %collective-permute-start.24 = (bf16[256,2048]{1,0:T(8,128)(2,1)}, bf16[256,2048]{1,0:T(8,128)(2,1)}, u32[]{:S(2)}, u32[]{:S(2)}) collective-permute-start(bf16[256,2048]{1,0:T(8,128)(2,1)} %collective-permute-done.19.refs_2_), channel_id=1, source_target_pairs={{0,1},{1,2},{2,3},{3,0},{4,5},{5,6},{6,7},{7,4},{8,9},{9,10},{10,1... | collective-permute-start | bytes 3145736 | tf_op jit(solution)/shard_map/ppermute | solution.py:302
  139.7 29.1 %collective-permute-start.27 = (bf16[256,1024]{1,0:T(8,128)(2,1)S(1)}, bf16[256,1024]{1,0:T(8,128)(2,1)}, u32[]{:S(2)}, u32[]{:S(2)}) collective-permute-start(bf16[256,1024]{1,0:T(8,128)(2,1)S(1)} %shard_map.254.refs_0_), channel_id=1, source_target_pairs={{0,8},{4,12},{8,0},{12,4},{16,24},{20,28},{24,16},{28,20},{1,9},{5... | collective-permute-start | bytes 1572872 | tf_op jit(solution)/shard_map/ppermute | solution.py:307
  140.3 28.5 %collective-permute-start.29 = (bf16[256,1024]{1,0:T(8,128)(2,1)}, bf16[256,1024]{1,0:T(8,128)(2,1)}, u32[]{:S(2)}, u32[]{:S(2)}) collective-permute-start(bf16[256,1024]{1,0:T(8,128)(2,1)} %collective-permute-done.28.refs_0_), channel_id=1, source_target_pairs={{0,16},{4,20},{8,24},{12,28},{16,0},{20,4},{24,8},{28,12},{1,17},{... | collective-permute-start | bytes 1572872 | tf_op jit(solution)/shard_map/ppermute | solution.py:307
  194.6 35.7 %collective-permute-start.38 = (bf16[512,1024]{1,0:T(8,128)(2,1)}, bf16[512,1024]{1,0:T(8,128)(2,1)}, u32[]{:S(2)}, u32[]{:S(2)}) collective-permute-start(bf16[512,1024]{1,0:T(8,128)(2,1)} %shard_map.262.refs_0_), channel_id=1, source_target_pairs={{0,16},{4,20},{8,24},{12,28},{16,0},{20,4},{24,8},{28,12},{1,17},{... | collective-permute-start | bytes 3145736 | tf_op jit(solution)/shard_map/ppermute | solution.py:307
  196.2 34.1 %collective-permute-start.39 = (bf16[512,1024]{1,0:T(8,128)(2,1)}, bf16[512,1024]{1,0:T(8,128)(2,1)}, u32[]{:S(2)}, u32[]{:S(2)}) collective-permute-start(bf16[512,1024]{1,0:T(8,128)(2,1)} %shard_map.263.refs_2_), channel_id=1, source_target_pairs={{0,8},{4,12},{8,0},{12,4},{16,24},{20,28},{24,16},{28,20},{1,9},{5... | collective-permute-start | bytes 3145736 | tf_op jit(solution)/shard_map/ppermute | solution.py:307
  231.8 24.8 %collective-permute-start.43 = (bf16[256,2048]{1,0:T(8,128)(2,1)S(1)}, bf16[256,2048]{1,0:T(8,128)(2,1)S(1)}, u32[]{:S(2)}, u32[]{:S(2)}) collective-permute-start(bf16[256,2048]{1,0:T(8,128)(2,1)S(1)} %shard_map.264.refs_0_), channel_id=1, source_target_pairs={{0,16},{4,20},{8,24},{12,28},{16,0},{20,4},{24,8},{28,12},{1,17},{... | collective-permute-start | bytes 3145736 | tf_op jit(solution)/shard_map/ppermute | solution.py:307
  233.5 23.6 %collective-permute-start.44 = (bf16[256,2048]{1,0:T(8,128)(2,1)S(1)}, bf16[256,2048]{1,0:T(8,128)(2,1)S(1)}, u32[]{:S(2)}, u32[]{:S(2)}) collective-permute-start(bf16[256,2048]{1,0:T(8,128)(2,1)S(1)} %shard_map.265.refs_0_), channel_id=1, source_target_pairs={{0,8},{4,12},{8,0},{12,4},{16,24},{20,28},{24,16},{28,20},{1,9},{5... | collective-permute-start | bytes 3145736 | tf_op jit(solution)/shard_map/ppermute | solution.py:307
  271.7 31.8 %collective-permute-start.47 = (bf16[256,2048]{1,0:T(8,128)(2,1)S(1)}, bf16[256,2048]{1,0:T(8,128)(2,1)S(1)}, u32[]{:S(2)}, u32[]{:S(2)}) collective-permute-start(bf16[256,2048]{1,0:T(8,128)(2,1)S(1)} %fusion.17.refs_0_), channel_id=1, source_target_pairs={{0,1},{1,2},{2,3},{3,0},{4,5},{5,6},{6,7},{7,4},{8,9},{9,10},{10,1... | collective-permute-start | bytes 3145736 | tf_op jit(solution)/shard_map/ppermute | solution.py:302
  303.5 27.5 %collective-permute-start.50 = (bf16[256,2048]{1,0:T(8,128)(2,1)S(1)}, bf16[256,2048]{1,0:T(8,128)(2,1)S(1)}, u32[]{:S(2)}, u32[]{:S(2)}) collective-permute-start(bf16[256,2048]{1,0:T(8,128)(2,1)S(1)} %collective-permute-done.47.refs_0_), channel_id=1, source_target_pairs={{0,1},{1,2},{2,3},{3,0},{4,5},{5,6},{6,7},{7,4},{8,9},{9,10},{10,1... | collective-permute-start | bytes 3145736 | tf_op jit(solution)/shard_map/ppermute | solution.py:302
  331.0 27.4 %collective-permute-start.52 = (bf16[256,2048]{1,0:T(8,128)(2,1)S(1)}, bf16[256,2048]{1,0:T(8,128)(2,1)S(1)}, u32[]{:S(2)}, u32[]{:S(2)}) collective-permute-start(bf16[256,2048]{1,0:T(8,128)(2,1)S(1)} %collective-permute-done.50.refs_0_), channel_id=1, source_target_pairs={{0,1},{1,2},{2,3},{3,0},{4,5},{5,6},{6,7},{7,4},{8,9},{9,10},{10,1... | collective-permute-start | bytes 3145736 | tf_op jit(solution)/shard_map/ppermute | solution.py:302
  331.0 27.4 %collective-permute-start.57 = (bf16[256,2048]{1,0:T(8,128)(2,1)S(1)}, bf16[256,2048]{1,0:T(8,128)(2,1)S(1)}, u32[]{:S(2)}, u32[]{:S(2)}) collective-permute-start(bf16[256,2048]{1,0:T(8,128)(2,1)S(1)} %slice.251), channel_id=1, source_target_pairs={{0,4},{4,0},{8,12},{12,8},{16,20},{20,16},{24,28},{28,24},{1,5},{5... | collective-permute-start | bytes 3145736 | tf_op jit(solution)/shard_map/ppermute | solution.py:307
  358.7 27.6 %collective-permute-start.58 = (bf16[256,2048]{1,0:T(8,128)(2,1)S(1)}, bf16[256,2048]{1,0:T(8,128)(2,1)S(1)}, u32[]{:S(2)}, u32[]{:S(2)}) collective-permute-start(bf16[256,2048]{1,0:T(8,128)(2,1)S(1)} %add_convert_fusion.7), channel_id=1, source_target_pairs={{0,1},{1,2},{2,3},{3,0},{4,5},{5,6},{6,7},{7,4},{8,9},{9,10},{10,1... | collective-permute-start | bytes 3145736 | tf_op jit(solution)/shard_map/ppermute | solution.py:302
  359.0 27.4 %collective-permute-start.56 = (bf16[256,2048]{1,0:T(8,128)(2,1)S(1)}, bf16[256,2048]{1,0:T(8,128)(2,1)S(1)}, u32[]{:S(2)}, u32[]{:S(2)}) collective-permute-start(bf16[256,2048]{1,0:T(8,128)(2,1)S(1)} %slice.250), channel_id=1, source_target_pairs={{0,4},{4,0},{8,12},{12,8},{16,20},{20,16},{24,28},{28,24},{1,5},{5... | collective-permute-start | bytes 3145736 | tf_op jit(solution)/shard_map/ppermute | solution.py:307
  386.9 26.6 %collective-permute-start.59 = (bf16[256,2048]{1,0:T(8,128)(2,1)S(1)}, bf16[256,2048]{1,0:T(8,128)(2,1)S(1)}, u32[]{:S(2)}, u32[]{:S(2)}) collective-permute-start(bf16[256,2048]{1,0:T(8,128)(2,1)S(1)} %add_convert_fusion.6), channel_id=1, source_target_pairs={{0,1},{1,2},{2,3},{3,0},{4,5},{5,6},{6,7},{7,4},{8,9},{9,10},{10,1... | collective-permute-start | bytes 3145736 | tf_op jit(solution)/shard_map/ppermute | solution.py:302
  387.1 26.4 %collective-permute-start.55 = (bf16[256,2048]{1,0:T(8,128)(2,1)S(1)}, bf16[256,2048]{1,0:T(8,128)(2,1)S(1)}, u32[]{:S(2)}, u32[]{:S(2)}) collective-permute-start(bf16[256,2048]{1,0:T(8,128)(2,1)S(1)} %slice.249), channel_id=1, source_target_pairs={{0,4},{4,0},{8,12},{12,8},{16,20},{20,16},{24,28},{28,24},{1,5},{5... | collective-permute-start | bytes 3145736 | tf_op jit(solution)/shard_map/ppermute | solution.py:307
  414.0 25.7 %collective-permute-start.60 = (bf16[256,2048]{1,0:T(8,128)(2,1)S(1)}, bf16[256,2048]{1,0:T(8,128)(2,1)S(1)}, u32[]{:S(2)}, u32[]{:S(2)}) collective-permute-start(bf16[256,2048]{1,0:T(8,128)(2,1)S(1)} %fusion.10), channel_id=1, source_target_pairs={{0,1},{1,2},{2,3},{3,0},{4,5},{5,6},{6,7},{7,4},{8,9},{9,10},{10,1... | collective-permute-start | bytes 3145736 | tf_op jit(solution)/shard_map/ppermute | solution.py:302
  414.1 25.7 %collective-permute-start.49 = (bf16[256,2048]{1,0:T(8,128)(2,1)S(1)}, bf16[256,2048]{1,0:T(8,128)(2,1)S(1)}, u32[]{:S(2)}, u32[]{:S(2)}) collective-permute-start(bf16[256,2048]{1,0:T(8,128)(2,1)S(1)} %slice.252), channel_id=1, source_target_pairs={{0,4},{4,0},{8,12},{12,8},{16,20},{20,16},{24,28},{28,24},{1,5},{5... | collective-permute-start | bytes 3145736 | tf_op jit(solution)/shard_map/ppermute | solution.py:307
  442.3 27.6 %collective-permute-start.61 = (bf16[256,2048]{1,0:T(8,128)(2,1)S(1)}, bf16[256,2048]{1,0:T(8,128)(2,1)S(1)}, u32[]{:S(2)}, u32[]{:S(2)}) collective-permute-start(bf16[256,2048]{1,0:T(8,128)(2,1)S(1)} %fusion.5.refs_0_), channel_id=1, source_target_pairs={{0,1},{1,2},{2,3},{3,0},{4,5},{5,6},{6,7},{7,4},{8,9},{9,10},{10,1... | collective-permute-start | bytes 3145736 | tf_op jit(solution)/shard_map/ppermute | solution.py:302
  469.9 27.8 %collective-permute-start.64 = (bf16[256,2048]{1,0:T(8,128)(2,1)S(1)}, bf16[256,2048]{1,0:T(8,128)(2,1)S(1)}, u32[]{:S(2)}, u32[]{:S(2)}) collective-permute-start(bf16[256,2048]{1,0:T(8,128)(2,1)S(1)} %collective-permute-done.61.refs_0_), channel_id=1, source_target_pairs={{0,1},{1,2},{2,3},{3,0},{4,5},{5,6},{6,7},{7,4},{8,9},{9,10},{10,1... | collective-permute-start | bytes 3145736 | tf_op jit(solution)/shard_map/ppermute | solution.py:302
  497.7 27.5 %collective-permute-start.66 = (bf16[256,2048]{1,0:T(8,128)(2,1)S(1)}, bf16[256,2048]{1,0:T(8,128)(2,1)S(1)}, u32[]{:S(2)}, u32[]{:S(2)}) collective-permute-start(bf16[256,2048]{1,0:T(8,128)(2,1)S(1)} %collective-permute-done.64.refs_0_), channel_id=1, source_target_pairs={{0,1},{1,2},{2,3},{3,0},{4,5},{5,6},{6,7},{7,4},{8,9},{9,10},{10,1... | collective-permute-start | bytes 3145736 | tf_op jit(solution)/shard_map/ppermute | solution.py:302
  497.9 38.4 %collective-permute-start.71 = (bf16[256,2048]{1,0:T(8,128)(2,1)}, bf16[256,2048]{1,0:T(8,128)(2,1)}, u32[]{:S(2)}, u32[]{:S(2)}) collective-permute-start(bf16[256,2048]{1,0:T(8,128)(2,1)} %slice.247), channel_id=1, source_target_pairs={{0,4},{4,0},{8,12},{12,8},{16,20},{20,16},{24,28},{28,24},{1,5},{5... | collective-permute-start | bytes 3145736 | tf_op jit(solution)/shard_map/ppermute | solution.py:307
  535.7 112.3 %collective-permute-start.63 = (bf16[256,2048]{1,0:T(8,128)(2,1)}, bf16[256,2048]{1,0:T(8,128)(2,1)}, u32[]{:S(2)}, u32[]{:S(2)}) collective-permute-start(bf16[256,2048]{1,0:T(8,128)(2,1)} %slice.248), channel_id=1, source_target_pairs={{0,4},{4,0},{8,12},{12,8},{16,20},{20,16},{24,28},{28,24},{1,5},{5... | collective-permute-start | bytes 3145736 | tf_op jit(solution)/shard_map/ppermute | solution.py:307
  539.4 27.9 %collective-permute-start.72 = (bf16[256,2048]{1,0:T(8,128)(2,1)}, bf16[256,2048]{1,0:T(8,128)(2,1)}, u32[]{:S(2)}, u32[]{:S(2)}) collective-permute-start(bf16[256,2048]{1,0:T(8,128)(2,1)} %add_convert_fusion.4), channel_id=1, source_target_pairs={{0,1},{1,2},{2,3},{3,0},{4,5},{5,6},{6,7},{7,4},{8,9},{9,10},{10,1... | collective-permute-start | bytes 3145736 | tf_op jit(solution)/shard_map/ppermute | solution.py:302
  539.6 27.7 %collective-permute-start.70 = (bf16[256,2048]{1,0:T(8,128)(2,1)}, bf16[256,2048]{1,0:T(8,128)(2,1)}, u32[]{:S(2)}, u32[]{:S(2)}) collective-permute-start(bf16[256,2048]{1,0:T(8,128)(2,1)} %slice.246), channel_id=1, source_target_pairs={{0,4},{4,0},{8,12},{12,8},{16,20},{20,16},{24,28},{28,24},{1,5},{5... | collective-permute-start | bytes 3145736 | tf_op jit(solution)/shard_map/ppermute | solution.py:307
  570.3 41.1 %collective-permute-start.73 = (bf16[256,2048]{1,0:T(8,128)(2,1)}, bf16[256,2048]{1,0:T(8,128)(2,1)}, u32[]{:S(2)}, u32[]{:S(2)}) collective-permute-start(bf16[256,2048]{1,0:T(8,128)(2,1)} %add_convert_fusion.3), channel_id=1, source_target_pairs={{0,1},{1,2},{2,3},{3,0},{4,5},{5,6},{6,7},{7,4},{8,9},{9,10},{10,1... | collective-permute-start | bytes 3145736 | tf_op jit(solution)/shard_map/ppermute | solution.py:302
  595.4 26.2 %collective-permute-start.75 = (bf16[2,256,1024]{2,1,0:T(8,128)(2,1)}, bf16[2,256,1024]{2,1,0:T(8,128)(2,1)S(1)}, u32[]{:S(2)}, u32[]{:S(2)}) collective-permute-start(bf16[2,256,1024]{2,1,0:T(8,128)(2,1)} %dynamic-slice_bitcast_fusion.7), channel_id=1, source_target_pairs={{0,8},{4,12},{8,0},{12,4},{16,24},{20,28},{24,16},{28,20},{1,9},{5... | collective-permute-start | bytes 3145736 | tf_op jit(solution)/shard_map/ppermute | solution.py:307
  597.4 35.0 %collective-permute-start.76 = (bf16[2,256,1024]{2,1,0:T(8,128)(2,1)}, bf16[2,256,1024]{2,1,0:T(8,128)(2,1)S(1)}, u32[]{:S(2)}, u32[]{:S(2)}) collective-permute-start(bf16[2,256,1024]{2,1,0:T(8,128)(2,1)} %dynamic-slice_bitcast_fusion.6), channel_id=1, source_target_pairs={{0,16},{4,20},{8,24},{12,28},{16,0},{20,4},{24,8},{28,12},{1,17},{... | collective-permute-start | bytes 3145736 | tf_op jit(solution)/shard_map/ppermute | solution.py:307
  611.3 32.3 %collective-permute-start.77 = (bf16[2,512,512]{2,1,0:T(8,128)(2,1)}, bf16[2,512,512]{2,1,0:T(8,128)(2,1)S(1)}, u32[]{:S(2)}, u32[]{:S(2)}) collective-permute-start(bf16[2,512,512]{2,1,0:T(8,128)(2,1)} %dynamic-slice_bitcast_fusion.5), channel_id=1, source_target_pairs={{0,8},{4,12},{8,0},{12,4},{16,24},{20,28},{24,16},{28,20},{1,9},{5... | collective-permute-start | bytes 3145736 | tf_op jit(solution)/shard_map/ppermute | solution.py:307
  612.4 33.3 %collective-permute-start.78 = (bf16[2,512,512]{2,1,0:T(8,128)(2,1)}, bf16[2,512,512]{2,1,0:T(8,128)(2,1)S(1)}, u32[]{:S(2)}, u32[]{:S(2)}) collective-permute-start(bf16[2,512,512]{2,1,0:T(8,128)(2,1)} %dynamic-slice_bitcast_fusion.4), channel_id=1, source_target_pairs={{0,16},{4,20},{8,24},{12,28},{16,0},{20,4},{24,8},{28,12},{1,17},{... | collective-permute-start | bytes 3145736 | tf_op jit(solution)/shard_map/ppermute | solution.py:307
  621.6 26.4 %collective-permute-start.74 = (bf16[256,2048]{1,0:T(8,128)(2,1)S(1)}, bf16[256,2048]{1,0:T(8,128)(2,1)S(1)}, u32[]{:S(2)}, u32[]{:S(2)}) collective-permute-start(bf16[256,2048]{1,0:T(8,128)(2,1)S(1)} %add_convert_fusion.2), channel_id=1, source_target_pairs={{0,1},{1,2},{2,3},{3,0},{4,5},{5,6},{6,7},{7,4},{8,9},{9,10},{10,1... | collective-permute-start | bytes 3145736 | tf_op jit(solution)/shard_map/ppermute | solution.py:302
  667.3 26.9 %collective-permute-start.84 = (bf16[2,512,512]{2,1,0:T(8,128)(2,1)}, bf16[2,512,512]{2,1,0:T(8,128)(2,1)}, u32[]{:S(2)}, u32[]{:S(2)}) collective-permute-start(bf16[2,512,512]{2,1,0:T(8,128)(2,1)} %dynamic-slice_bitcast_fusion.3), channel_id=1, source_target_pairs={{0,8},{4,12},{8,0},{12,4},{16,24},{20,28},{24,16},{28,20},{1,9},{5... | collective-permute-start | bytes 3145736 | tf_op jit(solution)/shard_map/ppermute | solution.py:307
  668.9 25.3 %collective-permute-start.85 = (bf16[2,512,512]{2,1,0:T(8,128)(2,1)}, bf16[2,512,512]{2,1,0:T(8,128)(2,1)}, u32[]{:S(2)}, u32[]{:S(2)}) collective-permute-start(bf16[2,512,512]{2,1,0:T(8,128)(2,1)} %dynamic-slice_bitcast_fusion.2), channel_id=1, source_target_pairs={{0,16},{4,20},{8,24},{12,28},{16,0},{20,4},{24,8},{28,12},{1,17},{... | collective-permute-start | bytes 3145736 | tf_op jit(solution)/shard_map/ppermute | solution.py:307
  694.2 49.5 %collective-permute-start.87 = (bf16[128,1024]{1,0:T(8,128)(2,1)S(1)}, bf16[128,1024]{1,0:T(8,128)(2,1)S(1)}, u32[]{:S(2)}, u32[]{:S(2)}) collective-permute-start(bf16[128,1024]{1,0:T(8,128)(2,1)S(1)} %get-tuple-element.360), channel_id=1, source_target_pairs={{0,1},{1,2},{2,3},{3,0},{4,5},{5,6},{6,7},{7,4},{8,9},{9,10},{10,1... | collective-permute-start | bytes 786440 | tf_op jit(solution)/shard_map/ppermute | solution.py:324
  706.0 38.4 %collective-permute-start.88 = (bf16[128,1024]{1,0:T(8,128)(2,1)S(1)}, bf16[128,1024]{1,0:T(8,128)(2,1)S(1)}, u32[]{:S(2)}, u32[]{:S(2)}) collective-permute-start(bf16[128,1024]{1,0:T(8,128)(2,1)S(1)} %get-tuple-element.361), channel_id=1, source_target_pairs={{0,2},{1,3},{2,0},{3,1},{4,6},{5,7},{6,4},{7,5},{8,10},{9,11},{10,... | collective-permute-start | bytes 786440 | tf_op jit(solution)/shard_map/ppermute | solution.py:324
  706.0 38.4 %collective-permute-start.89 = (bf16[128,1024]{1,0:T(8,128)(2,1)S(1)}, bf16[128,1024]{1,0:T(8,128)(2,1)S(1)}, u32[]{:S(2)}, u32[]{:S(2)}) collective-permute-start(bf16[128,1024]{1,0:T(8,128)(2,1)S(1)} %get-tuple-element.362), channel_id=1, source_target_pairs={{0,3},{1,0},{2,1},{3,2},{4,7},{5,4},{6,5},{7,6},{8,11},{9,8},{10,9... | collective-permute-start | bytes 786440 | tf_op jit(solution)/shard_map/ppermute | solution.py:324
  711.4 33.1 %collective-permute-start.90 = (bf16[512,512]{1,0:T(8,128)(2,1)}, bf16[512,512]{1,0:T(8,128)(2,1)}, u32[]{:S(2)}, u32[]{:S(2)}) collective-permute-start(bf16[512,512]{1,0:T(8,128)(2,1)} %fusion.30), channel_id=1, source_target_pairs={{0,16},{4,20},{8,24},{12,28},{16,0},{20,4},{24,8},{28,12},{1,17},{... | collective-permute-start | bytes 1572872 | tf_op jit(solution)/shard_map/ppermute | solution.py:307
  715.5 29.0 %collective-permute-start.91 = (bf16[512,512]{1,0:T(8,128)(2,1)}, bf16[512,512]{1,0:T(8,128)(2,1)}, u32[]{:S(2)}, u32[]{:S(2)}) collective-permute-start(bf16[512,512]{1,0:T(8,128)(2,1)} %fusion.31), channel_id=1, source_target_pairs={{0,8},{4,12},{8,0},{12,4},{16,24},{20,28},{24,16},{28,20},{1,9},{5... | collective-permute-start | bytes 1572872 | tf_op jit(solution)/shard_map/ppermute | solution.py:307
  758.7 35.4 %collective-permute-start.97 = (bf16[2,2,256,1152]{3,2,1,0:T(8,128)(2,1)}, bf16[2,2,256,1152]{3,2,1,0:T(8,128)(2,1)}, u32[]{:S(2)}, u32[]{:S(2)}) collective-permute-start(bf16[2,2,256,1152]{3,2,1,0:T(8,128)(2,1)} %dynamic-slice_bitcast_fusion), channel_id=1, source_target_pairs={{0,4},{4,0},{8,12},{12,8},{16,20},{20,16},{24,28},{28,24},{1,5},{5... | collective-permute-start | bytes 7077896 | tf_op jit(solution)/shard_map/ppermute | solution.py:307
  764.2 29.8 %collective-permute-start.96 = (bf16[2,2,256,1024]{3,2,0,1:T(8,128)(2,1)}, bf16[2,2,256,1024]{3,2,0,1:T(8,128)(2,1)}, u32[]{:S(2)}, u32[]{:S(2)}) collective-permute-start(bf16[2,2,256,1024]{3,2,0,1:T(8,128)(2,1)} %bitcast.261), channel_id=1, source_target_pairs={{0,4},{4,0},{8,12},{12,8},{16,20},{20,16},{24,28},{28,24},{1,5},{5... | collective-permute-start | bytes 6291464 | tf_op jit(solution)/shard_map/ppermute | solution.py:307
  824.9 36.3 %collective-permute-start.104 = (bf16[2,2,256,768]{3,2,0,1:T(8,128)(2,1)S(1)}, bf16[2,2,256,768]{3,2,0,1:T(8,128)(2,1)S(1)}, u32[]{:S(2)}, u32[]{:S(2)}) collective-permute-start(bf16[2,2,256,768]{3,2,0,1:T(8,128)(2,1)S(1)} %bitcast.302), channel_id=1, source_target_pairs={{0,4},{4,0},{8,12},{12,8},{16,20},{20,16},{24,28},{28,24},{1,5},{5... | collective-permute-start | bytes 4718600 | tf_op jit(solution)/shard_map/ppermute | solution.py:307
  826.3 34.9 %collective-permute-start.105 = (bf16[2,2,256,768]{3,2,1,0:T(8,128)(2,1)}, bf16[2,2,256,768]{3,2,1,0:T(8,128)(2,1)S(1)}, u32[]{:S(2)}, u32[]{:S(2)}) collective-permute-start(bf16[2,2,256,768]{3,2,1,0:T(8,128)(2,1)} %dynamic-slice_bitcast_fusion.1), channel_id=1, source_target_pairs={{0,4},{4,0},{8,12},{12,8},{16,20},{20,16},{24,28},{28,24},{1,5},{5... | collective-permute-start | bytes 4718600 | tf_op jit(solution)/shard_map/ppermute | solution.py:307
  831.2 30.0 %collective-permute-start.103 = (bf16[2,256,1152]{2,1,0:T(8,128)(2,1)S(1)}, bf16[2,256,1152]{2,1,0:T(8,128)(2,1)S(1)}, u32[]{:S(2)}, u32[]{:S(2)}) collective-permute-start(bf16[2,256,1152]{2,1,0:T(8,128)(2,1)S(1)} %fusion.18), channel_id=1, source_target_pairs={{0,16},{4,20},{8,24},{12,28},{16,0},{20,4},{24,8},{28,12},{1,17},{... | collective-permute-start | bytes 3538952 | tf_op jit(solution)/shard_map/ppermute | solution.py:307
  832.4 27.1 %collective-permute-start.98 = (bf16[256,2048]{1,0:T(8,128)(2,1)}, bf16[256,2048]{1,0:T(8,128)(2,1)}, u32[]{:S(2)}, u32[]{:S(2)}) collective-permute-start(bf16[256,2048]{1,0:T(8,128)(2,1)} %convolution_convert_fusion.5), channel_id=1, source_target_pairs={{0,1},{1,2},{2,3},{3,0},{4,5},{5,6},{6,7},{7,4},{8,9},{9,10},{10,1... | collective-permute-start | bytes 3145736 | tf_op jit(solution)/shard_map/ppermute | solution.py:302
  833.0 27.2 %collective-permute-start.102 = (bf16[2,256,1024]{2,1,0:T(8,128)(2,1)S(1)}, bf16[2,256,1024]{2,1,0:T(8,128)(2,1)}, u32[]{:S(2)}, u32[]{:S(2)}) collective-permute-start(bf16[2,256,1024]{2,1,0:T(8,128)(2,1)S(1)} %fusion.20), channel_id=1, source_target_pairs={{0,8},{4,12},{8,0},{12,4},{16,24},{20,28},{24,16},{28,20},{1,9},{5... | collective-permute-start | bytes 3145736 | tf_op jit(solution)/shard_map/ppermute | solution.py:307
  862.8 39.0 %collective-permute-start.106 = (bf16[256,2048]{1,0:T(8,128)(2,1)S(1)}, bf16[256,2048]{1,0:T(8,128)(2,1)S(1)}, u32[]{:S(2)}, u32[]{:S(2)}) collective-permute-start(bf16[256,2048]{1,0:T(8,128)(2,1)S(1)} %add_convert_fusion.1), channel_id=1, source_target_pairs={{0,1},{1,2},{2,3},{3,0},{4,5},{5,6},{6,7},{7,4},{8,9},{9,10},{10,1... | collective-permute-start | bytes 3145736 | tf_op jit(solution)/shard_map/ppermute | solution.py:302
  863.3 38.5 %collective-permute-start.107 = (bf16[2,256,768]{2,1,0:T(8,128)(2,1)S(1)}, bf16[2,256,768]{2,1,0:T(8,128)(2,1)S(1)}, u32[]{:S(2)}, u32[]{:S(2)}) collective-permute-start(bf16[2,256,768]{2,1,0:T(8,128)(2,1)S(1)} %fusion.25), channel_id=1, source_target_pairs={{0,8},{4,12},{8,0},{12,4},{16,24},{20,28},{24,16},{28,20},{1,9},{5... | collective-permute-start | bytes 2359304 | tf_op jit(solution)/shard_map/ppermute | solution.py:307
  865.3 36.5 %collective-permute-start.108 = (bf16[2,256,768]{2,1,0:T(8,128)(2,1)S(1)}, bf16[2,256,768]{2,1,0:T(8,128)(2,1)S(1)}, u32[]{:S(2)}, u32[]{:S(2)}) collective-permute-start(bf16[2,256,768]{2,1,0:T(8,128)(2,1)S(1)} %fusion.26), channel_id=1, source_target_pairs={{0,16},{4,20},{8,24},{12,28},{16,0},{20,4},{24,8},{28,12},{1,17},{... | collective-permute-start | bytes 2359304 | tf_op jit(solution)/shard_map/ppermute | solution.py:307
  874.5 27.3 %collective-permute-start.110 = (bf16[256,1152]{1,0:T(8,128)(2,1)S(1)}, bf16[256,1152]{1,0:T(8,128)(2,1)S(1)}, u32[]{:S(2)}, u32[]{:S(2)}) collective-permute-start(bf16[256,1152]{1,0:T(8,128)(2,1)S(1)} %fusion.27), channel_id=1, source_target_pairs={{0,8},{4,12},{8,0},{12,4},{16,24},{20,28},{24,16},{28,20},{1,9},{5... | collective-permute-start | bytes 1769480 | tf_op jit(solution)/shard_map/ppermute | solution.py:307
  875.2 25.6 %collective-permute-start.109 = (bf16[256,1024]{1,0:T(8,128)(2,1)S(1)}, bf16[256,1024]{1,0:T(8,128)(2,1)S(1)}, u32[]{:S(2)}, u32[]{:S(2)}) collective-permute-start(bf16[256,1024]{1,0:T(8,128)(2,1)S(1)} %fusion.32), channel_id=1, source_target_pairs={{0,16},{4,20},{8,24},{12,28},{16,0},{20,4},{24,8},{28,12},{1,17},{... | collective-permute-start | bytes 1572872 | tf_op jit(solution)/shard_map/ppermute | solution.py:307
  903.1 25.1 %collective-permute-start.111 = (bf16[256,2048]{1,0:T(8,128)(2,1)}, bf16[256,2048]{1,0:T(8,128)(2,1)}, u32[]{:S(2)}, u32[]{:S(2)}) collective-permute-start(bf16[256,2048]{1,0:T(8,128)(2,1)} %add_convert_fusion), channel_id=1, source_target_pairs={{0,1},{1,2},{2,3},{3,0},{4,5},{5,6},{6,7},{7,4},{8,9},{9,10},{10,1... | collective-permute-start | bytes 3145736 | tf_op jit(solution)/shard_map/ppermute | solution.py:302
  938.8 34.0 %collective-permute-start.118 = (bf16[64,2176]{1,0:T(8,128)(2,1)S(1)}, bf16[64,2176]{1,0:T(8,128)(2,1)S(1)}, u32[]{:S(2)}, u32[]{:S(2)}) collective-permute-start(bf16[64,2176]{1,0:T(8,128)(2,1)S(1)} %get-tuple-element.417), channel_id=1, source_target_pairs={{0,2},{1,3},{2,0},{3,1},{4,6},{5,7},{6,4},{7,5},{8,10},{9,11},{10,... | collective-permute-start | bytes 835592 | tf_op jit(solution)/shard_map/ppermute | solution.py:324
  939.2 33.6 %collective-permute-start.117 = (bf16[64,2176]{1,0:T(8,128)(2,1)S(1)}, bf16[64,2176]{1,0:T(8,128)(2,1)S(1)}, u32[]{:S(2)}, u32[]{:S(2)}) collective-permute-start(bf16[64,2176]{1,0:T(8,128)(2,1)S(1)} %get-tuple-element.416), channel_id=1, source_target_pairs={{0,1},{1,2},{2,3},{3,0},{4,5},{5,6},{6,7},{7,4},{8,9},{9,10},{10,1... | collective-permute-start | bytes 835592 | tf_op jit(solution)/shard_map/ppermute | solution.py:324
  (239 other events, 2375.4 us)

commit v5 on v4

--- a/solution.py
+++ b/solution.py
@@ -125,6 +125,83 @@
         out_shape=[shape] * 3,
         compiler_params=kernel_params(),
     )(raw, squares, cosine, sine_tab, gains)
+
+
+def ffn_backward_body(steps, left_ref, down_w, gate_ref, up_ref, gate_w, up_w, d_gate_ref, d_up_ref, share_ref):
+    step = pl.program_id(0)
+    d_inner = contract(left_ref[...], down_w[...], 1, 1)
+    gate = gate_ref[...]
+    sigmoid = jax.nn.sigmoid(gate)
+    d_gate = (d_inner * up_ref[...] * sigmoid * (1.0 + gate * (1.0 - sigmoid))).astype(bf16)
+    d_up = (d_inner * (gate * sigmoid)).astype(bf16)
+    d_gate_ref[...] = d_gate
+    d_up_ref[...] = d_up
+    share = contract(d_gate, gate_w[...], 1, 1) + contract(d_up, up_w[...], 1, 1)
+
+    @pl.when(step == 0)
+    def _():
+        share_ref[...] = share
+
+    if steps > 1:
+
+        @pl.when(step > 0)
+        def _():
+            share_ref[...] += share
+
+
+def ffn_backward(left, gate, up, w_down, w_gate, w_up):
+    rows, width = left.shape
+    extent = gate.shape[1]
+    tile = min(512, extent)
+    by_columns = vmem((rows, tile), lambda at: (0, at))
+    return pl.pallas_call(
+        functools.partial(ffn_backward_body, extent // tile),
+        grid=(extent // tile,),
+        in_specs=[
+            vmem(left.shape),
+            vmem((tile, width), lambda at: (at, 0)),
+            by_columns,
+            by_columns,
+            vmem((width, tile), lambda at: (0, at)),
+            vmem((width, tile), lambda at: (0, at)),
+        ],
+        out_specs=[by_columns, by_columns, vmem(left.shape)],
+        out_shape=[
+            jax.ShapeDtypeStruct(gate.shape, bf16),
+            jax.ShapeDtypeStruct(gate.shape, bf16),
+            jax.ShapeDtypeStruct(left.shape, f32),
+        ],
+        compiler_params=kernel_params(),
+        cost_estimate=pl.CostEstimate(
+            flops=6 * rows * width * extent, bytes_accessed=6 * width * extent, transcendentals=rows * extent
+        ),
+    )(left, w_down, gate, up, w_gate, w_up)
+
+
+def grad_halves_body(left_ref, right_ref, one_ref, two_ref):
+    total = contract(left_ref[...], right_ref[...], 0, 0).astype(bf16)
+    cut = one_ref.shape[1]
+    one_ref[...] = total[:, :cut]
+    two_ref[...] = total[:, cut:]
+
+
+def grad_halves(left, right, core):
+    bits = (lax.axis_size("dp") - 1).bit_length() - (not core)
+    (tokens, depth), cut = left.shape, right.shape[1] // 2
+    block = min(256, depth)
+    half = jax.ShapeDtypeStruct((depth, cut), bf16)
+    halves = pl.pallas_call(
+        grad_halves_body,
+        grid=(depth // block,),
+        in_specs=[vmem((tokens, block), lambda at: (0, at)), vmem(right.shape)],
+        out_specs=[vmem((block, cut), lambda at: (at, 0))] * 2,
+        out_shape=[half, half],
+        compiler_params=kernel_params(),
+        cost_estimate=pl.CostEstimate(
+            flops=4 * tokens * depth * cut, bytes_accessed=4 * tokens * depth, transcendentals=0
+        ),
+    )(left, right)
+    return [half.reshape((2,) * bits + (-1, cut)) for half in halves]
 
 
 def key_weights(query, key, seg_query, seg_key, first, count):
@@ -360,7 +437,7 @@
             write.wait()
 
 
-def assemble(pieces, parts, places, cuts=None):
+def assemble(pieces, parts, places, cuts=None, room=0):
     shape = (sum(rows for _, _, rows in parts), pieces[0].shape[1])
     several, cuts = cuts is not None, cuts or [(0, shape[1])]
     anywhere = pl.BlockSpec(memory_space=pl.ANY)
@@ -376,16 +453,16 @@
             pltpu.SemaphoreType.DMA((len(parts),)),
             pltpu.SemaphoreType.DMA((len(parts) * len(cuts),)),
         ],
-        compiler_params=pltpu.CompilerParams(vmem_limit_bytes=size + 2**20),
+        compiler_params=pltpu.CompilerParams(vmem_limit_bytes=max(room, size + 2**20)),
         cost_estimate=pl.CostEstimate(flops=0, bytes_accessed=2 * size, transcendentals=0),
     )(*pieces)
     return results if several else results[0]
 
 
-def stacked(pieces, parts=None):
-    parts = parts or [(at, 0, p.shape[0]) for at, p in enumerate(pieces)]
+def stacked(pieces, room=0):
+    parts = [(at, 0, p.shape[0]) for at, p in enumerate(pieces)]
     places = [sum(rows for _, _, rows in parts[:at]) for at in range(len(parts))]
-    return assemble(pieces, parts, lambda: places)
+    return assemble(pieces, parts, lambda: places, room=room)
 
 
 def in_order(slots, axis, first=0, rows=None):
@@ -460,32 +537,27 @@
         self.got = None
         return self.totals
 
-    def step(self):
+    def prepare(self):
         self.add()
-        got = []
-        for which, total in enumerate(self.totals):
-            bit = self.orders[which].pop(0)
+        self.away, self.bits = [], [order.pop(0) for order in self.orders]
+        for which, (total, bit) in enumerate(zip(self.totals, self.bits)):
             at = self.dims[which].index(bit)
             self.dims[which].remove(bit)
             mine = (lax.axis_index("dp") // bit) % 2
-            away = lax.dynamic_index_in_dim(total, 1 - mine, at, keepdims=False).astype(bf16)
-            got.append(flipped(away, bit))
+            self.away.append(lax.dynamic_index_in_dim(total, 1 - mine, at, keepdims=False).astype(bf16))
             self.totals[which] = lax.dynamic_index_in_dim(total, mine, at, keepdims=False)
-        self.got = got
+
+    def send(self):
+        self.got = [flipped(away, bit) for away, bit in zip(self.away, self.bits)]
+
+    def step(self):
+        self.prepare()
+        self.send()
 
     def finish(self):
         while self.orders[0]:
             self.step()
         return jnp.concatenate(self.add(), 1)
-
-
-def column_halves(grad, core, more=None):
-    bits = (lax.axis_size("dp") - 1).bit_length() - (not core)
-    cut = grad.shape[1] // 2
-    halves = [grad[:, :cut], grad[:, cut:]]
-    if more is not None:
-        halves[1] = jnp.concatenate([halves[1], more], 1)
-    return [half.reshape((2,) * bits + (-1, half.shape[1])) for half in halves]
 
 
 def small_sum(values, axis):
@@ -696,25 +768,24 @@
     a_scale = rms_scale(a_proj)
     hidden = tok_rows.astype(f32) + a_proj * a_scale * gain_attn
 
-    def ring(block, work, last=lambda: (), beside=lambda early: ()):
+    def ring(block, work, beside=lambda: ()):
         got, own = None, None
         for at in range(size):
             later = next_one(block, "seq") if at < size - 1 else None
             share = work(stacked([block, flipped(block, 1)]))
-            if later is None:
-                share, early = together(share, last())
             share, away = share[:rows], share[rows:].astype(bf16)
             if later is not None:
-                later, share, away = together(later, share, away)
+                later, share, away, got = together(later, share, away, got)
             share = share + flipped(away, 1).astype(f32)
             if at == 0:
                 own = share
             else:
                 if at > 1:
                     share = share + got.astype(f32)
-                got = next_one(share.astype(bf16), "seq")
+                send, later = together(share.astype(bf16), later)
+                got = next_one(send, "seq")
             block = later
-        got, extra = together(got, beside(early))
+        got, extra = together(got, beside(send))
         return own + got.astype(f32), extra
 
     h_slots, gates, ups, inners = [], [], [], []
@@ -729,7 +800,7 @@
         inners.append(inner)
         return product(inner, w_down_part)
 
-    m_proj, _ = ring(hidden.astype(bf16), forward)
+    m_proj, _ = ring(hidden.astype(bf16), forward, lambda send: ())
     m_scale = rms_scale(m_proj)
     out = (hidden + m_proj * m_scale * gain_ffn).astype(bf16).reshape(tokens.shape)
     grad_out = d_out.reshape(rows, width).astype(f32)
@@ -740,6 +811,12 @@
     def backward(dm_slot):
         at = len(dms)
         gate, up = gates[at], ups[at]
+        if at == size - 1:
+            d_gate, d_up, share = ffn_backward(dm_slot, gate, up, w_down_part, w_gate_part, w_up_part)
+            dms.append(dm_slot)
+            d_gates.append(d_gate)
+            d_ups.append(d_up)
+            return share
         d_inner = against(dm_slot, w_down_part)
         sigmoid_gate = jax.nn.sigmoid(gate)
         d_gate = (d_inner * up * sigmoid_gate * (1.0 + gate * (1.0 - sigmoid_gate))).astype(bf16)
@@ -749,20 +826,14 @@
         d_ups.append(d_up)
         return against(d_gate, w_gate_part) + against(d_up, w_up_part)
 
-    def down_grad():
-        return weight_grad(stacked(inners), stacked(dms)).astype(bf16)
-
-    def grads(d_down):
-        for grad in (d_down, weight_grad(h_alls[0], stacked(d_gates)).astype(bf16)):
-            cubes.append(CubeScatter(column_halves(grad, False)))
-            cubes[-1].step()
-        d_up = weight_grad(h_alls[0], stacked(d_ups)).astype(bf16)
-        return d_up, [cube.got for cube in cubes]
-
-    h_alls, cubes = [stacked(h_slots)], []
-    d_sum, (d_up, gots) = ring(dm_low, backward, down_grad, grads)
-    cube_down, cube_gate = cubes
-    cube_down.got, cube_gate.got = gots
+    def grads(send):
+        _, all_gates = together(send, stacked(d_gates, 56 * 2**20))
+        return grad_halves(h_all, all_gates, False)
+
+    h_all = stacked(h_slots, 56 * 2**20)
+    d_sum, d_gate = ring(dm_low, backward, grads)
+    cube_gate = CubeScatter(d_gate)
+    cube_gate.step()
 
     def ff_rows(total):
         core = lax.rem(lax.axis_index("dp"), 2)
@@ -791,7 +862,6 @@
             ],
         )
 
-    cube_gate.step()
     d_hidden = grad_out + d_sum
     d_gain_attn = jnp.sum(d_hidden * a_proj * a_scale, 0)
     da_low = norm_back(a_proj, a_scale, d_hidden * gain_attn).astype(bf16)
@@ -802,58 +872,74 @@
         bf16,
         lambda: [((0, 0, part_column(behind(ahead))), (ahead, 0, 0), (rows, part)) for ahead in slots],
     )
-    d_attended, cube_gate.got, d_up = together(d_attended, cube_gate.got, d_up)
+    all_ups = stacked(d_ups, 56 * 2**20)
+    d_attended, cube_gate.got, da_low, all_ups = together(d_attended, cube_gate.got, da_low, all_ups)
     d_attended = send_ahead(d_attended, "seq")
-    cube_up = CubeScatter(column_halves(d_up, False))
+    cube_gate.step()
+    d_up = grad_halves(h_all, all_ups, False)
+    d_w_out = grad_halves(attended, da_low, True)
+    d_attended, d_w_out, cube_gate.got, d_up = together(d_attended, d_w_out, cube_gate.got, d_up)
+    d_attended = in_order(d_attended, "seq")
+
+    cube_up = CubeScatter(d_up)
     cube_up.step()
-    d_w_out = weight_grad(attended, da_low).astype(bf16)
-    gate_send = ff_rows(cube_gate.finish())
-    d_attended, cube_up.got, d_w_out, gate_send = together(d_attended, cube_up.got, d_w_out, gate_send)
-    d_attended = in_order(d_attended, "seq")
-
-    gate_got = send_ahead(gate_send, "seq")
+    gate_got = send_ahead(ff_rows(cube_gate.finish()), "seq")
+    d_query, d_key, d_value = attend_back(query, key, value, d_attended, seg_ids)
+    d_query, gate_got, cube_up.got, d_w_out = together(d_query, gate_got, cube_up.got, d_w_out)
     cube_up.step()
-    d_query, d_key, d_value = attend_back(query, key, value, d_attended, seg_ids)
-    d_query, gate_got, cube_up.got = together(d_query, gate_got, cube_up.got)
-    up_send = ff_rows(cube_up.finish())
     dots, d_gain_qk = unrope(d_query, d_key, qkv, squares, cosine, sine_tab, gain_qk, width)
     dots = small_sum(dots.T, "seq")
-    d_gain_qk = lax.dynamic_update_slice_in_dim(jnp.zeros((2, width), f32), d_gain_qk, here * part, 1)
-    d_gains = jnp.concatenate([d_gain_qk, d_gain_attn[None], d_gain_ffn[None]], 0).T.astype(bf16)
-    d_gains = jnp.pad(d_gains, ((0, 0), (0, lanes - d_gains.shape[1])))
-    cube_out = CubeScatter(column_halves(d_w_out, True, d_gains), core=True)
+    dots, cube_up.got, d_w_out = together(dots, cube_up.got, d_w_out)
+    up_send = ff_rows(cube_up.finish())
+    up_got = send_ahead(up_send, "seq")
+    cube_out = CubeScatter(d_w_out, core=True)
     cube_out.step()
     d_qkv = raw_grad(d_query, d_key, d_value, qkv, squares, dots.T, cosine, sine_tab, gain_qk, width)
-    d_qkv, up_send, cube_out.got = together(d_qkv, up_send, cube_out.got)
     d_slots = relayout(
         [d_qkv],
         [(rows, 3 * part)] * size,
         bf16,
         lambda: [((0, part_row(before(back)), 0), (back, 0, 0), (rows, 3 * part)) for back in slots],
     )
-    got = next_one(against(d_slots[1], w_qkv).astype(bf16), "seq")
-    up_got = send_ahead(up_send, "seq")
-    cube_out.step()
-    cube_qkv = CubeScatter(column_halves(weight_grad(x_all, d_qkv).astype(bf16), True), core=True)
-    cube_qkv.step()
-    shares = [against(d_slots[back], w_qkv) for back in [*slots[2:], 0]]
-    got, up_got, cube_out.got, cube_qkv.got, shares = together(got, up_got, cube_out.got, cube_qkv.got, shares)
+    d_slots, cube_out.got = together(d_slots, cube_out.got)
+    cube_out.prepare()
+    first, d_qkv, d_slots, d_gain_qk, up_got, cube_out.away, dms, d_gain_attn = together(
+        against(d_slots[1], w_qkv).astype(bf16), d_qkv, d_slots, d_gain_qk, up_got, cube_out.away, dms, d_gain_attn
+    )
+    got = next_one(first, "seq")
+    cube_out.send()
+    d_gain_qk = lax.dynamic_update_slice_in_dim(jnp.zeros((2, width), f32), d_gain_qk, here * part, 1)
+    d_gains = jnp.concatenate([d_gain_qk, d_gain_attn[None], d_gain_ffn[None]], 0)
+    d_w_qkv = grad_halves(x_all, d_qkv, True)
+    shares = [against(d_slots[2], w_qkv)]
+    got, d_w_qkv, shares, cube_out.got, d_slots, dms, d_gains = together(
+        got, d_w_qkv, shares, cube_out.got, d_slots, dms, d_gains
+    )
+    cube_qkv = CubeScatter(d_w_qkv, core=True)
     for back in range(2, size):
         got = next_one((shares[back - 2] + got.astype(f32)).astype(bf16), "seq")
         if back == 2:
             cube_qkv.step()
             cube_out.step()
-            got, cube_qkv.got, cube_out.got = together(got, cube_qkv.got, cube_out.got)
+            shares += [against(d_slots[at], w_qkv) for at in [*slots[3:], 0]]
+            got, shares, cube_out.got, cube_qkv.got, dms = together(got, shares, cube_out.got, cube_qkv.got, dms)
         elif back == 3:
             cube_qkv.step()
-            out_send = row_blocks(cube_out.finish())
-            got, cube_qkv.got, out_send = together(got, cube_qkv.got, out_send)
-    out_got = send_ahead(out_send, "seq")
-    d_w_qkv = send_ahead(row_blocks(cube_qkv.finish()), "seq")
+            out_got = send_ahead(row_blocks(cube_out.finish()), "seq")
+            d_down = grad_halves(stacked(inners, 56 * 2**20), stacked(dms, 56 * 2**20), False)
+            got, cube_qkv.got, d_down = together(got, cube_qkv.got, d_down)
+            cube_down = CubeScatter(d_down)
+            cube_down.step()
+    d_w_qkv = row_blocks(cube_qkv.finish())
+    d_w_qkv, out_got, cube_down.got, d_gains = together(d_w_qkv, out_got, cube_down.got, d_gains)
+    d_w_qkv = send_ahead(d_w_qkv, "seq")
     d_down = cube_down.finish()
+    d_gains = small_sum(d_gains, "seq")
+    for bit in [1] + cube_bits()[0]:
+        d_gains = d_gains + flipped(d_gains.reshape(-1), bit).reshape(d_gains.shape)
+    d_gains = lax.dynamic_slice_in_dim(d_gains, (lax.axis_index("dp") * size + here) * own_rows, own_rows, 1)
     d_tokens = d_hidden + shares[-1] + got.astype(f32)
-    out_sum = sum(g.astype(f32) for g in out_got)
-    d_w_out, d_gains = out_sum[:, :width], out_sum[:, width : width + 4].T
+    d_w_out = sum(g.astype(f32) for g in out_got)
     d_w_qkv = relayout(
         d_w_qkv,
         [(own_rows, width)] * 3,

time: 982 us -> 952 us (0.969)
  Pallas kernels: 109 us -> 195 us
  matrix products: 139 us -> 79.6 us
  local copies, waits for them, and re-layouts: 111 us -> 62.4 us
  waiting for transfers between devices: 421 us -> 408 us
    pallas_call x0 -> x6, Pallas kernels: none -> 71 us  [the longest x5 56.5 us: grad_halves(): pl.pallas_call(grad_halves_body, grid=(depth // block,), in_specs=[vmem((...]
    dot_general x5 -> x0, matrix products: 47.9 us -> none  [weight_grad(): lax.dot_general(left, right, (((0,), (0,)), ((), ())), preferred_element_...]
    unnamed x352 -> x267, local copies, waits for them, and re-layouts: 62.2 us -> 36.5 us
    pallas_call x40, Pallas kernels: 46.9 us -> 64.8 us  [assemble(): pl.pallas_call(functools.partial(assemble_body, parts, places, len(pieces...]
    dot_general x17 -> x14, matrix products: 50.6 us -> 36.4 us  [against(): lax.dot_general(left, right, (((1,), (1,)), ((), ())), preferred_element_...]
    ppermute x27, waiting for transfers between devices: 79 us -> 65.6 us  [send_ahead(): lax.ppermute(blocks[step], axis, [(i, (i + step) % size) for i in range(s...]
    slice x7 -> x0, local copies, waits for them, and re-layouts: 11.4 us -> none  [the longest x5 9.81 us: column_halves(): halves = [grad[:, :cut], grad[:, cut:]]]
    ppermute x27, starting transfers between devices: 62.7 us -> 52.1 us  [send_ahead(): lax.ppermute(blocks[step], axis, [(i, (i + step) % size) for i in range(s...]
  transfers between devices with their start and end apart: 122 -> 128, of which waited for: 56 -> 64; matrix products, arithmetic and copies ran while one was open for 21% -> 13% of each run, Pallas kernels for 9% -> 20%
where the time goes in v5:
time: 952 us; the launch traced here: 944 us
  waiting for transfers between devices  408 us (43%)
  Pallas kernels  195 us (20%)
  starting transfers between devices  141 us (15%)
  matrix products  79.6 us (8%)
  local copies, waits for them, and re-layouts  62.4 us (7%)
  other arithmetic  54.4 us (6%)
    ppermute x18, waiting for transfers between devices, next_one(): return lax.ppermute(block, axis, [(i, (i + 1) % size) for i in range(size)])  221 us
    ppermute x71, waiting for transfers between devices, flipped(): return lax.ppermute(block, 'dp', [(i, i ^ bit) for i in range(size)])  109 us
    ppermute x27, waiting for transfers between devices, send_ahead(): lax.ppermute(blocks[step], axis, [(i, (i + step) % size) for i in range(s...  65.6 us
    pallas_call x40, Pallas kernels, assemble(): pl.pallas_call(functools.partial(assemble_body, parts, places, len(pieces...  64.8 us
    pallas_call x5, Pallas kernels, grad_halves(): pl.pallas_call(grad_halves_body, grid=(depth // block,), in_specs=[vmem((...  56.5 us
    ppermute x27, starting transfers between devices, send_ahead(): lax.ppermute(blocks[step], axis, [(i, (i + step) % size) for i in range(s...  52.1 us
    ppermute x71, starting transfers between devices, flipped(): return lax.ppermute(block, 'dp', [(i, i ^ bit) for i in range(size)])  48.2 us
    dot_general x14, matrix products, product(): return jnp.dot(left, right, preferred_element_type=f32)  43.2 us
  transfers between devices with their start and end apart: 128, of which 64 were waited for; matrix products, arithmetic and copies ran while one was open for 13% of the time, Pallas kernels for 20%

profile of v5, /device:TPU:0, one launch (start us, length us, event | category | flops | bytes accessed | tf_op | source)
XLA Modules:
  0.0 944.2 jit_solution(8258758298863974135)
XLA Ops:
  14.7 4.2 collective-permute-done.refs_1_
  19.0 7.4 collective-permute-done.1.refs_2_
  30.6 5.0 collective-permute-start.5
  38.0 6.0 collective-permute-done.5.refs_1_
  44.0 8.3 collective-permute-done.6.refs_2_
  57.4 6.1 collective-permute-start.10
  68.0 4.6 collective-permute-done.10.refs_1_
  75.1 6.9 collective-permute-done.11.refs_2_
  83.7 4.5 collective-permute-start.16
  91.6 12.4 %collective-permute-done.17.refs_1_ = bf16[256,1024]{1,0:T(8,128)(2,1)S(1)} collective-permute-done((bf16[256,1024]{1,0:T(8,128)(2,1)S(1)}, bf16[256,1024]{1,0:T(8,128)(2,1)S(1)}, u32[]{:S(2)}, u32[]{:S(2)}) %collective-permute-start.17) | collective-permute-done | bytes 524320 | tf_op jit(solution)/shard_map/ppermute | solution.py:384
  105.7 6.1 collective-permute-done.16.refs_1_
  119.5 8.8 collective-permute-done.20.refs_1_
  134.0 4.0 collective-permute-done.19.refs_2_
  146.7 4.7 shard_map.257
  155.2 13.7 %collective-permute-done.27.refs_1_ = bf16[256,1024]{1,0:T(8,128)(2,1)} collective-permute-done((bf16[256,1024]{1,0:T(8,128)(2,1)S(1)}, bf16[256,1024]{1,0:T(8,128)(2,1)}, u32[]{:S(2)}, u32[]{:S(2)}) %collective-permute-start.27) | collective-permute-done | bytes 524320 | tf_op jit(solution)/shard_map/ppermute | solution.py:384
  174.6 6.6 fusion.46.raw_ref
  197.8 8.8 collective-permute-done.34.refs_2_
  211.5 4.5 shard_map.258
  216.1 13.9 %shard_map.259.refs_0_ = bf16[1024,512]{1,0:T(8,128)(2,1)S(1)} custom-call(bf16[1024,512]{1,0:T(8,128)(2,1)S(1)} %get-tuple-element.339.q_ref, bf16[1024,512]{1,0:T(8,128)(2,1)S(1)} %get-tuple-element.340.k_ref, bf16[1024,512]{1,0:T(8,128)(2,1)S(1)} %get-tuple-element.341.v_ref, s32[1,1024]{1,0:T(1,128)S(1)} %copy-done.64, s32[1024,1]{1,0:T(8,128)S(1)} %copy.67.seg_k_ref), custom_call_target="tpu_custom_call" | custom-call | tf_op jit(solution)/shard_map/pallas_call | solution.py:241
  236.1 5.0 collective-permute-start.40
  244.8 3.9 shard_map.267.gate_w
  253.0 3.6 collective-permute-done.41.refs_2_
  272.7 6.3 collective-permute-start.47
  282.3 3.8 multiply_convert_fusion.9
  290.5 12.8 %collective-permute-done.47.refs_0_ = bf16[256,2048]{1,0:T(8,128)(2,1)S(1)} collective-permute-done((bf16[256,2048]{1,0:T(8,128)(2,1)S(1)}, bf16[256,2048]{1,0:T(8,128)(2,1)S(1)}, u32[]{:S(2)}, u32[]{:S(2)}) %collective-permute-start.47) | collective-permute-done | bytes 1048608 | tf_op jit(solution)/shard_map/ppermute | solution.py:379
  308.8 3.8 multiply_convert_fusion.8
  315.3 15.6 %collective-permute-done.50.refs_0_ = bf16[256,2048]{1,0:T(8,128)(2,1)S(1)} collective-permute-done((bf16[256,2048]{1,0:T(8,128)(2,1)S(1)}, bf16[256,2048]{1,0:T(8,128)(2,1)S(1)}, u32[]{:S(2)}, u32[]{:S(2)}) %collective-permute-start.50) | collective-permute-done | bytes 1048608 | tf_op jit(solution)/shard_map/ppermute | solution.py:379
  339.4 3.8 multiply_convert_fusion.7
  345.9 16.0 %collective-permute-done.53.refs_0_ = bf16[256,2048]{1,0:T(8,128)(2,1)S(1)} collective-permute-done((bf16[256,2048]{1,0:T(8,128)(2,1)S(1)}, bf16[256,2048]{1,0:T(8,128)(2,1)S(1)}, u32[]{:S(2)}, u32[]{:S(2)}) %collective-permute-start.53) | collective-permute-done | bytes 1048608 | tf_op jit(solution)/shard_map/ppermute | solution.py:379
  361.9 21.9 %collective-permute-done.55 = bf16[256,2048]{1,0:T(8,128)(2,1)S(1)} collective-permute-done((bf16[256,2048]{1,0:T(8,128)(2,1)S(1)}, bf16[256,2048]{1,0:T(8,128)(2,1)S(1)}, u32[]{:S(2)}, u32[]{:S(2)}) %collective-permute-start.55) | collective-permute-done | bytes 1048608 | tf_op jit(solution)/shard_map/ppermute | solution.py:379
  392.5 3.8 multiply_convert_fusion.6
  399.0 15.7 %collective-permute-done.59 = bf16[256,2048]{1,0:T(8,128)(2,1)S(1)} collective-permute-done((bf16[256,2048]{1,0:T(8,128)(2,1)S(1)}, bf16[256,2048]{1,0:T(8,128)(2,1)S(1)}, u32[]{:S(2)}, u32[]{:S(2)}) %collective-permute-start.59) | collective-permute-done | bytes 1048608 | tf_op jit(solution)/shard_map/ppermute | solution.py:379
  415.4 26.3 %collective-permute-done.60 = bf16[256,2048]{1,0:T(8,128)(2,1)S(1)} collective-permute-done((bf16[256,2048]{1,0:T(8,128)(2,1)S(1)}, bf16[256,2048]{1,0:T(8,128)(2,1)S(1)}, u32[]{:S(2)}, u32[]{:S(2)}) %collective-permute-start.60) | collective-permute-done | bytes 1048608 | tf_op jit(solution)/shard_map/ppermute | solution.py:379
  458.1 13.8 %collective-permute-done.61.refs_0_ = bf16[256,2048]{1,0:T(8,128)(2,1)S(1)} collective-permute-done((bf16[256,2048]{1,0:T(8,128)(2,1)S(1)}, bf16[256,2048]{1,0:T(8,128)(2,1)S(1)}, u32[]{:S(2)}, u32[]{:S(2)}) %collective-permute-start.61) | collective-permute-done | bytes 1048608 | tf_op jit(solution)/shard_map/ppermute | solution.py:379
  483.1 16.7 %collective-permute-done.64.refs_0_ = bf16[256,2048]{1,0:T(8,128)(2,1)S(1)} collective-permute-done((bf16[256,2048]{1,0:T(8,128)(2,1)S(1)}, bf16[256,2048]{1,0:T(8,128)(2,1)S(1)}, u32[]{:S(2)}, u32[]{:S(2)}) %collective-permute-start.64) | collective-permute-done | bytes 1048608 | tf_op jit(solution)/shard_map/ppermute | solution.py:379
  514.0 16.7 %collective-permute-done.67.refs_0_ = bf16[256,2048]{1,0:T(8,128)(2,1)S(1)} collective-permute-done((bf16[256,2048]{1,0:T(8,128)(2,1)S(1)}, bf16[256,2048]{1,0:T(8,128)(2,1)S(1)}, u32[]{:S(2)}, u32[]{:S(2)}) %collective-permute-start.67) | collective-permute-done | bytes 1048608 | tf_op jit(solution)/shard_map/ppermute | solution.py:379
  530.8 21.9 %collective-permute-done.69 = bf16[256,2048]{1,0:T(8,128)(2,1)S(1)} collective-permute-done((bf16[256,2048]{1,0:T(8,128)(2,1)S(1)}, bf16[256,2048]{1,0:T(8,128)(2,1)S(1)}, u32[]{:S(2)}, u32[]{:S(2)}) %collective-permute-start.69) | collective-permute-done | bytes 1048608 | tf_op jit(solution)/shard_map/ppermute | solution.py:379
  559.0 14.5 %shard_map.281 = (bf16[512,1024]{1,0:T(8,128)(2,1)S(1)}, bf16[512,1024]{1,0:T(8,128)(2,1)S(1)}, f32[512,2048]{1,0:T(8,128)}) custom-call(bf16[512,2048]{1,0:T(8,128)(2,1)S(1)} %shard_map.280.left_ref.refs_3_, bf16[1024,2048]{1,0:T(8,128)(2,1)} %copy-done.16, f32[512,1024]{1,0:T(8,128)} %copy-done.124, f32[512,1024]{1,0:T(8,128)} %get-tuple-element.593.up_ref, ...), custom_call_target="tpu_custom_call" | custom-call | flops 6442450944 | bytes 12582912 | tf_op jit(solution)/shard_map/pallas_call | solution.py:157
  576.2 7.2 collective-permute-done.73
  585.8 6.9 shard_map.282.left_ref
  592.8 3.3 shard_map.286.right_ref
  599.4 13.0 %shard_map.284 = (bf16[2048,512]{1,0:T(8,128)(2,1)S(1)}, bf16[2048,512]{1,0:T(8,128)(2,1)S(1)}) custom-call(bf16[2048,2048]{1,0:T(8,128)(2,1)} %shard_map.282.left_ref, bf16[2048,1024]{1,0:T(8,128)(2,1)} %shard_map.283.right_ref), custom_call_target="tpu_custom_call" | custom-call | flops 8589934592 | bytes 16777216 | tf_op jit(solution)/shard_map/pallas_call | solution.py:193
  625.5 13.9 %collective-permute-done.75 = bf16[2,512,512]{2,1,0:T(8,128)(2,1)S(1)} collective-permute-done((bf16[2,512,512]{2,1,0:T(8,128)(2,1)}, bf16[2,512,512]{2,1,0:T(8,128)(2,1)S(1)}, u32[]{:S(2)}, u32[]{:S(2)}) %collective-permute-start.75) | collective-permute-done | bytes 1048608 | tf_op jit(solution)/shard_map/ppermute | solution.py:384
  647.8 4.3 collective-permute-start.78
  652.1 12.9 %shard_map.288 = (bf16[2048,512]{1,0:T(8,128)(2,1)S(1)}, bf16[2048,512]{1,0:T(8,128)(2,1)S(1)}) custom-call(bf16[2048,2048]{1,0:T(8,128)(2,1)} %shard_map.282.left_ref, bf16[2048,1024]{1,0:T(8,128)(2,1)} %shard_map.286.right_ref), custom_call_target="tpu_custom_call" | custom-call | flops 8589934592 | bytes 16777216 | tf_op jit(solution)/shard_map/pallas_call | solution.py:193
  664.9 5.8 shard_map.287
  677.4 3.5 collective-permute-start.83
  684.9 20.1 %shard_map.290 = (bf16[1024,512]{1,0:T(8,128)(2,1)S(1)}, bf16[1024,512]{1,0:T(8,128)(2,1)S(1)}, bf16[1024,512]{1,0:T(8,128)(2,1)S(1)}) custom-call(bf16[1024,512]{1,0:T(8,128)(2,1)S(1)} %copy-done.23, bf16[1024,512]{1,0:T(8,128)(2,1)S(1)} %copy-done.25, bf16[1024,512]{1,0:T(8,128)(2,1)} %copy-done.26, bf16[1024,512]{1,0:T(8,128)(2,1)} %copy-done.21, ...), custom_call_target="tpu_custom_call" | custom-call | tf_op jit(solution)/shard_map/pallas_call | solution.py:285
  712.9 6.2 shard_map.292
  735.0 3.3 shard_map.297.left_ref
  742.6 6.1 shard_map.293.refs_0_.right_ref
  756.4 3.3 convert_add_fusion
  759.9 4.3 convert_add_fusion.1
  767.4 6.3 collective-permute-done.97.refs_2_
  775.0 6.1 collective-permute-start.99
  784.5 11.5 %shard_map.296 = (bf16[2048,768]{1,0:T(8,128)(2,1)S(1)}, bf16[2048,768]{1,0:T(8,128)(2,1)}) custom-call(bf16[1024,2048]{1,0:T(8,128)(2,1)} %copy-done.15, bf16[1024,1536]{1,0:T(8,128)(2,1)} %shard_map.293.refs_0_.right_ref), custom_call_target="tpu_custom_call" | custom-call | flops 6442450944 | bytes 8388608 | tf_op jit(solution)/shard_map/pallas_call | solution.py:193
  799.0 4.5 collective-permute-done.99
  821.8 17.6 %collective-permute-done.102 = bf16[256,2048]{1,0:T(8,128)(2,1)S(1)} collective-permute-done((bf16[256,2048]{1,0:T(8,128)(2,1)S(1)}, bf16[256,2048]{1,0:T(8,128)(2,1)S(1)}, u32[]{:S(2)}, u32[]{:S(2)}) %collective-permute-start.102) | collective-permute-done | bytes 1048608 | tf_op jit(solution)/shard_map/ppermute | solution.py:379
  849.2 7.0 shard_map.298.right_ref
  856.2 13.3 %shard_map.299 = (bf16[1024,1024]{1,0:T(8,128)(2,1)S(1)}, bf16[1024,1024]{1,0:T(8,128)(2,1)S(1)}) custom-call(bf16[2048,1024]{1,0:T(8,128)(2,1)} %shard_map.297.left_ref, bf16[2048,2048]{1,0:T(8,128)(2,1)} %shard_map.298.right_ref), custom_call_target="tpu_custom_call" | custom-call | flops 8589934592 | bytes 8388608 | tf_op jit(solution)/shard_map/pallas_call | solution.py:193
  869.4 3.8 collective-permute-done.107
  891.6 7.5 collective-permute-done.113
  899.3 11.3 %collective-permute-done.115 = bf16[2,256,1024]{2,1,0:T(8,128)(2,1)S(1)} collective-permute-done((bf16[2,256,1024]{2,1,0:T(8,128)(2,1)S(1)}, bf16[2,256,1024]{2,1,0:T(8,128)(2,1)S(1)}, u32[]{:S(2)}, u32[]{:S(2)}) %collective-permute-start.115) | collective-permute-done | bytes 1048608 | tf_op jit(solution)/shard_map/ppermute | solution.py:384
  930.8 7.0 collective-permute-done.118.refs_2_
  (680 shorter events, 367.6 us)
Async XLA Ops:
  2.1 24.3 %collective-permute-start.3 = (bf16[128,2048]{1,0:T(8,128)(2,1)S(1)}, bf16[128,2048]{1,0:T(8,128)(2,1)S(1)}, u32[]{:S(2)}, u32[]{:S(2)}) collective-permute-start(bf16[128,2048]{1,0:T(8,128)(2,1)S(1)} %get-tuple-element.569.refs_0_), channel_id=1, source_target_pairs={{0,8},{4,12},{8,0},{12,4},{16,24},{20,28},{24,16},{28,20},{1,9},{5... | collective-permute-start | bytes 1572872 | tf_op jit(solution)/shard_map/ppermute | solution.py:384
  5.1 21.3 %collective-permute-start.4 = (bf16[128,2048]{1,0:T(8,128)(2,1)S(1)}, bf16[128,2048]{1,0:T(8,128)(2,1)S(1)}, u32[]{:S(2)}, u32[]{:S(2)}) collective-permute-start(bf16[128,2048]{1,0:T(8,128)(2,1)S(1)} %get-tuple-element.568.refs_0_), channel_id=1, source_target_pairs={{0,16},{4,20},{8,24},{12,28},{16,0},{20,4},{24,8},{28,12},{1,17},{... | collective-permute-start | bytes 1572872 | tf_op jit(solution)/shard_map/ppermute | solution.py:384
  29.5 22.8 %collective-permute-start.8 = (bf16[128,1664]{1,0:T(8,128)(2,1)S(1)}, bf16[128,1664]{1,0:T(8,128)(2,1)S(1)}, u32[]{:S(2)}, u32[]{:S(2)}) collective-permute-start(bf16[128,1664]{1,0:T(8,128)(2,1)S(1)} %get-tuple-element.571.refs_0_), channel_id=1, source_target_pairs={{0,8},{4,12},{8,0},{12,4},{16,24},{20,28},{24,16},{28,20},{1,9},{5... | collective-permute-start | bytes 1277960 | tf_op jit(solution)/shard_map/ppermute | solution.py:384
  30.1 22.2 %collective-permute-start.9 = (bf16[128,1664]{1,0:T(8,128)(2,1)S(1)}, bf16[128,1664]{1,0:T(8,128)(2,1)S(1)}, u32[]{:S(2)}, u32[]{:S(2)}) collective-permute-start(bf16[128,1664]{1,0:T(8,128)(2,1)S(1)} %get-tuple-element.570.refs_0_), channel_id=1, source_target_pairs={{0,16},{4,20},{8,24},{12,28},{16,0},{20,4},{24,8},{28,12},{1,17},{... | collective-permute-start | bytes 1277960 | tf_op jit(solution)/shard_map/ppermute | solution.py:384
  53.3 30.4 %collective-permute-start.14 = (bf16[256,1664]{1,0:T(8,128)(2,1)S(1)}, bf16[256,1664]{1,0:T(8,128)(2,1)S(1)}, u32[]{:S(2)}, u32[]{:S(2)}) collective-permute-start(bf16[256,1664]{1,0:T(8,128)(2,1)S(1)} %shard_map.245.refs_0_), channel_id=1, source_target_pairs={{0,8},{4,12},{8,0},{12,4},{16,24},{20,28},{24,16},{28,20},{1,9},{5... | collective-permute-start | bytes 2555912 | tf_op jit(solution)/shard_map/ppermute | solution.py:384
  55.8 27.9 %collective-permute-start.13 = (bf16[256,1664]{1,0:T(8,128)(2,1)S(1)}, bf16[256,1664]{1,0:T(8,128)(2,1)S(1)}, u32[]{:S(2)}, u32[]{:S(2)}) collective-permute-start(bf16[256,1664]{1,0:T(8,128)(2,1)S(1)} %shard_map.244.refs_0_), channel_id=1, source_target_pairs={{0,16},{4,20},{8,24},{12,28},{16,0},{20,4},{24,8},{28,12},{1,17},{... | collective-permute-start | bytes 2555912 | tf_op jit(solution)/shard_map/ppermute | solution.py:384
  83.7 28.1 %collective-permute-start.16 = (bf16[256,2048]{1,0:T(8,128)(2,1)S(1)}, bf16[256,2048]{1,0:T(8,128)(2,1)S(1)}, u32[]{:S(2)}, u32[]{:S(2)}) collective-permute-start(bf16[256,2048]{1,0:T(8,128)(2,1)S(1)} %bitcast.246), channel_id=1, source_target_pairs={{0,1},{1,2},{2,3},{3,0},{4,5},{5,6},{6,7},{7,4},{8,9},{9,10},{10,1... | collective-permute-start | bytes 3145736 | tf_op jit(solution)/shard_map/ppermute | solution.py:379
  88.8 42.3 %collective-permute-start.23 = (bf16[512,1664]{1,0:T(8,128)(2,1)S(1)}, bf16[512,1664]{1,0:T(8,128)(2,1)S(1)}, u32[]{:S(2)}, u32[]{:S(2)}) collective-permute-start(bf16[512,1664]{1,0:T(8,128)(2,1)S(1)} %shard_map.251.refs_2_), channel_id=1, source_target_pairs={{0,4},{4,0},{8,12},{12,8},{16,20},{20,16},{24,28},{28,24},{1,5},{5... | collective-permute-start | bytes 5111816 | tf_op jit(solution)/shard_map/ppermute | solution.py:384
  89.5 43.3 %collective-permute-start.22 = (bf16[512,1664]{1,0:T(8,128)(2,1)S(1)}, bf16[512,1664]{1,0:T(8,128)(2,1)S(1)}, u32[]{:S(2)}, u32[]{:S(2)}) collective-permute-start(bf16[512,1664]{1,0:T(8,128)(2,1)S(1)} %shard_map.250.refs_0_), channel_id=1, source_target_pairs={{0,4},{4,0},{8,12},{12,8},{16,20},{20,16},{24,28},{28,24},{1,5},{5... | collective-permute-start | bytes 5111816 | tf_op jit(solution)/shard_map/ppermute | solution.py:384
  104.0 24.3 %collective-permute-start.20 = (bf16[256,2048]{1,0:T(8,128)(2,1)S(1)}, bf16[256,2048]{1,0:T(8,128)(2,1)S(1)}, u32[]{:S(2)}, u32[]{:S(2)}) collective-permute-start(bf16[256,2048]{1,0:T(8,128)(2,1)S(1)} %shard_map.248.refs_0_), channel_id=1, source_target_pairs={{0,16},{4,20},{8,24},{12,28},{16,0},{20,4},{24,8},{28,12},{1,17},{... | collective-permute-start | bytes 3145736 | tf_op jit(solution)/shard_map/ppermute | solution.py:384
  104.5 24.8 %collective-permute-start.21 = (bf16[256,2048]{1,0:T(8,128)(2,1)S(1)}, bf16[256,2048]{1,0:T(8,128)(2,1)S(1)}, u32[]{:S(2)}, u32[]{:S(2)}) collective-permute-start(bf16[256,2048]{1,0:T(8,128)(2,1)S(1)} %shard_map.249.refs_2_), channel_id=1, source_target_pairs={{0,8},{4,12},{8,0},{12,4},{16,24},{20,28},{24,16},{28,20},{1,9},{5... | collective-permute-start | bytes 3145736 | tf_op jit(solution)/shard_map/ppermute | solution.py:384
  111.9 26.2 %collective-permute-start.19 = (bf16[256,2048]{1,0:T(8,128)(2,1)S(1)}, bf16[256,2048]{1,0:T(8,128)(2,1)}, u32[]{:S(2)}, u32[]{:S(2)}) collective-permute-start(bf16[256,2048]{1,0:T(8,128)(2,1)S(1)} %collective-permute-done.16.refs_1_), channel_id=1, source_target_pairs={{0,1},{1,2},{2,3},{3,0},{4,5},{5,6},{6,7},{7,4},{8,9},{9,10},{10,1... | collective-permute-start | bytes 3145736 | tf_op jit(solution)/shard_map/ppermute | solution.py:379
  130.3 38.5 %collective-permute-start.25 = (bf16[512,1024]{1,0:T(8,128)(2,1)}, bf16[512,1024]{1,0:T(8,128)(2,1)}, u32[]{:S(2)}, u32[]{:S(2)}) collective-permute-start(bf16[512,1024]{1,0:T(8,128)(2,1)} %shard_map.252.refs_0_), channel_id=1, source_target_pairs={{0,16},{4,20},{8,24},{12,28},{16,0},{20,4},{24,8},{28,12},{1,17},{... | collective-permute-start | bytes 3145736 | tf_op jit(solution)/shard_map/ppermute | solution.py:384
  132.3 36.6 %collective-permute-start.26 = (bf16[512,1024]{1,0:T(8,128)(2,1)}, bf16[512,1024]{1,0:T(8,128)(2,1)}, u32[]{:S(2)}, u32[]{:S(2)}) collective-permute-start(bf16[512,1024]{1,0:T(8,128)(2,1)} %shard_map.253.refs_2_), channel_id=1, source_target_pairs={{0,8},{4,12},{8,0},{12,4},{16,24},{20,28},{24,16},{28,20},{1,9},{5... | collective-permute-start | bytes 3145736 | tf_op jit(solution)/shard_map/ppermute | solution.py:384
  138.1 30.8 %collective-permute-start.24 = (bf16[256,2048]{1,0:T(8,128)(2,1)}, bf16[256,2048]{1,0:T(8,128)(2,1)}, u32[]{:S(2)}, u32[]{:S(2)}) collective-permute-start(bf16[256,2048]{1,0:T(8,128)(2,1)} %collective-permute-done.19.refs_2_), channel_id=1, source_target_pairs={{0,1},{1,2},{2,3},{3,0},{4,5},{5,6},{6,7},{7,4},{8,9},{9,10},{10,1... | collective-permute-start | bytes 3145736 | tf_op jit(solution)/shard_map/ppermute | solution.py:379
  139.8 29.1 %collective-permute-start.27 = (bf16[256,1024]{1,0:T(8,128)(2,1)S(1)}, bf16[256,1024]{1,0:T(8,128)(2,1)}, u32[]{:S(2)}, u32[]{:S(2)}) collective-permute-start(bf16[256,1024]{1,0:T(8,128)(2,1)S(1)} %shard_map.254.refs_0_), channel_id=1, source_target_pairs={{0,8},{4,12},{8,0},{12,4},{16,24},{20,28},{24,16},{28,20},{1,9},{5... | collective-permute-start | bytes 1572872 | tf_op jit(solution)/shard_map/ppermute | solution.py:384
  140.4 28.5 %collective-permute-start.29 = (bf16[256,1024]{1,0:T(8,128)(2,1)}, bf16[256,1024]{1,0:T(8,128)(2,1)}, u32[]{:S(2)}, u32[]{:S(2)}) collective-permute-start(bf16[256,1024]{1,0:T(8,128)(2,1)} %collective-permute-done.28.refs_0_), channel_id=1, source_target_pairs={{0,16},{4,20},{8,24},{12,28},{16,0},{20,4},{24,8},{28,12},{1,17},{... | collective-permute-start | bytes 1572872 | tf_op jit(solution)/shard_map/ppermute | solution.py:384
  195.5 35.5 %collective-permute-start.39 = (bf16[512,1024]{1,0:T(8,128)(2,1)}, bf16[512,1024]{1,0:T(8,128)(2,1)}, u32[]{:S(2)}, u32[]{:S(2)}) collective-permute-start(bf16[512,1024]{1,0:T(8,128)(2,1)} %shard_map.263.refs_2_), channel_id=1, source_target_pairs={{0,8},{4,12},{8,0},{12,4},{16,24},{20,28},{24,16},{28,20},{1,9},{5... | collective-permute-start | bytes 3145736 | tf_op jit(solution)/shard_map/ppermute | solution.py:384
  196.1 35.0 %collective-permute-start.38 = (bf16[512,1024]{1,0:T(8,128)(2,1)}, bf16[512,1024]{1,0:T(8,128)(2,1)}, u32[]{:S(2)}, u32[]{:S(2)}) collective-permute-start(bf16[512,1024]{1,0:T(8,128)(2,1)} %shard_map.262.refs_0_), channel_id=1, source_target_pairs={{0,16},{4,20},{8,24},{12,28},{16,0},{20,4},{24,8},{28,12},{1,17},{... | collective-permute-start | bytes 3145736 | tf_op jit(solution)/shard_map/ppermute | solution.py:384
  208.8 22.3 %collective-permute-start.36 = (bf16[128,2048]{1,0:T(8,128)(2,1)}, bf16[128,2048]{1,0:T(8,128)(2,1)}, u32[]{:S(2)}, u32[]{:S(2)}) collective-permute-start(bf16[128,2048]{1,0:T(8,128)(2,1)} %get-tuple-element.567.refs_0_), channel_id=1, source_target_pairs={{0,8},{4,12},{8,0},{12,4},{16,24},{20,28},{24,16},{28,20},{1,9},{5... | collective-permute-start | bytes 1572872 | tf_op jit(solution)/shard_map/ppermute | solution.py:384
  209.3 21.8 %collective-permute-start.37 = (bf16[128,2048]{1,0:T(8,128)(2,1)}, bf16[128,2048]{1,0:T(8,128)(2,1)}, u32[]{:S(2)}, u32[]{:S(2)}) collective-permute-start(bf16[128,2048]{1,0:T(8,128)(2,1)} %get-tuple-element.566.refs_0_), channel_id=1, source_target_pairs={{0,16},{4,20},{8,24},{12,28},{16,0},{20,4},{24,8},{28,12},{1,17},{... | collective-permute-start | bytes 1572872 | tf_op jit(solution)/shard_map/ppermute | solution.py:384
  232.6 24.0 %collective-permute-start.44 = (bf16[256,2048]{1,0:T(8,128)(2,1)S(1)}, bf16[256,2048]{1,0:T(8,128)(2,1)S(1)}, u32[]{:S(2)}, u32[]{:S(2)}) collective-permute-start(bf16[256,2048]{1,0:T(8,128)(2,1)S(1)} %shard_map.265.refs_0_), channel_id=1, source_target_pairs={{0,8},{4,12},{8,0},{12,4},{16,24},{20,28},{24,16},{28,20},{1,9},{5... | collective-permute-start | bytes 3145736 | tf_op jit(solution)/shard_map/ppermute | solution.py:384
  235.4 22.7 %collective-permute-start.43 = (bf16[256,2048]{1,0:T(8,128)(2,1)S(1)}, bf16[256,2048]{1,0:T(8,128)(2,1)S(1)}, u32[]{:S(2)}, u32[]{:S(2)}) collective-permute-start(bf16[256,2048]{1,0:T(8,128)(2,1)S(1)} %shard_map.264.refs_0_), channel_id=1, source_target_pairs={{0,16},{4,20},{8,24},{12,28},{16,0},{20,4},{24,8},{28,12},{1,17},{... | collective-permute-start | bytes 3145736 | tf_op jit(solution)/shard_map/ppermute | solution.py:384
  272.7 30.7 %collective-permute-start.47 = (bf16[256,2048]{1,0:T(8,128)(2,1)S(1)}, bf16[256,2048]{1,0:T(8,128)(2,1)S(1)}, u32[]{:S(2)}, u32[]{:S(2)}) collective-permute-start(bf16[256,2048]{1,0:T(8,128)(2,1)S(1)} %fusion.14.refs_0_), channel_id=1, source_target_pairs={{0,1},{1,2},{2,3},{3,0},{4,5},{5,6},{6,7},{7,4},{8,9},{9,10},{10,1... | collective-permute-start | bytes 3145736 | tf_op jit(solution)/shard_map/ppermute | solution.py:379
  303.4 27.5 %collective-permute-start.50 = (bf16[256,2048]{1,0:T(8,128)(2,1)S(1)}, bf16[256,2048]{1,0:T(8,128)(2,1)S(1)}, u32[]{:S(2)}, u32[]{:S(2)}) collective-permute-start(bf16[256,2048]{1,0:T(8,128)(2,1)S(1)} %collective-permute-done.47.refs_0_), channel_id=1, source_target_pairs={{0,1},{1,2},{2,3},{3,0},{4,5},{5,6},{6,7},{7,4},{8,9},{9,10},{10,1... | collective-permute-start | bytes 3145736 | tf_op jit(solution)/shard_map/ppermute | solution.py:379
  334.1 27.8 %collective-permute-start.53 = (bf16[256,2048]{1,0:T(8,128)(2,1)S(1)}, bf16[256,2048]{1,0:T(8,128)(2,1)S(1)}, u32[]{:S(2)}, u32[]{:S(2)}) collective-permute-start(bf16[256,2048]{1,0:T(8,128)(2,1)S(1)} %collective-permute-done.50.refs_0_), channel_id=1, source_target_pairs={{0,1},{1,2},{2,3},{3,0},{4,5},{5,6},{6,7},{7,4},{8,9},{9,10},{10,1... | collective-permute-start | bytes 3145736 | tf_op jit(solution)/shard_map/ppermute | solution.py:379
  334.1 49.7 %collective-permute-start.55 = (bf16[256,2048]{1,0:T(8,128)(2,1)S(1)}, bf16[256,2048]{1,0:T(8,128)(2,1)S(1)}, u32[]{:S(2)}, u32[]{:S(2)}) collective-permute-start(bf16[256,2048]{1,0:T(8,128)(2,1)S(1)} %add_convert_fusion.7), channel_id=1, source_target_pairs={{0,1},{1,2},{2,3},{3,0},{4,5},{5,6},{6,7},{7,4},{8,9},{9,10},{10,1... | collective-permute-start | bytes 3145736 | tf_op jit(solution)/shard_map/ppermute | solution.py:379
  387.2 27.5 %collective-permute-start.59 = (bf16[256,2048]{1,0:T(8,128)(2,1)S(1)}, bf16[256,2048]{1,0:T(8,128)(2,1)S(1)}, u32[]{:S(2)}, u32[]{:S(2)}) collective-permute-start(bf16[256,2048]{1,0:T(8,128)(2,1)S(1)} %add_convert_fusion.6), channel_id=1, source_target_pairs={{0,1},{1,2},{2,3},{3,0},{4,5},{5,6},{6,7},{7,4},{8,9},{9,10},{10,1... | collective-permute-start | bytes 3145736 | tf_op jit(solution)/shard_map/ppermute | solution.py:379
  415.2 26.5 %collective-permute-start.60 = (bf16[256,2048]{1,0:T(8,128)(2,1)S(1)}, bf16[256,2048]{1,0:T(8,128)(2,1)S(1)}, u32[]{:S(2)}, u32[]{:S(2)}) collective-permute-start(bf16[256,2048]{1,0:T(8,128)(2,1)S(1)} %fusion.8), channel_id=1, source_target_pairs={{0,1},{1,2},{2,3},{3,0},{4,5},{5,6},{6,7},{7,4},{8,9},{9,10},{10,1... | collective-permute-start | bytes 3145736 | tf_op jit(solution)/shard_map/ppermute | solution.py:379
  415.3 26.4 %collective-permute-start.49 = (bf16[256,2048]{1,0:T(8,128)(2,1)S(1)}, bf16[256,2048]{1,0:T(8,128)(2,1)S(1)}, u32[]{:S(2)}, u32[]{:S(2)}) collective-permute-start(bf16[256,2048]{1,0:T(8,128)(2,1)S(1)} %slice.193), channel_id=1, source_target_pairs={{0,4},{4,0},{8,12},{12,8},{16,20},{20,16},{24,28},{28,24},{1,5},{5... | collective-permute-start | bytes 3145736 | tf_op jit(solution)/shard_map/ppermute | solution.py:384
  444.3 27.6 %collective-permute-start.61 = (bf16[256,2048]{1,0:T(8,128)(2,1)S(1)}, bf16[256,2048]{1,0:T(8,128)(2,1)S(1)}, u32[]{:S(2)}, u32[]{:S(2)}) collective-permute-start(bf16[256,2048]{1,0:T(8,128)(2,1)S(1)} %fusion.3.refs_0_), channel_id=1, source_target_pairs={{0,1},{1,2},{2,3},{3,0},{4,5},{5,6},{6,7},{7,4},{8,9},{9,10},{10,1... | collective-permute-start | bytes 3145736 | tf_op jit(solution)/shard_map/ppermute | solution.py:379
  471.9 27.9 %collective-permute-start.64 = (bf16[256,2048]{1,0:T(8,128)(2,1)S(1)}, bf16[256,2048]{1,0:T(8,128)(2,1)S(1)}, u32[]{:S(2)}, u32[]{:S(2)}) collective-permute-start(bf16[256,2048]{1,0:T(8,128)(2,1)S(1)} %collective-permute-done.61.refs_0_), channel_id=1, source_target_pairs={{0,1},{1,2},{2,3},{3,0},{4,5},{5,6},{6,7},{7,4},{8,9},{9,10},{10,1... | collective-permute-start | bytes 3145736 | tf_op jit(solution)/shard_map/ppermute | solution.py:379
  503.0 27.8 %collective-permute-start.67 = (bf16[256,2048]{1,0:T(8,128)(2,1)S(1)}, bf16[256,2048]{1,0:T(8,128)(2,1)S(1)}, u32[]{:S(2)}, u32[]{:S(2)}) collective-permute-start(bf16[256,2048]{1,0:T(8,128)(2,1)S(1)} %collective-permute-done.64.refs_0_), channel_id=1, source_target_pairs={{0,1},{1,2},{2,3},{3,0},{4,5},{5,6},{6,7},{7,4},{8,9},{9,10},{10,1... | collective-permute-start | bytes 3145736 | tf_op jit(solution)/shard_map/ppermute | solution.py:379
  503.0 49.7 %collective-permute-start.69 = (bf16[256,2048]{1,0:T(8,128)(2,1)S(1)}, bf16[256,2048]{1,0:T(8,128)(2,1)S(1)}, u32[]{:S(2)}, u32[]{:S(2)}) collective-permute-start(bf16[256,2048]{1,0:T(8,128)(2,1)S(1)} %add_convert_fusion.4), channel_id=1, source_target_pairs={{0,1},{1,2},{2,3},{3,0},{4,5},{5,6},{6,7},{7,4},{8,9},{9,10},{10,1... | collective-permute-start | bytes 3145736 | tf_op jit(solution)/shard_map/ppermute | solution.py:379
  556.1 27.2 %collective-permute-start.73 = (bf16[256,2048]{1,0:T(8,128)(2,1)S(1)}, bf16[256,2048]{1,0:T(8,128)(2,1)S(1)}, u32[]{:S(2)}, u32[]{:S(2)}) collective-permute-start(bf16[256,2048]{1,0:T(8,128)(2,1)S(1)} %add_convert_fusion.3), channel_id=1, source_target_pairs={{0,1},{1,2},{2,3},{3,0},{4,5},{5,6},{6,7},{7,4},{8,9},{9,10},{10,1... | collective-permute-start | bytes 3145736 | tf_op jit(solution)/shard_map/ppermute | solution.py:379
  585.4 27.1 %collective-permute-start.74 = (bf16[256,2048]{1,0:T(8,128)(2,1)S(1)}, bf16[256,2048]{1,0:T(8,128)(2,1)}, u32[]{:S(2)}, u32[]{:S(2)}) collective-permute-start(bf16[256,2048]{1,0:T(8,128)(2,1)S(1)} %add_convert_fusion.2), channel_id=1, source_target_pairs={{0,1},{1,2},{2,3},{3,0},{4,5},{5,6},{6,7},{7,4},{8,9},{9,10},{10,1... | collective-permute-start | bytes 3145736 | tf_op jit(solution)/shard_map/ppermute | solution.py:379
  592.7 24.1 %collective-permute-start.63 = (bf16[256,2048]{1,0:T(8,128)(2,1)}, bf16[256,2048]{1,0:T(8,128)(2,1)}, u32[]{:S(2)}, u32[]{:S(2)}) collective-permute-start(bf16[256,2048]{1,0:T(8,128)(2,1)} %slice.189), channel_id=1, source_target_pairs={{0,4},{4,0},{8,12},{12,8},{16,20},{20,16},{24,28},{28,24},{1,5},{5... | collective-permute-start | bytes 3145736 | tf_op jit(solution)/shard_map/ppermute | solution.py:384
  613.6 25.8 %collective-permute-start.75 = (bf16[2,512,512]{2,1,0:T(8,128)(2,1)}, bf16[2,512,512]{2,1,0:T(8,128)(2,1)S(1)}, u32[]{:S(2)}, u32[]{:S(2)}) collective-permute-start(bf16[2,512,512]{2,1,0:T(8,128)(2,1)} %dynamic-slice_bitcast_fusion.7), channel_id=1, source_target_pairs={{0,8},{4,12},{8,0},{12,4},{16,24},{20,28},{24,16},{28,20},{1,9},{5... | collective-permute-start | bytes 3145736 | tf_op jit(solution)/shard_map/ppermute | solution.py:384
  615.1 25.5 %collective-permute-start.76 = (bf16[2,512,512]{2,1,0:T(8,128)(2,1)}, bf16[2,512,512]{2,1,0:T(8,128)(2,1)S(1)}, u32[]{:S(2)}, u32[]{:S(2)}) collective-permute-start(bf16[2,512,512]{2,1,0:T(8,128)(2,1)} %dynamic-slice_bitcast_fusion.6), channel_id=1, source_target_pairs={{0,16},{4,20},{8,24},{12,28},{16,0},{20,4},{24,8},{28,12},{1,17},{... | collective-permute-start | bytes 3145736 | tf_op jit(solution)/shard_map/ppermute | solution.py:384
  644.1 26.7 %collective-permute-start.81 = (bf16[512,512]{1,0:T(8,128)(2,1)}, bf16[512,512]{1,0:T(8,128)(2,1)}, u32[]{:S(2)}, u32[]{:S(2)}) collective-permute-start(bf16[512,512]{1,0:T(8,128)(2,1)} %fusion.25), channel_id=1, source_target_pairs={{0,8},{4,12},{8,0},{12,4},{16,24},{20,28},{24,16},{28,20},{1,9},{5... | collective-permute-start | bytes 1572872 | tf_op jit(solution)/shard_map/ppermute | solution.py:384
  646.0 24.8 %collective-permute-start.80 = (bf16[512,512]{1,0:T(8,128)(2,1)S(1)}, bf16[512,512]{1,0:T(8,128)(2,1)S(1)}, u32[]{:S(2)}, u32[]{:S(2)}) collective-permute-start(bf16[512,512]{1,0:T(8,128)(2,1)S(1)} %fusion.24), channel_id=1, source_target_pairs={{0,16},{4,20},{8,24},{12,28},{16,0},{20,4},{24,8},{28,12},{1,17},{... | collective-permute-start | bytes 1572872 | tf_op jit(solution)/shard_map/ppermute | solution.py:384
  647.8 23.0 %collective-permute-start.77 = (bf16[256,512]{1,0:T(8,128)(2,1)S(1)}, bf16[256,512]{1,0:T(8,128)(2,1)S(1)}, u32[]{:S(2)}, u32[]{:S(2)}) collective-permute-start(bf16[256,512]{1,0:T(8,128)(2,1)S(1)} %get-tuple-element.415), channel_id=1, source_target_pairs={{0,1},{1,2},{2,3},{3,0},{4,5},{5,6},{6,7},{7,4},{8,9},{9,10},{10,1... | collective-permute-start | bytes 786440 | tf_op jit(solution)/shard_map/ppermute | solution.py:401
  647.8 23.0 %collective-permute-start.78 = (bf16[256,512]{1,0:T(8,128)(2,1)S(1)}, bf16[256,512]{1,0:T(8,128)(2,1)S(1)}, u32[]{:S(2)}, u32[]{:S(2)}) collective-permute-start(bf16[256,512]{1,0:T(8,128)(2,1)S(1)} %get-tuple-element.416), channel_id=1, source_target_pairs={{0,2},{1,3},{2,0},{3,1},{4,6},{5,7},{6,4},{7,5},{8,10},{9,11},{10,... | collective-permute-start | bytes 786440 | tf_op jit(solution)/shard_map/ppermute | solution.py:401
  673.1 32.0 %collective-permute-start.86 = (bf16[2,512,512]{2,1,0:T(8,128)(2,1)}, bf16[2,512,512]{2,1,0:T(8,128)(2,1)S(1)}, u32[]{:S(2)}, u32[]{:S(2)}) collective-permute-start(bf16[2,512,512]{2,1,0:T(8,128)(2,1)} %dynamic-slice_bitcast_fusion.5), channel_id=1, source_target_pairs={{0,8},{4,12},{8,0},{12,4},{16,24},{20,28},{24,16},{28,20},{1,9},{5... | collective-permute-start | bytes 3145736 | tf_op jit(solution)/shard_map/ppermute | solution.py:384
  674.7 30.5 %collective-permute-start.87 = (bf16[2,512,512]{2,1,0:T(8,128)(2,1)}, bf16[2,512,512]{2,1,0:T(8,128)(2,1)}, u32[]{:S(2)}, u32[]{:S(2)}) collective-permute-start(bf16[2,512,512]{2,1,0:T(8,128)(2,1)} %dynamic-slice_bitcast_fusion.4), channel_id=1, source_target_pairs={{0,16},{4,20},{8,24},{12,28},{16,0},{20,4},{24,8},{28,12},{1,17},{... | collective-permute-start | bytes 3145736 | tf_op jit(solution)/shard_map/ppermute | solution.py:384
  677.4 27.7 %collective-permute-start.83 = (bf16[128,1024]{1,0:T(8,128)(2,1)S(1)}, bf16[128,1024]{1,0:T(8,128)(2,1)S(1)}, u32[]{:S(2)}, u32[]{:S(2)}) collective-permute-start(bf16[128,1024]{1,0:T(8,128)(2,1)S(1)} %get-tuple-element.434), channel_id=1, source_target_pairs={{0,1},{1,2},{2,3},{3,0},{4,5},{5,6},{6,7},{7,4},{8,9},{9,10},{10,1... | collective-permute-start | bytes 786440 | tf_op jit(solution)/shard_map/ppermute | solution.py:401
  680.9 24.2 %collective-permute-start.84 = (bf16[128,1024]{1,0:T(8,128)(2,1)S(1)}, bf16[128,1024]{1,0:T(8,128)(2,1)S(1)}, u32[]{:S(2)}, u32[]{:S(2)}) collective-permute-start(bf16[128,1024]{1,0:T(8,128)(2,1)S(1)} %get-tuple-element.435), channel_id=1, source_target_pairs={{0,2},{1,3},{2,0},{3,1},{4,6},{5,7},{6,4},{7,5},{8,10},{9,11},{10,... | collective-permute-start | bytes 786440 | tf_op jit(solution)/shard_map/ppermute | solution.py:401
  680.9 24.2 %collective-permute-start.85 = (bf16[128,1024]{1,0:T(8,128)(2,1)S(1)}, bf16[128,1024]{1,0:T(8,128)(2,1)S(1)}, u32[]{:S(2)}, u32[]{:S(2)}) collective-permute-start(bf16[128,1024]{1,0:T(8,128)(2,1)S(1)} %get-tuple-element.436), channel_id=1, source_target_pairs={{0,3},{1,0},{2,1},{3,2},{4,7},{5,4},{6,5},{7,6},{8,11},{9,8},{10,9... | collective-permute-start | bytes 786440 | tf_op jit(solution)/shard_map/ppermute | solution.py:401
  728.9 27.5 %collective-permute-start.93 = (bf16[2,2,256,1024]{3,2,0,1:T(8,128)(2,1)}, bf16[2,2,256,1024]{3,2,0,1:T(8,128)(2,1)}, u32[]{:S(2)}, u32[]{:S(2)}) collective-permute-start(bf16[2,2,256,1024]{3,2,0,1:T(8,128)(2,1)} %copy_bitcast_fusion), channel_id=1, source_target_pairs={{0,4},{4,0},{8,12},{12,8},{16,20},{20,16},{24,28},{28,24},{1,5},{5... | collective-permute-start | bytes 6291464 | tf_op jit(solution)/shard_map/ppermute | solution.py:384
  730.4 26.0 %collective-permute-start.94 = (bf16[2,2,256,1024]{3,2,1,0:T(8,128)(2,1)}, bf16[2,2,256,1024]{3,2,1,0:T(8,128)(2,1)}, u32[]{:S(2)}, u32[]{:S(2)}) collective-permute-start(bf16[2,2,256,1024]{3,2,1,0:T(8,128)(2,1)} %dynamic-slice_bitcast_fusion), channel_id=1, source_target_pairs={{0,4},{4,0},{8,12},{12,8},{16,20},{20,16},{24,28},{28,24},{1,5},{5... | collective-permute-start | bytes 6291464 | tf_op jit(solution)/shard_map/ppermute | solution.py:384
  773.7 25.1 %collective-permute-start.100 = (bf16[2,256,1024]{2,1,0:T(8,128)(2,1)S(1)}, bf16[2,256,1024]{2,1,0:T(8,128)(2,1)}, u32[]{:S(2)}, u32[]{:S(2)}) collective-permute-start(bf16[2,256,1024]{2,1,0:T(8,128)(2,1)S(1)} %fusion.16), channel_id=1, source_target_pairs={{0,8},{4,12},{8,0},{12,4},{16,24},{20,28},{24,16},{28,20},{1,9},{5... | collective-permute-start | bytes 3145736 | tf_op jit(solution)/shard_map/ppermute | solution.py:384
  774.2 24.8 %collective-permute-start.101 = (bf16[2,256,1024]{2,1,0:T(8,128)(2,1)S(1)}, bf16[2,256,1024]{2,1,0:T(8,128)(2,1)}, u32[]{:S(2)}, u32[]{:S(2)}) collective-permute-start(bf16[2,256,1024]{2,1,0:T(8,128)(2,1)S(1)} %fusion.17), channel_id=1, source_target_pairs={{0,16},{4,20},{8,24},{12,28},{16,0},{20,4},{24,8},{28,12},{1,17},{... | collective-permute-start | bytes 3145736 | tf_op jit(solution)/shard_map/ppermute | solution.py:384
  775.0 28.6 %collective-permute-start.99 = (bf16[256,2048]{1,0:T(8,128)(2,1)}, bf16[256,2048]{1,0:T(8,128)(2,1)S(1)}, u32[]{:S(2)}, u32[]{:S(2)}) collective-permute-start(bf16[256,2048]{1,0:T(8,128)(2,1)} %convolution_convert_fusion), channel_id=1, source_target_pairs={{0,1},{1,2},{2,3},{3,0},{4,5},{5,6},{6,7},{7,4},{8,9},{9,10},{10,1... | collective-permute-start | bytes 3145736 | tf_op jit(solution)/shard_map/ppermute | solution.py:379
  811.4 28.0 %collective-permute-start.105 = (bf16[2,2,256,768]{3,2,0,1:T(8,128)(2,1)S(1)}, bf16[2,2,256,768]{3,2,0,1:T(8,128)(2,1)S(1)}, u32[]{:S(2)}, u32[]{:S(2)}) collective-permute-start(bf16[2,2,256,768]{3,2,0,1:T(8,128)(2,1)S(1)} %copy_bitcast_fusion.1), channel_id=1, source_target_pairs={{0,4},{4,0},{8,12},{12,8},{16,20},{20,16},{24,28},{28,24},{1,5},{5... | collective-permute-start | bytes 4718600 | tf_op jit(solution)/shard_map/ppermute | solution.py:384
  811.6 27.8 %collective-permute-start.106 = (bf16[2,2,256,768]{3,2,1,0:T(8,128)(2,1)S(1)}, bf16[2,2,256,768]{3,2,1,0:T(8,128)(2,1)S(1)}, u32[]{:S(2)}, u32[]{:S(2)}) collective-permute-start(bf16[2,2,256,768]{3,2,1,0:T(8,128)(2,1)S(1)} %dynamic-slice_bitcast_fusion.1), channel_id=1, source_target_pairs={{0,4},{4,0},{8,12},{12,8},{16,20},{20,16},{24,28},{28,24},{1,5},{5... | collective-permute-start | bytes 4718600 | tf_op jit(solution)/shard_map/ppermute | solution.py:384
  813.0 26.5 %collective-permute-start.102 = (bf16[256,2048]{1,0:T(8,128)(2,1)S(1)}, bf16[256,2048]{1,0:T(8,128)(2,1)S(1)}, u32[]{:S(2)}, u32[]{:S(2)}) collective-permute-start(bf16[256,2048]{1,0:T(8,128)(2,1)S(1)} %add_convert_fusion.1), channel_id=1, source_target_pairs={{0,1},{1,2},{2,3},{3,0},{4,5},{5,6},{6,7},{7,4},{8,9},{9,10},{10,1... | collective-permute-start | bytes 3145736 | tf_op jit(solution)/shard_map/ppermute | solution.py:379
  841.7 49.8 %collective-permute-start.112 = (bf16[64,2048]{1,0:T(8,128)(2,1)S(1)}, bf16[64,2048]{1,0:T(8,128)(2,1)}, u32[]{:S(2)}, u32[]{:S(2)}) collective-permute-start(bf16[64,2048]{1,0:T(8,128)(2,1)S(1)} %get-tuple-element.517), channel_id=1, source_target_pairs={{0,1},{1,2},{2,3},{3,0},{4,5},{5,6},{6,7},{7,4},{8,9},{9,10},{10,1... | collective-permute-start | bytes 786440 | tf_op jit(solution)/shard_map/ppermute | solution.py:401
  844.1 25.3 %collective-permute-start.109 = (bf16[2,256,768]{2,1,0:T(8,128)(2,1)S(1)}, bf16[2,256,768]{2,1,0:T(8,128)(2,1)}, u32[]{:S(2)}, u32[]{:S(2)}) collective-permute-start(bf16[2,256,768]{2,1,0:T(8,128)(2,1)S(1)} %fusion.23), channel_id=1, source_target_pairs={{0,16},{4,20},{8,24},{12,28},{16,0},{20,4},{24,8},{28,12},{1,17},{... | collective-permute-start | bytes 2359304 | tf_op jit(solution)/shard_map/ppermute | solution.py:384
  846.7 26.5 %collective-permute-start.107 = (bf16[256,2048]{1,0:T(8,128)(2,1)}, bf16[256,2048]{1,0:T(8,128)(2,1)}, u32[]{:S(2)}, u32[]{:S(2)}) collective-permute-start(bf16[256,2048]{1,0:T(8,128)(2,1)} %add_convert_fusion), channel_id=1, source_target_pairs={{0,1},{1,2},{2,3},{3,0},{4,5},{5,6},{6,7},{7,4},{8,9},{9,10},{10,1... | collective-permute-start | bytes 3145736 | tf_op jit(solution)/shard_map/ppermute | solution.py:379
  848.5 20.9 %collective-permute-start.108 = (bf16[2,256,768]{2,1,0:T(8,128)(2,1)}, bf16[2,256,768]{2,1,0:T(8,128)(2,1)}, u32[]{:S(2)}, u32[]{:S(2)}) collective-permute-start(bf16[2,256,768]{2,1,0:T(8,128)(2,1)} %fusion.22), channel_id=1, source_target_pairs={{0,8},{4,12},{8,0},{12,4},{16,24},{20,28},{24,16},{28,20},{1,9},{5... | collective-permute-start | bytes 2359304 | tf_op jit(solution)/shard_map/ppermute | solution.py:384
  878.9 31.7 %collective-permute-start.115 = (bf16[2,256,1024]{2,1,0:T(8,128)(2,1)S(1)}, bf16[2,256,1024]{2,1,0:T(8,128)(2,1)S(1)}, u32[]{:S(2)}, u32[]{:S(2)}) collective-permute-start(bf16[2,256,1024]{2,1,0:T(8,128)(2,1)S(1)} %dynamic-slice_bitcast_fusion.3), channel_id=1, source_target_pairs={{0,8},{4,12},{8,0},{12,4},{16,24},{20,28},{24,16},{28,20},{1,9},{5... | collective-permute-start | bytes 3145736 | tf_op jit(solution)/shard_map/ppermute | solution.py:384
  880.4 30.2 %collective-permute-start.116 = (bf16[2,256,1024]{2,1,0:T(8,128)(2,1)S(1)}, bf16[2,256,1024]{2,1,0:T(8,128)(2,1)S(1)}, u32[]{:S(2)}, u32[]{:S(2)}) collective-permute-start(bf16[2,256,1024]{2,1,0:T(8,128)(2,1)S(1)} %dynamic-slice_bitcast_fusion.2), channel_id=1, source_target_pairs={{0,16},{4,20},{8,24},{12,28},{16,0},{20,4},{24,8},{28,12},{1,17},{... | collective-permute-start | bytes 3145736 | tf_op jit(solution)/shard_map/ppermute | solution.py:384
  915.7 24.4 %collective-permute-start.126 = (bf16[256,1024]{1,0:T(8,128)(2,1)}, bf16[256,1024]{1,0:T(8,128)(2,1)}, u32[]{:S(2)}, u32[]{:S(2)}) collective-permute-start(bf16[256,1024]{1,0:T(8,128)(2,1)} %fusion.30), channel_id=1, source_target_pairs={{0,16},{4,20},{8,24},{12,28},{16,0},{20,4},{24,8},{28,12},{1,17},{... | collective-permute-start | bytes 1572872 | tf_op jit(solution)/shard_map/ppermute | solution.py:384
  919.8 21.5 %collective-permute-start.127 = (bf16[256,1024]{1,0:T(8,128)(2,1)}, bf16[256,1024]{1,0:T(8,128)(2,1)}, u32[]{:S(2)}, u32[]{:S(2)}) collective-permute-start(bf16[256,1024]{1,0:T(8,128)(2,1)} %fusion.31), channel_id=1, source_target_pairs={{0,8},{4,12},{8,0},{12,4},{16,24},{20,28},{24,16},{28,20},{1,9},{5... | collective-permute-start | bytes 1572872 | tf_op jit(solution)/shard_map/ppermute | solution.py:384
  (198 other events, 1711.2 us)

commit v6 on v5

--- a/solution.py
+++ b/solution.py
@@ -769,10 +769,10 @@
     hidden = tok_rows.astype(f32) + a_proj * a_scale * gain_attn
 
     def ring(block, work, beside=lambda: ()):
-        got, own = None, None
+        got, own, held = None, None, block
         for at in range(size):
             later = next_one(block, "seq") if at < size - 1 else None
-            share = work(stacked([block, flipped(block, 1)]))
+            share = work(stacked([held, flipped(held, 1)]))
             share, away = share[:rows], share[rows:].astype(bf16)
             if later is not None:
                 later, share, away, got = together(later, share, away, got)
@@ -782,9 +782,9 @@
             else:
                 if at > 1:
                     share = share + got.astype(f32)
-                send, later = together(share.astype(bf16), later)
+                send, held = together(share.astype(bf16), later)
                 got = next_one(send, "seq")
-            block = later
+            block, held = later, later if at == 0 else held
         got, extra = together(got, beside(send))
         return own + got.astype(f32), extra
 
@@ -800,7 +800,7 @@
         inners.append(inner)
         return product(inner, w_down_part)
 
-    m_proj, _ = ring(hidden.astype(bf16), forward, lambda send: ())
+    m_proj, h_all = ring(hidden.astype(bf16), forward, lambda send: stacked(h_slots, 56 * 2**20))
     m_scale = rms_scale(m_proj)
     out = (hidden + m_proj * m_scale * gain_ffn).astype(bf16).reshape(tokens.shape)
     grad_out = d_out.reshape(rows, width).astype(f32)
@@ -830,7 +830,6 @@
         _, all_gates = together(send, stacked(d_gates, 56 * 2**20))
         return grad_halves(h_all, all_gates, False)
 
-    h_all = stacked(h_slots, 56 * 2**20)
     d_sum, d_gate = ring(dm_low, backward, grads)
     cube_gate = CubeScatter(d_gate)
     cube_gate.step()
@@ -928,16 +927,20 @@
             out_got = send_ahead(row_blocks(cube_out.finish()), "seq")
             d_down = grad_halves(stacked(inners, 56 * 2**20), stacked(dms, 56 * 2**20), False)
             got, cube_qkv.got, d_down = together(got, cube_qkv.got, d_down)
-            cube_down = CubeScatter(d_down)
-            cube_down.step()
+    cube_qkv.step()
+    cube_qkv.got, d_down = together(cube_qkv.got, d_down)
+    cube_down = CubeScatter(d_down)
+    cube_down.step()
     d_w_qkv = row_blocks(cube_qkv.finish())
-    d_w_qkv, out_got, cube_down.got, d_gains = together(d_w_qkv, out_got, cube_down.got, d_gains)
+    d_w_qkv, out_got = together(d_w_qkv, out_got)
     d_w_qkv = send_ahead(d_w_qkv, "seq")
     d_down = cube_down.finish()
-    d_gains = small_sum(d_gains, "seq")
+    d_gains = small_sum(d_gains.reshape(-1), "seq")
     for bit in [1] + cube_bits()[0]:
-        d_gains = d_gains + flipped(d_gains.reshape(-1), bit).reshape(d_gains.shape)
-    d_gains = lax.dynamic_slice_in_dim(d_gains, (lax.axis_index("dp") * size + here) * own_rows, own_rows, 1)
+        d_gains = d_gains + flipped(d_gains, bit)
+    d_gains = lax.dynamic_slice_in_dim(
+        d_gains.reshape(4, width), (lax.axis_index("dp") * size + here) * own_rows, own_rows, 1
+    )
     d_tokens = d_hidden + shares[-1] + got.astype(f32)
     d_w_out = sum(g.astype(f32) for g in out_got)
     d_w_qkv = relayout(

time: 952 us -> 942 us (0.989)
  waiting for transfers between devices: 408 us -> 379 us
  local copies, waits for them, and re-layouts: 62.4 us -> 74.2 us
    ppermute x18, waiting for transfers between devices: 221 us -> 205 us  [next_one(): return lax.ppermute(block, axis, [(i, (i + 1) % size) for i in range(size)])]
    ppermute x27, waiting for transfers between devices: 65.6 us -> 56.1 us  [send_ahead(): lax.ppermute(blocks[step], axis, [(i, (i + step) % size) for i in range(s...]
    unnamed x267 -> x285, local copies, waits for them, and re-layouts: 36.5 us -> 39.4 us
  transfers between devices with their start and end apart: 128 -> 128, of which waited for: 64 -> 62; matrix products, arithmetic and copies ran while one was open for 13% -> 15% of each run, Pallas kernels for 20% -> 20%
where the time goes in v6:
time: 942 us; the launch traced here: 936 us
  waiting for transfers between devices  379 us (40%)
  Pallas kernels  193 us (20%)
  starting transfers between devices  148 us (16%)
  matrix products  81.2 us (9%)
  local copies, waits for them, and re-layouts  74.2 us (8%)
  other arithmetic  56.4 us (6%)
    ppermute x18, waiting for transfers between devices, next_one(): return lax.ppermute(block, axis, [(i, (i + 1) % size) for i in range(size)])  205 us
    ppermute x71, waiting for transfers between devices, flipped(): return lax.ppermute(block, 'dp', [(i, i ^ bit) for i in range(size)])  106 us
    pallas_call x40, Pallas kernels, assemble(): pl.pallas_call(functools.partial(assemble_body, parts, places, len(pieces...  62.8 us
    ppermute x27, starting transfers between devices, send_ahead(): lax.ppermute(blocks[step], axis, [(i, (i + step) % size) for i in range(s...  60.6 us
    pallas_call x5, Pallas kernels, grad_halves(): pl.pallas_call(grad_halves_body, grid=(depth // block,), in_specs=[vmem((...  56.5 us
    ppermute x27, waiting for transfers between devices, send_ahead(): lax.ppermute(blocks[step], axis, [(i, (i + step) % size) for i in range(s...  56.1 us
    ppermute x71, starting transfers between devices, flipped(): return lax.ppermute(block, 'dp', [(i, i ^ bit) for i in range(size)])  47.9 us
    dot_general x14, matrix products, product(): return jnp.dot(left, right, preferred_element_type=f32)  43.4 us
  transfers between devices with their start and end apart: 128, of which 62 were waited for; matrix products, arithmetic and copies ran while one was open for 15% of the time, Pallas kernels for 20%

profile of v6, /device:TPU:0, one launch (start us, length us, event | category | flops | bytes accessed | tf_op | source)
XLA Modules:
  0.0 935.5 jit_solution(7150974468718897974)
XLA Ops:
  14.7 4.2 collective-permute-done.refs_1_
  19.0 7.4 collective-permute-done.1.refs_2_
  30.6 5.0 collective-permute-start.5
  38.0 6.0 collective-permute-done.5.refs_1_
  44.0 8.3 collective-permute-done.6.refs_2_
  57.4 6.1 collective-permute-start.10
  68.0 4.6 collective-permute-done.10.refs_1_
  75.1 6.9 collective-permute-done.11.refs_2_
  83.7 4.5 collective-permute-start.16
  91.6 12.4 %collective-permute-done.17.refs_1_ = bf16[256,1024]{1,0:T(8,128)(2,1)S(1)} collective-permute-done((bf16[256,1024]{1,0:T(8,128)(2,1)S(1)}, bf16[256,1024]{1,0:T(8,128)(2,1)S(1)}, u32[]{:S(2)}, u32[]{:S(2)}) %collective-permute-start.17) | collective-permute-done | bytes 524320 | tf_op jit(solution)/shard_map/ppermute | solution.py:384
  105.7 6.1 collective-permute-done.16.refs_1_
  119.6 8.7 collective-permute-done.20.refs_1_
  134.0 4.1 collective-permute-done.19.refs_2_
  146.7 4.7 shard_map.257
  155.2 13.6 %collective-permute-done.27.refs_1_ = bf16[256,1024]{1,0:T(8,128)(2,1)} collective-permute-done((bf16[256,1024]{1,0:T(8,128)(2,1)S(1)}, bf16[256,1024]{1,0:T(8,128)(2,1)}, u32[]{:S(2)}, u32[]{:S(2)}) %collective-permute-start.27) | collective-permute-done | bytes 524320 | tf_op jit(solution)/shard_map/ppermute | solution.py:384
  174.6 6.6 fusion.46.raw_ref
  197.7 8.8 collective-permute-done.34.refs_2_
  211.5 4.5 shard_map.258
  216.0 13.9 %shard_map.259.refs_0_ = bf16[1024,512]{1,0:T(8,128)(2,1)S(1)} custom-call(bf16[1024,512]{1,0:T(8,128)(2,1)S(1)} %get-tuple-element.342.q_ref, bf16[1024,512]{1,0:T(8,128)(2,1)S(1)} %get-tuple-element.343.k_ref, bf16[1024,512]{1,0:T(8,128)(2,1)S(1)} %get-tuple-element.344.v_ref, s32[1,1024]{1,0:T(1,128)S(1)} %copy-done.68, s32[1024,1]{1,0:T(8,128)S(1)} %copy.67.seg_k_ref), custom_call_target="tpu_custom_call" | custom-call | tf_op jit(solution)/shard_map/pallas_call | solution.py:241
  236.0 5.1 collective-permute-start.40
  271.8 6.3 collective-permute-start.47
  281.5 3.9 multiply_convert_fusion.9
  290.9 11.7 %collective-permute-done.47.refs_0_ = bf16[256,2048]{1,0:T(8,128)(2,1)S(1)} collective-permute-done((bf16[256,2048]{1,0:T(8,128)(2,1)S(1)}, bf16[256,2048]{1,0:T(8,128)(2,1)S(1)}, u32[]{:S(2)}, u32[]{:S(2)}) %collective-permute-start.47) | collective-permute-done | bytes 1048608 | tf_op jit(solution)/shard_map/ppermute | solution.py:379
  307.9 3.8 multiply_convert_fusion.8
  314.5 15.6 %collective-permute-done.50.refs_0_ = bf16[256,2048]{1,0:T(8,128)(2,1)S(1)} collective-permute-done((bf16[256,2048]{1,0:T(8,128)(2,1)S(1)}, bf16[256,2048]{1,0:T(8,128)(2,1)S(1)}, u32[]{:S(2)}, u32[]{:S(2)}) %collective-permute-start.50) | collective-permute-done | bytes 1048608 | tf_op jit(solution)/shard_map/ppermute | solution.py:379
  338.5 3.8 multiply_convert_fusion.7
  346.1 15.0 %collective-permute-done.52.refs_0_ = bf16[256,2048]{1,0:T(8,128)(2,1)S(1)} collective-permute-done((bf16[256,2048]{1,0:T(8,128)(2,1)S(1)}, bf16[256,2048]{1,0:T(8,128)(2,1)S(1)}, u32[]{:S(2)}, u32[]{:S(2)}) %collective-permute-start.52) | collective-permute-done | bytes 1048608 | tf_op jit(solution)/shard_map/ppermute | solution.py:379
  361.0 21.9 %collective-permute-done.55 = bf16[256,2048]{1,0:T(8,128)(2,1)S(1)} collective-permute-done((bf16[256,2048]{1,0:T(8,128)(2,1)S(1)}, bf16[256,2048]{1,0:T(8,128)(2,1)S(1)}, u32[]{:S(2)}, u32[]{:S(2)}) %collective-permute-start.55) | collective-permute-done | bytes 1048608 | tf_op jit(solution)/shard_map/ppermute | solution.py:379
  391.6 3.8 multiply_convert_fusion.6
  398.2 15.7 %collective-permute-done.59 = bf16[256,2048]{1,0:T(8,128)(2,1)S(1)} collective-permute-done((bf16[256,2048]{1,0:T(8,128)(2,1)S(1)}, bf16[256,2048]{1,0:T(8,128)(2,1)S(1)}, u32[]{:S(2)}, u32[]{:S(2)}) %collective-permute-start.59) | collective-permute-done | bytes 1048608 | tf_op jit(solution)/shard_map/ppermute | solution.py:379
  414.5 7.1 shard_map.277.left_ref
  421.6 19.2 %collective-permute-done.60 = bf16[256,2048]{1,0:T(8,128)(2,1)S(1)} collective-permute-done((bf16[256,2048]{1,0:T(8,128)(2,1)S(1)}, bf16[256,2048]{1,0:T(8,128)(2,1)S(1)}, u32[]{:S(2)}, u32[]{:S(2)}) %collective-permute-start.60) | collective-permute-done | bytes 1048608 | tf_op jit(solution)/shard_map/ppermute | solution.py:379
  457.4 13.1 %collective-permute-done.61.refs_0_ = bf16[256,2048]{1,0:T(8,128)(2,1)S(1)} collective-permute-done((bf16[256,2048]{1,0:T(8,128)(2,1)S(1)}, bf16[256,2048]{1,0:T(8,128)(2,1)S(1)}, u32[]{:S(2)}, u32[]{:S(2)}) %collective-permute-start.61) | collective-permute-done | bytes 1048608 | tf_op jit(solution)/shard_map/ppermute | solution.py:379
  481.7 16.6 %collective-permute-done.64.refs_0_ = bf16[256,2048]{1,0:T(8,128)(2,1)S(1)} collective-permute-done((bf16[256,2048]{1,0:T(8,128)(2,1)S(1)}, bf16[256,2048]{1,0:T(8,128)(2,1)S(1)}, u32[]{:S(2)}, u32[]{:S(2)}) %collective-permute-start.64) | collective-permute-done | bytes 1048608 | tf_op jit(solution)/shard_map/ppermute | solution.py:379
  512.5 16.8 %collective-permute-done.66.refs_0_ = bf16[256,2048]{1,0:T(8,128)(2,1)S(1)} collective-permute-done((bf16[256,2048]{1,0:T(8,128)(2,1)S(1)}, bf16[256,2048]{1,0:T(8,128)(2,1)S(1)}, u32[]{:S(2)}, u32[]{:S(2)}) %collective-permute-start.66) | collective-permute-done | bytes 1048608 | tf_op jit(solution)/shard_map/ppermute | solution.py:379
  529.3 21.9 %collective-permute-done.69 = bf16[256,2048]{1,0:T(8,128)(2,1)S(1)} collective-permute-done((bf16[256,2048]{1,0:T(8,128)(2,1)S(1)}, bf16[256,2048]{1,0:T(8,128)(2,1)S(1)}, u32[]{:S(2)}, u32[]{:S(2)}) %collective-permute-start.69) | collective-permute-done | bytes 1048608 | tf_op jit(solution)/shard_map/ppermute | solution.py:379
  557.4 14.6 %shard_map.282 = (bf16[512,1024]{1,0:T(8,128)(2,1)S(1)}, bf16[512,1024]{1,0:T(8,128)(2,1)S(1)}, f32[512,2048]{1,0:T(8,128)}) custom-call(bf16[512,2048]{1,0:T(8,128)(2,1)S(1)} %shard_map.281.left_ref.refs_3_, bf16[1024,2048]{1,0:T(8,128)(2,1)} %copy-done.16, f32[512,1024]{1,0:T(8,128)} %copy-done.127, f32[512,1024]{1,0:T(8,128)} %get-tuple-element.599.up_ref, ...), custom_call_target="tpu_custom_call" | custom-call | flops 6442450944 | bytes 12582912 | tf_op jit(solution)/shard_map/pallas_call | solution.py:157
  574.7 7.1 collective-permute-done.73
  584.3 3.3 shard_map.286.right_ref
  590.9 13.0 %shard_map.284 = (bf16[2048,512]{1,0:T(8,128)(2,1)S(1)}, bf16[2048,512]{1,0:T(8,128)(2,1)S(1)}) custom-call(bf16[2048,2048]{1,0:T(8,128)(2,1)} %shard_map.277.left_ref, bf16[2048,1024]{1,0:T(8,128)(2,1)} %shard_map.283.right_ref), custom_call_target="tpu_custom_call" | custom-call | flops 8589934592 | bytes 16777216 | tf_op jit(solution)/shard_map/pallas_call | solution.py:193
  604.0 6.7 collective-permute-done.74
  623.6 12.0 %collective-permute-done.75 = bf16[2,512,512]{2,1,0:T(8,128)(2,1)S(1)} collective-permute-done((bf16[2,512,512]{2,1,0:T(8,128)(2,1)}, bf16[2,512,512]{2,1,0:T(8,128)(2,1)S(1)}, u32[]{:S(2)}, u32[]{:S(2)}) %collective-permute-start.75) | collective-permute-done | bytes 1048608 | tf_op jit(solution)/shard_map/ppermute | solution.py:384
  644.1 3.8 collective-permute-start.79
  647.9 12.9 %shard_map.288 = (bf16[2048,512]{1,0:T(8,128)(2,1)S(1)}, bf16[2048,512]{1,0:T(8,128)(2,1)S(1)}) custom-call(bf16[2048,2048]{1,0:T(8,128)(2,1)} %shard_map.277.left_ref, bf16[2048,1024]{1,0:T(8,128)(2,1)} %shard_map.286.right_ref), custom_call_target="tpu_custom_call" | custom-call | flops 8589934592 | bytes 16777216 | tf_op jit(solution)/shard_map/pallas_call | solution.py:193
  660.8 5.9 shard_map.287
  679.9 20.1 %shard_map.290 = (bf16[1024,512]{1,0:T(8,128)(2,1)S(1)}, bf16[1024,512]{1,0:T(8,128)(2,1)S(1)}, bf16[1024,512]{1,0:T(8,128)(2,1)S(1)}) custom-call(bf16[1024,512]{1,0:T(8,128)(2,1)S(1)} %copy-done.27, bf16[1024,512]{1,0:T(8,128)(2,1)S(1)} %copy-done.29, bf16[1024,512]{1,0:T(8,128)(2,1)} %copy-done.30, bf16[1024,512]{1,0:T(8,128)(2,1)} %copy-done.25, ...), custom_call_target="tpu_custom_call" | custom-call | tf_op jit(solution)/shard_map/pallas_call | solution.py:285
  707.9 6.2 shard_map.292
  729.8 3.3 shard_map.297.left_ref
  737.4 6.1 shard_map.293.refs_0_.right_ref
  751.4 3.3 convert_add_fusion
  754.9 4.3 convert_add_fusion.1
  764.4 4.2 collective-permute-done.97.refs_2_
  769.7 6.1 collective-permute-start.99
  780.5 11.5 %shard_map.296 = (bf16[2048,768]{1,0:T(8,128)(2,1)S(1)}, bf16[2048,768]{1,0:T(8,128)(2,1)}) custom-call(bf16[1024,2048]{1,0:T(8,128)(2,1)} %copy-done.15, bf16[1024,1536]{1,0:T(8,128)(2,1)} %shard_map.293.refs_0_.right_ref), custom_call_target="tpu_custom_call" | custom-call | flops 6442450944 | bytes 8388608 | tf_op jit(solution)/shard_map/pallas_call | solution.py:193
  794.0 4.6 collective-permute-done.99
  830.7 7.4 collective-permute-done.103
  838.2 5.6 collective-permute-done.102
  853.8 7.1 shard_map.298.right_ref
  862.2 13.3 %shard_map.299 = (bf16[1024,1024]{1,0:T(8,128)(2,1)S(1)}, bf16[1024,1024]{1,0:T(8,128)(2,1)S(1)}) custom-call(bf16[2048,1024]{1,0:T(8,128)(2,1)} %shard_map.297.left_ref, bf16[2048,2048]{1,0:T(8,128)(2,1)} %shard_map.298.right_ref), custom_call_target="tpu_custom_call" | custom-call | flops 8589934592 | bytes 8388608 | tf_op jit(solution)/shard_map/pallas_call | solution.py:193
  875.4 3.8 collective-permute-done.107
  887.8 3.4 collective-permute-start.114
  899.7 6.4 collective-permute-done.113
  906.1 9.4 %collective-permute-start.115 = (bf16[64,1536]{1,0:T(8,128)(2,1)S(1)}, bf16[64,1536]{1,0:T(8,128)(2,1)S(1)}, u32[]{:S(2)}, u32[]{:S(2)}) collective-permute-start(bf16[64,1536]{1,0:T(8,128)(2,1)S(1)} %get-tuple-element.530), channel_id=1, source_target_pairs={{0,1},{1,2},{2,3},{3,0},{4,5},{5,6},{6,7},{7,4},{8,9},{9,10},{10,1... | collective-permute-start | bytes 589832 | tf_op jit(solution)/shard_map/ppermute | solution.py:401
  928.7 3.4 collective-permute-done.125
  (698 shorter events, 385.3 us)
Async XLA Ops:
  2.1 24.3 %collective-permute-start.3 = (bf16[128,2048]{1,0:T(8,128)(2,1)S(1)}, bf16[128,2048]{1,0:T(8,128)(2,1)S(1)}, u32[]{:S(2)}, u32[]{:S(2)}) collective-permute-start(bf16[128,2048]{1,0:T(8,128)(2,1)S(1)} %get-tuple-element.575.refs_0_), channel_id=1, source_target_pairs={{0,8},{4,12},{8,0},{12,4},{16,24},{20,28},{24,16},{28,20},{1,9},{5... | collective-permute-start | bytes 1572872 | tf_op jit(solution)/shard_map/ppermute | solution.py:384
  5.1 21.3 %collective-permute-start.4 = (bf16[128,2048]{1,0:T(8,128)(2,1)S(1)}, bf16[128,2048]{1,0:T(8,128)(2,1)S(1)}, u32[]{:S(2)}, u32[]{:S(2)}) collective-permute-start(bf16[128,2048]{1,0:T(8,128)(2,1)S(1)} %get-tuple-element.574.refs_0_), channel_id=1, source_target_pairs={{0,16},{4,20},{8,24},{12,28},{16,0},{20,4},{24,8},{28,12},{1,17},{... | collective-permute-start | bytes 1572872 | tf_op jit(solution)/shard_map/ppermute | solution.py:384
  29.5 22.8 %collective-permute-start.8 = (bf16[128,1664]{1,0:T(8,128)(2,1)S(1)}, bf16[128,1664]{1,0:T(8,128)(2,1)S(1)}, u32[]{:S(2)}, u32[]{:S(2)}) collective-permute-start(bf16[128,1664]{1,0:T(8,128)(2,1)S(1)} %get-tuple-element.577.refs_0_), channel_id=1, source_target_pairs={{0,8},{4,12},{8,0},{12,4},{16,24},{20,28},{24,16},{28,20},{1,9},{5... | collective-permute-start | bytes 1277960 | tf_op jit(solution)/shard_map/ppermute | solution.py:384
  30.1 22.2 %collective-permute-start.9 = (bf16[128,1664]{1,0:T(8,128)(2,1)S(1)}, bf16[128,1664]{1,0:T(8,128)(2,1)S(1)}, u32[]{:S(2)}, u32[]{:S(2)}) collective-permute-start(bf16[128,1664]{1,0:T(8,128)(2,1)S(1)} %get-tuple-element.576.refs_0_), channel_id=1, source_target_pairs={{0,16},{4,20},{8,24},{12,28},{16,0},{20,4},{24,8},{28,12},{1,17},{... | collective-permute-start | bytes 1277960 | tf_op jit(solution)/shard_map/ppermute | solution.py:384
  53.3 30.4 %collective-permute-start.14 = (bf16[256,1664]{1,0:T(8,128)(2,1)S(1)}, bf16[256,1664]{1,0:T(8,128)(2,1)S(1)}, u32[]{:S(2)}, u32[]{:S(2)}) collective-permute-start(bf16[256,1664]{1,0:T(8,128)(2,1)S(1)} %shard_map.245.refs_0_), channel_id=1, source_target_pairs={{0,8},{4,12},{8,0},{12,4},{16,24},{20,28},{24,16},{28,20},{1,9},{5... | collective-permute-start | bytes 2555912 | tf_op jit(solution)/shard_map/ppermute | solution.py:384
  55.8 27.9 %collective-permute-start.13 = (bf16[256,1664]{1,0:T(8,128)(2,1)S(1)}, bf16[256,1664]{1,0:T(8,128)(2,1)S(1)}, u32[]{:S(2)}, u32[]{:S(2)}) collective-permute-start(bf16[256,1664]{1,0:T(8,128)(2,1)S(1)} %shard_map.244.refs_0_), channel_id=1, source_target_pairs={{0,16},{4,20},{8,24},{12,28},{16,0},{20,4},{24,8},{28,12},{1,17},{... | collective-permute-start | bytes 2555912 | tf_op jit(solution)/shard_map/ppermute | solution.py:384
  83.7 28.1 %collective-permute-start.16 = (bf16[256,2048]{1,0:T(8,128)(2,1)S(1)}, bf16[256,2048]{1,0:T(8,128)(2,1)S(1)}, u32[]{:S(2)}, u32[]{:S(2)}) collective-permute-start(bf16[256,2048]{1,0:T(8,128)(2,1)S(1)} %bitcast.246), channel_id=1, source_target_pairs={{0,1},{1,2},{2,3},{3,0},{4,5},{5,6},{6,7},{7,4},{8,9},{9,10},{10,1... | collective-permute-start | bytes 3145736 | tf_op jit(solution)/shard_map/ppermute | solution.py:379
  88.8 42.2 %collective-permute-start.23 = (bf16[512,1664]{1,0:T(8,128)(2,1)S(1)}, bf16[512,1664]{1,0:T(8,128)(2,1)S(1)}, u32[]{:S(2)}, u32[]{:S(2)}) collective-permute-start(bf16[512,1664]{1,0:T(8,128)(2,1)S(1)} %shard_map.251.refs_2_), channel_id=1, source_target_pairs={{0,4},{4,0},{8,12},{12,8},{16,20},{20,16},{24,28},{28,24},{1,5},{5... | collective-permute-start | bytes 5111816 | tf_op jit(solution)/shard_map/ppermute | solution.py:384
  89.5 43.2 %collective-permute-start.22 = (bf16[512,1664]{1,0:T(8,128)(2,1)S(1)}, bf16[512,1664]{1,0:T(8,128)(2,1)S(1)}, u32[]{:S(2)}, u32[]{:S(2)}) collective-permute-start(bf16[512,1664]{1,0:T(8,128)(2,1)S(1)} %shard_map.250.refs_0_), channel_id=1, source_target_pairs={{0,4},{4,0},{8,12},{12,8},{16,20},{20,16},{24,28},{28,24},{1,5},{5... | collective-permute-start | bytes 5111816 | tf_op jit(solution)/shard_map/ppermute | solution.py:384
  104.0 24.3 %collective-permute-start.20 = (bf16[256,2048]{1,0:T(8,128)(2,1)S(1)}, bf16[256,2048]{1,0:T(8,128)(2,1)S(1)}, u32[]{:S(2)}, u32[]{:S(2)}) collective-permute-start(bf16[256,2048]{1,0:T(8,128)(2,1)S(1)} %shard_map.248.refs_0_), channel_id=1, source_target_pairs={{0,16},{4,20},{8,24},{12,28},{16,0},{20,4},{24,8},{28,12},{1,17},{... | collective-permute-start | bytes 3145736 | tf_op jit(solution)/shard_map/ppermute | solution.py:384
  104.5 24.8 %collective-permute-start.21 = (bf16[256,2048]{1,0:T(8,128)(2,1)S(1)}, bf16[256,2048]{1,0:T(8,128)(2,1)S(1)}, u32[]{:S(2)}, u32[]{:S(2)}) collective-permute-start(bf16[256,2048]{1,0:T(8,128)(2,1)S(1)} %shard_map.249.refs_2_), channel_id=1, source_target_pairs={{0,8},{4,12},{8,0},{12,4},{16,24},{20,28},{24,16},{28,20},{1,9},{5... | collective-permute-start | bytes 3145736 | tf_op jit(solution)/shard_map/ppermute | solution.py:384
  111.9 26.2 %collective-permute-start.19 = (bf16[256,2048]{1,0:T(8,128)(2,1)S(1)}, bf16[256,2048]{1,0:T(8,128)(2,1)}, u32[]{:S(2)}, u32[]{:S(2)}) collective-permute-start(bf16[256,2048]{1,0:T(8,128)(2,1)S(1)} %collective-permute-done.16.refs_1_), channel_id=1, source_target_pairs={{0,1},{1,2},{2,3},{3,0},{4,5},{5,6},{6,7},{7,4},{8,9},{9,10},{10,1... | collective-permute-start | bytes 3145736 | tf_op jit(solution)/shard_map/ppermute | solution.py:379
  130.3 38.5 %collective-permute-start.25 = (bf16[512,1024]{1,0:T(8,128)(2,1)}, bf16[512,1024]{1,0:T(8,128)(2,1)}, u32[]{:S(2)}, u32[]{:S(2)}) collective-permute-start(bf16[512,1024]{1,0:T(8,128)(2,1)} %shard_map.252.refs_0_), channel_id=1, source_target_pairs={{0,16},{4,20},{8,24},{12,28},{16,0},{20,4},{24,8},{28,12},{1,17},{... | collective-permute-start | bytes 3145736 | tf_op jit(solution)/shard_map/ppermute | solution.py:384
  132.2 36.6 %collective-permute-start.26 = (bf16[512,1024]{1,0:T(8,128)(2,1)}, bf16[512,1024]{1,0:T(8,128)(2,1)}, u32[]{:S(2)}, u32[]{:S(2)}) collective-permute-start(bf16[512,1024]{1,0:T(8,128)(2,1)} %shard_map.253.refs_2_), channel_id=1, source_target_pairs={{0,8},{4,12},{8,0},{12,4},{16,24},{20,28},{24,16},{28,20},{1,9},{5... | collective-permute-start | bytes 3145736 | tf_op jit(solution)/shard_map/ppermute | solution.py:384
  138.1 30.8 %collective-permute-start.24 = (bf16[256,2048]{1,0:T(8,128)(2,1)}, bf16[256,2048]{1,0:T(8,128)(2,1)}, u32[]{:S(2)}, u32[]{:S(2)}) collective-permute-start(bf16[256,2048]{1,0:T(8,128)(2,1)} %collective-permute-done.19.refs_2_), channel_id=1, source_target_pairs={{0,1},{1,2},{2,3},{3,0},{4,5},{5,6},{6,7},{7,4},{8,9},{9,10},{10,1... | collective-permute-start | bytes 3145736 | tf_op jit(solution)/shard_map/ppermute | solution.py:379
  139.8 29.0 %collective-permute-start.27 = (bf16[256,1024]{1,0:T(8,128)(2,1)S(1)}, bf16[256,1024]{1,0:T(8,128)(2,1)}, u32[]{:S(2)}, u32[]{:S(2)}) collective-permute-start(bf16[256,1024]{1,0:T(8,128)(2,1)S(1)} %shard_map.254.refs_0_), channel_id=1, source_target_pairs={{0,8},{4,12},{8,0},{12,4},{16,24},{20,28},{24,16},{28,20},{1,9},{5... | collective-permute-start | bytes 1572872 | tf_op jit(solution)/shard_map/ppermute | solution.py:384
  140.4 28.4 %collective-permute-start.29 = (bf16[256,1024]{1,0:T(8,128)(2,1)}, bf16[256,1024]{1,0:T(8,128)(2,1)}, u32[]{:S(2)}, u32[]{:S(2)}) collective-permute-start(bf16[256,1024]{1,0:T(8,128)(2,1)} %collective-permute-done.28.refs_0_), channel_id=1, source_target_pairs={{0,16},{4,20},{8,24},{12,28},{16,0},{20,4},{24,8},{28,12},{1,17},{... | collective-permute-start | bytes 1572872 | tf_op jit(solution)/shard_map/ppermute | solution.py:384
  195.5 35.5 %collective-permute-start.39 = (bf16[512,1024]{1,0:T(8,128)(2,1)}, bf16[512,1024]{1,0:T(8,128)(2,1)}, u32[]{:S(2)}, u32[]{:S(2)}) collective-permute-start(bf16[512,1024]{1,0:T(8,128)(2,1)} %shard_map.263.refs_2_), channel_id=1, source_target_pairs={{0,8},{4,12},{8,0},{12,4},{16,24},{20,28},{24,16},{28,20},{1,9},{5... | collective-permute-start | bytes 3145736 | tf_op jit(solution)/shard_map/ppermute | solution.py:384
  196.1 35.0 %collective-permute-start.38 = (bf16[512,1024]{1,0:T(8,128)(2,1)}, bf16[512,1024]{1,0:T(8,128)(2,1)}, u32[]{:S(2)}, u32[]{:S(2)}) collective-permute-start(bf16[512,1024]{1,0:T(8,128)(2,1)} %shard_map.262.refs_0_), channel_id=1, source_target_pairs={{0,16},{4,20},{8,24},{12,28},{16,0},{20,4},{24,8},{28,12},{1,17},{... | collective-permute-start | bytes 3145736 | tf_op jit(solution)/shard_map/ppermute | solution.py:384
  208.7 22.3 %collective-permute-start.36 = (bf16[128,2048]{1,0:T(8,128)(2,1)}, bf16[128,2048]{1,0:T(8,128)(2,1)}, u32[]{:S(2)}, u32[]{:S(2)}) collective-permute-start(bf16[128,2048]{1,0:T(8,128)(2,1)} %get-tuple-element.573.refs_0_), channel_id=1, source_target_pairs={{0,8},{4,12},{8,0},{12,4},{16,24},{20,28},{24,16},{28,20},{1,9},{5... | collective-permute-start | bytes 1572872 | tf_op jit(solution)/shard_map/ppermute | solution.py:384
  209.2 21.8 %collective-permute-start.37 = (bf16[128,2048]{1,0:T(8,128)(2,1)}, bf16[128,2048]{1,0:T(8,128)(2,1)}, u32[]{:S(2)}, u32[]{:S(2)}) collective-permute-start(bf16[128,2048]{1,0:T(8,128)(2,1)} %get-tuple-element.572.refs_0_), channel_id=1, source_target_pairs={{0,16},{4,20},{8,24},{12,28},{16,0},{20,4},{24,8},{28,12},{1,17},{... | collective-permute-start | bytes 1572872 | tf_op jit(solution)/shard_map/ppermute | solution.py:384
  232.5 24.0 %collective-permute-start.44 = (bf16[256,2048]{1,0:T(8,128)(2,1)S(1)}, bf16[256,2048]{1,0:T(8,128)(2,1)S(1)}, u32[]{:S(2)}, u32[]{:S(2)}) collective-permute-start(bf16[256,2048]{1,0:T(8,128)(2,1)S(1)} %shard_map.265.refs_0_), channel_id=1, source_target_pairs={{0,8},{4,12},{8,0},{12,4},{16,24},{20,28},{24,16},{28,20},{1,9},{5... | collective-permute-start | bytes 3145736 | tf_op jit(solution)/shard_map/ppermute | solution.py:384
  235.4 22.7 %collective-permute-start.43 = (bf16[256,2048]{1,0:T(8,128)(2,1)S(1)}, bf16[256,2048]{1,0:T(8,128)(2,1)S(1)}, u32[]{:S(2)}, u32[]{:S(2)}) collective-permute-start(bf16[256,2048]{1,0:T(8,128)(2,1)S(1)} %shard_map.264.refs_0_), channel_id=1, source_target_pairs={{0,16},{4,20},{8,24},{12,28},{16,0},{20,4},{24,8},{28,12},{1,17},{... | collective-permute-start | bytes 3145736 | tf_op jit(solution)/shard_map/ppermute | solution.py:384
  271.8 30.7 %collective-permute-start.47 = (bf16[256,2048]{1,0:T(8,128)(2,1)S(1)}, bf16[256,2048]{1,0:T(8,128)(2,1)S(1)}, u32[]{:S(2)}, u32[]{:S(2)}) collective-permute-start(bf16[256,2048]{1,0:T(8,128)(2,1)S(1)} %fusion.14.refs_0_), channel_id=1, source_target_pairs={{0,1},{1,2},{2,3},{3,0},{4,5},{5,6},{6,7},{7,4},{8,9},{9,10},{10,1... | collective-permute-start | bytes 3145736 | tf_op jit(solution)/shard_map/ppermute | solution.py:379
  302.5 27.5 %collective-permute-start.50 = (bf16[256,2048]{1,0:T(8,128)(2,1)S(1)}, bf16[256,2048]{1,0:T(8,128)(2,1)S(1)}, u32[]{:S(2)}, u32[]{:S(2)}) collective-permute-start(bf16[256,2048]{1,0:T(8,128)(2,1)S(1)} %collective-permute-done.47.refs_0_), channel_id=1, source_target_pairs={{0,1},{1,2},{2,3},{3,0},{4,5},{5,6},{6,7},{7,4},{8,9},{9,10},{10,1... | collective-permute-start | bytes 3145736 | tf_op jit(solution)/shard_map/ppermute | solution.py:379
  333.2 27.8 %collective-permute-start.52 = (bf16[256,2048]{1,0:T(8,128)(2,1)S(1)}, bf16[256,2048]{1,0:T(8,128)(2,1)S(1)}, u32[]{:S(2)}, u32[]{:S(2)}) collective-permute-start(bf16[256,2048]{1,0:T(8,128)(2,1)S(1)} %collective-permute-done.50.refs_0_), channel_id=1, source_target_pairs={{0,1},{1,2},{2,3},{3,0},{4,5},{5,6},{6,7},{7,4},{8,9},{9,10},{10,1... | collective-permute-start | bytes 3145736 | tf_op jit(solution)/shard_map/ppermute | solution.py:379
  333.2 49.7 %collective-permute-start.55 = (bf16[256,2048]{1,0:T(8,128)(2,1)S(1)}, bf16[256,2048]{1,0:T(8,128)(2,1)S(1)}, u32[]{:S(2)}, u32[]{:S(2)}) collective-permute-start(bf16[256,2048]{1,0:T(8,128)(2,1)S(1)} %add_convert_fusion.7), channel_id=1, source_target_pairs={{0,1},{1,2},{2,3},{3,0},{4,5},{5,6},{6,7},{7,4},{8,9},{9,10},{10,1... | collective-permute-start | bytes 3145736 | tf_op jit(solution)/shard_map/ppermute | solution.py:379
  386.3 27.5 %collective-permute-start.59 = (bf16[256,2048]{1,0:T(8,128)(2,1)S(1)}, bf16[256,2048]{1,0:T(8,128)(2,1)S(1)}, u32[]{:S(2)}, u32[]{:S(2)}) collective-permute-start(bf16[256,2048]{1,0:T(8,128)(2,1)S(1)} %add_convert_fusion.6), channel_id=1, source_target_pairs={{0,1},{1,2},{2,3},{3,0},{4,5},{5,6},{6,7},{7,4},{8,9},{9,10},{10,1... | collective-permute-start | bytes 3145736 | tf_op jit(solution)/shard_map/ppermute | solution.py:379
  414.4 26.5 %collective-permute-start.60 = (bf16[256,2048]{1,0:T(8,128)(2,1)S(1)}, bf16[256,2048]{1,0:T(8,128)(2,1)S(1)}, u32[]{:S(2)}, u32[]{:S(2)}) collective-permute-start(bf16[256,2048]{1,0:T(8,128)(2,1)S(1)} %fusion.8), channel_id=1, source_target_pairs={{0,1},{1,2},{2,3},{3,0},{4,5},{5,6},{6,7},{7,4},{8,9},{9,10},{10,1... | collective-permute-start | bytes 3145736 | tf_op jit(solution)/shard_map/ppermute | solution.py:379
  414.4 26.4 %collective-permute-start.49 = (bf16[256,2048]{1,0:T(8,128)(2,1)}, bf16[256,2048]{1,0:T(8,128)(2,1)S(1)}, u32[]{:S(2)}, u32[]{:S(2)}) collective-permute-start(bf16[256,2048]{1,0:T(8,128)(2,1)} %slice.193), channel_id=1, source_target_pairs={{0,4},{4,0},{8,12},{12,8},{16,20},{20,16},{24,28},{28,24},{1,5},{5... | collective-permute-start | bytes 3145736 | tf_op jit(solution)/shard_map/ppermute | solution.py:384
  442.8 27.6 %collective-permute-start.61 = (bf16[256,2048]{1,0:T(8,128)(2,1)S(1)}, bf16[256,2048]{1,0:T(8,128)(2,1)S(1)}, u32[]{:S(2)}, u32[]{:S(2)}) collective-permute-start(bf16[256,2048]{1,0:T(8,128)(2,1)S(1)} %fusion.3.refs_0_), channel_id=1, source_target_pairs={{0,1},{1,2},{2,3},{3,0},{4,5},{5,6},{6,7},{7,4},{8,9},{9,10},{10,1... | collective-permute-start | bytes 3145736 | tf_op jit(solution)/shard_map/ppermute | solution.py:379
  470.5 27.9 %collective-permute-start.64 = (bf16[256,2048]{1,0:T(8,128)(2,1)S(1)}, bf16[256,2048]{1,0:T(8,128)(2,1)S(1)}, u32[]{:S(2)}, u32[]{:S(2)}) collective-permute-start(bf16[256,2048]{1,0:T(8,128)(2,1)S(1)} %collective-permute-done.61.refs_0_), channel_id=1, source_target_pairs={{0,1},{1,2},{2,3},{3,0},{4,5},{5,6},{6,7},{7,4},{8,9},{9,10},{10,1... | collective-permute-start | bytes 3145736 | tf_op jit(solution)/shard_map/ppermute | solution.py:379
  501.5 27.8 %collective-permute-start.66 = (bf16[256,2048]{1,0:T(8,128)(2,1)S(1)}, bf16[256,2048]{1,0:T(8,128)(2,1)S(1)}, u32[]{:S(2)}, u32[]{:S(2)}) collective-permute-start(bf16[256,2048]{1,0:T(8,128)(2,1)S(1)} %collective-permute-done.64.refs_0_), channel_id=1, source_target_pairs={{0,1},{1,2},{2,3},{3,0},{4,5},{5,6},{6,7},{7,4},{8,9},{9,10},{10,1... | collective-permute-start | bytes 3145736 | tf_op jit(solution)/shard_map/ppermute | solution.py:379
  501.5 49.7 %collective-permute-start.69 = (bf16[256,2048]{1,0:T(8,128)(2,1)S(1)}, bf16[256,2048]{1,0:T(8,128)(2,1)S(1)}, u32[]{:S(2)}, u32[]{:S(2)}) collective-permute-start(bf16[256,2048]{1,0:T(8,128)(2,1)S(1)} %add_convert_fusion.4), channel_id=1, source_target_pairs={{0,1},{1,2},{2,3},{3,0},{4,5},{5,6},{6,7},{7,4},{8,9},{9,10},{10,1... | collective-permute-start | bytes 3145736 | tf_op jit(solution)/shard_map/ppermute | solution.py:379
  554.6 27.2 %collective-permute-start.73 = (bf16[256,2048]{1,0:T(8,128)(2,1)S(1)}, bf16[256,2048]{1,0:T(8,128)(2,1)S(1)}, u32[]{:S(2)}, u32[]{:S(2)}) collective-permute-start(bf16[256,2048]{1,0:T(8,128)(2,1)S(1)} %add_convert_fusion.3), channel_id=1, source_target_pairs={{0,1},{1,2},{2,3},{3,0},{4,5},{5,6},{6,7},{7,4},{8,9},{9,10},{10,1... | collective-permute-start | bytes 3145736 | tf_op jit(solution)/shard_map/ppermute | solution.py:379
  583.9 26.8 %collective-permute-start.74 = (bf16[256,2048]{1,0:T(8,128)(2,1)S(1)}, bf16[256,2048]{1,0:T(8,128)(2,1)}, u32[]{:S(2)}, u32[]{:S(2)}) collective-permute-start(bf16[256,2048]{1,0:T(8,128)(2,1)S(1)} %add_convert_fusion.2), channel_id=1, source_target_pairs={{0,1},{1,2},{2,3},{3,0},{4,5},{5,6},{6,7},{7,4},{8,9},{9,10},{10,1... | collective-permute-start | bytes 3145736 | tf_op jit(solution)/shard_map/ppermute | solution.py:379
  584.2 30.7 %collective-permute-start.63 = (bf16[256,2048]{1,0:T(8,128)(2,1)}, bf16[256,2048]{1,0:T(8,128)(2,1)}, u32[]{:S(2)}, u32[]{:S(2)}) collective-permute-start(bf16[256,2048]{1,0:T(8,128)(2,1)} %slice.189), channel_id=1, source_target_pairs={{0,4},{4,0},{8,12},{12,8},{16,20},{20,16},{24,28},{28,24},{1,5},{5... | collective-permute-start | bytes 3145736 | tf_op jit(solution)/shard_map/ppermute | solution.py:384
  611.7 23.9 %collective-permute-start.75 = (bf16[2,512,512]{2,1,0:T(8,128)(2,1)}, bf16[2,512,512]{2,1,0:T(8,128)(2,1)S(1)}, u32[]{:S(2)}, u32[]{:S(2)}) collective-permute-start(bf16[2,512,512]{2,1,0:T(8,128)(2,1)} %dynamic-slice_bitcast_fusion.7), channel_id=1, source_target_pairs={{0,8},{4,12},{8,0},{12,4},{16,24},{20,28},{24,16},{28,20},{1,9},{5... | collective-permute-start | bytes 3145736 | tf_op jit(solution)/shard_map/ppermute | solution.py:384
  613.3 23.6 %collective-permute-start.76 = (bf16[2,512,512]{2,1,0:T(8,128)(2,1)}, bf16[2,512,512]{2,1,0:T(8,128)(2,1)S(1)}, u32[]{:S(2)}, u32[]{:S(2)}) collective-permute-start(bf16[2,512,512]{2,1,0:T(8,128)(2,1)} %dynamic-slice_bitcast_fusion.6), channel_id=1, source_target_pairs={{0,16},{4,20},{8,24},{12,28},{16,0},{20,4},{24,8},{28,12},{1,17},{... | collective-permute-start | bytes 3145736 | tf_op jit(solution)/shard_map/ppermute | solution.py:384
  640.4 26.2 %collective-permute-start.81 = (bf16[512,512]{1,0:T(8,128)(2,1)}, bf16[512,512]{1,0:T(8,128)(2,1)}, u32[]{:S(2)}, u32[]{:S(2)}) collective-permute-start(bf16[512,512]{1,0:T(8,128)(2,1)} %fusion.25), channel_id=1, source_target_pairs={{0,8},{4,12},{8,0},{12,4},{16,24},{20,28},{24,16},{28,20},{1,9},{5... | collective-permute-start | bytes 1572872 | tf_op jit(solution)/shard_map/ppermute | solution.py:384
  642.4 24.3 %collective-permute-start.80 = (bf16[512,512]{1,0:T(8,128)(2,1)S(1)}, bf16[512,512]{1,0:T(8,128)(2,1)S(1)}, u32[]{:S(2)}, u32[]{:S(2)}) collective-permute-start(bf16[512,512]{1,0:T(8,128)(2,1)S(1)} %fusion.24), channel_id=1, source_target_pairs={{0,16},{4,20},{8,24},{12,28},{16,0},{20,4},{24,8},{28,12},{1,17},{... | collective-permute-start | bytes 1572872 | tf_op jit(solution)/shard_map/ppermute | solution.py:384
  644.1 22.6 %collective-permute-start.77 = (bf16[256,512]{1,0:T(8,128)(2,1)S(1)}, bf16[256,512]{1,0:T(8,128)(2,1)S(1)}, u32[]{:S(2)}, u32[]{:S(2)}) collective-permute-start(bf16[256,512]{1,0:T(8,128)(2,1)S(1)} %get-tuple-element.420), channel_id=1, source_target_pairs={{0,1},{1,2},{2,3},{3,0},{4,5},{5,6},{6,7},{7,4},{8,9},{9,10},{10,1... | collective-permute-start | bytes 786440 | tf_op jit(solution)/shard_map/ppermute | solution.py:401
  644.1 22.6 %collective-permute-start.78 = (bf16[256,512]{1,0:T(8,128)(2,1)S(1)}, bf16[256,512]{1,0:T(8,128)(2,1)S(1)}, u32[]{:S(2)}, u32[]{:S(2)}) collective-permute-start(bf16[256,512]{1,0:T(8,128)(2,1)S(1)} %get-tuple-element.421), channel_id=1, source_target_pairs={{0,2},{1,3},{2,0},{3,1},{4,6},{5,7},{6,4},{7,5},{8,10},{9,11},{10,... | collective-permute-start | bytes 786440 | tf_op jit(solution)/shard_map/ppermute | solution.py:401
  644.1 22.6 %collective-permute-start.79 = (bf16[256,512]{1,0:T(8,128)(2,1)S(1)}, bf16[256,512]{1,0:T(8,128)(2,1)S(1)}, u32[]{:S(2)}, u32[]{:S(2)}) collective-permute-start(bf16[256,512]{1,0:T(8,128)(2,1)S(1)} %get-tuple-element.422), channel_id=1, source_target_pairs={{0,3},{1,0},{2,1},{3,2},{4,7},{5,4},{6,5},{7,6},{8,11},{9,8},{10,9... | collective-permute-start | bytes 786440 | tf_op jit(solution)/shard_map/ppermute | solution.py:401
  669.0 31.1 %collective-permute-start.86 = (bf16[2,512,512]{2,1,0:T(8,128)(2,1)}, bf16[2,512,512]{2,1,0:T(8,128)(2,1)S(1)}, u32[]{:S(2)}, u32[]{:S(2)}) collective-permute-start(bf16[2,512,512]{2,1,0:T(8,128)(2,1)} %dynamic-slice_bitcast_fusion.5), channel_id=1, source_target_pairs={{0,8},{4,12},{8,0},{12,4},{16,24},{20,28},{24,16},{28,20},{1,9},{5... | collective-permute-start | bytes 3145736 | tf_op jit(solution)/shard_map/ppermute | solution.py:384
  670.6 29.5 %collective-permute-start.87 = (bf16[2,512,512]{2,1,0:T(8,128)(2,1)}, bf16[2,512,512]{2,1,0:T(8,128)(2,1)}, u32[]{:S(2)}, u32[]{:S(2)}) collective-permute-start(bf16[2,512,512]{2,1,0:T(8,128)(2,1)} %dynamic-slice_bitcast_fusion.4), channel_id=1, source_target_pairs={{0,16},{4,20},{8,24},{12,28},{16,0},{20,4},{24,8},{28,12},{1,17},{... | collective-permute-start | bytes 3145736 | tf_op jit(solution)/shard_map/ppermute | solution.py:384
  673.3 26.7 %collective-permute-start.83 = (bf16[128,1024]{1,0:T(8,128)(2,1)S(1)}, bf16[128,1024]{1,0:T(8,128)(2,1)S(1)}, u32[]{:S(2)}, u32[]{:S(2)}) collective-permute-start(bf16[128,1024]{1,0:T(8,128)(2,1)S(1)} %get-tuple-element.439), channel_id=1, source_target_pairs={{0,1},{1,2},{2,3},{3,0},{4,5},{5,6},{6,7},{7,4},{8,9},{9,10},{10,1... | collective-permute-start | bytes 786440 | tf_op jit(solution)/shard_map/ppermute | solution.py:401
  674.3 25.7 %collective-permute-start.84 = (bf16[128,1024]{1,0:T(8,128)(2,1)S(1)}, bf16[128,1024]{1,0:T(8,128)(2,1)S(1)}, u32[]{:S(2)}, u32[]{:S(2)}) collective-permute-start(bf16[128,1024]{1,0:T(8,128)(2,1)S(1)} %get-tuple-element.440), channel_id=1, source_target_pairs={{0,2},{1,3},{2,0},{3,1},{4,6},{5,7},{6,4},{7,5},{8,10},{9,11},{10,... | collective-permute-start | bytes 786440 | tf_op jit(solution)/shard_map/ppermute | solution.py:401
  675.4 24.6 %collective-permute-start.85 = (bf16[128,1024]{1,0:T(8,128)(2,1)S(1)}, bf16[128,1024]{1,0:T(8,128)(2,1)S(1)}, u32[]{:S(2)}, u32[]{:S(2)}) collective-permute-start(bf16[128,1024]{1,0:T(8,128)(2,1)S(1)} %get-tuple-element.441), channel_id=1, source_target_pairs={{0,3},{1,0},{2,1},{3,2},{4,7},{5,4},{6,5},{7,6},{8,11},{9,8},{10,9... | collective-permute-start | bytes 786440 | tf_op jit(solution)/shard_map/ppermute | solution.py:401
  723.7 27.7 %collective-permute-start.93 = (bf16[2,2,256,1024]{3,2,0,1:T(8,128)(2,1)}, bf16[2,2,256,1024]{3,2,0,1:T(8,128)(2,1)}, u32[]{:S(2)}, u32[]{:S(2)}) collective-permute-start(bf16[2,2,256,1024]{3,2,0,1:T(8,128)(2,1)} %copy_bitcast_fusion), channel_id=1, source_target_pairs={{0,4},{4,0},{8,12},{12,8},{16,20},{20,16},{24,28},{28,24},{1,5},{5... | collective-permute-start | bytes 6291464 | tf_op jit(solution)/shard_map/ppermute | solution.py:384
  725.2 26.2 %collective-permute-start.94 = (bf16[2,2,256,1024]{3,2,1,0:T(8,128)(2,1)}, bf16[2,2,256,1024]{3,2,1,0:T(8,128)(2,1)}, u32[]{:S(2)}, u32[]{:S(2)}) collective-permute-start(bf16[2,2,256,1024]{3,2,1,0:T(8,128)(2,1)} %dynamic-slice_bitcast_fusion), channel_id=1, source_target_pairs={{0,4},{4,0},{8,12},{12,8},{16,20},{20,16},{24,28},{28,24},{1,5},{5... | collective-permute-start | bytes 6291464 | tf_op jit(solution)/shard_map/ppermute | solution.py:384
  748.8 19.7 %collective-permute-start.97 = (bf16[128,1024]{1,0:T(8,128)(2,1)S(1)}, bf16[128,1024]{1,0:T(8,128)(2,1)S(1)}, u32[]{:S(2)}, u32[]{:S(2)}) collective-permute-start(bf16[128,1024]{1,0:T(8,128)(2,1)S(1)} %get-tuple-element.470), channel_id=1, source_target_pairs={{0,2},{1,3},{2,0},{3,1},{4,6},{5,7},{6,4},{7,5},{8,10},{9,11},{10,... | collective-permute-start | bytes 786440 | tf_op jit(solution)/shard_map/ppermute | solution.py:401
  768.5 25.2 %collective-permute-start.100 = (bf16[2,256,1024]{2,1,0:T(8,128)(2,1)}, bf16[2,256,1024]{2,1,0:T(8,128)(2,1)S(1)}, u32[]{:S(2)}, u32[]{:S(2)}) collective-permute-start(bf16[2,256,1024]{2,1,0:T(8,128)(2,1)} %fusion.16), channel_id=1, source_target_pairs={{0,8},{4,12},{8,0},{12,4},{16,24},{20,28},{24,16},{28,20},{1,9},{5... | collective-permute-start | bytes 3145736 | tf_op jit(solution)/shard_map/ppermute | solution.py:384
  769.1 24.9 %collective-permute-start.101 = (bf16[2,256,1024]{2,1,0:T(8,128)(2,1)}, bf16[2,256,1024]{2,1,0:T(8,128)(2,1)S(1)}, u32[]{:S(2)}, u32[]{:S(2)}) collective-permute-start(bf16[2,256,1024]{2,1,0:T(8,128)(2,1)} %fusion.17), channel_id=1, source_target_pairs={{0,16},{4,20},{8,24},{12,28},{16,0},{20,4},{24,8},{28,12},{1,17},{... | collective-permute-start | bytes 3145736 | tf_op jit(solution)/shard_map/ppermute | solution.py:384
  769.7 28.9 %collective-permute-start.99 = (bf16[256,2048]{1,0:T(8,128)(2,1)}, bf16[256,2048]{1,0:T(8,128)(2,1)S(1)}, u32[]{:S(2)}, u32[]{:S(2)}) collective-permute-start(bf16[256,2048]{1,0:T(8,128)(2,1)} %convolution_convert_fusion), channel_id=1, source_target_pairs={{0,1},{1,2},{2,3},{3,0},{4,5},{5,6},{6,7},{7,4},{8,9},{9,10},{10,1... | collective-permute-start | bytes 3145736 | tf_op jit(solution)/shard_map/ppermute | solution.py:379
  806.2 24.6 %collective-permute-start.104 = (bf16[256,1024]{1,0:T(8,128)(2,1)}, bf16[256,1024]{1,0:T(8,128)(2,1)}, u32[]{:S(2)}, u32[]{:S(2)}) collective-permute-start(bf16[256,1024]{1,0:T(8,128)(2,1)} %fusion.29), channel_id=1, source_target_pairs={{0,8},{4,12},{8,0},{12,4},{16,24},{20,28},{24,16},{28,20},{1,9},{5... | collective-permute-start | bytes 1572872 | tf_op jit(solution)/shard_map/ppermute | solution.py:384
  812.1 31.7 %collective-permute-start.105 = (bf16[2,2,256,768]{3,2,0,1:T(8,128)(2,1)}, bf16[2,2,256,768]{3,2,0,1:T(8,128)(2,1)}, u32[]{:S(2)}, u32[]{:S(2)}) collective-permute-start(bf16[2,2,256,768]{3,2,0,1:T(8,128)(2,1)} %copy_bitcast_fusion.1), channel_id=1, source_target_pairs={{0,4},{4,0},{8,12},{12,8},{16,20},{20,16},{24,28},{28,24},{1,5},{5... | collective-permute-start | bytes 4718600 | tf_op jit(solution)/shard_map/ppermute | solution.py:384
  814.6 29.2 %collective-permute-start.106 = (bf16[2,2,256,768]{3,2,1,0:T(8,128)(2,1)}, bf16[2,2,256,768]{3,2,1,0:T(8,128)(2,1)}, u32[]{:S(2)}, u32[]{:S(2)}) collective-permute-start(bf16[2,2,256,768]{3,2,1,0:T(8,128)(2,1)} %dynamic-slice_bitcast_fusion.1), channel_id=1, source_target_pairs={{0,4},{4,0},{8,12},{12,8},{16,20},{20,16},{24,28},{28,24},{1,5},{5... | collective-permute-start | bytes 4718600 | tf_op jit(solution)/shard_map/ppermute | solution.py:384
  816.6 27.2 %collective-permute-start.102 = (bf16[256,2048]{1,0:T(8,128)(2,1)}, bf16[256,2048]{1,0:T(8,128)(2,1)}, u32[]{:S(2)}, u32[]{:S(2)}) collective-permute-start(bf16[256,2048]{1,0:T(8,128)(2,1)} %add_convert_fusion.1), channel_id=1, source_target_pairs={{0,1},{1,2},{2,3},{3,0},{4,5},{5,6},{6,7},{7,4},{8,9},{9,10},{10,1... | collective-permute-start | bytes 3145736 | tf_op jit(solution)/shard_map/ppermute | solution.py:379
  847.0 28.4 %collective-permute-start.109 = (bf16[2,256,768]{2,1,0:T(8,128)(2,1)}, bf16[2,256,768]{2,1,0:T(8,128)(2,1)}, u32[]{:S(2)}, u32[]{:S(2)}) collective-permute-start(bf16[2,256,768]{2,1,0:T(8,128)(2,1)} %fusion.23), channel_id=1, source_target_pairs={{0,16},{4,20},{8,24},{12,28},{16,0},{20,4},{24,8},{28,12},{1,17},{... | collective-permute-start | bytes 2359304 | tf_op jit(solution)/shard_map/ppermute | solution.py:384
  851.4 24.1 %collective-permute-start.108 = (bf16[2,256,768]{2,1,0:T(8,128)(2,1)}, bf16[2,256,768]{2,1,0:T(8,128)(2,1)}, u32[]{:S(2)}, u32[]{:S(2)}) collective-permute-start(bf16[2,256,768]{2,1,0:T(8,128)(2,1)} %fusion.22), channel_id=1, source_target_pairs={{0,8},{4,12},{8,0},{12,4},{16,24},{20,28},{24,16},{28,20},{1,9},{5... | collective-permute-start | bytes 2359304 | tf_op jit(solution)/shard_map/ppermute | solution.py:384
  853.5 25.7 %collective-permute-start.107 = (bf16[256,2048]{1,0:T(8,128)(2,1)S(1)}, bf16[256,2048]{1,0:T(8,128)(2,1)S(1)}, u32[]{:S(2)}, u32[]{:S(2)}) collective-permute-start(bf16[256,2048]{1,0:T(8,128)(2,1)S(1)} %add_convert_fusion), channel_id=1, source_target_pairs={{0,1},{1,2},{2,3},{3,0},{4,5},{5,6},{6,7},{7,4},{8,9},{9,10},{10,1... | collective-permute-start | bytes 3145736 | tf_op jit(solution)/shard_map/ppermute | solution.py:379
  894.9 23.0 %collective-permute-start.124 = (bf16[2,256,1024]{2,1,0:T(8,128)(2,1)}, bf16[2,256,1024]{2,1,0:T(8,128)(2,1)}, u32[]{:S(2)}, u32[]{:S(2)}) collective-permute-start(bf16[2,256,1024]{2,1,0:T(8,128)(2,1)} %dynamic-slice_bitcast_fusion.3), channel_id=1, source_target_pairs={{0,8},{4,12},{8,0},{12,4},{16,24},{20,28},{24,16},{28,20},{1,9},{5... | collective-permute-start | bytes 3145736 | tf_op jit(solution)/shard_map/ppermute | solution.py:384
  897.6 23.5 %collective-permute-start.126 = (bf16[2,256,1024]{2,1,0:T(8,128)(2,1)S(1)}, bf16[2,256,1024]{2,1,0:T(8,128)(2,1)S(1)}, u32[]{:S(2)}, u32[]{:S(2)}) collective-permute-start(bf16[2,256,1024]{2,1,0:T(8,128)(2,1)S(1)} %dynamic-slice_bitcast_fusion.2), channel_id=1, source_target_pairs={{0,16},{4,20},{8,24},{12,28},{16,0},{20,4},{24,8},{28,12},{1,17},{... | collective-permute-start | bytes 3145736 | tf_op jit(solution)/shard_map/ppermute | solution.py:384
  (207 other events, 1496.6 us)

commit v7 on v6

--- a/solution.py
+++ b/solution.py
@@ -711,9 +711,8 @@
             cube_qkv.set(more)
         elif at == size - 2:
             cube_up.step()
-            x_next, new, more, w_out_own = together(x_next, cube_gate.new, cube_up.new, w_out)
+            x_next, new, w_out_own = together(x_next, cube_gate.new, w_out)
             cube_gate.set(new)
-            cube_up.set(more)
         x_slots.append(x_next)
     cube_qkv.finish()
     w_qkv, gains = cube_join(
@@ -721,17 +720,16 @@
     )
 
     x_all = in_order(x_slots, "seq")
-    out_got = share_out(w_out_own, "seq")
-    cube_up.step()
     qkv = product(x_all, w_qkv)
     squares = jnp.stack([jnp.sum(jnp.square(qkv[:, first : first + part]), -1) for first in (0, part)], 0)
     squares = small_sum(squares, "seq")
     gains = gains[:, :4].T.astype(f32)
     gain_attn, gain_ffn = gains[2], gains[3]
     gain_qk = lax.dynamic_slice_in_dim(gains[:2], here * part, part, 1)
-    squares, out_got, gain_qk = together(squares, out_got, gain_qk)
-    cube_out = CubeGather(two_parts(out_got), core=True)
-    cube_out.step()
+    squares, gain_qk, w_out_own, new = together(squares, gain_qk, w_out_own, cube_up.new)
+    cube_up.set(new)
+    out_got = share_out(w_out_own, "seq")
+    cube_up.step()
     squares = squares.T
     query, key, value = query_key(qkv, squares, cosine, sine_tab, gain_qk, width)
     seg_ids = segments.reshape(total_len)
@@ -742,10 +740,12 @@
         bf16,
         lambda: [((0, part_row(behind(ahead)), 0), (ahead, 0, 0), (rows, part)) for ahead in slots],
     )
-    attended, new, more = together(attended, cube_out.new, cube_up.new)
-    cube_out.set(new)
-    cube_up.set(more)
+    attended, out_got, new = together(attended, out_got, cube_up.new)
+    cube_up.set(new)
     attended = send_ahead(attended, "seq")
+    cube_out = CubeGather(two_parts(out_got), core=True)
+    cube_out.step()
+    cube_out.set(cube_out.new)
     cube_out.step()
     for cube in (cube_down, cube_gate, cube_up):
         cube.finish()

time: 942 us -> 929 us (0.986)
  starting transfers between devices: 148 us -> 138 us
    unnamed x285 -> x297, local copies, waits for them, and re-layouts: 39.4 us -> 42.4 us
  transfers between devices with their start and end apart: 128 -> 128, of which waited for: 62 -> 64; matrix products, arithmetic and copies ran while one was open for 15% -> 15% of each run, Pallas kernels for 20% -> 20%
where the time goes in v7:
time: 929 us; the launch traced here: 922 us
  waiting for transfers between devices  376 us (40%)
  Pallas kernels  191 us (21%)
  starting transfers between devices  138 us (15%)
  matrix products  81.2 us (9%)
  local copies, waits for them, and re-layouts  76.3 us (8%)
  other arithmetic  56.5 us (6%)
    ppermute x18, waiting for transfers between devices, next_one(): return lax.ppermute(block, axis, [(i, (i + 1) % size) for i in range(size)])  212 us
    ppermute x71, waiting for transfers between devices, flipped(): return lax.ppermute(block, 'dp', [(i, i ^ bit) for i in range(size)])  106 us
    pallas_call x40, Pallas kernels, assemble(): pl.pallas_call(functools.partial(assemble_body, parts, places, len(pieces...  60.7 us
    ppermute x27, starting transfers between devices, send_ahead(): lax.ppermute(blocks[step], axis, [(i, (i + step) % size) for i in range(s...  57.8 us
    pallas_call x5, Pallas kernels, grad_halves(): pl.pallas_call(grad_halves_body, grid=(depth // block,), in_specs=[vmem((...  56.6 us
    ppermute x27, waiting for transfers between devices, send_ahead(): lax.ppermute(blocks[step], axis, [(i, (i + step) % size) for i in range(s...  54 us
    ppermute x71, starting transfers between devices, flipped(): return lax.ppermute(block, 'dp', [(i, i ^ bit) for i in range(size)])  47.1 us
    dot_general x14, matrix products, product(): return jnp.dot(left, right, preferred_element_type=f32)  43.4 us
  transfers between devices with their start and end apart: 128, of which 64 were waited for; matrix products, arithmetic and copies ran while one was open for 15% of the time, Pallas kernels for 20%

profile of v7, /device:TPU:0, one launch (start us, length us, event | category | flops | bytes accessed | tf_op | source)
XLA Modules:
  0.0 922.5 jit_solution(13116179599305529003)
XLA Ops:
  14.7 4.2 collective-permute-done.refs_1_
  19.0 7.4 collective-permute-done.1.refs_2_
  30.7 5.0 collective-permute-start.5
  38.1 6.0 collective-permute-done.5.refs_1_
  44.1 8.3 collective-permute-done.6.refs_2_
  57.4 6.1 collective-permute-start.10
  68.1 4.6 collective-permute-done.10.refs_1_
  75.1 6.9 collective-permute-done.11.refs_2_
  83.8 4.5 collective-permute-start.16
  91.6 12.4 %collective-permute-done.17.refs_1_ = bf16[256,1024]{1,0:T(8,128)(2,1)S(1)} collective-permute-done((bf16[256,1024]{1,0:T(8,128)(2,1)S(1)}, bf16[256,1024]{1,0:T(8,128)(2,1)S(1)}, u32[]{:S(2)}, u32[]{:S(2)}) %collective-permute-start.17) | collective-permute-done | bytes 524320 | tf_op jit(solution)/shard_map/ppermute | solution.py:384
  105.8 6.1 collective-permute-done.16.refs_1_
  118.1 10.2 %collective-permute-done.20.refs_1_ = bf16[256,2048]{1,0:T(8,128)(2,1)S(1)} collective-permute-done((bf16[256,2048]{1,0:T(8,128)(2,1)S(1)}, bf16[256,2048]{1,0:T(8,128)(2,1)S(1)}, u32[]{:S(2)}, u32[]{:S(2)}) %collective-permute-start.20) | collective-permute-done | bytes 1048608 | tf_op jit(solution)/shard_map/ppermute | solution.py:384
  133.8 4.3 collective-permute-done.19.refs_2_
  149.3 4.7 shard_map.255
  158.6 5.3 collective-permute-done.24.refs_3_
  169.6 6.6 fusion.46.raw_ref
  193.0 4.5 shard_map.258
  197.6 13.9 %shard_map.259.refs_0_ = bf16[1024,512]{1,0:T(8,128)(2,1)S(1)} custom-call(bf16[1024,512]{1,0:T(8,128)(2,1)S(1)} %get-tuple-element.341.q_ref, bf16[1024,512]{1,0:T(8,128)(2,1)S(1)} %get-tuple-element.342.k_ref, bf16[1024,512]{1,0:T(8,128)(2,1)S(1)} %get-tuple-element.343.v_ref, s32[1,1024]{1,0:T(1,128)S(1)} %copy-done.72, s32[1024,1]{1,0:T(8,128)S(1)} %copy.67.seg_k_ref), custom_call_target="tpu_custom_call" | custom-call | tf_op jit(solution)/shard_map/pallas_call | solution.py:241
  217.0 8.5 collective-permute-done.43.refs_1_
  261.0 3.5 collective-permute-start.47
  267.8 3.9 multiply_convert_fusion.9
  277.2 12.6 %collective-permute-done.47.refs_0_ = bf16[256,2048]{1,0:T(8,128)(2,1)S(1)} collective-permute-done((bf16[256,2048]{1,0:T(8,128)(2,1)S(1)}, bf16[256,2048]{1,0:T(8,128)(2,1)S(1)}, u32[]{:S(2)}, u32[]{:S(2)}) %collective-permute-start.47) | collective-permute-done | bytes 1048608 | tf_op jit(solution)/shard_map/ppermute | solution.py:379
  295.2 3.8 multiply_convert_fusion.8
  301.8 15.6 %collective-permute-done.50.refs_0_ = bf16[256,2048]{1,0:T(8,128)(2,1)S(1)} collective-permute-done((bf16[256,2048]{1,0:T(8,128)(2,1)S(1)}, bf16[256,2048]{1,0:T(8,128)(2,1)S(1)}, u32[]{:S(2)}, u32[]{:S(2)}) %collective-permute-start.50) | collective-permute-done | bytes 1048608 | tf_op jit(solution)/shard_map/ppermute | solution.py:379
  325.8 3.8 multiply_convert_fusion.7
  333.4 15.0 %collective-permute-done.52.refs_0_ = bf16[256,2048]{1,0:T(8,128)(2,1)S(1)} collective-permute-done((bf16[256,2048]{1,0:T(8,128)(2,1)S(1)}, bf16[256,2048]{1,0:T(8,128)(2,1)S(1)}, u32[]{:S(2)}, u32[]{:S(2)}) %collective-permute-start.52) | collective-permute-done | bytes 1048608 | tf_op jit(solution)/shard_map/ppermute | solution.py:379
  348.3 21.9 %collective-permute-done.55 = bf16[256,2048]{1,0:T(8,128)(2,1)S(1)} collective-permute-done((bf16[256,2048]{1,0:T(8,128)(2,1)S(1)}, bf16[256,2048]{1,0:T(8,128)(2,1)S(1)}, u32[]{:S(2)}, u32[]{:S(2)}) %collective-permute-start.55) | collective-permute-done | bytes 1048608 | tf_op jit(solution)/shard_map/ppermute | solution.py:379
  378.9 3.8 multiply_convert_fusion.6
  385.4 15.7 %collective-permute-done.59 = bf16[256,2048]{1,0:T(8,128)(2,1)S(1)} collective-permute-done((bf16[256,2048]{1,0:T(8,128)(2,1)S(1)}, bf16[256,2048]{1,0:T(8,128)(2,1)S(1)}, u32[]{:S(2)}, u32[]{:S(2)}) %collective-permute-start.59) | collective-permute-done | bytes 1048608 | tf_op jit(solution)/shard_map/ppermute | solution.py:379
  401.8 7.1 shard_map.277.left_ref
  408.9 19.2 %collective-permute-done.60 = bf16[256,2048]{1,0:T(8,128)(2,1)S(1)} collective-permute-done((bf16[256,2048]{1,0:T(8,128)(2,1)S(1)}, bf16[256,2048]{1,0:T(8,128)(2,1)S(1)}, u32[]{:S(2)}, u32[]{:S(2)}) %collective-permute-start.60) | collective-permute-done | bytes 1048608 | tf_op jit(solution)/shard_map/ppermute | solution.py:379
  444.7 13.1 %collective-permute-done.61.refs_0_ = bf16[256,2048]{1,0:T(8,128)(2,1)S(1)} collective-permute-done((bf16[256,2048]{1,0:T(8,128)(2,1)S(1)}, bf16[256,2048]{1,0:T(8,128)(2,1)S(1)}, u32[]{:S(2)}, u32[]{:S(2)}) %collective-permute-start.61) | collective-permute-done | bytes 1048608 | tf_op jit(solution)/shard_map/ppermute | solution.py:379
  469.0 16.6 %collective-permute-done.64.refs_0_ = bf16[256,2048]{1,0:T(8,128)(2,1)S(1)} collective-permute-done((bf16[256,2048]{1,0:T(8,128)(2,1)S(1)}, bf16[256,2048]{1,0:T(8,128)(2,1)S(1)}, u32[]{:S(2)}, u32[]{:S(2)}) %collective-permute-start.64) | collective-permute-done | bytes 1048608 | tf_op jit(solution)/shard_map/ppermute | solution.py:379
  499.8 16.8 %collective-permute-done.66.refs_0_ = bf16[256,2048]{1,0:T(8,128)(2,1)S(1)} collective-permute-done((bf16[256,2048]{1,0:T(8,128)(2,1)S(1)}, bf16[256,2048]{1,0:T(8,128)(2,1)S(1)}, u32[]{:S(2)}, u32[]{:S(2)}) %collective-permute-start.66) | collective-permute-done | bytes 1048608 | tf_op jit(solution)/shard_map/ppermute | solution.py:379
  516.6 21.9 %collective-permute-done.69 = bf16[256,2048]{1,0:T(8,128)(2,1)S(1)} collective-permute-done((bf16[256,2048]{1,0:T(8,128)(2,1)S(1)}, bf16[256,2048]{1,0:T(8,128)(2,1)S(1)}, u32[]{:S(2)}, u32[]{:S(2)}) %collective-permute-start.69) | collective-permute-done | bytes 1048608 | tf_op jit(solution)/shard_map/ppermute | solution.py:379
  544.7 14.5 %shard_map.282 = (bf16[512,1024]{1,0:T(8,128)(2,1)S(1)}, bf16[512,1024]{1,0:T(8,128)(2,1)S(1)}, f32[512,2048]{1,0:T(8,128)}) custom-call(bf16[512,2048]{1,0:T(8,128)(2,1)S(1)} %shard_map.281.left_ref.refs_3_, bf16[1024,2048]{1,0:T(8,128)(2,1)} %copy-done.16, f32[512,1024]{1,0:T(8,128)} %copy-done.133, f32[512,1024]{1,0:T(8,128)} %get-tuple-element.597.up_ref, ...), custom_call_target="tpu_custom_call" | custom-call | flops 6442450944 | bytes 12582912 | tf_op jit(solution)/shard_map/pallas_call | solution.py:157
  562.0 7.1 collective-permute-done.73
  571.6 3.3 shard_map.286.right_ref
  574.9 3.3 shard_map.283.right_ref
  578.2 13.0 %shard_map.284 = (bf16[2048,512]{1,0:T(8,128)(2,1)S(1)}, bf16[2048,512]{1,0:T(8,128)(2,1)S(1)}) custom-call(bf16[2048,2048]{1,0:T(8,128)(2,1)} %shard_map.277.left_ref, bf16[2048,1024]{1,0:T(8,128)(2,1)} %shard_map.283.right_ref), custom_call_target="tpu_custom_call" | custom-call | flops 8589934592 | bytes 16777216 | tf_op jit(solution)/shard_map/pallas_call | solution.py:193
  591.3 6.7 collective-permute-done.74
  611.2 11.7 %collective-permute-done.75 = bf16[2,512,512]{2,1,0:T(8,128)(2,1)S(1)} collective-permute-done((bf16[2,512,512]{2,1,0:T(8,128)(2,1)}, bf16[2,512,512]{2,1,0:T(8,128)(2,1)S(1)}, u32[]{:S(2)}, u32[]{:S(2)}) %collective-permute-start.75) | collective-permute-done | bytes 1048608 | tf_op jit(solution)/shard_map/ppermute | solution.py:384
  630.5 3.8 collective-permute-start.79
  634.3 12.9 %shard_map.288 = (bf16[2048,512]{1,0:T(8,128)(2,1)S(1)}, bf16[2048,512]{1,0:T(8,128)(2,1)S(1)}) custom-call(bf16[2048,2048]{1,0:T(8,128)(2,1)} %shard_map.277.left_ref, bf16[2048,1024]{1,0:T(8,128)(2,1)} %shard_map.286.right_ref), custom_call_target="tpu_custom_call" | custom-call | flops 8589934592 | bytes 16777216 | tf_op jit(solution)/shard_map/pallas_call | solution.py:193
  647.2 5.9 shard_map.287
  667.4 20.1 %shard_map.290 = (bf16[1024,512]{1,0:T(8,128)(2,1)S(1)}, bf16[1024,512]{1,0:T(8,128)(2,1)S(1)}, bf16[1024,512]{1,0:T(8,128)(2,1)S(1)}) custom-call(bf16[1024,512]{1,0:T(8,128)(2,1)S(1)} %copy-done.27, bf16[1024,512]{1,0:T(8,128)(2,1)S(1)} %copy-done.29, bf16[1024,512]{1,0:T(8,128)(2,1)} %copy-done.30, bf16[1024,512]{1,0:T(8,128)(2,1)} %copy-done.25, ...), custom_call_target="tpu_custom_call" | custom-call | tf_op jit(solution)/shard_map/pallas_call | solution.py:285
  694.3 6.2 shard_map.292
  716.2 3.3 shard_map.297.left_ref
  723.8 6.1 shard_map.293.refs_0_.right_ref
  737.8 3.3 convert_add_fusion
  741.3 4.3 convert_add_fusion.1
  750.7 4.2 collective-permute-done.97.refs_2_
  757.2 6.1 collective-permute-start.99
  768.0 11.6 %shard_map.296 = (bf16[2048,768]{1,0:T(8,128)(2,1)S(1)}, bf16[2048,768]{1,0:T(8,128)(2,1)}) custom-call(bf16[1024,2048]{1,0:T(8,128)(2,1)} %copy-done.15, bf16[1024,1536]{1,0:T(8,128)(2,1)} %shard_map.293.refs_0_.right_ref), custom_call_target="tpu_custom_call" | custom-call | flops 6442450944 | bytes 8388608 | tf_op jit(solution)/shard_map/pallas_call | solution.py:193
  781.6 4.6 collective-permute-done.99
  817.1 8.1 collective-permute-done.103
  825.2 5.6 collective-permute-done.102
  841.3 7.1 shard_map.298.right_ref
  849.7 13.3 %shard_map.299 = (bf16[1024,1024]{1,0:T(8,128)(2,1)S(1)}, bf16[1024,1024]{1,0:T(8,128)(2,1)S(1)}) custom-call(bf16[2048,1024]{1,0:T(8,128)(2,1)} %shard_map.297.left_ref, bf16[2048,2048]{1,0:T(8,128)(2,1)} %shard_map.298.right_ref), custom_call_target="tpu_custom_call" | custom-call | flops 8589934592 | bytes 8388608 | tf_op jit(solution)/shard_map/pallas_call | solution.py:193
  863.0 3.8 collective-permute-done.107
  874.8 3.4 collective-permute-start.114
  887.1 6.0 collective-permute-done.113
  893.1 9.4 %collective-permute-start.115 = (bf16[64,1536]{1,0:T(8,128)(2,1)S(1)}, bf16[64,1536]{1,0:T(8,128)(2,1)S(1)}, u32[]{:S(2)}, u32[]{:S(2)}) collective-permute-start(bf16[64,1536]{1,0:T(8,128)(2,1)S(1)} %get-tuple-element.528), channel_id=1, source_target_pairs={{0,1},{1,2},{2,3},{3,0},{4,5},{5,6},{6,7},{7,4},{8,9},{9,10},{10,1... | collective-permute-start | bytes 589832 | tf_op jit(solution)/shard_map/ppermute | solution.py:401
  915.7 3.4 collective-permute-done.125
  (711 shorter events, 382.8 us)
Async XLA Ops:
  2.1 24.3 %collective-permute-start.3 = (bf16[128,2048]{1,0:T(8,128)(2,1)S(1)}, bf16[128,2048]{1,0:T(8,128)(2,1)S(1)}, u32[]{:S(2)}, u32[]{:S(2)}) collective-permute-start(bf16[128,2048]{1,0:T(8,128)(2,1)S(1)} %get-tuple-element.573.refs_0_), channel_id=1, source_target_pairs={{0,8},{4,12},{8,0},{12,4},{16,24},{20,28},{24,16},{28,20},{1,9},{5... | collective-permute-start | bytes 1572872 | tf_op jit(solution)/shard_map/ppermute | solution.py:384
  5.1 22.1 %collective-permute-start.4 = (bf16[128,2048]{1,0:T(8,128)(2,1)S(1)}, bf16[128,2048]{1,0:T(8,128)(2,1)S(1)}, u32[]{:S(2)}, u32[]{:S(2)}) collective-permute-start(bf16[128,2048]{1,0:T(8,128)(2,1)S(1)} %get-tuple-element.572.refs_0_), channel_id=1, source_target_pairs={{0,16},{4,20},{8,24},{12,28},{16,0},{20,4},{24,8},{28,12},{1,17},{... | collective-permute-start | bytes 1572872 | tf_op jit(solution)/shard_map/ppermute | solution.py:384
  29.6 22.8 %collective-permute-start.8 = (bf16[128,1664]{1,0:T(8,128)(2,1)S(1)}, bf16[128,1664]{1,0:T(8,128)(2,1)S(1)}, u32[]{:S(2)}, u32[]{:S(2)}) collective-permute-start(bf16[128,1664]{1,0:T(8,128)(2,1)S(1)} %get-tuple-element.575.refs_0_), channel_id=1, source_target_pairs={{0,8},{4,12},{8,0},{12,4},{16,24},{20,28},{24,16},{28,20},{1,9},{5... | collective-permute-start | bytes 1277960 | tf_op jit(solution)/shard_map/ppermute | solution.py:384
  30.2 22.2 %collective-permute-start.9 = (bf16[128,1664]{1,0:T(8,128)(2,1)S(1)}, bf16[128,1664]{1,0:T(8,128)(2,1)S(1)}, u32[]{:S(2)}, u32[]{:S(2)}) collective-permute-start(bf16[128,1664]{1,0:T(8,128)(2,1)S(1)} %get-tuple-element.574.refs_0_), channel_id=1, source_target_pairs={{0,16},{4,20},{8,24},{12,28},{16,0},{20,4},{24,8},{28,12},{1,17},{... | collective-permute-start | bytes 1277960 | tf_op jit(solution)/shard_map/ppermute | solution.py:384
  53.3 30.4 %collective-permute-start.14 = (bf16[256,1664]{1,0:T(8,128)(2,1)S(1)}, bf16[256,1664]{1,0:T(8,128)(2,1)S(1)}, u32[]{:S(2)}, u32[]{:S(2)}) collective-permute-start(bf16[256,1664]{1,0:T(8,128)(2,1)S(1)} %shard_map.245.refs_0_), channel_id=1, source_target_pairs={{0,8},{4,12},{8,0},{12,4},{16,24},{20,28},{24,16},{28,20},{1,9},{5... | collective-permute-start | bytes 2555912 | tf_op jit(solution)/shard_map/ppermute | solution.py:384
  55.9 27.9 %collective-permute-start.13 = (bf16[256,1664]{1,0:T(8,128)(2,1)S(1)}, bf16[256,1664]{1,0:T(8,128)(2,1)S(1)}, u32[]{:S(2)}, u32[]{:S(2)}) collective-permute-start(bf16[256,1664]{1,0:T(8,128)(2,1)S(1)} %shard_map.244.refs_0_), channel_id=1, source_target_pairs={{0,16},{4,20},{8,24},{12,28},{16,0},{20,4},{24,8},{28,12},{1,17},{... | collective-permute-start | bytes 2555912 | tf_op jit(solution)/shard_map/ppermute | solution.py:384
  83.8 28.1 %collective-permute-start.16 = (bf16[256,2048]{1,0:T(8,128)(2,1)S(1)}, bf16[256,2048]{1,0:T(8,128)(2,1)S(1)}, u32[]{:S(2)}, u32[]{:S(2)}) collective-permute-start(bf16[256,2048]{1,0:T(8,128)(2,1)S(1)} %bitcast.246), channel_id=1, source_target_pairs={{0,1},{1,2},{2,3},{3,0},{4,5},{5,6},{6,7},{7,4},{8,9},{9,10},{10,1... | collective-permute-start | bytes 3145736 | tf_op jit(solution)/shard_map/ppermute | solution.py:379
  88.9 42.5 %collective-permute-start.23 = (bf16[512,1664]{1,0:T(8,128)(2,1)S(1)}, bf16[512,1664]{1,0:T(8,128)(2,1)S(1)}, u32[]{:S(2)}, u32[]{:S(2)}) collective-permute-start(bf16[512,1664]{1,0:T(8,128)(2,1)S(1)} %shard_map.251.refs_2_), channel_id=1, source_target_pairs={{0,4},{4,0},{8,12},{12,8},{16,20},{20,16},{24,28},{28,24},{1,5},{5... | collective-permute-start | bytes 5111816 | tf_op jit(solution)/shard_map/ppermute | solution.py:384
  89.6 43.0 %collective-permute-start.22 = (bf16[512,1664]{1,0:T(8,128)(2,1)S(1)}, bf16[512,1664]{1,0:T(8,128)(2,1)S(1)}, u32[]{:S(2)}, u32[]{:S(2)}) collective-permute-start(bf16[512,1664]{1,0:T(8,128)(2,1)S(1)} %shard_map.250.refs_0_), channel_id=1, source_target_pairs={{0,4},{4,0},{8,12},{12,8},{16,20},{20,16},{24,28},{28,24},{1,5},{5... | collective-permute-start | bytes 5111816 | tf_op jit(solution)/shard_map/ppermute | solution.py:384
  104.0 24.3 %collective-permute-start.20 = (bf16[256,2048]{1,0:T(8,128)(2,1)S(1)}, bf16[256,2048]{1,0:T(8,128)(2,1)S(1)}, u32[]{:S(2)}, u32[]{:S(2)}) collective-permute-start(bf16[256,2048]{1,0:T(8,128)(2,1)S(1)} %shard_map.248.refs_0_), channel_id=1, source_target_pairs={{0,16},{4,20},{8,24},{12,28},{16,0},{20,4},{24,8},{28,12},{1,17},{... | collective-permute-start | bytes 3145736 | tf_op jit(solution)/shard_map/ppermute | solution.py:384
  104.5 25.3 %collective-permute-start.21 = (bf16[256,2048]{1,0:T(8,128)(2,1)S(1)}, bf16[256,2048]{1,0:T(8,128)(2,1)S(1)}, u32[]{:S(2)}, u32[]{:S(2)}) collective-permute-start(bf16[256,2048]{1,0:T(8,128)(2,1)S(1)} %shard_map.249.refs_2_), channel_id=1, source_target_pairs={{0,8},{4,12},{8,0},{12,4},{16,24},{20,28},{24,16},{28,20},{1,9},{5... | collective-permute-start | bytes 3145736 | tf_op jit(solution)/shard_map/ppermute | solution.py:384
  111.9 26.2 %collective-permute-start.19 = (bf16[256,2048]{1,0:T(8,128)(2,1)S(1)}, bf16[256,2048]{1,0:T(8,128)(2,1)}, u32[]{:S(2)}, u32[]{:S(2)}) collective-permute-start(bf16[256,2048]{1,0:T(8,128)(2,1)S(1)} %collective-permute-done.16.refs_1_), channel_id=1, source_target_pairs={{0,1},{1,2},{2,3},{3,0},{4,5},{5,6},{6,7},{7,4},{8,9},{9,10},{10,1... | collective-permute-start | bytes 3145736 | tf_op jit(solution)/shard_map/ppermute | solution.py:379
  129.3 29.2 %collective-permute-start.25 = (bf16[512,1024]{1,0:T(8,128)(2,1)}, bf16[512,1024]{1,0:T(8,128)(2,1)}, u32[]{:S(2)}, u32[]{:S(2)}) collective-permute-start(bf16[512,1024]{1,0:T(8,128)(2,1)} %shard_map.252.refs_0_), channel_id=1, source_target_pairs={{0,16},{4,20},{8,24},{12,28},{16,0},{20,4},{24,8},{28,12},{1,17},{... | collective-permute-start | bytes 3145736 | tf_op jit(solution)/shard_map/ppermute | solution.py:384
  130.8 27.7 %collective-permute-start.26 = (bf16[512,1024]{1,0:T(8,128)(2,1)}, bf16[512,1024]{1,0:T(8,128)(2,1)}, u32[]{:S(2)}, u32[]{:S(2)}) collective-permute-start(bf16[512,1024]{1,0:T(8,128)(2,1)} %shard_map.253.refs_2_), channel_id=1, source_target_pairs={{0,8},{4,12},{8,0},{12,4},{16,24},{20,28},{24,16},{28,20},{1,9},{5... | collective-permute-start | bytes 3145736 | tf_op jit(solution)/shard_map/ppermute | solution.py:384
  138.1 25.8 %collective-permute-start.24 = (bf16[256,2048]{1,0:T(8,128)(2,1)}, bf16[256,2048]{1,0:T(8,128)(2,1)}, u32[]{:S(2)}, u32[]{:S(2)}) collective-permute-start(bf16[256,2048]{1,0:T(8,128)(2,1)} %collective-permute-done.19.refs_2_), channel_id=1, source_target_pairs={{0,1},{1,2},{2,3},{3,0},{4,5},{5,6},{6,7},{7,4},{8,9},{9,10},{10,1... | collective-permute-start | bytes 3145736 | tf_op jit(solution)/shard_map/ppermute | solution.py:379
  142.4 40.3 %collective-permute-start.30 = (bf16[256,1024]{1,0:T(8,128)(2,1)S(1)}, bf16[256,1024]{1,0:T(8,128)(2,1)}, u32[]{:S(2)}, u32[]{:S(2)}) collective-permute-start(bf16[256,1024]{1,0:T(8,128)(2,1)S(1)} %shard_map.256.refs_0_), channel_id=1, source_target_pairs={{0,8},{4,12},{8,0},{12,4},{16,24},{20,28},{24,16},{28,20},{1,9},{5... | collective-permute-start | bytes 1572872 | tf_op jit(solution)/shard_map/ppermute | solution.py:384
  143.0 39.8 %collective-permute-start.32 = (bf16[256,1024]{1,0:T(8,128)(2,1)}, bf16[256,1024]{1,0:T(8,128)(2,1)}, u32[]{:S(2)}, u32[]{:S(2)}) collective-permute-start(bf16[256,1024]{1,0:T(8,128)(2,1)} %collective-permute-done.31.refs_0_), channel_id=1, source_target_pairs={{0,16},{4,20},{8,24},{12,28},{16,0},{20,4},{24,8},{28,12},{1,17},{... | collective-permute-start | bytes 1572872 | tf_op jit(solution)/shard_map/ppermute | solution.py:384
  184.9 27.7 %collective-permute-start.37 = (bf16[512,1024]{1,0:T(8,128)(2,1)}, bf16[512,1024]{1,0:T(8,128)(2,1)}, u32[]{:S(2)}, u32[]{:S(2)}) collective-permute-start(bf16[512,1024]{1,0:T(8,128)(2,1)} %shard_map.262.refs_2_), channel_id=1, source_target_pairs={{0,8},{4,12},{8,0},{12,4},{16,24},{20,28},{24,16},{28,20},{1,9},{5... | collective-permute-start | bytes 3145736 | tf_op jit(solution)/shard_map/ppermute | solution.py:384
  187.6 25.0 %collective-permute-start.36 = (bf16[512,1024]{1,0:T(8,128)(2,1)}, bf16[512,1024]{1,0:T(8,128)(2,1)}, u32[]{:S(2)}, u32[]{:S(2)}) collective-permute-start(bf16[512,1024]{1,0:T(8,128)(2,1)} %shard_map.261.refs_0_), channel_id=1, source_target_pairs={{0,16},{4,20},{8,24},{12,28},{16,0},{20,4},{24,8},{28,12},{1,17},{... | collective-permute-start | bytes 3145736 | tf_op jit(solution)/shard_map/ppermute | solution.py:384
  188.1 24.4 %collective-permute-start.33 = (bf16[64,2048]{1,0:T(8,128)(2,1)S(1)}, bf16[64,2048]{1,0:T(8,128)(2,1)}, u32[]{:S(2)}, u32[]{:S(2)}) collective-permute-start(bf16[64,2048]{1,0:T(8,128)(2,1)S(1)} %copy-done.71), channel_id=1, source_target_pairs={{0,1},{1,2},{2,3},{3,0},{4,5},{5,6},{6,7},{7,4},{8,9},{9,10},{10,1... | collective-permute-start | bytes 786440 | tf_op jit(solution)/shard_map/ppermute | solution.py:408
  190.2 22.4 %collective-permute-start.34 = (bf16[64,2048]{1,0:T(8,128)(2,1)S(1)}, bf16[64,2048]{1,0:T(8,128)(2,1)}, u32[]{:S(2)}, u32[]{:S(2)}) collective-permute-start(bf16[64,2048]{1,0:T(8,128)(2,1)S(1)} %copy-done.71), channel_id=1, source_target_pairs={{0,2},{1,3},{2,0},{3,1},{4,6},{5,7},{6,4},{7,5},{8,10},{9,11},{10,... | collective-permute-start | bytes 786440 | tf_op jit(solution)/shard_map/ppermute | solution.py:408
  192.0 20.6 %collective-permute-start.35 = (bf16[64,2048]{1,0:T(8,128)(2,1)S(1)}, bf16[64,2048]{1,0:T(8,128)(2,1)}, u32[]{:S(2)}, u32[]{:S(2)}) collective-permute-start(bf16[64,2048]{1,0:T(8,128)(2,1)S(1)} %copy-done.71), channel_id=1, source_target_pairs={{0,3},{1,0},{2,1},{3,2},{4,7},{5,4},{6,5},{7,6},{8,11},{9,8},{10,9... | collective-permute-start | bytes 786440 | tf_op jit(solution)/shard_map/ppermute | solution.py:408
  225.7 21.5 %collective-permute-start.44 = (bf16[256,2048]{1,0:T(8,128)(2,1)S(1)}, bf16[256,2048]{1,0:T(8,128)(2,1)S(1)}, u32[]{:S(2)}, u32[]{:S(2)}) collective-permute-start(bf16[256,2048]{1,0:T(8,128)(2,1)S(1)} %shard_map.265.refs_0_), channel_id=1, source_target_pairs={{0,8},{4,12},{8,0},{12,4},{16,24},{20,28},{24,16},{28,20},{1,9},{5... | collective-permute-start | bytes 3145736 | tf_op jit(solution)/shard_map/ppermute | solution.py:384
  261.0 28.8 %collective-permute-start.47 = (bf16[256,2048]{1,0:T(8,128)(2,1)S(1)}, bf16[256,2048]{1,0:T(8,128)(2,1)S(1)}, u32[]{:S(2)}, u32[]{:S(2)}) collective-permute-start(bf16[256,2048]{1,0:T(8,128)(2,1)S(1)} %fusion.14.refs_0_), channel_id=1, source_target_pairs={{0,1},{1,2},{2,3},{3,0},{4,5},{5,6},{6,7},{7,4},{8,9},{9,10},{10,1... | collective-permute-start | bytes 3145736 | tf_op jit(solution)/shard_map/ppermute | solution.py:379
  289.8 27.5 %collective-permute-start.50 = (bf16[256,2048]{1,0:T(8,128)(2,1)S(1)}, bf16[256,2048]{1,0:T(8,128)(2,1)S(1)}, u32[]{:S(2)}, u32[]{:S(2)}) collective-permute-start(bf16[256,2048]{1,0:T(8,128)(2,1)S(1)} %collective-permute-done.47.refs_0_), channel_id=1, source_target_pairs={{0,1},{1,2},{2,3},{3,0},{4,5},{5,6},{6,7},{7,4},{8,9},{9,10},{10,1... | collective-permute-start | bytes 3145736 | tf_op jit(solution)/shard_map/ppermute | solution.py:379
  320.5 27.8 %collective-permute-start.52 = (bf16[256,2048]{1,0:T(8,128)(2,1)S(1)}, bf16[256,2048]{1,0:T(8,128)(2,1)S(1)}, u32[]{:S(2)}, u32[]{:S(2)}) collective-permute-start(bf16[256,2048]{1,0:T(8,128)(2,1)S(1)} %collective-permute-done.50.refs_0_), channel_id=1, source_target_pairs={{0,1},{1,2},{2,3},{3,0},{4,5},{5,6},{6,7},{7,4},{8,9},{9,10},{10,1... | collective-permute-start | bytes 3145736 | tf_op jit(solution)/shard_map/ppermute | solution.py:379
  320.5 49.7 %collective-permute-start.55 = (bf16[256,2048]{1,0:T(8,128)(2,1)S(1)}, bf16[256,2048]{1,0:T(8,128)(2,1)S(1)}, u32[]{:S(2)}, u32[]{:S(2)}) collective-permute-start(bf16[256,2048]{1,0:T(8,128)(2,1)S(1)} %add_convert_fusion.7), channel_id=1, source_target_pairs={{0,1},{1,2},{2,3},{3,0},{4,5},{5,6},{6,7},{7,4},{8,9},{9,10},{10,1... | collective-permute-start | bytes 3145736 | tf_op jit(solution)/shard_map/ppermute | solution.py:379
  373.6 27.5 %collective-permute-start.59 = (bf16[256,2048]{1,0:T(8,128)(2,1)S(1)}, bf16[256,2048]{1,0:T(8,128)(2,1)S(1)}, u32[]{:S(2)}, u32[]{:S(2)}) collective-permute-start(bf16[256,2048]{1,0:T(8,128)(2,1)S(1)} %add_convert_fusion.6), channel_id=1, source_target_pairs={{0,1},{1,2},{2,3},{3,0},{4,5},{5,6},{6,7},{7,4},{8,9},{9,10},{10,1... | collective-permute-start | bytes 3145736 | tf_op jit(solution)/shard_map/ppermute | solution.py:379
  401.7 26.5 %collective-permute-start.60 = (bf16[256,2048]{1,0:T(8,128)(2,1)S(1)}, bf16[256,2048]{1,0:T(8,128)(2,1)S(1)}, u32[]{:S(2)}, u32[]{:S(2)}) collective-permute-start(bf16[256,2048]{1,0:T(8,128)(2,1)S(1)} %fusion.8), channel_id=1, source_target_pairs={{0,1},{1,2},{2,3},{3,0},{4,5},{5,6},{6,7},{7,4},{8,9},{9,10},{10,1... | collective-permute-start | bytes 3145736 | tf_op jit(solution)/shard_map/ppermute | solution.py:379
  401.7 26.4 %collective-permute-start.49 = (bf16[256,2048]{1,0:T(8,128)(2,1)}, bf16[256,2048]{1,0:T(8,128)(2,1)S(1)}, u32[]{:S(2)}, u32[]{:S(2)}) collective-permute-start(bf16[256,2048]{1,0:T(8,128)(2,1)} %slice.193), channel_id=1, source_target_pairs={{0,4},{4,0},{8,12},{12,8},{16,20},{20,16},{24,28},{28,24},{1,5},{5... | collective-permute-start | bytes 3145736 | tf_op jit(solution)/shard_map/ppermute | solution.py:384
  430.1 27.7 %collective-permute-start.61 = (bf16[256,2048]{1,0:T(8,128)(2,1)S(1)}, bf16[256,2048]{1,0:T(8,128)(2,1)S(1)}, u32[]{:S(2)}, u32[]{:S(2)}) collective-permute-start(bf16[256,2048]{1,0:T(8,128)(2,1)S(1)} %fusion.3.refs_0_), channel_id=1, source_target_pairs={{0,1},{1,2},{2,3},{3,0},{4,5},{5,6},{6,7},{7,4},{8,9},{9,10},{10,1... | collective-permute-start | bytes 3145736 | tf_op jit(solution)/shard_map/ppermute | solution.py:379
  457.8 27.9 %collective-permute-start.64 = (bf16[256,2048]{1,0:T(8,128)(2,1)S(1)}, bf16[256,2048]{1,0:T(8,128)(2,1)S(1)}, u32[]{:S(2)}, u32[]{:S(2)}) collective-permute-start(bf16[256,2048]{1,0:T(8,128)(2,1)S(1)} %collective-permute-done.61.refs_0_), channel_id=1, source_target_pairs={{0,1},{1,2},{2,3},{3,0},{4,5},{5,6},{6,7},{7,4},{8,9},{9,10},{10,1... | collective-permute-start | bytes 3145736 | tf_op jit(solution)/shard_map/ppermute | solution.py:379
  488.8 27.8 %collective-permute-start.66 = (bf16[256,2048]{1,0:T(8,128)(2,1)S(1)}, bf16[256,2048]{1,0:T(8,128)(2,1)S(1)}, u32[]{:S(2)}, u32[]{:S(2)}) collective-permute-start(bf16[256,2048]{1,0:T(8,128)(2,1)S(1)} %collective-permute-done.64.refs_0_), channel_id=1, source_target_pairs={{0,1},{1,2},{2,3},{3,0},{4,5},{5,6},{6,7},{7,4},{8,9},{9,10},{10,1... | collective-permute-start | bytes 3145736 | tf_op jit(solution)/shard_map/ppermute | solution.py:379
  488.8 49.7 %collective-permute-start.69 = (bf16[256,2048]{1,0:T(8,128)(2,1)S(1)}, bf16[256,2048]{1,0:T(8,128)(2,1)S(1)}, u32[]{:S(2)}, u32[]{:S(2)}) collective-permute-start(bf16[256,2048]{1,0:T(8,128)(2,1)S(1)} %add_convert_fusion.4), channel_id=1, source_target_pairs={{0,1},{1,2},{2,3},{3,0},{4,5},{5,6},{6,7},{7,4},{8,9},{9,10},{10,1... | collective-permute-start | bytes 3145736 | tf_op jit(solution)/shard_map/ppermute | solution.py:379
  541.9 27.2 %collective-permute-start.73 = (bf16[256,2048]{1,0:T(8,128)(2,1)S(1)}, bf16[256,2048]{1,0:T(8,128)(2,1)S(1)}, u32[]{:S(2)}, u32[]{:S(2)}) collective-permute-start(bf16[256,2048]{1,0:T(8,128)(2,1)S(1)} %add_convert_fusion.3), channel_id=1, source_target_pairs={{0,1},{1,2},{2,3},{3,0},{4,5},{5,6},{6,7},{7,4},{8,9},{9,10},{10,1... | collective-permute-start | bytes 3145736 | tf_op jit(solution)/shard_map/ppermute | solution.py:379
  571.2 26.8 %collective-permute-start.74 = (bf16[256,2048]{1,0:T(8,128)(2,1)S(1)}, bf16[256,2048]{1,0:T(8,128)(2,1)}, u32[]{:S(2)}, u32[]{:S(2)}) collective-permute-start(bf16[256,2048]{1,0:T(8,128)(2,1)S(1)} %add_convert_fusion.2), channel_id=1, source_target_pairs={{0,1},{1,2},{2,3},{3,0},{4,5},{5,6},{6,7},{7,4},{8,9},{9,10},{10,1... | collective-permute-start | bytes 3145736 | tf_op jit(solution)/shard_map/ppermute | solution.py:379
  571.5 31.0 %collective-permute-start.63 = (bf16[256,2048]{1,0:T(8,128)(2,1)}, bf16[256,2048]{1,0:T(8,128)(2,1)}, u32[]{:S(2)}, u32[]{:S(2)}) collective-permute-start(bf16[256,2048]{1,0:T(8,128)(2,1)} %slice.189), channel_id=1, source_target_pairs={{0,4},{4,0},{8,12},{12,8},{16,20},{20,16},{24,28},{28,24},{1,5},{5... | collective-permute-start | bytes 3145736 | tf_op jit(solution)/shard_map/ppermute | solution.py:384
  599.0 23.9 %collective-permute-start.75 = (bf16[2,512,512]{2,1,0:T(8,128)(2,1)}, bf16[2,512,512]{2,1,0:T(8,128)(2,1)S(1)}, u32[]{:S(2)}, u32[]{:S(2)}) collective-permute-start(bf16[2,512,512]{2,1,0:T(8,128)(2,1)} %dynamic-slice_bitcast_fusion.7), channel_id=1, source_target_pairs={{0,8},{4,12},{8,0},{12,4},{16,24},{20,28},{24,16},{28,20},{1,9},{5... | collective-permute-start | bytes 3145736 | tf_op jit(solution)/shard_map/ppermute | solution.py:384
  600.9 23.6 %collective-permute-start.76 = (bf16[2,512,512]{2,1,0:T(8,128)(2,1)}, bf16[2,512,512]{2,1,0:T(8,128)(2,1)S(1)}, u32[]{:S(2)}, u32[]{:S(2)}) collective-permute-start(bf16[2,512,512]{2,1,0:T(8,128)(2,1)} %dynamic-slice_bitcast_fusion.6), channel_id=1, source_target_pairs={{0,16},{4,20},{8,24},{12,28},{16,0},{20,4},{24,8},{28,12},{1,17},{... | collective-permute-start | bytes 3145736 | tf_op jit(solution)/shard_map/ppermute | solution.py:384
  628.0 25.1 %collective-permute-start.81 = (bf16[512,512]{1,0:T(8,128)(2,1)}, bf16[512,512]{1,0:T(8,128)(2,1)}, u32[]{:S(2)}, u32[]{:S(2)}) collective-permute-start(bf16[512,512]{1,0:T(8,128)(2,1)} %fusion.25), channel_id=1, source_target_pairs={{0,8},{4,12},{8,0},{12,4},{16,24},{20,28},{24,16},{28,20},{1,9},{5... | collective-permute-start | bytes 1572872 | tf_op jit(solution)/shard_map/ppermute | solution.py:384
  629.6 23.4 %collective-permute-start.80 = (bf16[512,512]{1,0:T(8,128)(2,1)S(1)}, bf16[512,512]{1,0:T(8,128)(2,1)S(1)}, u32[]{:S(2)}, u32[]{:S(2)}) collective-permute-start(bf16[512,512]{1,0:T(8,128)(2,1)S(1)} %fusion.24), channel_id=1, source_target_pairs={{0,16},{4,20},{8,24},{12,28},{16,0},{20,4},{24,8},{28,12},{1,17},{... | collective-permute-start | bytes 1572872 | tf_op jit(solution)/shard_map/ppermute | solution.py:384
  630.5 22.6 %collective-permute-start.77 = (bf16[256,512]{1,0:T(8,128)(2,1)S(1)}, bf16[256,512]{1,0:T(8,128)(2,1)S(1)}, u32[]{:S(2)}, u32[]{:S(2)}) collective-permute-start(bf16[256,512]{1,0:T(8,128)(2,1)S(1)} %get-tuple-element.418), channel_id=1, source_target_pairs={{0,1},{1,2},{2,3},{3,0},{4,5},{5,6},{6,7},{7,4},{8,9},{9,10},{10,1... | collective-permute-start | bytes 786440 | tf_op jit(solution)/shard_map/ppermute | solution.py:401
  630.5 22.6 %collective-permute-start.78 = (bf16[256,512]{1,0:T(8,128)(2,1)S(1)}, bf16[256,512]{1,0:T(8,128)(2,1)S(1)}, u32[]{:S(2)}, u32[]{:S(2)}) collective-permute-start(bf16[256,512]{1,0:T(8,128)(2,1)S(1)} %get-tuple-element.419), channel_id=1, source_target_pairs={{0,2},{1,3},{2,0},{3,1},{4,6},{5,7},{6,4},{7,5},{8,10},{9,11},{10,... | collective-permute-start | bytes 786440 | tf_op jit(solution)/shard_map/ppermute | solution.py:401
  630.5 22.6 %collective-permute-start.79 = (bf16[256,512]{1,0:T(8,128)(2,1)S(1)}, bf16[256,512]{1,0:T(8,128)(2,1)S(1)}, u32[]{:S(2)}, u32[]{:S(2)}) collective-permute-start(bf16[256,512]{1,0:T(8,128)(2,1)S(1)} %get-tuple-element.420), channel_id=1, source_target_pairs={{0,3},{1,0},{2,1},{3,2},{4,7},{5,4},{6,5},{7,6},{8,11},{9,8},{10,9... | collective-permute-start | bytes 786440 | tf_op jit(solution)/shard_map/ppermute | solution.py:401
  655.4 32.3 %collective-permute-start.86 = (bf16[2,512,512]{2,1,0:T(8,128)(2,1)}, bf16[2,512,512]{2,1,0:T(8,128)(2,1)S(1)}, u32[]{:S(2)}, u32[]{:S(2)}) collective-permute-start(bf16[2,512,512]{2,1,0:T(8,128)(2,1)} %dynamic-slice_bitcast_fusion.5), channel_id=1, source_target_pairs={{0,8},{4,12},{8,0},{12,4},{16,24},{20,28},{24,16},{28,20},{1,9},{5... | collective-permute-start | bytes 3145736 | tf_op jit(solution)/shard_map/ppermute | solution.py:384
  658.1 29.5 %collective-permute-start.87 = (bf16[2,512,512]{2,1,0:T(8,128)(2,1)}, bf16[2,512,512]{2,1,0:T(8,128)(2,1)}, u32[]{:S(2)}, u32[]{:S(2)}) collective-permute-start(bf16[2,512,512]{2,1,0:T(8,128)(2,1)} %dynamic-slice_bitcast_fusion.4), channel_id=1, source_target_pairs={{0,16},{4,20},{8,24},{12,28},{16,0},{20,4},{24,8},{28,12},{1,17},{... | collective-permute-start | bytes 3145736 | tf_op jit(solution)/shard_map/ppermute | solution.py:384
  660.8 26.7 %collective-permute-start.83 = (bf16[128,1024]{1,0:T(8,128)(2,1)S(1)}, bf16[128,1024]{1,0:T(8,128)(2,1)S(1)}, u32[]{:S(2)}, u32[]{:S(2)}) collective-permute-start(bf16[128,1024]{1,0:T(8,128)(2,1)S(1)} %get-tuple-element.437), channel_id=1, source_target_pairs={{0,1},{1,2},{2,3},{3,0},{4,5},{5,6},{6,7},{7,4},{8,9},{9,10},{10,1... | collective-permute-start | bytes 786440 | tf_op jit(solution)/shard_map/ppermute | solution.py:401
  661.9 25.7 %collective-permute-start.84 = (bf16[128,1024]{1,0:T(8,128)(2,1)S(1)}, bf16[128,1024]{1,0:T(8,128)(2,1)S(1)}, u32[]{:S(2)}, u32[]{:S(2)}) collective-permute-start(bf16[128,1024]{1,0:T(8,128)(2,1)S(1)} %get-tuple-element.438), channel_id=1, source_target_pairs={{0,2},{1,3},{2,0},{3,1},{4,6},{5,7},{6,4},{7,5},{8,10},{9,11},{10,... | collective-permute-start | bytes 786440 | tf_op jit(solution)/shard_map/ppermute | solution.py:401
  663.0 24.6 %collective-permute-start.85 = (bf16[128,1024]{1,0:T(8,128)(2,1)S(1)}, bf16[128,1024]{1,0:T(8,128)(2,1)S(1)}, u32[]{:S(2)}, u32[]{:S(2)}) collective-permute-start(bf16[128,1024]{1,0:T(8,128)(2,1)S(1)} %get-tuple-element.439), channel_id=1, source_target_pairs={{0,3},{1,0},{2,1},{3,2},{4,7},{5,4},{6,5},{7,6},{8,11},{9,8},{10,9... | collective-permute-start | bytes 786440 | tf_op jit(solution)/shard_map/ppermute | solution.py:401
  710.1 27.7 %collective-permute-start.93 = (bf16[2,2,256,1024]{3,2,0,1:T(8,128)(2,1)}, bf16[2,2,256,1024]{3,2,0,1:T(8,128)(2,1)}, u32[]{:S(2)}, u32[]{:S(2)}) collective-permute-start(bf16[2,2,256,1024]{3,2,0,1:T(8,128)(2,1)} %copy_bitcast_fusion), channel_id=1, source_target_pairs={{0,4},{4,0},{8,12},{12,8},{16,20},{20,16},{24,28},{28,24},{1,5},{5... | collective-permute-start | bytes 6291464 | tf_op jit(solution)/shard_map/ppermute | solution.py:384
  711.6 26.2 %collective-permute-start.94 = (bf16[2,2,256,1024]{3,2,1,0:T(8,128)(2,1)}, bf16[2,2,256,1024]{3,2,1,0:T(8,128)(2,1)}, u32[]{:S(2)}, u32[]{:S(2)}) collective-permute-start(bf16[2,2,256,1024]{3,2,1,0:T(8,128)(2,1)} %dynamic-slice_bitcast_fusion), channel_id=1, source_target_pairs={{0,4},{4,0},{8,12},{12,8},{16,20},{20,16},{24,28},{28,24},{1,5},{5... | collective-permute-start | bytes 6291464 | tf_op jit(solution)/shard_map/ppermute | solution.py:384
  735.2 19.7 %collective-permute-start.97 = (bf16[128,1024]{1,0:T(8,128)(2,1)S(1)}, bf16[128,1024]{1,0:T(8,128)(2,1)S(1)}, u32[]{:S(2)}, u32[]{:S(2)}) collective-permute-start(bf16[128,1024]{1,0:T(8,128)(2,1)S(1)} %get-tuple-element.468), channel_id=1, source_target_pairs={{0,2},{1,3},{2,0},{3,1},{4,6},{5,7},{6,4},{7,5},{8,10},{9,11},{10,... | collective-permute-start | bytes 786440 | tf_op jit(solution)/shard_map/ppermute | solution.py:401
  754.9 25.2 %collective-permute-start.100 = (bf16[2,256,1024]{2,1,0:T(8,128)(2,1)}, bf16[2,256,1024]{2,1,0:T(8,128)(2,1)S(1)}, u32[]{:S(2)}, u32[]{:S(2)}) collective-permute-start(bf16[2,256,1024]{2,1,0:T(8,128)(2,1)} %fusion.16), channel_id=1, source_target_pairs={{0,8},{4,12},{8,0},{12,4},{16,24},{20,28},{24,16},{28,20},{1,9},{5... | collective-permute-start | bytes 3145736 | tf_op jit(solution)/shard_map/ppermute | solution.py:384
  756.6 24.9 %collective-permute-start.101 = (bf16[2,256,1024]{2,1,0:T(8,128)(2,1)}, bf16[2,256,1024]{2,1,0:T(8,128)(2,1)S(1)}, u32[]{:S(2)}, u32[]{:S(2)}) collective-permute-start(bf16[2,256,1024]{2,1,0:T(8,128)(2,1)} %fusion.17), channel_id=1, source_target_pairs={{0,16},{4,20},{8,24},{12,28},{16,0},{20,4},{24,8},{28,12},{1,17},{... | collective-permute-start | bytes 3145736 | tf_op jit(solution)/shard_map/ppermute | solution.py:384
  757.2 28.9 %collective-permute-start.99 = (bf16[256,2048]{1,0:T(8,128)(2,1)}, bf16[256,2048]{1,0:T(8,128)(2,1)S(1)}, u32[]{:S(2)}, u32[]{:S(2)}) collective-permute-start(bf16[256,2048]{1,0:T(8,128)(2,1)} %convolution_convert_fusion), channel_id=1, source_target_pairs={{0,1},{1,2},{2,3},{3,0},{4,5},{5,6},{6,7},{7,4},{8,9},{9,10},{10,1... | collective-permute-start | bytes 3145736 | tf_op jit(solution)/shard_map/ppermute | solution.py:379
  793.8 23.4 %collective-permute-start.104 = (bf16[256,1024]{1,0:T(8,128)(2,1)}, bf16[256,1024]{1,0:T(8,128)(2,1)}, u32[]{:S(2)}, u32[]{:S(2)}) collective-permute-start(bf16[256,1024]{1,0:T(8,128)(2,1)} %fusion.29), channel_id=1, source_target_pairs={{0,8},{4,12},{8,0},{12,4},{16,24},{20,28},{24,16},{28,20},{1,9},{5... | collective-permute-start | bytes 1572872 | tf_op jit(solution)/shard_map/ppermute | solution.py:384
  799.1 31.7 %collective-permute-start.105 = (bf16[2,2,256,768]{3,2,0,1:T(8,128)(2,1)}, bf16[2,2,256,768]{3,2,0,1:T(8,128)(2,1)}, u32[]{:S(2)}, u32[]{:S(2)}) collective-permute-start(bf16[2,2,256,768]{3,2,0,1:T(8,128)(2,1)} %copy_bitcast_fusion.1), channel_id=1, source_target_pairs={{0,4},{4,0},{8,12},{12,8},{16,20},{20,16},{24,28},{28,24},{1,5},{5... | collective-permute-start | bytes 4718600 | tf_op jit(solution)/shard_map/ppermute | solution.py:384
  801.6 29.1 %collective-permute-start.106 = (bf16[2,2,256,768]{3,2,1,0:T(8,128)(2,1)}, bf16[2,2,256,768]{3,2,1,0:T(8,128)(2,1)}, u32[]{:S(2)}, u32[]{:S(2)}) collective-permute-start(bf16[2,2,256,768]{3,2,1,0:T(8,128)(2,1)} %dynamic-slice_bitcast_fusion.1), channel_id=1, source_target_pairs={{0,4},{4,0},{8,12},{12,8},{16,20},{20,16},{24,28},{28,24},{1,5},{5... | collective-permute-start | bytes 4718600 | tf_op jit(solution)/shard_map/ppermute | solution.py:384
  803.6 27.2 %collective-permute-start.102 = (bf16[256,2048]{1,0:T(8,128)(2,1)}, bf16[256,2048]{1,0:T(8,128)(2,1)}, u32[]{:S(2)}, u32[]{:S(2)}) collective-permute-start(bf16[256,2048]{1,0:T(8,128)(2,1)} %add_convert_fusion.1), channel_id=1, source_target_pairs={{0,1},{1,2},{2,3},{3,0},{4,5},{5,6},{6,7},{7,4},{8,9},{9,10},{10,1... | collective-permute-start | bytes 3145736 | tf_op jit(solution)/shard_map/ppermute | solution.py:379
  834.0 29.0 %collective-permute-start.109 = (bf16[2,256,768]{2,1,0:T(8,128)(2,1)}, bf16[2,256,768]{2,1,0:T(8,128)(2,1)}, u32[]{:S(2)}, u32[]{:S(2)}) collective-permute-start(bf16[2,256,768]{2,1,0:T(8,128)(2,1)} %fusion.23), channel_id=1, source_target_pairs={{0,16},{4,20},{8,24},{12,28},{16,0},{20,4},{24,8},{28,12},{1,17},{... | collective-permute-start | bytes 2359304 | tf_op jit(solution)/shard_map/ppermute | solution.py:384
  837.7 25.3 %collective-permute-start.108 = (bf16[2,256,768]{2,1,0:T(8,128)(2,1)}, bf16[2,256,768]{2,1,0:T(8,128)(2,1)}, u32[]{:S(2)}, u32[]{:S(2)}) collective-permute-start(bf16[2,256,768]{2,1,0:T(8,128)(2,1)} %fusion.22), channel_id=1, source_target_pairs={{0,8},{4,12},{8,0},{12,4},{16,24},{20,28},{24,16},{28,20},{1,9},{5... | collective-permute-start | bytes 2359304 | tf_op jit(solution)/shard_map/ppermute | solution.py:384
  841.1 25.7 %collective-permute-start.107 = (bf16[256,2048]{1,0:T(8,128)(2,1)S(1)}, bf16[256,2048]{1,0:T(8,128)(2,1)S(1)}, u32[]{:S(2)}, u32[]{:S(2)}) collective-permute-start(bf16[256,2048]{1,0:T(8,128)(2,1)S(1)} %add_convert_fusion), channel_id=1, source_target_pairs={{0,1},{1,2},{2,3},{3,0},{4,5},{5,6},{6,7},{7,4},{8,9},{9,10},{10,1... | collective-permute-start | bytes 3145736 | tf_op jit(solution)/shard_map/ppermute | solution.py:379
  881.8 23.1 %collective-permute-start.124 = (bf16[2,256,1024]{2,1,0:T(8,128)(2,1)}, bf16[2,256,1024]{2,1,0:T(8,128)(2,1)}, u32[]{:S(2)}, u32[]{:S(2)}) collective-permute-start(bf16[2,256,1024]{2,1,0:T(8,128)(2,1)} %dynamic-slice_bitcast_fusion.3), channel_id=1, source_target_pairs={{0,8},{4,12},{8,0},{12,4},{16,24},{20,28},{24,16},{28,20},{1,9},{5... | collective-permute-start | bytes 3145736 | tf_op jit(solution)/shard_map/ppermute | solution.py:384
  885.0 23.0 %collective-permute-start.126 = (bf16[2,256,1024]{2,1,0:T(8,128)(2,1)S(1)}, bf16[2,256,1024]{2,1,0:T(8,128)(2,1)S(1)}, u32[]{:S(2)}, u32[]{:S(2)}) collective-permute-start(bf16[2,256,1024]{2,1,0:T(8,128)(2,1)S(1)} %dynamic-slice_bitcast_fusion.2), channel_id=1, source_target_pairs={{0,16},{4,20},{8,24},{12,28},{16,0},{20,4},{24,8},{28,12},{1,17},{... | collective-permute-start | bytes 3145736 | tf_op jit(solution)/shard_map/ppermute | solution.py:384
  (214 other events, 1565.5 us)
